TPU v7x, 32 devices: a whole 2x2x4 slice. The times are simulated.
32 devices in a mesh: dp: 4 (over y, x), seq: 8 (over z, core).
Axes of the slice: x: 2, y: 2, z: 4, core: 2. Of those that a mesh axis runs over, the one named last changes fastest.
Arguments:
- tokens: bfloat16 [4, 1024, 768], P('dp', 'seq'), may hold values from -6 to 6
- tie_index: int32 [4], P('dp'), may hold values from 0 to 1, as said below
- first_gain: bfloat16 [2, 768], P(None, ('dp', 'seq')), may hold values from 0.25 to 1.75
- first_shift: bfloat16 [2, 768], P(None, ('dp', 'seq')), may hold values from -4 to 4
- qkv_weight: bfloat16 [2, 768, 2304], P(None, ('dp', 'seq')), may hold values from -0.21875 to 0.21875
- qv_bias: bfloat16 [2, 1536], P(None, ('dp', 'seq')), may hold values from -6 to 6
- out_weight: bfloat16 [2, 768, 768], P(None, ('dp', 'seq')), may hold values from -3 to 3
- out_bias: bfloat16 [2, 768], P(None, ('dp', 'seq')), may hold values from -4 to 4
- second_gain: bfloat16 [2, 768], P(None, ('dp', 'seq')), may hold values from 0.25 to 1.75
- second_shift: bfloat16 [2, 768], P(None, ('dp', 'seq')), may hold values from -4 to 4
- fc_weight: bfloat16 [2, 768, 3072], P(None, ('dp', 'seq')), may hold values from -0.21875 to 0.21875
- fc_bias: bfloat16 [2, 3072], P(None, ('dp', 'seq')), may hold values from -6 to 6
- proj_weight: bfloat16 [2, 3072, 768], P(None, ('dp', 'seq')), may hold values from -0.109375 to 0.109375
- proj_bias: bfloat16 [2, 768], P(None, ('dp', 'seq')), may hold values from -4 to 4
- cotangent: bfloat16 [4, 1024, 768], P('dp', 'seq'), may hold values from -6 to 6
Outputs:
- layer_out: bfloat16 [4, 1024, 768], P('dp', 'seq')
- input_grad: bfloat16 [4, 1024, 768], P('dp', 'seq')
- grad_first_gain: float32 [2, 768], P(None, ('dp', 'seq'))
- grad_first_shift: float32 [2, 768], P(None, ('dp', 'seq'))
- grad_qkv_weight: float32 [2, 768, 2304], P(None, ('dp', 'seq'))
- grad_qv_bias: float32 [2, 1536], P(None, ('dp', 'seq'))
- grad_out_weight: float32 [2, 768, 768], P(None, ('dp', 'seq'))
- grad_out_bias: float32 [2, 768], P(None, ('dp', 'seq'))
- grad_second_gain: float32 [2, 768], P(None, ('dp', 'seq'))
- grad_second_shift: float32 [2, 768], P(None, ('dp', 'seq'))
- grad_fc_weight: float32 [2, 768, 3072], P(None, ('dp', 'seq'))
- grad_fc_bias: float32 [2, 3072], P(None, ('dp', 'seq'))
- grad_proj_weight: float32 [2, 3072, 768], P(None, ('dp', 'seq'))
- grad_proj_bias: float32 [2, 768], P(None, ('dp', 'seq'))
Inputs may be any that keep to these rules, and one draw needn't show every extreme that they name: `tie_index`: each of the 2 shared blocks is picked by exactly 2 sequences.
All inputs are finite; a program needn't handle non-finite values.
Results may differ from a plain program's by a relative error of at most 0.017.
Values may be sent and summed in bfloat16 or wider, within the bound.
No kernel may reach another device: no remote copies, remote signals or barrier semaphores. Data moves between devices by JAX's collectives and lax.ppermute only.
A program may use at most 384 MiB of HBM per device.

v0:
```python
import math

import jax
import jax.numpy as jnp
from jax import lax
from jax.sharding import PartitionSpec as P

HEADS = 12
HEAD_DIM = 64
BLOCK = 256


epsilon = 1e-05
neg_large = -1e30


def norm_apply(values, norm_gain, norm_shift):
    row_mean = jnp.mean(values, -1, keepdims=True)
    centred = values - row_mean
    row_var = jnp.mean(centred * centred, -1, keepdims=True)
    return centred * lax.rsqrt(row_var + epsilon) * norm_gain + norm_shift


def gelu_tanh(values):
    return jax.nn.gelu(values, approximate=True)


def select_all(gathered, chosen):
    return tuple(
        (lax.dynamic_index_in_dim(stacked, chosen, 0, keepdims=False) for stacked in gathered)
    )


def add_block(totals, update, chosen):
    current = lax.dynamic_index_in_dim(totals, chosen, 0, keepdims=True)
    return lax.dynamic_update_index_in_dim(totals, current + update[None], chosen, 0)


def split_three(values):
    upper_part = values.astype(jnp.bfloat16)
    rest_one = values - lax.optimization_barrier(upper_part).astype(jnp.float32)
    middle_part = rest_one.astype(jnp.bfloat16)
    lower_part = (rest_one - lax.optimization_barrier(middle_part).astype(jnp.float32)).astype(
        jnp.bfloat16
    )
    return (upper_part, middle_part, lower_part)


def to_heads(flat_rows, head_count):
    return flat_rows.reshape(
        flat_rows.shape[0], flat_rows.shape[1], head_count, flat_rows.shape[2] // head_count
    )


def allowed_mask(query_pos, key_pos, block_len):
    return (key_pos[None, :] // block_len <= query_pos[:, None] // block_len)[None, :, None, :]


def make_forward_step(query_heads, positions, block_len, score_scale):
    last_block = positions[-1] // block_len
    head_count = query_heads.shape[2]

    def fold_step(carried, shard_piece, start_row):
        key_piece, value_piece = shard_piece
        key_count = key_piece.shape[1]
        step_len = math.gcd(key_count, 512)

        def one_part(fold_state, offset):
            key_heads = to_heads(
                lax.dynamic_slice_in_dim(key_piece, offset, step_len, 1), head_count
            )
            value_heads = to_heads(
                lax.dynamic_slice_in_dim(value_piece, offset, step_len, 1), head_count
            )
            key_pos = offset + jnp.arange(step_len, dtype=jnp.int32)

            def update(state_in):
                top_old, total_old, sum_old = state_in
                scores = (
                    jnp.einsum(
                        "sqhe,skhe->sqhk",
                        query_heads,
                        key_heads,
                        preferred_element_type=jnp.float32,
                    )
                    * score_scale
                )
                allowed = allowed_mask(positions, key_pos, block_len)
                top_new = jnp.maximum(top_old, jnp.max(jnp.where(allowed, scores, neg_large), -1))
                exp_scores = jnp.where(allowed, jnp.exp(scores - top_new[..., None]), 0.0)
                rescale = jnp.exp(top_old - top_new)
                total_new = total_old * rescale + jnp.sum(exp_scores, -1)
                sum_new = sum_old * rescale[..., None] + jnp.einsum(
                    "sqhk,skhe->sqhe",
                    exp_scores.astype(jnp.bfloat16),
                    value_heads,
                    preferred_element_type=jnp.float32,
                )
                return (top_new, total_new, sum_new)

            return (
                lax.cond(
                    offset // block_len <= last_block, update, lambda state_in: state_in, fold_state
                ),
                None,
            )

        offsets = jnp.arange(key_count // step_len, dtype=jnp.int32) * step_len
        return lax.scan(one_part, carried, offsets)[0]

    return fold_step


def make_query_step(
    query_heads, grad_heads, log_total, delta_rows, positions, block_len, score_scale
):
    last_block = positions[-1] // block_len
    head_count = query_heads.shape[2]

    def fold_step(carried, shard_piece, start_row):
        key_piece, value_piece = shard_piece
        key_count = key_piece.shape[1]
        step_len = math.gcd(key_count, 512)

        def one_part(fold_state, offset):
            key_heads = to_heads(
                lax.dynamic_slice_in_dim(key_piece, offset, step_len, 1), head_count
            )
            value_heads = to_heads(
                lax.dynamic_slice_in_dim(value_piece, offset, step_len, 1), head_count
            )
            key_pos = offset + jnp.arange(step_len, dtype=jnp.int32)

            def update(state_in):
                scores = (
                    jnp.einsum(
                        "sqhe,skhe->sqhk",
                        query_heads,
                        key_heads,
                        preferred_element_type=jnp.float32,
                    )
                    * score_scale
                )
                allowed = allowed_mask(positions, key_pos, block_len)
                probs_all = jnp.where(allowed, jnp.exp(scores - log_total[..., None]), 0.0)
                grad_probs = jnp.einsum(
                    "sqhe,skhe->sqhk", grad_heads, value_heads, preferred_element_type=jnp.float32
                )
                grad_scores = (probs_all * (grad_probs - delta_rows[..., None])).astype(
                    jnp.bfloat16
                )
                return state_in + jnp.einsum(
                    "sqhk,skhe->sqhe", grad_scores, key_heads, preferred_element_type=jnp.float32
                )

            return (
                lax.cond(
                    offset // block_len <= last_block, update, lambda state_in: state_in, fold_state
                ),
                None,
            )

        offsets = jnp.arange(key_count // step_len, dtype=jnp.int32) * step_len
        return lax.scan(one_part, carried, offsets)[0]

    return fold_step


def make_key_step(key_heads, value_heads, positions, block_len, score_scale):
    first_block = positions[0] // block_len
    head_count = key_heads.shape[2]

    def fold_step(carried, shard_piece, start_row):
        query_piece, grad_piece, stats_piece = shard_piece
        seq_count, query_count, model_width = query_piece.shape
        step_len = math.gcd(query_count, 512)

        def one_part(fold_state, offset):
            query_part = to_heads(
                lax.dynamic_slice_in_dim(query_piece, offset, step_len, 1), head_count
            )
            grad_part = to_heads(
                lax.dynamic_slice_in_dim(grad_piece, offset, step_len, 1), head_count
            )
            stats_part = lax.dynamic_slice_in_dim(stats_piece, offset, step_len, 1).astype(
                jnp.float32
            )
            stats_part = stats_part.reshape(seq_count, step_len, 6, head_count)
            log_total = stats_part[:, :, 0] + stats_part[:, :, 1] + stats_part[:, :, 2]
            delta_rows = stats_part[:, :, 3] + stats_part[:, :, 4] + stats_part[:, :, 5]
            query_pos = offset + jnp.arange(step_len, dtype=jnp.int32)

            def update(state_in):
                key_grad, value_grad = state_in
                scores = (
                    jnp.einsum(
                        "sqhe,skhe->sqhk", query_part, key_heads, preferred_element_type=jnp.float32
                    )
                    * score_scale
                )
                allowed = allowed_mask(query_pos, positions, block_len)
                probs_all = jnp.where(allowed, jnp.exp(scores - log_total[..., None]), 0.0)
                grad_probs = jnp.einsum(
                    "sqhe,skhe->sqhk", grad_part, value_heads, preferred_element_type=jnp.float32
                )
                grad_scores = (probs_all * (grad_probs - delta_rows[..., None])).astype(
                    jnp.bfloat16
                )
                value_grad = value_grad + jnp.einsum(
                    "sqhk,sqhe->skhe",
                    probs_all.astype(jnp.bfloat16),
                    grad_part,
                    preferred_element_type=jnp.float32,
                )
                key_grad = key_grad + jnp.einsum(
                    "sqhk,sqhe->skhe", grad_scores, query_part, preferred_element_type=jnp.float32
                )
                return (key_grad, value_grad)

            last_query = (offset + step_len - 1) // block_len
            return (
                lax.cond(last_query >= first_block, update, lambda state_in: state_in, fold_state),
                None,
            )

        offsets = jnp.arange(query_count // step_len, dtype=jnp.int32) * step_len
        return lax.scan(one_part, carried, offsets)[0]

    return fold_step


def per_device(
    tokens,
    tie_index,
    first_gain,
    first_shift,
    qkv_weight,
    qv_bias,
    out_weight,
    out_bias,
    second_gain,
    second_shift,
    fc_weight,
    fc_bias,
    proj_weight,
    proj_bias,
    cotangent,
):
    gathered = (
        lax.all_gather(first_gain, ("dp", "seq"), axis=1, tiled=True),
        lax.all_gather(first_shift, ("dp", "seq"), axis=1, tiled=True),
        lax.all_gather(qkv_weight, ("dp", "seq"), axis=1, tiled=True),
        lax.all_gather(qv_bias, ("dp", "seq"), axis=1, tiled=True),
        lax.all_gather(out_weight, ("dp", "seq"), axis=1, tiled=True),
        lax.all_gather(out_bias, ("dp", "seq"), axis=1, tiled=True),
        lax.all_gather(second_gain, ("dp", "seq"), axis=1, tiled=True),
        lax.all_gather(second_shift, ("dp", "seq"), axis=1, tiled=True),
        lax.all_gather(fc_weight, ("dp", "seq"), axis=1, tiled=True),
        lax.all_gather(fc_bias, ("dp", "seq"), axis=1, tiled=True),
        lax.all_gather(proj_weight, ("dp", "seq"), axis=1, tiled=True),
        lax.all_gather(proj_bias, ("dp", "seq"), axis=1, tiled=True),
    )
    seq_count, tok_count, model_width = tokens.shape
    head_count = HEADS
    block_len = BLOCK
    score_scale = 1.0 / math.sqrt(HEAD_DIM)
    positions = lax.axis_index("seq") * tok_count + jnp.arange(tok_count, dtype=jnp.int32)
    member = 0
    gain_one, shift_one, w_qkv, bias_qv = select_all(gathered[0:4], tie_index[member])
    inputs = tokens[member].astype(jnp.float32)
    normed = norm_apply(inputs, gain_one, shift_one).astype(jnp.bfloat16)
    qkv_rows = jnp.dot(normed, w_qkv, preferred_element_type=jnp.float32)
    normed_list = [normed]
    query_list = [(qkv_rows[:, :model_width] + bias_qv[:model_width]).astype(jnp.bfloat16)]
    key_list = [qkv_rows[:, model_width : 2 * model_width].astype(jnp.bfloat16)]
    value_list = [(qkv_rows[:, 2 * model_width :] + bias_qv[model_width:]).astype(jnp.bfloat16)]
    query_all = jnp.stack(query_list)
    key_all = jnp.stack(key_list)
    value_all = jnp.stack(value_list)
    query_heads = to_heads(query_all, head_count)
    head_dim = query_heads.shape[3]
    stat_shape = (seq_count, tok_count, head_count)
    start_state = (
        jnp.full(stat_shape, neg_large, jnp.float32),
        jnp.zeros(stat_shape, jnp.float32),
        jnp.zeros(stat_shape + (head_dim,), jnp.float32),
    )
    forward_step = make_forward_step(query_heads, positions, block_len, score_scale)
    top_score, total_weight, weighted_sum = forward_step(
        start_state,
        (
            lax.all_gather(key_all, "seq", axis=1, tiled=True),
            lax.all_gather(value_all, "seq", axis=1, tiled=True),
        ),
        jnp.int32(0),
    )
    attn_heads = weighted_sum / total_weight[..., None]
    log_total = top_score + jnp.log(total_weight)
    attended = attn_heads.reshape(seq_count, tok_count, model_width).astype(jnp.bfloat16)
    member = 0
    w_out, bias_out, gain_two, shift_two, w_fc, bias_fc, w_proj, bias_proj = select_all(
        gathered[4:12], tie_index[member]
    )
    inputs = tokens[member].astype(jnp.float32)
    middle = (
        inputs + jnp.dot(attended[member], w_out, preferred_element_type=jnp.float32) + bias_out
    )
    normed_two = norm_apply(middle, gain_two, shift_two).astype(jnp.bfloat16)
    hidden_pre = jnp.dot(normed_two, w_fc, preferred_element_type=jnp.float32) + bias_fc
    hidden = gelu_tanh(hidden_pre).astype(jnp.bfloat16)
    layer_rows = [
        (middle + jnp.dot(hidden, w_proj, preferred_element_type=jnp.float32) + bias_proj).astype(
            jnp.bfloat16
        )
    ]
    saved_mlp = [(middle, normed_two, hidden_pre, hidden)]
    layer_out = jnp.stack(layer_rows)
    whole_back = (
        lax.all_gather(first_gain, ("dp", "seq"), axis=1, tiled=True),
        lax.all_gather(first_shift, ("dp", "seq"), axis=1, tiled=True),
        lax.all_gather(qkv_weight, ("dp", "seq"), axis=1, tiled=True),
        lax.all_gather(qv_bias, ("dp", "seq"), axis=1, tiled=True),
        lax.all_gather(out_weight, ("dp", "seq"), axis=1, tiled=True),
        lax.all_gather(out_bias, ("dp", "seq"), axis=1, tiled=True),
        lax.all_gather(second_gain, ("dp", "seq"), axis=1, tiled=True),
        lax.all_gather(second_shift, ("dp", "seq"), axis=1, tiled=True),
        lax.all_gather(fc_weight, ("dp", "seq"), axis=1, tiled=True),
        lax.all_gather(fc_bias, ("dp", "seq"), axis=1, tiled=True),
        lax.all_gather(proj_weight, ("dp", "seq"), axis=1, tiled=True),
        lax.all_gather(proj_bias, ("dp", "seq"), axis=1, tiled=True),
    )
    grad_totals = [jnp.zeros(stacked.shape, jnp.float32) for stacked in whole_back]
    member = 0
    chosen = tie_index[member]
    w_out, bias_out, gain_two, shift_two, w_fc, bias_fc, w_proj, bias_proj = select_all(
        whole_back[4:12], chosen
    )
    middle, normed_two, hidden_pre, hidden = saved_mlp[member]
    upstream = cotangent[member].astype(jnp.float32)
    upstream_low = upstream.astype(jnp.bfloat16)
    grad_hidden = jnp.einsum("td,fd->tf", upstream_low, w_proj, preferred_element_type=jnp.float32)
    gelu_pull = jax.vjp(gelu_tanh, hidden_pre)[1]
    grad_pre = gelu_pull(grad_hidden)[0].astype(jnp.bfloat16)
    grad_normed = jnp.einsum("tf,df->td", grad_pre, w_fc, preferred_element_type=jnp.float32)
    norm_pull = jax.vjp(
        norm_apply, middle, gain_two.astype(jnp.float32), shift_two.astype(jnp.float32)
    )[1]
    grad_middle, grad_gain, grad_shift = norm_pull(grad_normed)
    grad_middle = grad_middle + upstream
    middle_low = grad_middle.astype(jnp.bfloat16)
    attn_grads = [
        jnp.einsum("te,de->td", middle_low, w_out, preferred_element_type=jnp.float32).astype(
            jnp.bfloat16
        )
    ]
    middle_grads = [grad_middle]
    updates = (
        jnp.einsum("td,te->de", attended[member], middle_low, preferred_element_type=jnp.float32),
        jnp.sum(grad_middle, 0),
        grad_gain,
        grad_shift,
        jnp.einsum("td,tf->df", normed_two, grad_pre, preferred_element_type=jnp.float32),
        jnp.sum(grad_pre.astype(jnp.float32), 0),
        jnp.einsum("tf,td->fd", hidden, upstream_low, preferred_element_type=jnp.float32),
        jnp.sum(upstream, 0),
    )
    for slot_index, update in enumerate(updates):
        grad_totals[4 + slot_index] = add_block(grad_totals[4 + slot_index], update, chosen)
    grad_attn_all = jnp.stack(attn_grads)
    grad_heads = to_heads(grad_attn_all, head_count)
    delta_rows = jnp.sum(grad_heads.astype(jnp.float32) * attn_heads, -1)
    query_step = make_query_step(
        query_heads, grad_heads, log_total, delta_rows, positions, block_len, score_scale
    )
    zero_heads = jnp.zeros(stat_shape + (head_dim,), jnp.float32)
    grad_query = query_step(
        zero_heads,
        (
            lax.all_gather(key_all, "seq", axis=1, tiled=True),
            lax.all_gather(value_all, "seq", axis=1, tiled=True),
        ),
        jnp.int32(0),
    )
    row_stats = jnp.stack(split_three(log_total) + split_three(delta_rows), 2).reshape(
        seq_count, tok_count, 6 * head_count
    )
    key_step = make_key_step(
        to_heads(key_all, head_count),
        to_heads(value_all, head_count),
        positions,
        block_len,
        score_scale,
    )
    grad_key, grad_value = key_step(
        (zero_heads, zero_heads),
        (
            lax.all_gather(query_all, "seq", axis=1, tiled=True),
            lax.all_gather(grad_attn_all, "seq", axis=1, tiled=True),
            lax.all_gather(row_stats, "seq", axis=1, tiled=True),
        ),
        jnp.int32(0),
    )
    flat_shape = (seq_count, tok_count, model_width)
    grad_query = (grad_query * score_scale).reshape(flat_shape).astype(jnp.bfloat16)
    grad_key = (grad_key * score_scale).reshape(flat_shape).astype(jnp.bfloat16)
    grad_value = grad_value.reshape(flat_shape).astype(jnp.bfloat16)
    member = 0
    chosen = tie_index[member]
    gain_one, shift_one, w_qkv, bias_qv = select_all(whole_back[0:4], chosen)
    grad_mixed = jnp.concatenate([grad_query[member], grad_key[member], grad_value[member]], 1)
    grad_normed = jnp.einsum("te,de->td", grad_mixed, w_qkv, preferred_element_type=jnp.float32)
    norm_pull = jax.vjp(
        norm_apply,
        tokens[member].astype(jnp.float32),
        gain_one.astype(jnp.float32),
        shift_one.astype(jnp.float32),
    )[1]
    grad_inputs, grad_gain, grad_shift = norm_pull(grad_normed)
    input_rows = [(grad_inputs + middle_grads[member]).astype(jnp.bfloat16)]
    updates = (
        grad_gain,
        grad_shift,
        jnp.einsum(
            "td,te->de", normed_list[member], grad_mixed, preferred_element_type=jnp.float32
        ),
        jnp.concatenate(
            [
                jnp.sum(grad_query[member].astype(jnp.float32), 0),
                jnp.sum(grad_value[member].astype(jnp.float32), 0),
            ]
        ),
    )
    for slot_index, update in enumerate(updates):
        grad_totals[slot_index] = add_block(grad_totals[slot_index], update, chosen)
    input_grad = jnp.stack(input_rows)
    shard_grads = tuple(
        (
            lax.psum_scatter(grad_totals[0], ("dp", "seq"), scatter_dimension=1, tiled=True),
            lax.psum_scatter(grad_totals[1], ("dp", "seq"), scatter_dimension=1, tiled=True),
            lax.psum_scatter(grad_totals[2], ("dp", "seq"), scatter_dimension=1, tiled=True),
            lax.psum_scatter(grad_totals[3], ("dp", "seq"), scatter_dimension=1, tiled=True),
            lax.psum_scatter(grad_totals[4], ("dp", "seq"), scatter_dimension=1, tiled=True),
            lax.psum_scatter(grad_totals[5], ("dp", "seq"), scatter_dimension=1, tiled=True),
            lax.psum_scatter(grad_totals[6], ("dp", "seq"), scatter_dimension=1, tiled=True),
            lax.psum_scatter(grad_totals[7], ("dp", "seq"), scatter_dimension=1, tiled=True),
            lax.psum_scatter(grad_totals[8], ("dp", "seq"), scatter_dimension=1, tiled=True),
            lax.psum_scatter(grad_totals[9], ("dp", "seq"), scatter_dimension=1, tiled=True),
            lax.psum_scatter(grad_totals[10], ("dp", "seq"), scatter_dimension=1, tiled=True),
            lax.psum_scatter(grad_totals[11], ("dp", "seq"), scatter_dimension=1, tiled=True),
        )
    )
    return (layer_out, input_grad) + shard_grads


def solution(mesh):
    in_specs = (
        P("dp", "seq", None),
        P("dp"),
        P(None, ("dp", "seq")),
        P(None, ("dp", "seq")),
        P(None, ("dp", "seq"), None),
        P(None, ("dp", "seq")),
        P(None, ("dp", "seq"), None),
        P(None, ("dp", "seq")),
        P(None, ("dp", "seq")),
        P(None, ("dp", "seq")),
        P(None, ("dp", "seq"), None),
        P(None, ("dp", "seq")),
        P(None, ("dp", "seq"), None),
        P(None, ("dp", "seq")),
        P("dp", "seq", None),
    )
    out_specs = (
        P("dp", "seq", None),
        P("dp", "seq", None),
        P(None, ("dp", "seq")),
        P(None, ("dp", "seq")),
        P(None, ("dp", "seq"), None),
        P(None, ("dp", "seq")),
        P(None, ("dp", "seq"), None),
        P(None, ("dp", "seq")),
        P(None, ("dp", "seq")),
        P(None, ("dp", "seq")),
        P(None, ("dp", "seq"), None),
        P(None, ("dp", "seq")),
        P(None, ("dp", "seq"), None),
        P(None, ("dp", "seq")),
    )
    return jax.shard_map(
        per_device, mesh=mesh, in_specs=in_specs, out_specs=out_specs, check_vma=False
    )
```

profile of v0, /device:TPU:0, one launch (start us, length us, event | category | flops | bytes accessed | tf_op | source)
XLA Modules:
  0.0 1401.1 jit_solution(10741595637575591213)
XLA Ops:
  8.6 43.2 %all-gather.4 = bf16[32,24,2]{1,2,0:T(2,128)(2,1)S(1)} all-gather(bf16[1,24,2]{1,2,0:T(2,128)(2,1)} %bitcast.477), channel_id=1, replica_groups=mesh['dp'=4,'seq'=8] {'dp','seq'}, dimensions={0}, use_global_device_ids=true | all-gather | bytes 3168 | tf_op jit(solution)/shard_map/all_gather | solution.py:250
  52.0 36.9 %all-gather.5 = bf16[32,24,2]{1,2,0:T(2,128)(2,1)S(1)} all-gather(bf16[1,24,2]{1,2,0:T(2,128)(2,1)} %bitcast.478), channel_id=1, replica_groups=mesh['dp'=4,'seq'=8] {'dp','seq'}, dimensions={0}, use_global_device_ids=true | all-gather | bytes 3168 | tf_op jit(solution)/shard_map/all_gather | solution.py:251
  88.9 38.0 %all-gather.6 = bf16[32,48,2]{1,2,0:T(2,128)(2,1)S(1)} all-gather(bf16[1,48,2]{1,2,0:T(2,128)(2,1)} %bitcast.479), channel_id=1, replica_groups=mesh['dp'=4,'seq'=8] {'dp','seq'}, dimensions={0}, use_global_device_ids=true | all-gather | bytes 6336 | tf_op jit(solution)/shard_map/all_gather | solution.py:253
  129.4 2.8 fusion.107
  138.8 36.5 %all-gather.7 = bf16[32,24,2]{1,2,0:T(2,128)(2,1)S(1)} all-gather(bf16[1,24,2]{1,2,0:T(2,128)(2,1)S(1)} %bitcast.480), channel_id=1, replica_groups=mesh['dp'=4,'seq'=8] {'dp','seq'}, dimensions={0}, use_global_device_ids=true | all-gather | bytes 3168 | tf_op jit(solution)/shard_map/all_gather | solution.py:255
  175.4 38.0 %all-gather.8 = bf16[32,24,2]{1,2,0:T(2,128)(2,1)S(1)} all-gather(bf16[1,24,2]{1,2,0:T(2,128)(2,1)S(1)} %bitcast.481), channel_id=1, replica_groups=mesh['dp'=4,'seq'=8] {'dp','seq'}, dimensions={0}, use_global_device_ids=true | all-gather | bytes 3168 | tf_op jit(solution)/shard_map/all_gather | solution.py:256
  213.5 36.5 %all-gather.9 = bf16[32,24,2]{1,2,0:T(2,128)(2,1)S(1)} all-gather(bf16[1,24,2]{1,2,0:T(2,128)(2,1)S(1)} %bitcast.482), channel_id=1, replica_groups=mesh['dp'=4,'seq'=8] {'dp','seq'}, dimensions={0}, use_global_device_ids=true | all-gather | bytes 3168 | tf_op jit(solution)/shard_map/all_gather | solution.py:257
  250.1 38.0 %all-gather.10 = bf16[32,96,2]{1,2,0:T(2,128)(2,1)S(1)} all-gather(bf16[1,96,2]{1,2,0:T(2,128)(2,1)S(1)} %bitcast.483), channel_id=1, replica_groups=mesh['dp'=4,'seq'=8] {'dp','seq'}, dimensions={0}, use_global_device_ids=true | all-gather | bytes 12672 | tf_op jit(solution)/shard_map/all_gather | solution.py:259
  289.2 2.6 copy.91
  291.8 2.8 copy.90
  294.7 14.7 %while.51 = (s32[]{:T(128)}, f32[1,128,12]{1,2,0:T(8,128)S(1)}, f32[1,128,12]{1,2,0:T(8,128)S(1)}, f32[1,128,12,64]{1,3,2,0:T(8,128)S(1)}, s32[2]{0:T(128)}, /*i...) while((s32[]{:T(128)}, f32[1,128,12]{1,2,0:T(8,128)S(1)}, ...), condition=%wide.region_7.8_spmd.clone, body=%wide.region_2.7_spmd.clone.sunk | while | flops 210254352 | bytes 15510010 | solution.py:109
  294.7 1.3 dynamic_slice.242
  298.6 6.8 conditional.9
  300.8 2.3 constant_dynamic-slice_fusion
  305.4 1.2 dynamic_slice.242
  309.5 1.8 fusion.213
  311.5 14.1 %all-gather.25.cloned.1.call-done = bf16[2,768,3072]{2,1,0:T(8,128)(2,1)} async-done(((bf16[2,24,3072]{2,1,0:T(8,128)(2,1)}), bf16[2,768,3072]{2,1,0:T(8,128)(2,1)}) %all-gather.25.cloned.1.call-update) | async-done | bytes 9437200 | tf_op jit(solution)/shard_map/all_gather | solution.py:258
  325.6 3.2 fusion.99
  328.8 80.6 %all-gather.27.cloned.1.call-done = bf16[2,3072,768]{2,1,0:T(8,128)(2,1)} async-done(((bf16[2,96,768]{2,1,0:T(8,128)(2,1)}), bf16[2,3072,768]{2,1,0:T(8,128)(2,1)}) %all-gather.27.cloned.1.call-update) | async-done | bytes 9437200 | tf_op jit(solution)/shard_map/all_gather | solution.py:260
  409.4 5.0 convert_reduce_fusion
  414.5 2.3 multiply_reduce_fusion
  417.2 1.3 fusion.130
  423.0 12.4 all-gather.33.cloned.1.call-done
  435.4 2.6 copy.103
  442.6 18.8 %while.52 = (s32[]{:T(128)}, f32[1,128,12,64]{1,3,2,0:T(8,128)}, s32[2]{0:T(128)}, s32[]{:T(128)}, bf16[1,1024,768]{1,2,0:T(8,128)(2,1)}, /*index=5*/bf16[1,128,...) while((s32[]{:T(128)}, f32[1,128,12,64]{1,3,2,0:T(8,128)}, ...), condition=%wide.region_16.17_spmd.clone, body=%wide.region_13.16_spmd.clone.sunk | while | flops 306882592 | bytes 16275958 | solution.py:164
  442.6 1.3 dynamic_slice.243
  446.4 11.1 conditional.10
  449.1 3.1 constant_dynamic-slice_fusion.2
  453.8 3.8 fusion.40
  457.6 1.3 dynamic_slice.243
  461.5 1.7 convert_reduce_fusion.4
  467.2 1.7 copy.119
  468.9 24.0 %all_gather.73 = bf16[1,1024,72]{1,2,0:T(8,128)(2,1)} all-gather(bf16[1,128,72]{1,2,0:T(8,128)(2,1)S(1)} %reshape.677), channel_id=1, replica_groups=mesh['dp'=4,'seq'=8] {'seq'}, dimensions={1}, use_global_device_ids=true | all-gather | bytes 165888 | tf_op jit(solution)/shard_map/all_gather | solution.py:399
  493.0 2.6 copy.104
  497.2 36.6 %while.53 = (s32[]{:T(128)}, f32[1,128,12,64]{1,3,2,0:T(8,128)}, f32[1,128,12,64]{1,3,2,0:T(8,128)}, s32[2]{0:T(128)}, s32[]{:T(128)}, /*index=5*/bf16[1,1024,72...) while((s32[]{:T(128)}, f32[1,128,12,64]{1,3,2,0:T(8,128)}, ...), condition=%wide.region_20.21_spmd.clone, body=%wide.region_17.20_spmd.clone.sunk | while | flops 410851360 | bytes 22571612 | solution.py:227
  497.2 1.3 dynamic_slice.245
  502.2 13.4 conditional.11
  503.2 3.1 constant_dynamic-slice_fusion.4
  507.9 4.6 fusion.74
  512.5 3.1 fusion.71
  520.6 13.2 conditional.11
  521.6 3.0 constant_dynamic-slice_fusion.4
  526.1 4.6 fusion.74
  530.8 3.1 fusion.71
  535.2 1.3 copy.111
  536.6 2.5 broadcast_in_dim.168
  539.1 2.0 bitcast_dynamic-update-slice_fusion.3
  542.5 5.9 broadcast_in_dim.164
  548.4 4.1 bitcast_dynamic-update-slice_fusion.2
  552.7 7.7 broadcast_in_dim.175
  560.4 5.2 bitcast_dynamic-update-slice_fusion
  565.7 8.8 broadcast_in_dim.171
  574.6 5.1 bitcast_dynamic-update-slice_fusion.1
  580.3 36.8 %all-gather.11 = bf16[32,24,2]{1,2,0:T(2,128)(2,1)S(1)} all-gather(bf16[1,24,2]{1,2,0:T(2,128)(2,1)S(1)} %bitcast.484), channel_id=1, replica_groups=mesh['dp'=4,'seq'=8] {'dp','seq'}, dimensions={0}, use_global_device_ids=true | all-gather | bytes 3168 | tf_op jit(solution)/shard_map/all_gather | solution.py:261
  617.5 4.2 fusion.136
  621.7 1.4 copy.120
  623.2 3.6 fusion.208
  628.3 39.9 %all-reduce.6 = (f32[2,768]{1,0:T(2,128)S(1)}, f32[2,768]{1,0:T(2,128)S(1)}, f32[2,768]{1,0:T(2,128)S(1)}, f32[2,768]{1,0:T(2,128)S(1)}, f32[2,768]{1,0:T(2,128)S(1)}, /*index=5*/f32[2,768]{1,0:T(2,128)S(1)}) all-reduce(f32[2,768]{1,0:T(2,128)S(1)} %dynamic_update_slice.43, ...), channel_id=6, replica_groups=mesh['dp'=4,'seq'=8] {'dp','seq'}, use_global_device_ids=true, to_apply=%region_24.25.clone | all-reduce | flops 9216 | bytes 73728
  672.0 16.5 %reduce-scatter.25.cloned.1.call-done = f32[48,2]{1,0:T(8,128)} async-done(((f32[1536,2]{1,0:T(8,128)}), f32[48,2]{1,0:T(8,128)}) %reduce-scatter.25.cloned.1.call-update) | async-done | bytes 400
  688.5 1.4 copy.112
  689.8 110.8 %reduce-scatter.19.cloned.1.call-done = f32[2,24,768]{2,1,0:T(8,128)} async-done(((f32[2,768,768]{2,1,0:T(8,128)}), f32[2,24,768]{2,1,0:T(8,128)}) %reduce-scatter.19.cloned.1.call-update) | async-done | bytes 147472 | tf_op jit(solution)/shard_map/reduce_scatter | solution.py:442
  800.7 169.5 %reduce-scatter.17.cloned.1.call-done = f32[2,24,2304]{2,1,0:T(8,128)} async-done(((f32[2,768,2304]{2,1,0:T(8,128)}), f32[2,24,2304]{2,1,0:T(8,128)}) %reduce-scatter.17.cloned.1.call-update) | async-done | bytes 442384 | tf_op jit(solution)/shard_map/reduce_scatter | solution.py:440
  970.2 211.9 %reduce-scatter.23.cloned.1.call-done = f32[2,96,768]{2,1,0:T(8,128)} async-done(((f32[2,3072,768]{2,1,0:T(8,128)}), f32[2,96,768]{2,1,0:T(8,128)}) %reduce-scatter.23.cloned.1.call-update) | async-done | bytes 589840 | tf_op jit(solution)/shard_map/reduce_scatter | solution.py:448
  1182.1 212.0 %reduce-scatter.21.cloned.1.call-done = f32[2,24,3072]{2,1,0:T(8,128)} async-done(((f32[2,768,3072]{2,1,0:T(8,128)}), f32[2,24,3072]{2,1,0:T(8,128)}) %reduce-scatter.21.cloned.1.call-update) | async-done | bytes 589840 | tf_op jit(solution)/shard_map/reduce_scatter | solution.py:446
  (292 shorter events, 45.1 us)
Async XLA Ops:
  7.2 122.2 %all-gather.21.cloned.1.call-start = ((), (), s32[]{:S(2)}) async-start(), calls=%async_computation.6 | async-start | bytes 7299072 | tf_op jit(solution)/shard_map/all_gather | solution.py:252
  7.9 281.3 %all-gather.31.cloned.1.call-start = ((), (), s32[]{:S(2)}) async-start(), calls=%async_computation.15 | async-start | bytes 1769472 | tf_op jit(solution)/shard_map/all_gather | solution.py:293
  127.1 5.1 copy-start.29
  128.2 4.0 copy-start.34
  129.3 2.9 copy-start.50
  129.3 2.9 copy-start.42
  132.2 6.6 copy-start.52
  132.2 43.2 %copy-start.53 = (bf16[2,24]{1,0:T(2,128)(2,1)S(1)}, bf16[2,24]{1,0:T(2,128)(2,1)}, u32[]{:S(2)}) copy-start(bf16[2,24]{1,0:T(2,128)(2,1)} %param.35) | copy-start | bytes 292
  132.3 81.2 %copy-start.54 = (bf16[2,24]{1,0:T(2,128)(2,1)S(1)}, bf16[2,24]{1,0:T(2,128)(2,1)}, u32[]{:S(2)}) copy-start(bf16[2,24]{1,0:T(2,128)(2,1)} %param.36) | copy-start | bytes 292
  132.3 117.8 %copy-start.55 = (bf16[2,96]{1,0:T(2,128)(2,1)S(1)}, bf16[2,96]{1,0:T(2,128)(2,1)}, u32[]{:S(2)}) copy-start(bf16[2,96]{1,0:T(2,128)(2,1)} %param.38) | copy-start | bytes 1156
  133.0 155.9 %copy-start.18 = (bf16[128,768]{1,0:T(8,128)(2,1)}, bf16[128,768]{1,0:T(8,128)(2,1)S(1)}, u32[]{:S(2)}) copy-start(bf16[128,768]{1,0:T(8,128)(2,1)S(1)} %get-tuple-element.1284) | copy-start | bytes 589828
  133.0 158.8 %all-gather.29.cloned.1.call-start = ((), (), s32[]{:S(2)}) async-start(), calls=%async_computation.14 | async-start | bytes 1769472 | tf_op jit(solution)/shard_map/all_gather | solution.py:292
  133.8 175.6 %all-gather.23.cloned.1.call-start = ((), (), s32[]{:S(2)}) async-start(), calls=%async_computation.7 | async-start | bytes 2433024 | tf_op jit(solution)/shard_map/all_gather | solution.py:254
  134.4 191.2 %all-gather.25.cloned.1.call-start = ((), (), s32[]{:S(2)}) async-start(), calls=%async_computation.8 | async-start | bytes 9732096 | tf_op jit(solution)/shard_map/all_gather | solution.py:258
  135.0 274.5 %all-gather.27.cloned.1.call-start = ((), (), s32[]{:S(2)}) async-start(), calls=%async_computation.9 | async-start | bytes 9732096 | tf_op jit(solution)/shard_map/all_gather | solution.py:260
  135.6 299.8 %all-gather.33.cloned.1.call-start = ((), (), s32[]{:S(2)}) async-start(), calls=%async_computation.16 | async-start | bytes 1769472 | tf_op jit(solution)/shard_map/all_gather | solution.py:397
  288.2 37.3 %copy-start.27 = (f32[768]{0:T(1024)}, f32[768]{0:T(1024)S(1)}, u32[]{:S(2)}) copy-start(f32[768]{0:T(1024)S(1)} %get-tuple-element.1297) | copy-start | bytes 9220
  289.0 204.0 %all-gather.35.cloned.1.call-start = ((), (), s32[]{:S(2)}) async-start(), calls=%async_computation.17 | async-start | bytes 1769472 | tf_op jit(solution)/shard_map/all_gather | solution.py:398
  294.7 14.8 %copy-start.4 = (bf16[1,128,768]{2,1,0:T(8,128)(2,1)S(1)}, bf16[1,128,768]{2,1,0:T(8,128)(2,1)}, u32[]{:S(2)}) copy-start(bf16[1,128,768]{2,1,0:T(8,128)(2,1)} %param.27) | copy-start | bytes 589828
  309.4 16.1 %copy-start.16 = (bf16[1,128,12,64]{1,3,2,0:T(8,128)(2,1)}, bf16[1,128,12,64]{1,3,2,0:T(8,128)(2,1)S(1)}, u32[]{:S(2)}) copy-start(bf16[1,128,12,64]{1,3,2,0:T(8,128)(2,1)S(1)} %fusion.173) | copy-start | bytes 589828
  311.2 105.6 %copy-start.2 = (f32[128,768]{1,0:T(8,128)}, f32[128,768]{1,0:T(8,128)S(1)}, u32[]{:S(2)}) copy-start(f32[128,768]{1,0:T(8,128)S(1)} %get-tuple-element.1289) | copy-start | bytes 1179652
  311.2 105.6 %copy-start.37 = (f32[128]{0:T(128)}, f32[128]{0:T(128)S(1)}, u32[]{:S(2)}) copy-start(f32[128]{0:T(128)S(1)} %broadcast_multiply_fusion) | copy-start | bytes 1540
  311.4 105.4 %copy-start.45 = (f32[128]{0:T(128)}, f32[128]{0:T(128)S(1)}, u32[]{:S(2)}) copy-start(f32[128]{0:T(128)S(1)} %fusion.203) | copy-start | bytes 1540
  325.6 83.9 %copy-start.11 = (bf16[1,128,768]{2,1,0:T(8,128)(2,1)S(1)}, bf16[1,128,768]{2,1,0:T(8,128)(2,1)}, u32[]{:S(2)}) copy-start(bf16[1,128,768]{2,1,0:T(8,128)(2,1)} %param.41) | copy-start | bytes 589828
  328.8 85.7 %copy-start.6 = (f32[128,3072]{1,0:T(8,128)}, f32[128,3072]{1,0:T(8,128)S(1)}, u32[]{:S(2)}) copy-start(f32[128,3072]{1,0:T(8,128)S(1)} %fusion.99) | copy-start | bytes 4718596
  409.4 5.1 copy-start.5
  414.5 2.6 copy-start.15
  416.8 4.5 copy-start.19
  416.8 5.3 copy-start.20
  417.1 20.9 %copy-start.9 = (f32[128,768]{1,0:T(8,128)}, f32[128,768]{1,0:T(8,128)S(1)}, u32[]{:S(2)}) copy-start(f32[128,768]{1,0:T(8,128)S(1)} %get-tuple-element.1265) | copy-start | bytes 1179652
  417.1 20.8 %copy-start.47 = (f32[128]{0:T(128)}, f32[128]{0:T(128)S(1)}, u32[]{:S(2)}) copy-start(f32[128]{0:T(128)S(1)} %negate_multiply_fusion.1) | copy-start | bytes 1540
  418.4 21.6 %copy-start.21 = (bf16[128,768]{1,0:T(8,128)(2,1)S(1)}, bf16[128,768]{1,0:T(8,128)(2,1)}, u32[]{:S(2)}) copy-start(bf16[128,768]{1,0:T(8,128)(2,1)} %fusion.130) | copy-start | bytes 589828
  418.5 203.2 %reduce-scatter.27.cloned.1.call-start = ((), (), s32[]{:S(2)}) async-start(), calls=%async_computation.19 | async-start | bytes 1622016
  492.9 195.5 %reduce-scatter.25.cloned.1.call-start = ((), (), s32[]{:S(2)}) async-start(), calls=%async_computation.18 | async-start | bytes 811008
  497.2 37.9 %copy-start.41 = (f32[768]{0:T(1024)S(1)}, f32[768]{0:T(1024)}, u32[]{:S(2)}) copy-start(f32[768]{0:T(1024)} %reduce_sum.204) | copy-start | bytes 9220
  502.2 5.0 copy-start.8
  520.6 4.9 copy-start.8
  535.0 13.4 copy-start.24
  536.5 2.6 copy-start.10
  536.5 264.2 %reduce-scatter.19.cloned.1.call-start = ((), (), s32[]{:S(2)}) async-start(), calls=%async_computation.11 | async-start | bytes 4866048 | tf_op jit(solution)/shard_map/reduce_scatter | solution.py:442
  541.1 429.1 %reduce-scatter.17.cloned.1.call-start = ((), (), s32[]{:S(2)}) async-start(), calls=%async_computation.10 | async-start | bytes 14598144 | tf_op jit(solution)/shard_map/reduce_scatter | solution.py:440
  542.4 6.0 copy-start.26
  542.4 6.0 copy-start.22
  542.4 6.0 copy-start.30
  542.5 6.0 copy-start.35
  542.5 6.0 copy-start.43
  552.6 7.7 copy-start.7
  552.6 629.5 %reduce-scatter.23.cloned.1.call-start = ((), (), s32[]{:S(2)}) async-start(), calls=%async_computation.13 | async-start | bytes 19464192 | tf_op jit(solution)/shard_map/reduce_scatter | solution.py:448
  565.6 8.9 copy-start.3
  565.6 8.9 copy-start.14
  565.6 8.9 copy-start.28
  565.6 8.9 copy-start.38
  565.6 828.5 %reduce-scatter.21.cloned.1.call-start = ((), (), s32[]{:S(2)}) async-start(), calls=%async_computation.12 | async-start | bytes 19464192 | tf_op jit(solution)/shard_map/reduce_scatter | solution.py:446
  565.7 8.8 copy-start.46
  579.7 37.6 %copy-start.40 = (f32[768]{0:T(1024)S(1)}, f32[768]{0:T(1024)}, u32[]{:S(2)}) copy-start(f32[768]{0:T(1024)} %get-tuple-element.1175) | copy-start | bytes 9220
  579.7 37.6 %copy-start.39 = (f32[768]{0:T(1024)S(1)}, f32[768]{0:T(1024)}, u32[]{:S(2)}) copy-start(f32[768]{0:T(1024)} %get-tuple-element.1179) | copy-start | bytes 9220
  617.4 4.2 copy-start.32
  617.5 5.6 copy-start.23
  617.5 5.6 copy-start.25
  617.5 5.6 copy-start.36
  623.1 3.6 copy-start.51
  623.1 3.6 copy-start.44
  623.1 3.9 copy-start.49
  623.1 5.1 copy-start.33
  (9 other events, 16.0 us)
Sparse Core Ops, SparseCore 0:
  11.2 75.4 all-gather.20
  133.2 21.3 all-gather.30
  156.8 24.5 all-gather.28
  184.4 57.0 all-gather.22
  244.6 80.9 all-gather.24
  328.6 80.7 all-gather.26
  411.6 23.6 all-gather.32
  437.0 24.5 all-gather.34
  493.1 95.8 reduce-scatter.26
  594.0 94.4 reduce-scatter.24
  694.5 106.1 reduce-scatter.18
  808.1 162.0 reduce-scatter.16
  978.3 203.7 reduce-scatter.22
  1190.1 204.0 reduce-scatter.20
where the time goes:
time: 1410 us; the launch traced here: 1400 us
  waiting for transfers between devices  830 us (59%)
  blocking collectives  368 us (26%)
  local copies, waits for them, and re-layouts  79.7 us (6%)
  matrix products  63.4 us (4%)
  between operations  21.2 us (2%)
  other arithmetic  19 us (1%)
  loops' own time  18.5 us (1%)
    reduce_scatter x1, waiting for transfers between devices, per_device(): lax.psum_scatter(grad_totals[8], ('dp', 'seq'), scatter_dimension=1, tile...  212 us
    reduce_scatter x1, waiting for transfers between devices, per_device(): lax.psum_scatter(grad_totals[10], ('dp', 'seq'), scatter_dimension=1, til...  212 us
    reduce_scatter x1, waiting for transfers between devices, per_device(): lax.psum_scatter(grad_totals[2], ('dp', 'seq'), scatter_dimension=1, tile...  170 us
    reduce_scatter x1, waiting for transfers between devices, per_device(): lax.psum_scatter(grad_totals[4], ('dp', 'seq'), scatter_dimension=1, tile...  111 us
    all_gather x1, waiting for transfers between devices, per_device(): lax.all_gather(proj_weight, ('dp', 'seq'), axis=1, tiled=True)  80.6 us
    all_gather x1, blocking collectives, per_device(): lax.all_gather(first_gain, ('dp', 'seq'), axis=1, tiled=True)  43.2 us
    unnamed x1, blocking collectives  39.9 us
    all_gather x1, blocking collectives, per_device(): lax.all_gather(fc_bias, ('dp', 'seq'), axis=1, tiled=True)  38 us
  transfers between devices with their start and end apart: 14, of which 8 were waited for; matrix products, arithmetic and copies ran while one was open for 11% of the time, Pallas kernels for 0%

commit v1 on v0

v1 whole, which is shorter than its diff:
```python
import functools
import math

import jax
import jax.numpy as jnp
from jax import lax
from jax.experimental import pallas as pl
from jax.experimental.pallas import tpu as pltpu
from jax.sharding import PartitionSpec as P

HEADS = 12
HEAD_DIM = 64
BLOCK = 256

epsilon = 1e-05
bf16 = jnp.bfloat16
f32 = jnp.float32


def dot(a, b, ca, cb):
    return lax.dot_general(a, b, (((ca,), (cb,)), ((), ())), preferred_element_type=f32)


def norm_parts(values):
    row_mean = jnp.mean(values, -1, keepdims=True)
    centred = values - row_mean
    row_var = jnp.mean(centred * centred, -1, keepdims=True)
    scale = lax.rsqrt(row_var + epsilon)
    return centred * scale, scale


def norm_back(normal, scale, gain, grad):
    scaled = grad * gain
    return scale * (
        scaled
        - jnp.mean(scaled, -1, keepdims=True)
        - normal * jnp.mean(scaled * normal, -1, keepdims=True)
    )


def head_mask(rows, width, head):
    lane = lax.broadcasted_iota(jnp.int32, (rows, width), 1)
    return (lane >= head * HEAD_DIM) & (lane < (head + 1) * HEAD_DIM)


def attend_kernel(masked, rank_ref, q_ref, k_ref, v_ref, w_ref, *refs):
    bias_ref = refs[0] if masked else None
    a_ref, *out_refs = refs[1:] if masked else refs
    sums_ref = out_refs.pop()
    chunks, group, size, width = k_ref.shape
    for chunk in range(chunks):
        count = (chunk + 1) * group * size
        keys = k_ref[: chunk + 1].reshape(count, width)
        values = v_ref[: chunk + 1].reshape(count, width)
        values_t = values.T
        query = q_ref[chunk]
        parts = []
        for head in range(width // HEAD_DIM):
            part = jnp.where(head_mask(size, width, head), query, jnp.zeros_like(query))
            scores = dot(keys, part, 1, 1)
            if masked:
                early = count - group * size
                scores = jnp.concatenate([scores[:early], scores[early:] + bias_ref[...]], 0) if early else scores + bias_ref[...]
            top = jnp.max(scores, 0, keepdims=True)
            raised = jnp.exp(scores - top)
            total = jnp.sum(raised, 0, keepdims=True)
            mixed = dot(
                values_t[head * HEAD_DIM : (head + 1) * HEAD_DIM], raised.astype(bf16), 1, 0
            )
            parts.append(mixed / total)
        attended = jnp.concatenate(parts, 0).T.astype(bf16)
        a_ref[chunk] = attended
        sums_ref[chunk] = dot(attended, w_ref[...], 1, 0).astype(bf16)
    rank = rank_ref[0]
    for step, out_ref in enumerate(out_refs):
        out_ref[...] = sums_ref[lax.rem(rank + step, chunks)]


def attend_back_kernel(masked, q_ref, k_ref, v_ref, g_ref, *refs):
    bias_ref = refs[0] if masked else None
    dq_ref, dk_ref, dv_ref = refs[1:] if masked else refs
    chunks, group, size, width = k_ref.shape
    heads = width // HEAD_DIM
    score_scale = 1.0 / math.sqrt(HEAD_DIM)
    for chunk in range(chunks - 1, -1, -1):
        count = (chunk + 1) * group * size
        keys = k_ref[: chunk + 1].reshape(count, width)
        values = v_ref[: chunk + 1].reshape(count, width)
        keys_t = keys.T
        query = q_ref[chunk]
        grad = g_ref[chunk]
        parts, probs_all, grads_all, query_all, grad_all = [], [], [], [], []
        for head in range(heads):
            lanes = head_mask(size, width, head)
            query_part = jnp.where(lanes, query, jnp.zeros_like(query))
            grad_part = jnp.where(lanes, grad, jnp.zeros_like(grad))
            scores = dot(keys, query_part, 1, 1)
            if masked:
                early = count - group * size
                scores = jnp.concatenate([scores[:early], scores[early:] + bias_ref[...]], 0) if early else scores + bias_ref[...]
            top = jnp.max(scores, 0, keepdims=True)
            raised = jnp.exp(scores - top)
            probs = raised * (1.0 / jnp.sum(raised, 0, keepdims=True))
            grad_probs = dot(values, grad_part, 1, 1)
            delta = jnp.sum(probs * grad_probs, 0, keepdims=True)
            grad_scores = (probs * (grad_probs - delta)).astype(bf16)
            parts.append(
                dot(keys_t[head * HEAD_DIM : (head + 1) * HEAD_DIM], grad_scores, 1, 0)
            )
            probs_all.append(probs.astype(bf16))
            grads_all.append(grad_scores)
            query_all.append(query_part)
            grad_all.append(grad_part)
        dq_ref[chunk] = (jnp.concatenate(parts, 0).T * score_scale).astype(bf16)
        key_grad = dot(jnp.concatenate(grads_all, 1), jnp.concatenate(query_all, 0), 1, 0)
        value_grad = dot(jnp.concatenate(probs_all, 1), jnp.concatenate(grad_all, 0), 1, 0)
        key_grad = key_grad.reshape(chunk + 1, group, size, width)
        value_grad = value_grad.reshape(chunk + 1, group, size, width)
        if chunk == chunks - 1:
            dk_ref[...] = key_grad
            dv_ref[...] = value_grad
        else:
            dk_ref[: chunk + 1] = dk_ref[: chunk + 1] + key_grad
            dv_ref[: chunk + 1] = dv_ref[: chunk + 1] + value_grad


VMEM = pl.BlockSpec(memory_space=pltpu.VMEM)
SMEM = pl.BlockSpec(memory_space=pltpu.SMEM)
PARAMS = pltpu.CompilerParams(vmem_limit_bytes=56 * 1024 * 1024)


def attend(rank, query, keys, values, weight, bias):
    chunks, group, size, width = keys.shape
    model = weight.shape[1]
    extra = () if bias is None else (bias,)
    outs = pl.pallas_call(
        functools.partial(attend_kernel, bias is not None),
        out_shape=[jax.ShapeDtypeStruct((chunks, size, width), bf16)]
        + [jax.ShapeDtypeStruct((size, model), bf16)] * chunks,
        in_specs=[SMEM] + [VMEM] * (4 + len(extra)),
        out_specs=[VMEM] * (1 + chunks),
        scratch_shapes=[pltpu.VMEM((chunks, size, model), bf16)],
        compiler_params=PARAMS,
        name="attend",
    )(rank, query, keys, values, weight, *extra)
    return outs[0], outs[1:]


def attend_back(query, keys, values, grad, bias):
    chunks, group, size, width = keys.shape
    extra = () if bias is None else (bias,)
    return pl.pallas_call(
        functools.partial(attend_back_kernel, bias is not None),
        out_shape=[
            jax.ShapeDtypeStruct((chunks, size, width), bf16),
            jax.ShapeDtypeStruct(keys.shape, f32),
            jax.ShapeDtypeStruct(keys.shape, f32),
        ],
        in_specs=[VMEM] * (4 + len(extra)),
        out_specs=[VMEM] * 3,
        compiler_params=PARAMS,
        name="attend_back",
    )(query, keys, values, grad, *extra)


def per_device(
    n_dp,
    n_seq,
    tokens,
    tie_index,
    first_gain,
    first_shift,
    qkv_weight,
    qv_bias,
    out_weight,
    out_bias,
    second_gain,
    second_shift,
    fc_weight,
    fc_bias,
    proj_weight,
    proj_bias,
    cotangent,
):
    ranks, planes, group = n_dp, n_dp, n_seq // n_dp
    axes = ("dp", "seq")
    size, model = tokens.shape[1:]
    ties, rows = qkv_weight.shape[:2]
    inner = fc_weight.shape[2]
    width = model // ranks
    part = inner // ranks
    heads_here = HEADS // ranks
    score_scale = 1.0 / math.sqrt(HEAD_DIM)
    rank = lax.axis_index("dp")
    place = lax.axis_index("seq")
    plane, member = place // group, place % group

    def route(where):
        pairs = []
        for a in range(ranks):
            for b in range(planes):
                for c in range(group):
                    x, y, z = where(a, b, c)
                    pairs.append(
                        (a * n_seq + b * group + c, x * n_seq + y * group + z)
                    )
        return pairs

    swap = route(lambda a, b, c: (b, a, c))
    to_rank = [route(lambda a, b, c, k=k: ((a + k) % ranks, b, c)) for k in range(ranks)]
    to_plane = [route(lambda a, b, c, k=k: (a, (b + k) % planes, c)) for k in range(planes)]
    to_member = [route(lambda a, b, c, k=k: (a, b, (c + k) % group)) for k in range(group)]

    def send(values, pairs):
        return lax.ppermute(values, axes, pairs)

    def pick(stacked, index, axis=0):
        return lax.dynamic_index_in_dim(stacked, index, axis, keepdims=False)

    def turn(parts, start):
        count = len(parts)
        if count == 1:
            return jnp.stack(parts)
        if count == 2:
            first = jnp.where(start == 0, parts[0], parts[1])
            second = jnp.where(start == 0, parts[1], parts[0])
            return jnp.stack([first, second])
        stacked = jnp.stack(parts + parts)
        return lax.dynamic_slice_in_dim(stacked, (count - start) % count, count, 0)

    def from_ranks(pieces):
        return turn(
            [pick(pieces, rank)]
            + [
                send(pick(pieces, (rank + ranks - k) % ranks), to_rank[ranks - k])
                for k in range(1, ranks)
            ],
            rank,
        )

    def from_planes(piece_of):
        return [piece_of(plane)] + [
            send(piece_of((plane + planes - k) % planes), to_plane[planes - k])
            for k in range(1, planes)
        ]

    def from_members(piece):
        return [piece] + [send(piece, to_member[group - k]) for k in range(1, group)]

    tie_parts = [tie_index] + [send(tie_index, to_rank[ranks - k]) for k in range(1, ranks)]
    tie_rel = jnp.concatenate(tie_parts)
    tie_of = lambda seq: tie_rel[(seq + ranks - rank) % ranks]
    chosen = tie_of(plane)

    tokens_own = send(tokens[0], swap)
    grad_own = send(cotangent[0], swap)

    small = jnp.concatenate(
        [
            first_gain,
            first_shift,
            out_bias,
            second_gain,
            second_shift,
            proj_bias,
            qv_bias,
            fc_bias,
        ],
        1,
    )
    extra = 8
    small_rows = jnp.pad(small[:, None], ((0, 0), (0, extra - 1), (0, 3 * width - small.shape[1])))
    qkv_cols = qkv_weight.reshape(ties, rows, 3, ranks, width).transpose(3, 0, 1, 2, 4)
    qkv_cols = qkv_cols.reshape(ranks, ties, rows, 3 * width)
    qkv_cols = jnp.concatenate(
        [qkv_cols, jnp.broadcast_to(small_rows[None], (ranks,) + small_rows.shape)], 2
    )
    fc_cols = fc_weight.reshape(ties, rows, ranks, part).transpose(2, 0, 1, 3)
    qkv_rank = from_ranks(qkv_cols)
    fc_rank = from_ranks(fc_cols)

    def whole(piece_of):
        planes_here = turn(from_planes(piece_of), plane)
        return turn(from_members(planes_here), member)

    qkv_all = whole(lambda seq: pick(qkv_rank, tie_of(seq), 1)).transpose(2, 1, 0, 3, 4)
    w_qkv = qkv_all[..., :rows, :].reshape(model, 3 * width)
    small_all = qkv_all[..., rows, : 12 * rows].reshape(-1, 12 * rows)
    vectors = small_all[:, : 6 * rows].reshape(-1, 6, rows).transpose(1, 0, 2).reshape(6, model)
    vectors = vectors.astype(f32)
    gain_one, shift_one, bias_out, gain_two, shift_two, bias_proj = [
        vectors[k : k + 1] for k in range(6)
    ]
    bias_qv = small_all[:, 6 * rows : 8 * rows].reshape(2, ranks, width).astype(f32)
    bias_qv = pick(bias_qv, rank, 1)
    bias_fc = pick(small_all[:, 8 * rows :].reshape(ranks, 1, part), rank).astype(f32)

    out_all = whole(lambda seq: pick(out_weight, tie_of(seq)))
    w_out = out_all.transpose(1, 0, 2, 3).reshape(width, model)
    fc_all = whole(lambda seq: pick(fc_rank, tie_of(seq), 1)).transpose(2, 1, 0, 3, 4)
    w_fc = fc_all.reshape(model, part)
    proj_all = whole(lambda seq: pick(proj_weight, tie_of(seq)))
    w_proj = proj_all.transpose(1, 0, 2, 3).reshape(part, model)

    tokens_all = lax.all_gather(tokens_own, "dp", axis=0, tiled=True)
    normal_all, _ = norm_parts(tokens_all.astype(f32))
    normed = (normal_all * gain_one + shift_one).astype(bf16)
    mixed = dot(normed, w_qkv, 1, 0)
    query = (mixed[:, :width] + bias_qv[:1]).astype(bf16)
    key = mixed[:, width : 2 * width].astype(bf16)
    value = (mixed[:, 2 * width :] + bias_qv[1:]).astype(bf16)
    query = (query * jnp.asarray(score_scale, bf16)).reshape(ranks, size, width)
    pair = jnp.stack([key, value]).reshape(2, ranks, size, width)
    pairs = jnp.stack(from_members(pair), 2)
    keys, values = pairs[0], pairs[1]
    bias = None
    if group * size > BLOCK:
        owners = (member + jnp.arange(group)) % group
        seen = owners // (BLOCK // size) <= member // (BLOCK // size)
        bias = jnp.repeat(jnp.where(seen, 0.0, -1e30), size)[:, None].astype(f32)
        bias = jnp.broadcast_to(bias, (group * size, size))
    attended, sums = attend(rank.reshape(1).astype(jnp.int32), query, keys, values, w_out, bias)

    def spread(parts):
        total = parts[0].astype(f32)
        for k in range(1, ranks):
            total = total + send(parts[k], to_rank[k]).astype(f32)
        return total

    def by_step(values):
        stacked = values.reshape(ranks, size, model)
        return [pick(stacked, (rank + k) % ranks) for k in range(ranks)]

    middle = tokens_own.astype(f32) + spread(sums) + bias_out
    normal_two, scale_two = norm_parts(middle)
    normed_two_own = (normal_two * gain_two + shift_two).astype(bf16)
    normed_two = lax.all_gather(normed_two_own, "dp", axis=0, tiled=True)
    grad_all = lax.all_gather(grad_own, "dp", axis=0, tiled=True)
    hidden_pre = dot(normed_two, w_fc, 1, 0) + bias_fc
    root = math.sqrt(2.0 / math.pi)
    squared = hidden_pre * hidden_pre
    bent = jnp.tanh(root * hidden_pre * (1.0 + 0.044715 * squared))
    hidden = (0.5 * hidden_pre * (1.0 + bent)).astype(bf16)
    slope = 0.5 * (1.0 + bent) + 0.5 * hidden_pre * (1.0 - bent * bent) * root * (
        1.0 + 3.0 * 0.044715 * squared
    )
    layer_sums = dot(hidden, w_proj, 1, 0).astype(bf16)
    layer_own = (middle + spread(by_step(layer_sums)) + bias_proj).astype(bf16)
    layer_out = send(layer_own, swap)[None]

    grad_hidden = dot(grad_all, w_proj, 1, 1)
    grad_pre = (grad_hidden * slope).astype(bf16)
    second_sums = dot(grad_pre, w_fc, 1, 1)
    grad_second = spread(by_step(second_sums.astype(bf16)))
    upstream = grad_own.astype(f32)
    grad_middle = upstream + norm_back(normal_two, scale_two, gain_two, grad_second)
    middle_low_own = grad_middle.astype(bf16)
    middle_low = lax.all_gather(middle_low_own, "dp", axis=0, tiled=True)
    grad_attended = dot(middle_low, w_out, 1, 1).astype(bf16).reshape(ranks, size, width)
    grad_query, grad_keys, grad_values = attend_back(query, keys, values, grad_attended, bias)
    pair = jnp.stack([grad_keys, grad_values])
    total = pair[:, :, 0]
    for k in range(1, group):
        total = total + send(pair[:, :, k].astype(bf16), to_member[k]).astype(f32)
    total = total.astype(bf16).reshape(2, ranks * size, width)
    grad_query = grad_query.reshape(ranks * size, width)
    grad_mixed = jnp.concatenate([grad_query, total[0], total[1]], 1)
    first_sums = dot(grad_mixed, w_qkv, 1, 1)
    grad_first = spread(by_step(first_sums.astype(bf16)))
    normal_one, scale_one = norm_parts(tokens_own.astype(f32))
    input_own = (grad_middle + norm_back(normal_one, scale_one, gain_one, grad_first)).astype(bf16)
    input_grad = send(input_own, swap)[None]

    def over_members(pieces):
        axis = pieces.ndim - 3
        total = pick(pieces, member, axis)
        for k in range(1, group):
            total = total + send(pick(pieces, (member + k) % group, axis), to_member[k])
        return total

    def over_planes(pieces):
        parts = [pick(pieces, plane)] + [
            send(pick(pieces, (plane + k) % planes), to_plane[k]) for k in range(1, planes)
        ]
        sums_here = []
        for block in range(ties):
            total = 0.0
            for k in range(planes):
                source = (plane + planes - k) % planes
                total = total + jnp.where(tie_of(source) == block, parts[k].astype(f32), 0.0)
            sums_here.append(total)
        return jnp.stack(sums_here)

    by_owner = (ranks, planes, group)
    grad_w_proj = dot(hidden, grad_all, 0, 0).reshape(planes, group, -1, model)
    grad_proj_weight = over_planes(over_members(grad_w_proj).astype(bf16))
    grad_w_fc = dot(normed_two, grad_pre, 0, 0).reshape(by_owner + (rows, part))
    fc_owner = over_members(grad_w_fc).astype(bf16).transpose(1, 0, 2, 3)
    fc_back = from_ranks(over_planes(fc_owner).astype(bf16).transpose(1, 0, 2, 3))
    grad_fc_weight = fc_back.transpose(1, 2, 0, 3).reshape(ties, rows, inner).astype(f32)
    attended_flat = attended.reshape(ranks * size, width)
    grad_w_out = dot(attended_flat, middle_low, 0, 0).reshape(planes, group, rows, model)
    grad_out_weight = over_planes(over_members(grad_w_out).astype(bf16))

    second_normal = normed_two.astype(f32)
    own_sums = jnp.stack([grad_middle.sum(0), upstream.sum(0)])
    vector_grads = jnp.stack(
        [
            jnp.sum(first_sums * normal_all, 0),
            jnp.sum(first_sums, 0),
            own_sums[0],
            jnp.sum(grad_second * normal_two, 0),
            jnp.sum(grad_second, 0),
            own_sums[1],
        ]
    )
    mine = jnp.arange(ranks) == rank
    qv_sums = jnp.stack([grad_query.astype(f32).sum(0), total[1].astype(f32).sum(0)])
    qv_sums = jnp.where(mine[None, :, None], qv_sums[:, None], 0.0).reshape(-1, 2 * rows)
    fc_sums = grad_pre.astype(f32).sum(0)
    fc_sums = jnp.where(mine[:, None], fc_sums[None], 0.0).reshape(-1, 4 * rows)
    vector_grads = vector_grads.reshape(6, -1, rows).transpose(1, 0, 2).reshape(-1, 6 * rows)
    small_grads = jnp.concatenate([vector_grads, qv_sums, fc_sums], 1)
    small_grads = jnp.pad(
        small_grads.reshape(by_owner + (1, 12 * rows)),
        ((0, 0),) * 3 + ((0, extra - 1), (0, 3 * width - 12 * rows)),
    )
    grad_w_qkv = dot(normed, grad_mixed, 0, 0).reshape(by_owner + (rows, 3 * width))
    qkv_owner = over_members(jnp.concatenate([grad_w_qkv, small_grads], 3)).astype(bf16)
    qkv_back = over_planes(qkv_owner.transpose(1, 0, 2, 3)).astype(bf16)
    qkv_back = from_ranks(qkv_back.transpose(1, 0, 2, 3)).astype(f32)
    grad_qkv_weight = qkv_back[:, :, :rows].reshape(ranks, ties, rows, 3, width)
    grad_qkv_weight = grad_qkv_weight.transpose(1, 2, 3, 0, 4).reshape(ties, rows, 3 * model)
    small_back = qkv_back[:, :, rows, : 12 * rows].sum(0)
    vec = [small_back[:, k * rows : (k + 1) * rows] for k in range(6)]
    return (
        layer_out,
        input_grad,
        vec[0],
        vec[1],
        grad_qkv_weight,
        small_back[:, 6 * rows : 8 * rows],
        grad_out_weight,
        vec[2],
        vec[3],
        vec[4],
        grad_fc_weight,
        small_back[:, 8 * rows :],
        grad_proj_weight,
        vec[5],
    )


def solution(mesh):
    both = ("dp", "seq")
    token_spec = P("dp", "seq", None)
    vector = P(None, both)
    matrix = P(None, both, None)
    param_specs = (
        vector,
        vector,
        matrix,
        vector,
        matrix,
        vector,
        vector,
        vector,
        matrix,
        vector,
        matrix,
        vector,
    )
    return jax.shard_map(
        functools.partial(per_device, mesh.shape["dp"], mesh.shape["seq"]),
        mesh=mesh,
        in_specs=(token_spec, P("dp")) + param_specs + (token_spec,),
        out_specs=(token_spec, token_spec) + param_specs,
        check_vma=False,
    )
```

time: 1410 us -> 356 us (0.25)
  waiting for transfers between devices: 830 us -> 58.4 us
  blocking collectives: 368 us -> 52 us
  starting transfers between devices: 1.2 us -> 97.8 us
  matrix products: 63.4 us -> 13.6 us
  local copies, waits for them, and re-layouts: 79.7 us -> 58.1 us
  Pallas kernels: 0 us -> 18.7 us
  loops' own time: 18.5 us -> 0 us
  other arithmetic: 19 us -> 34.4 us
    reduce_scatter x4 -> x0, waiting for transfers between devices: 704 us -> none  [the longest x1 212 us: per_device(): lax.psum_scatter(grad_totals[8], ('dp', 'seq'), scatter_dimension=1, tile...]
    all_gather x9 -> x4, blocking collectives: 328 us -> 52 us  [the longest x1 15.9 us: per_device(): middle_low = lax.all_gather(middle_low_own, 'dp', axis=0, tiled=True)]
    all_gather x8 -> x0, waiting for transfers between devices: 107 us -> none  [the longest x1 80.6 us: per_device(): lax.all_gather(proj_weight, ('dp', 'seq'), axis=1, tiled=True)]
    ppermute x0 -> x65, starting transfers between devices: none -> 97.8 us  [send(): return lax.ppermute(values, axes, pairs)]
    ppermute x0 -> x65, waiting for transfers between devices: none -> 58.4 us  [send(): return lax.ppermute(values, axes, pairs)]
    dot_general x22 -> x11, matrix products: 63.4 us -> 13.6 us  [dot(): lax.dot_general(a, b, (((ca,), (cb,)), ((), ())), preferred_element_type=...]
    unnamed x1 -> x0, blocking collectives: 39.9 us -> none
    broadcast_in_dim x11 -> x2, local copies, waits for them, and re-layouts: 25 us -> 0.09 us  [the longest x1 0.08 us: per_device(): fc_sums = jnp.where(mine[:, None], fc_sums[None], 0.0).reshape(-1, 4 * rows)]
  transfers between devices with their start and end apart: 14 -> 65, of which waited for: 8 -> 18; matrix products, arithmetic and copies ran while one was open for 11% -> 23% of each run, Pallas kernels for 0% -> 5%
where the time goes in v1:
time: 356 us; the launch traced here: 349 us
  starting transfers between devices  97.8 us (27%)
  waiting for transfers between devices  58.4 us (16%)
  local copies, waits for them, and re-layouts  58.1 us (16%)
  blocking collectives  52 us (15%)
  other arithmetic  34.4 us (10%)
  Pallas kernels  18.7 us (5%)
  between operations  16.3 us (5%)
  matrix products  13.6 us (4%)
    ppermute x65, starting transfers between devices, send(): return lax.ppermute(values, axes, pairs)  97.8 us
    ppermute x65, waiting for transfers between devices, send(): return lax.ppermute(values, axes, pairs)  58.4 us
    unnamed x183, local copies, waits for them, and re-layouts  21.5 us
    all_gather x1, blocking collectives, per_device(): middle_low = lax.all_gather(middle_low_own, 'dp', axis=0, tiled=True)  15.9 us
    all_gather x1, blocking collectives, per_device(): tokens_all = lax.all_gather(tokens_own, 'dp', axis=0, tiled=True)  14.1 us
    dot_general x11, matrix products, dot(): lax.dot_general(a, b, (((ca,), (cb,)), ((), ())), preferred_element_type=...  13.6 us
    all_gather x1, blocking collectives, per_device(): normed_two = lax.all_gather(normed_two_own, 'dp', axis=0, tiled=True)  11.1 us
    pallas_call x1, Pallas kernels, attend_back(): pl.pallas_call(functools.partial(attend_back_kernel, bias is not None), o...  11 us
  transfers between devices with their start and end apart: 65, of which 18 were waited for; matrix products, arithmetic and copies ran while one was open for 23% of the time, Pallas kernels for 5%

profile of v1, /device:TPU:0, one launch (start us, length us, event | category | flops | bytes accessed | tf_op | source)
XLA Modules:
  0.0 349.5 jit_solution(9894839847698171838)
XLA Ops:
  0.6 3.0 collective-permute-start.6
  3.6 1.5 collective-permute-start.5
  5.2 1.4 collective-permute-start.4
  10.5 1.5 collective-permute-start.2
  16.9 1.6 collective-permute-start
  18.5 1.9 pad_add_fusion
  28.8 6.5 %collective-permute-start.12 = (bf16[24,768]{1,0:T(8,128)(2,1)S(1)}, bf16[24,768]{1,0:T(8,128)(2,1)S(1)}, u32[]{:S(2)}, u32[]{:S(2)}) collective-permute-start(bf16[24,768]{1,0:T(8,128)(2,1)S(1)} %get-tuple-element.123), channel_id=1, source_target_pairs={{0,6},{1,7},{2,0},{3,1},{4,2},{5,3},{6,4},{7,5},{8,14},{9,15},{10,... | collective-permute-start | bytes 110600 | tf_op jit(solution)/shard_map/ppermute | solution.py:215
  41.4 4.8 %collective-permute-done.13 = bf16[24,768]{1,0:T(8,128)(2,1)S(1)} collective-permute-done((bf16[24,768]{1,0:T(8,128)(2,1)S(1)}, bf16[24,768]{1,0:T(8,128)(2,1)S(1)}, u32[]{:S(2)}, u32[]{:S(2)}) %collective-permute-start.13) | collective-permute-done | bytes 36896 | tf_op jit(solution)/shard_map/ppermute | solution.py:215
  46.2 5.7 %collective-permute-done.14 = bf16[24,768]{1,0:T(8,128)(2,1)S(1)} collective-permute-done((bf16[24,768]{1,0:T(8,128)(2,1)S(1)}, bf16[24,768]{1,0:T(8,128)(2,1)S(1)}, u32[]{:S(2)}, u32[]{:S(2)}) %collective-permute-start.14) | collective-permute-done | bytes 36896 | tf_op jit(solution)/shard_map/ppermute | solution.py:215
  52.4 1.9 collective-permute-start.20
  56.0 1.6 collective-permute-start.34
  57.6 5.9 %collective-permute-start.26 = (bf16[96,768]{1,0:T(8,128)(2,1)S(1)}, bf16[96,768]{1,0:T(8,128)(2,1)S(1)}, u32[]{:S(2)}, u32[]{:S(2)}) collective-permute-start(bf16[96,768]{1,0:T(8,128)(2,1)S(1)} %copy-done.36), channel_id=1, source_target_pairs={{0,6},{1,7},{2,0},{3,1},{4,2},{5,3},{6,4},{7,5},{8,14},{9,15},{10,... | collective-permute-start | bytes 442376 | tf_op jit(solution)/shard_map/ppermute | solution.py:215
  71.7 6.5 %collective-permute-done.26 = bf16[96,768]{1,0:T(8,128)(2,1)S(1)} collective-permute-done((bf16[96,768]{1,0:T(8,128)(2,1)S(1)}, bf16[96,768]{1,0:T(8,128)(2,1)S(1)}, u32[]{:S(2)}, u32[]{:S(2)}) %collective-permute-start.26) | collective-permute-done | bytes 147488 | tf_op jit(solution)/shard_map/ppermute | solution.py:215
  82.3 2.8 collective-permute-start.22
  85.1 14.1 %all_gather.12 = bf16[512,768]{1,0:T(8,128)(2,1)S(1)} all-gather(bf16[128,768]{1,0:T(8,128)(2,1)S(1)} %collective-permute-done), channel_id=1, replica_groups=mesh['dp'=4,'seq'=8] {'dp'}, dimensions={0}, use_global_device_ids=true | all-gather | bytes 983040 | tf_op jit(solution)/shard_map/all_gather | solution.py:305
  100.5 10.9 %all_gather.14 = bf16[512,768]{1,0:T(8,128)(2,1)} all-gather(bf16[128,768]{1,0:T(8,128)(2,1)S(1)} %collective-permute-done.34), channel_id=1, replica_groups=mesh['dp'=4,'seq'=8] {'dp'}, dimensions={0}, use_global_device_ids=true | all-gather | bytes 983040 | tf_op jit(solution)/shard_map/all_gather | solution.py:338
  111.4 1.8 collective-permute-start.24
  114.1 4.7 %collective-permute-done.24 = bf16[4,24,768]{2,1,0:T(8,128)(2,1)S(1)} collective-permute-done((bf16[4,24,768]{2,1,0:T(8,128)(2,1)S(1)}, bf16[4,24,768]{2,1,0:T(8,128)(2,1)S(1)}, u32[]{:S(2)}, u32[]{:S(2)}) %collective-permute-start.24) | collective-permute-done | bytes 147488 | tf_op jit(solution)/shard_map/ppermute | solution.py:215
  123.3 2.0 fusion.126
  133.8 7.7 %attend.1 = (bf16[4,128,192]{2,1,0:T(8,128)(2,1)}, bf16[128,768]{1,0:T(8,128)(2,1)}, bf16[128,768]{1,0:T(8,128)(2,1)}, bf16[128,768]{1,0:T(8,128)(2,1)}, bf16[128,768]{1,0:T(8,128)(2,1)}) custom-call(s32[1]{0:T(128)} %bitcast.1.rank_ref, bf16[4,128,192]{2,1,0:T(8,128)(2,1)} %bitcast.509, bf16[4,2,128,192]{3,2,1,0:T(8,128)(2,1)} %get-tuple-element.56.k_ref, ...), custom_call_target="tpu_custom_call" | custom-call | tf_op jit(solution)/shard_map/attend/pallas_call | solution.py:136
  141.6 1.5 collective-permute-start.18
  143.0 1.3 collective-permute-start.17
  149.5 4.8 %collective-permute-done.17 = bf16[128,768]{1,0:T(8,128)(2,1)S(1)} collective-permute-done((bf16[128,768]{1,0:T(8,128)(2,1)}, bf16[128,768]{1,0:T(8,128)(2,1)S(1)}, u32[]{:S(2)}, u32[]{:S(2)}) %collective-permute-start.17) | collective-permute-done | bytes 196640 | tf_op jit(solution)/shard_map/ppermute | solution.py:215
  155.0 1.7 fusion.134
  157.0 11.1 %all_gather.13 = bf16[512,768]{1,0:T(8,128)(2,1)S(1)} all-gather(bf16[128,768]{1,0:T(8,128)(2,1)S(1)} %add_convert_fusion), channel_id=1, replica_groups=mesh['dp'=4,'seq'=8] {'dp'}, dimensions={0}, use_global_device_ids=true | all-gather | bytes 983040 | tf_op jit(solution)/shard_map/all_gather | solution.py:337
  170.6 1.4 convert_reduce_fusion.1
  173.6 2.3 fusion.128
  176.8 1.5 collective-permute-start.37
  180.3 2.4 collective-permute-start.32
  188.5 1.6 collective-permute-done.36
  190.1 2.1 multiply_reduce_fusion
  192.3 3.3 collective-permute-done.31
  195.6 2.7 fusion.131
  198.3 3.1 collective-permute-start.33
  201.4 15.9 %all_gather.15 = bf16[512,768]{1,0:T(8,128)(2,1)S(1)} all-gather(bf16[128,768]{1,0:T(8,128)(2,1)S(1)} %convert_element_type.286), channel_id=1, replica_groups=mesh['dp'=4,'seq'=8] {'dp'}, dimensions={0}, use_global_device_ids=true | all-gather | bytes 983040 | tf_op jit(solution)/shard_map/all_gather | solution.py:358
  219.9 11.0 %attend_back.1 = (bf16[4,128,192]{2,1,0:T(8,128)(2,1)}, f32[4,2,128,192]{3,2,1,0:T(8,128)}, f32[4,2,128,192]{3,2,1,0:T(8,128)}) custom-call(bf16[4,128,192]{2,1,0:T(8,128)(2,1)} %bitcast.510, bf16[4,2,128,192]{3,2,1,0:T(8,128)(2,1)} %get-tuple-element.56.k_ref, bf16[4,2,128,192]{3,2,1,0:T(8,128)(2,1)} %get-tuple-element.55.v_ref, bf16[4,128,192]{2,1,0:T(8,128)(2,1)} %bitcast.520), custom_call_target="tpu_custom_call" | custom-call | tf_op jit(solution)/shard_map/attend_back/pallas_call | solution.py:152
  230.9 2.1 fusion.24
  235.2 3.5 %collective-permute-start.52 = (bf16[24,768]{1,0:T(8,128)(2,1)}, bf16[24,768]{1,0:T(8,128)(2,1)}, u32[]{:S(2)}, u32[]{:S(2)}) collective-permute-start(bf16[24,768]{1,0:T(8,128)(2,1)} %get-tuple-element.113), channel_id=1, source_target_pairs={{0,4},{1,5},{2,6},{3,7},{4,0},{5,1},{6,2},{7,3},{8,12},{9,13},{10,... | collective-permute-start | bytes 110600 | tf_op jit(solution)/shard_map/ppermute | solution.py:215
  239.7 1.4 stack.329
  241.1 1.4 stack.330
  242.4 1.4 stack.331
  243.8 1.4 stack.332
  247.2 1.5 fusion.20
  250.1 1.5 fusion.129
  253.4 1.4 collective-permute-start.41
  258.1 1.4 stack.328
  263.3 2.1 fusion.81
  266.0 1.5 fusion.130
  269.1 1.5 fusion.15
  270.7 11.2 %collective-permute-start.57 = (bf16[4,24,768]{2,1,0:T(8,128)(2,1)S(1)}, bf16[4,24,768]{2,1,0:T(8,128)(2,1)S(1)}, u32[]{:S(2)}, u32[]{:S(2)}) collective-permute-start(bf16[4,24,768]{2,1,0:T(8,128)(2,1)S(1)} %get-tuple-element.80), channel_id=1, source_target_pairs={{0,6},{1,7},{2,0},{3,1},{4,2},{5,3},{6,4},{7,5},{8,14},{9,15},{10,... | collective-permute-start | bytes 442376 | tf_op jit(solution)/shard_map/ppermute | solution.py:215
  281.9 6.2 %collective-permute-start.56 = (bf16[4,24,768]{2,1,0:T(8,128)(2,1)S(1)}, bf16[4,24,768]{2,1,0:T(8,128)(2,1)S(1)}, u32[]{:S(2)}, u32[]{:S(2)}) collective-permute-start(bf16[4,24,768]{2,1,0:T(8,128)(2,1)S(1)} %get-tuple-element.81), channel_id=1, source_target_pairs={{0,4},{1,5},{2,6},{3,7},{4,0},{5,1},{6,2},{7,3},{8,12},{9,13},{10,... | collective-permute-start | bytes 442376 | tf_op jit(solution)/shard_map/ppermute | solution.py:215
  288.1 1.4 fusion.16
  290.7 11.1 %collective-permute-start.63 = (bf16[96,768]{1,0:T(8,128)(2,1)S(1)}, bf16[96,768]{1,0:T(8,128)(2,1)S(1)}, u32[]{:S(2)}, u32[]{:S(2)}) collective-permute-start(bf16[96,768]{1,0:T(8,128)(2,1)S(1)} %get-tuple-element.77), channel_id=1, source_target_pairs={{0,4},{1,5},{2,6},{3,7},{4,0},{5,1},{6,2},{7,3},{8,12},{9,13},{10,... | collective-permute-start | bytes 442376 | tf_op jit(solution)/shard_map/ppermute | solution.py:215
  301.8 5.4 %collective-permute-done.56 = bf16[4,24,768]{2,1,0:T(8,128)(2,1)S(1)} collective-permute-done((bf16[4,24,768]{2,1,0:T(8,128)(2,1)S(1)}, bf16[4,24,768]{2,1,0:T(8,128)(2,1)S(1)}, u32[]{:S(2)}, u32[]{:S(2)}) %collective-permute-start.56) | collective-permute-done | bytes 147488 | tf_op jit(solution)/shard_map/ppermute | solution.py:215
  307.5 1.5 collective-permute-start.58
  308.9 1.8 collective-permute-start.59
  313.9 3.1 collective-permute-done.60
  317.3 3.6 %collective-permute-start.46 = (bf16[4,32,576]{2,1,0:T(8,128)(2,1)S(1)}, bf16[4,32,576]{2,1,0:T(8,128)(2,1)S(1)}, u32[]{:S(2)}, u32[]{:S(2)}) collective-permute-start(bf16[4,32,576]{2,1,0:T(8,128)(2,1)S(1)} %get-tuple-element.71), channel_id=1, source_target_pairs={{0,6},{1,7},{2,0},{3,1},{4,2},{5,3},{6,4},{7,5},{8,14},{9,15},{10,... | collective-permute-start | bytes 442376 | tf_op jit(solution)/shard_map/ppermute | solution.py:215
  322.5 3.1 collective-permute-done.46
  325.6 8.1 %collective-permute-done.45 = bf16[4,32,576]{2,1,0:T(8,128)(2,1)S(1)} collective-permute-done((bf16[4,32,576]{2,1,0:T(8,128)(2,1)S(1)}, bf16[4,32,576]{2,1,0:T(8,128)(2,1)S(1)}, u32[]{:S(2)}, u32[]{:S(2)}) %collective-permute-start.45) | collective-permute-done | bytes 147488 | tf_op jit(solution)/shard_map/ppermute | solution.py:215
  334.1 3.5 %collective-permute-start.48 = (bf16[2,32,576]{2,1,0:T(8,128)(2,1)S(1)}, bf16[2,32,576]{2,1,0:T(8,128)(2,1)S(1)}, u32[]{:S(2)}, u32[]{:S(2)}) collective-permute-start(bf16[2,32,576]{2,1,0:T(8,128)(2,1)S(1)} %get-tuple-element.90), channel_id=1, source_target_pairs={{0,16},{1,17},{2,18},{3,19},{4,20},{5,21},{6,22},{7,23},{8,24},{9,... | collective-permute-start | bytes 221192 | tf_op jit(solution)/shard_map/ppermute | solution.py:215
  338.8 1.7 collective-permute-done.48
  340.5 2.4 collective-permute-done.49
  346.9 1.6 copy.199
  (416 shorter events, 89.6 us)
Async XLA Ops:
  0.6 16.2 %collective-permute-start.6 = (s32[1]{0:T(128)}, s32[1]{0:T(128)}, u32[]{:S(2)}, u32[]{:S(2)}) collective-permute-start(s32[1]{0:T(128)} %param.16), channel_id=1, source_target_pairs={{0,8},{1,9},{2,10},{3,11},{4,12},{5,13},{6,14},{7,15},{8,16},{9,17... | collective-permute-start | bytes 20 | tf_op jit(solution)/shard_map/ppermute | solution.py:215
  3.6 13.3 %collective-permute-start.5 = (s32[1]{0:T(128)}, s32[1]{0:T(128)}, u32[]{:S(2)}, u32[]{:S(2)}) collective-permute-start(s32[1]{0:T(128)} %param.16), channel_id=1, source_target_pairs={{0,16},{1,17},{2,18},{3,19},{4,20},{5,21},{6,22},{7,23},{8,24},{9,... | collective-permute-start | bytes 20 | tf_op jit(solution)/shard_map/ppermute | solution.py:215
  5.2 13.3 %collective-permute-start.4 = (s32[1]{0:T(128)}, s32[1]{0:T(128)}, u32[]{:S(2)}, u32[]{:S(2)}) collective-permute-start(s32[1]{0:T(128)} %param.16), channel_id=1, source_target_pairs={{0,24},{1,25},{2,26},{3,27},{4,28},{5,29},{6,30},{7,31},{8,0},{9,1... | collective-permute-start | bytes 20 | tf_op jit(solution)/shard_map/ppermute | solution.py:215
  9.9 42.4 %collective-permute-start.1 = (bf16[2,32,576]{2,1,0:T(8,128)(2,1)}, bf16[2,32,576]{2,1,0:T(8,128)(2,1)S(1)}, u32[]{:S(2)}, u32[]{:S(2)}) collective-permute-start(bf16[2,32,576]{2,1,0:T(8,128)(2,1)} %get-tuple-element.93), channel_id=1, source_target_pairs={{0,24},{1,25},{2,26},{3,27},{4,28},{5,29},{6,30},{7,31},{8,0},{9,1... | collective-permute-start | bytes 221192 | tf_op jit(solution)/shard_map/ppermute | solution.py:215
  10.5 43.8 %collective-permute-start.2 = (bf16[2,32,576]{2,1,0:T(8,128)(2,1)}, bf16[2,32,576]{2,1,0:T(8,128)(2,1)}, u32[]{:S(2)}, u32[]{:S(2)}) collective-permute-start(bf16[2,32,576]{2,1,0:T(8,128)(2,1)} %get-tuple-element.94), channel_id=1, source_target_pairs={{0,16},{1,17},{2,18},{3,19},{4,20},{5,21},{6,22},{7,23},{8,24},{9,... | collective-permute-start | bytes 221192 | tf_op jit(solution)/shard_map/ppermute | solution.py:215
  16.8 39.1 %collective-permute-start.3 = (bf16[2,32,576]{2,1,0:T(8,128)(2,1)}, bf16[2,32,576]{2,1,0:T(8,128)(2,1)S(1)}, u32[]{:S(2)}, u32[]{:S(2)}) collective-permute-start(bf16[2,32,576]{2,1,0:T(8,128)(2,1)} %get-tuple-element.91), channel_id=1, source_target_pairs={{0,8},{1,9},{2,10},{3,11},{4,12},{5,13},{6,14},{7,15},{8,16},{9,17... | collective-permute-start | bytes 221192 | tf_op jit(solution)/shard_map/ppermute | solution.py:215
  16.9 65.4 %collective-permute-start = (bf16[128,768]{1,0:T(8,128)(2,1)}, bf16[128,768]{1,0:T(8,128)(2,1)S(1)}, u32[]{:S(2)}, u32[]{:S(2)}) collective-permute-start(bf16[128,768]{1,0:T(8,128)(2,1)} %bitcast), channel_id=1, source_target_pairs={{0,0},{1,1},{2,8},{3,9},{4,16},{5,17},{6,24},{7,25},{8,2},{9,3},{1... | collective-permute-start | bytes 589832 | tf_op jit(solution)/shard_map/ppermute | solution.py:215
  28.8 12.5 %collective-permute-start.12 = (bf16[24,768]{1,0:T(8,128)(2,1)S(1)}, bf16[24,768]{1,0:T(8,128)(2,1)S(1)}, u32[]{:S(2)}, u32[]{:S(2)}) collective-permute-start(bf16[24,768]{1,0:T(8,128)(2,1)S(1)} %get-tuple-element.123), channel_id=1, source_target_pairs={{0,6},{1,7},{2,0},{3,1},{4,2},{5,3},{6,4},{7,5},{8,14},{9,15},{10,... | collective-permute-start | bytes 110600 | tf_op jit(solution)/shard_map/ppermute | solution.py:215
  41.3 4.9 %collective-permute-start.13 = (bf16[24,768]{1,0:T(8,128)(2,1)S(1)}, bf16[24,768]{1,0:T(8,128)(2,1)S(1)}, u32[]{:S(2)}, u32[]{:S(2)}) collective-permute-start(bf16[24,768]{1,0:T(8,128)(2,1)S(1)} %get-tuple-element.124), channel_id=1, source_target_pairs={{0,4},{1,5},{2,6},{3,7},{4,0},{5,1},{6,2},{7,3},{8,12},{9,13},{10,... | collective-permute-start | bytes 110600 | tf_op jit(solution)/shard_map/ppermute | solution.py:215
  46.2 5.8 %collective-permute-start.14 = (bf16[24,768]{1,0:T(8,128)(2,1)S(1)}, bf16[24,768]{1,0:T(8,128)(2,1)S(1)}, u32[]{:S(2)}, u32[]{:S(2)}) collective-permute-start(bf16[24,768]{1,0:T(8,128)(2,1)S(1)} %get-tuple-element.121), channel_id=1, source_target_pairs={{0,2},{1,3},{2,4},{3,5},{4,6},{5,7},{6,0},{7,1},{8,10},{9,11},{10,... | collective-permute-start | bytes 110600 | tf_op jit(solution)/shard_map/ppermute | solution.py:215
  52.0 5.6 %collective-permute-start.19 = (bf16[2,24,768]{2,1,0:T(8,128)(2,1)}, bf16[2,24,768]{2,1,0:T(8,128)(2,1)S(1)}, u32[]{:S(2)}, u32[]{:S(2)}) collective-permute-start(bf16[2,24,768]{2,1,0:T(8,128)(2,1)} %bitcast.543), channel_id=1, source_target_pairs={{0,24},{1,25},{2,26},{3,27},{4,28},{5,29},{6,30},{7,31},{8,0},{9,1... | collective-permute-start | bytes 221192 | tf_op jit(solution)/shard_map/ppermute | solution.py:215
  52.4 11.8 %collective-permute-start.20 = (bf16[2,24,768]{2,1,0:T(8,128)(2,1)}, bf16[2,24,768]{2,1,0:T(8,128)(2,1)S(1)}, u32[]{:S(2)}, u32[]{:S(2)}) collective-permute-start(bf16[2,24,768]{2,1,0:T(8,128)(2,1)} %bitcast.542), channel_id=1, source_target_pairs={{0,16},{1,17},{2,18},{3,19},{4,20},{5,21},{6,22},{7,23},{8,24},{9,... | collective-permute-start | bytes 221192 | tf_op jit(solution)/shard_map/ppermute | solution.py:215
  54.3 10.5 %collective-permute-start.21 = (bf16[2,24,768]{2,1,0:T(8,128)(2,1)}, bf16[2,24,768]{2,1,0:T(8,128)(2,1)S(1)}, u32[]{:S(2)}, u32[]{:S(2)}) collective-permute-start(bf16[2,24,768]{2,1,0:T(8,128)(2,1)} %bitcast.541), channel_id=1, source_target_pairs={{0,8},{1,9},{2,10},{3,11},{4,12},{5,13},{6,14},{7,15},{8,16},{9,17... | collective-permute-start | bytes 221192 | tf_op jit(solution)/shard_map/ppermute | solution.py:215
  56.0 44.5 %collective-permute-start.34 = (bf16[128,768]{1,0:T(8,128)(2,1)}, bf16[128,768]{1,0:T(8,128)(2,1)S(1)}, u32[]{:S(2)}, u32[]{:S(2)}) collective-permute-start(bf16[128,768]{1,0:T(8,128)(2,1)} %bitcast.550), channel_id=1, source_target_pairs={{0,0},{1,1},{2,8},{3,9},{4,16},{5,17},{6,24},{7,25},{8,2},{9,3},{1... | collective-permute-start | bytes 589832 | tf_op jit(solution)/shard_map/ppermute | solution.py:215
  57.6 20.6 %collective-permute-start.26 = (bf16[96,768]{1,0:T(8,128)(2,1)S(1)}, bf16[96,768]{1,0:T(8,128)(2,1)S(1)}, u32[]{:S(2)}, u32[]{:S(2)}) collective-permute-start(bf16[96,768]{1,0:T(8,128)(2,1)S(1)} %copy-done.36), channel_id=1, source_target_pairs={{0,6},{1,7},{2,0},{3,1},{4,2},{5,3},{6,4},{7,5},{8,14},{9,15},{10,... | collective-permute-start | bytes 442376 | tf_op jit(solution)/shard_map/ppermute | solution.py:215
  64.1 14.1 %collective-permute-start.27 = (bf16[96,768]{1,0:T(8,128)(2,1)S(1)}, bf16[96,768]{1,0:T(8,128)(2,1)S(1)}, u32[]{:S(2)}, u32[]{:S(2)}) collective-permute-start(bf16[96,768]{1,0:T(8,128)(2,1)S(1)} %copy-done.35), channel_id=1, source_target_pairs={{0,4},{1,5},{2,6},{3,7},{4,0},{5,1},{6,2},{7,3},{8,12},{9,13},{10,... | collective-permute-start | bytes 442376 | tf_op jit(solution)/shard_map/ppermute | solution.py:215
  64.8 13.5 %collective-permute-start.28 = (bf16[96,768]{1,0:T(8,128)(2,1)S(1)}, bf16[96,768]{1,0:T(8,128)(2,1)S(1)}, u32[]{:S(2)}, u32[]{:S(2)}) collective-permute-start(bf16[96,768]{1,0:T(8,128)(2,1)S(1)} %copy-done.34), channel_id=1, source_target_pairs={{0,2},{1,3},{2,4},{3,5},{4,6},{5,7},{6,0},{7,1},{8,10},{9,11},{10,... | collective-permute-start | bytes 442376 | tf_op jit(solution)/shard_map/ppermute | solution.py:215
  78.2 2.2 collective-permute-start.15
  78.3 33.1 %collective-permute-start.7 = (bf16[4,32,576]{2,1,0:T(8,128)(2,1)S(1)}, bf16[4,32,576]{2,1,0:T(8,128)(2,1)S(1)}, u32[]{:S(2)}, u32[]{:S(2)}) collective-permute-start(bf16[4,32,576]{2,1,0:T(8,128)(2,1)S(1)} %get-tuple-element.75), channel_id=1, source_target_pairs={{0,6},{1,7},{2,0},{3,1},{4,2},{5,3},{6,4},{7,5},{8,14},{9,15},{10,... | collective-permute-start | bytes 442376 | tf_op jit(solution)/shard_map/ppermute | solution.py:215
  78.4 34.8 %collective-permute-start.8 = (bf16[4,32,576]{2,1,0:T(8,128)(2,1)S(1)}, bf16[4,32,576]{2,1,0:T(8,128)(2,1)S(1)}, u32[]{:S(2)}, u32[]{:S(2)}) collective-permute-start(bf16[4,32,576]{2,1,0:T(8,128)(2,1)S(1)} %get-tuple-element.74), channel_id=1, source_target_pairs={{0,4},{1,5},{2,6},{3,7},{4,0},{5,1},{6,2},{7,3},{8,12},{9,13},{10,... | collective-permute-start | bytes 442376 | tf_op jit(solution)/shard_map/ppermute | solution.py:215
  80.4 32.9 %collective-permute-start.9 = (bf16[4,32,576]{2,1,0:T(8,128)(2,1)S(1)}, bf16[4,32,576]{2,1,0:T(8,128)(2,1)S(1)}, u32[]{:S(2)}, u32[]{:S(2)}) collective-permute-start(bf16[4,32,576]{2,1,0:T(8,128)(2,1)S(1)} %get-tuple-element.73), channel_id=1, source_target_pairs={{0,2},{1,3},{2,4},{3,5},{4,6},{5,7},{6,0},{7,1},{8,10},{9,11},{10,... | collective-permute-start | bytes 442376 | tf_op jit(solution)/shard_map/ppermute | solution.py:215
  82.3 31.8 %collective-permute-start.22 = (bf16[4,24,768]{2,1,0:T(8,128)(2,1)S(1)}, bf16[4,24,768]{2,1,0:T(8,128)(2,1)S(1)}, u32[]{:S(2)}, u32[]{:S(2)}) collective-permute-start(bf16[4,24,768]{2,1,0:T(8,128)(2,1)S(1)} %get-tuple-element.84), channel_id=1, source_target_pairs={{0,6},{1,7},{2,0},{3,1},{4,2},{5,3},{6,4},{7,5},{8,14},{9,15},{10,... | collective-permute-start | bytes 442376 | tf_op jit(solution)/shard_map/ppermute | solution.py:215
  100.5 13.7 %collective-permute-start.23 = (bf16[4,24,768]{2,1,0:T(8,128)(2,1)S(1)}, bf16[4,24,768]{2,1,0:T(8,128)(2,1)S(1)}, u32[]{:S(2)}, u32[]{:S(2)}) collective-permute-start(bf16[4,24,768]{2,1,0:T(8,128)(2,1)S(1)} %get-tuple-element.83), channel_id=1, source_target_pairs={{0,4},{1,5},{2,6},{3,7},{4,0},{5,1},{6,2},{7,3},{8,12},{9,13},{10,... | collective-permute-start | bytes 442376 | tf_op jit(solution)/shard_map/ppermute | solution.py:215
  111.4 7.5 %collective-permute-start.24 = (bf16[4,24,768]{2,1,0:T(8,128)(2,1)S(1)}, bf16[4,24,768]{2,1,0:T(8,128)(2,1)S(1)}, u32[]{:S(2)}, u32[]{:S(2)}) collective-permute-start(bf16[4,24,768]{2,1,0:T(8,128)(2,1)S(1)} %get-tuple-element.82), channel_id=1, source_target_pairs={{0,2},{1,3},{2,4},{3,5},{4,6},{5,7},{6,0},{7,1},{8,10},{9,11},{10,... | collective-permute-start | bytes 442376 | tf_op jit(solution)/shard_map/ppermute | solution.py:215
  113.2 15.2 %collective-permute-start.29 = (bf16[4,96,768]{2,1,0:T(8,128)(2,1)}, bf16[4,96,768]{2,1,0:T(8,128)(2,1)}, u32[]{:S(2)}, u32[]{:S(2)}) collective-permute-start(bf16[4,96,768]{2,1,0:T(8,128)(2,1)} %constant_dynamic-slice_fusion.1), channel_id=1, source_target_pairs={{0,1},{1,0},{2,3},{3,2},{4,5},{5,4},{6,7},{7,6},{8,9},{9,8},{10,11... | collective-permute-start | bytes 1769480 | tf_op jit(solution)/shard_map/ppermute | solution.py:215
  113.5 7.6 %collective-permute-start.10 = (bf16[4,4,32,576]{3,2,0,1:T(8,128)(2,1)S(1)}, bf16[4,4,32,576]{3,2,0,1:T(8,128)(2,1)S(1)}, u32[]{:S(2)}, u32[]{:S(2)}) collective-permute-start(bf16[4,4,32,576]{3,2,0,1:T(8,128)(2,1)S(1)} %constant_dynamic-slice_fusion.10), channel_id=1, source_target_pairs={{0,1},{1,0},{2,3},{3,2},{4,5},{5,4},{6,7},{7,6},{8,9},{9,8},{10,11... | collective-permute-start | bytes 1769480 | tf_op jit(solution)/shard_map/ppermute | solution.py:215
  120.8 24.1 %collective-permute-start.25 = (bf16[4,4,24,768]{3,2,0,1:T(8,128)(2,1)}, bf16[4,4,24,768]{3,2,0,1:T(8,128)(2,1)}, u32[]{:S(2)}, u32[]{:S(2)}) collective-permute-start(bf16[4,4,24,768]{3,2,0,1:T(8,128)(2,1)} %constant_dynamic-slice_fusion.3), channel_id=1, source_target_pairs={{0,1},{1,0},{2,3},{3,2},{4,5},{5,4},{6,7},{7,6},{8,9},{9,8},{10,11... | collective-permute-start | bytes 1769480 | tf_op jit(solution)/shard_map/ppermute | solution.py:215
  128.1 3.4 collective-permute-start.11
  141.6 7.9 %collective-permute-start.18 = (bf16[128,768]{1,0:T(8,128)(2,1)}, bf16[128,768]{1,0:T(8,128)(2,1)S(1)}, u32[]{:S(2)}, u32[]{:S(2)}) collective-permute-start(bf16[128,768]{1,0:T(8,128)(2,1)} %get-tuple-element.25), channel_id=1, source_target_pairs={{0,24},{1,25},{2,26},{3,27},{4,28},{5,29},{6,30},{7,31},{8,0},{9,1... | collective-permute-start | bytes 589832 | tf_op jit(solution)/shard_map/ppermute | solution.py:215
  143.0 11.2 %collective-permute-start.17 = (bf16[128,768]{1,0:T(8,128)(2,1)}, bf16[128,768]{1,0:T(8,128)(2,1)S(1)}, u32[]{:S(2)}, u32[]{:S(2)}) collective-permute-start(bf16[128,768]{1,0:T(8,128)(2,1)} %get-tuple-element.24), channel_id=1, source_target_pairs={{0,16},{1,17},{2,18},{3,19},{4,20},{5,21},{6,22},{7,23},{8,24},{9,... | collective-permute-start | bytes 589832 | tf_op jit(solution)/shard_map/ppermute | solution.py:215
  144.4 9.9 %collective-permute-start.16 = (bf16[128,768]{1,0:T(8,128)(2,1)}, bf16[128,768]{1,0:T(8,128)(2,1)S(1)}, u32[]{:S(2)}, u32[]{:S(2)}) collective-permute-start(bf16[128,768]{1,0:T(8,128)(2,1)} %get-tuple-element.23), channel_id=1, source_target_pairs={{0,8},{1,9},{2,10},{3,11},{4,12},{5,13},{6,14},{7,15},{8,16},{9,17... | collective-permute-start | bytes 589832 | tf_op jit(solution)/shard_map/ppermute | solution.py:215
  176.8 11.7 %collective-permute-start.37 = (bf16[128,768]{1,0:T(8,128)(2,1)}, bf16[128,768]{1,0:T(8,128)(2,1)}, u32[]{:S(2)}, u32[]{:S(2)}) collective-permute-start(bf16[128,768]{1,0:T(8,128)(2,1)} %get-tuple-element.65), channel_id=1, source_target_pairs={{0,24},{1,25},{2,26},{3,27},{4,28},{5,29},{6,30},{7,31},{8,0},{9,1... | collective-permute-start | bytes 589832 | tf_op jit(solution)/shard_map/ppermute | solution.py:215
  178.2 11.9 %collective-permute-start.36 = (bf16[128,768]{1,0:T(8,128)(2,1)}, bf16[128,768]{1,0:T(8,128)(2,1)}, u32[]{:S(2)}, u32[]{:S(2)}) collective-permute-start(bf16[128,768]{1,0:T(8,128)(2,1)} %get-tuple-element.66), channel_id=1, source_target_pairs={{0,16},{1,17},{2,18},{3,19},{4,20},{5,21},{6,22},{7,23},{8,24},{9,... | collective-permute-start | bytes 589832 | tf_op jit(solution)/shard_map/ppermute | solution.py:215
  178.9 11.2 %collective-permute-start.35 = (bf16[128,768]{1,0:T(8,128)(2,1)}, bf16[128,768]{1,0:T(8,128)(2,1)}, u32[]{:S(2)}, u32[]{:S(2)}) collective-permute-start(bf16[128,768]{1,0:T(8,128)(2,1)} %get-tuple-element.64), channel_id=1, source_target_pairs={{0,8},{1,9},{2,10},{3,11},{4,12},{5,13},{6,14},{7,15},{8,16},{9,17... | collective-permute-start | bytes 589832 | tf_op jit(solution)/shard_map/ppermute | solution.py:215
  180.3 12.0 %collective-permute-start.32 = (bf16[128,768]{1,0:T(8,128)(2,1)}, bf16[128,768]{1,0:T(8,128)(2,1)}, u32[]{:S(2)}, u32[]{:S(2)}) collective-permute-start(bf16[128,768]{1,0:T(8,128)(2,1)} %get-tuple-element.68), channel_id=1, source_target_pairs={{0,24},{1,25},{2,26},{3,27},{4,28},{5,29},{6,30},{7,31},{8,0},{9,1... | collective-permute-start | bytes 589832 | tf_op jit(solution)/shard_map/ppermute | solution.py:215
  182.7 12.9 %collective-permute-start.31 = (bf16[128,768]{1,0:T(8,128)(2,1)}, bf16[128,768]{1,0:T(8,128)(2,1)}, u32[]{:S(2)}, u32[]{:S(2)}) collective-permute-start(bf16[128,768]{1,0:T(8,128)(2,1)} %get-tuple-element.69), channel_id=1, source_target_pairs={{0,16},{1,17},{2,18},{3,19},{4,20},{5,21},{6,22},{7,23},{8,24},{9,... | collective-permute-start | bytes 589832 | tf_op jit(solution)/shard_map/ppermute | solution.py:215
  188.5 7.1 %collective-permute-start.30 = (bf16[128,768]{1,0:T(8,128)(2,1)S(1)}, bf16[128,768]{1,0:T(8,128)(2,1)S(1)}, u32[]{:S(2)}, u32[]{:S(2)}) collective-permute-start(bf16[128,768]{1,0:T(8,128)(2,1)S(1)} %copy-done.31), channel_id=1, source_target_pairs={{0,8},{1,9},{2,10},{3,11},{4,12},{5,13},{6,14},{7,15},{8,16},{9,17... | collective-permute-start | bytes 589832 | tf_op jit(solution)/shard_map/ppermute | solution.py:215
  198.3 46.9 %collective-permute-start.33 = (bf16[128,768]{1,0:T(8,128)(2,1)}, bf16[128,768]{1,0:T(8,128)(2,1)}, u32[]{:S(2)}, u32[]{:S(2)}) collective-permute-start(bf16[128,768]{1,0:T(8,128)(2,1)} %get-tuple-element.87), channel_id=1, source_target_pairs={{0,0},{1,1},{2,8},{3,9},{4,16},{5,17},{6,24},{7,25},{8,2},{9,3},{1... | collective-permute-start | bytes 589832 | tf_op jit(solution)/shard_map/ppermute | solution.py:215
  218.6 14.9 %collective-permute-start.50 = (f32[4,24,768]{2,1,0:T(8,128)}, f32[4,24,768]{2,1,0:T(8,128)}, u32[]{:S(2)}, u32[]{:S(2)}) collective-permute-start(f32[4,24,768]{2,1,0:T(8,128)} %dynamic-slice_bitcast_fusion.2), channel_id=1, source_target_pairs={{0,1},{1,0},{2,3},{3,2},{4,5},{5,4},{6,7},{7,6},{8,9},{9,8},{10,11... | collective-permute-start | bytes 884744 | tf_op jit(solution)/shard_map/ppermute | solution.py:215
  233.0 14.2 %collective-permute-start.38 = (bf16[2,4,128,192]{3,2,1,0:T(8,128)(2,1)}, bf16[2,4,128,192]{3,2,1,0:T(8,128)(2,1)}, u32[]{:S(2)}, u32[]{:S(2)}) collective-permute-start(bf16[2,4,128,192]{3,2,1,0:T(8,128)(2,1)} %fusion.24), channel_id=1, source_target_pairs={{0,1},{1,0},{2,3},{3,2},{4,5},{5,4},{6,7},{7,6},{8,9},{9,8},{10,11... | collective-permute-start | bytes 1179656 | tf_op jit(solution)/shard_map/ppermute | solution.py:215
  235.2 9.9 %collective-permute-start.51 = (bf16[24,768]{1,0:T(8,128)(2,1)}, bf16[24,768]{1,0:T(8,128)(2,1)}, u32[]{:S(2)}, u32[]{:S(2)}) collective-permute-start(bf16[24,768]{1,0:T(8,128)(2,1)} %get-tuple-element.114), channel_id=1, source_target_pairs={{0,2},{1,3},{2,4},{3,5},{4,6},{5,7},{6,0},{7,1},{8,10},{9,11},{10,... | collective-permute-start | bytes 110600 | tf_op jit(solution)/shard_map/ppermute | solution.py:215
  235.2 10.4 %collective-permute-start.52 = (bf16[24,768]{1,0:T(8,128)(2,1)}, bf16[24,768]{1,0:T(8,128)(2,1)}, u32[]{:S(2)}, u32[]{:S(2)}) collective-permute-start(bf16[24,768]{1,0:T(8,128)(2,1)} %get-tuple-element.113), channel_id=1, source_target_pairs={{0,4},{1,5},{2,6},{3,7},{4,0},{5,1},{6,2},{7,3},{8,12},{9,13},{10,... | collective-permute-start | bytes 110600 | tf_op jit(solution)/shard_map/ppermute | solution.py:215
  238.7 6.9 %collective-permute-start.53 = (bf16[24,768]{1,0:T(8,128)(2,1)}, bf16[24,768]{1,0:T(8,128)(2,1)}, u32[]{:S(2)}, u32[]{:S(2)}) collective-permute-start(bf16[24,768]{1,0:T(8,128)(2,1)} %get-tuple-element.112), channel_id=1, source_target_pairs={{0,6},{1,7},{2,0},{3,1},{4,2},{5,3},{6,4},{7,5},{8,14},{9,15},{10,... | collective-permute-start | bytes 110600 | tf_op jit(solution)/shard_map/ppermute | solution.py:215
  245.1 24.0 %collective-permute-start.54 = (f32[4,4,24,768]{3,2,1,0:T(8,128)}, f32[4,4,24,768]{3,2,1,0:T(8,128)}, u32[]{:S(2)}, u32[]{:S(2)}) collective-permute-start(f32[4,4,24,768]{3,2,1,0:T(8,128)} %dynamic-slice_bitcast_fusion.1), channel_id=1, source_target_pairs={{0,1},{1,0},{2,3},{3,2},{4,5},{5,4},{6,7},{7,6},{8,9},{9,8},{10,11... | collective-permute-start | bytes 3538952 | tf_op jit(solution)/shard_map/ppermute | solution.py:215
  245.1 43.0 %collective-permute-start.61 = (f32[4,96,768]{2,1,0:T(8,128)}, f32[4,96,768]{2,1,0:T(8,128)}, u32[]{:S(2)}, u32[]{:S(2)}) collective-permute-start(f32[4,96,768]{2,1,0:T(8,128)} %dynamic-slice_bitcast_fusion), channel_id=1, source_target_pairs={{0,1},{1,0},{2,3},{3,2},{4,5},{5,4},{6,7},{7,6},{8,9},{9,8},{10,11... | collective-permute-start | bytes 3538952 | tf_op jit(solution)/shard_map/ppermute | solution.py:215
  253.4 12.1 %collective-permute-start.41 = (bf16[128,768]{1,0:T(8,128)(2,1)}, bf16[128,768]{1,0:T(8,128)(2,1)}, u32[]{:S(2)}, u32[]{:S(2)}) collective-permute-start(bf16[128,768]{1,0:T(8,128)(2,1)} %get-tuple-element.62), channel_id=1, source_target_pairs={{0,24},{1,25},{2,26},{3,27},{4,28},{5,29},{6,30},{7,31},{8,0},{9,1... | collective-permute-start | bytes 589832 | tf_op jit(solution)/shard_map/ppermute | solution.py:215
  254.8 11.1 %collective-permute-start.40 = (bf16[128,768]{1,0:T(8,128)(2,1)}, bf16[128,768]{1,0:T(8,128)(2,1)}, u32[]{:S(2)}, u32[]{:S(2)}) collective-permute-start(bf16[128,768]{1,0:T(8,128)(2,1)} %get-tuple-element.63), channel_id=1, source_target_pairs={{0,16},{1,17},{2,18},{3,19},{4,20},{5,21},{6,22},{7,23},{8,24},{9,... | collective-permute-start | bytes 589832 | tf_op jit(solution)/shard_map/ppermute | solution.py:215
  255.3 10.6 %collective-permute-start.39 = (bf16[128,768]{1,0:T(8,128)(2,1)}, bf16[128,768]{1,0:T(8,128)(2,1)}, u32[]{:S(2)}, u32[]{:S(2)}) collective-permute-start(bf16[128,768]{1,0:T(8,128)(2,1)} %get-tuple-element.61), channel_id=1, source_target_pairs={{0,8},{1,9},{2,10},{3,11},{4,12},{5,13},{6,14},{7,15},{8,16},{9,17... | collective-permute-start | bytes 589832 | tf_op jit(solution)/shard_map/ppermute | solution.py:215
  269.0 48.1 %collective-permute-start.43 = (f32[4,4,32,576]{3,2,1,0:T(8,128)S(1)}, f32[4,4,32,576]{3,2,1,0:T(8,128)S(1)}, u32[]{:S(2)}, u32[]{:S(2)}) collective-permute-start(f32[4,4,32,576]{3,2,1,0:T(8,128)S(1)} %fusion.10), channel_id=1, source_target_pairs={{0,1},{1,0},{2,3},{3,2},{4,5},{5,4},{6,7},{7,6},{8,9},{9,8},{10,11... | collective-permute-start | bytes 3538952 | tf_op jit(solution)/shard_map/ppermute | solution.py:215
  270.7 20.0 %collective-permute-start.57 = (bf16[4,24,768]{2,1,0:T(8,128)(2,1)S(1)}, bf16[4,24,768]{2,1,0:T(8,128)(2,1)S(1)}, u32[]{:S(2)}, u32[]{:S(2)}) collective-permute-start(bf16[4,24,768]{2,1,0:T(8,128)(2,1)S(1)} %get-tuple-element.80), channel_id=1, source_target_pairs={{0,6},{1,7},{2,0},{3,1},{4,2},{5,3},{6,4},{7,5},{8,14},{9,15},{10,... | collective-permute-start | bytes 442376 | tf_op jit(solution)/shard_map/ppermute | solution.py:215
  281.9 25.4 %collective-permute-start.56 = (bf16[4,24,768]{2,1,0:T(8,128)(2,1)S(1)}, bf16[4,24,768]{2,1,0:T(8,128)(2,1)S(1)}, u32[]{:S(2)}, u32[]{:S(2)}) collective-permute-start(bf16[4,24,768]{2,1,0:T(8,128)(2,1)S(1)} %get-tuple-element.81), channel_id=1, source_target_pairs={{0,4},{1,5},{2,6},{3,7},{4,0},{5,1},{6,2},{7,3},{8,12},{9,13},{10,... | collective-permute-start | bytes 442376 | tf_op jit(solution)/shard_map/ppermute | solution.py:215
  288.1 19.1 %collective-permute-start.55 = (bf16[4,24,768]{2,1,0:T(8,128)(2,1)S(1)}, bf16[4,24,768]{2,1,0:T(8,128)(2,1)S(1)}, u32[]{:S(2)}, u32[]{:S(2)}) collective-permute-start(bf16[4,24,768]{2,1,0:T(8,128)(2,1)S(1)} %get-tuple-element.79), channel_id=1, source_target_pairs={{0,2},{1,3},{2,4},{3,5},{4,6},{5,7},{6,0},{7,1},{8,10},{9,11},{10,... | collective-permute-start | bytes 442376 | tf_op jit(solution)/shard_map/ppermute | solution.py:215
  289.6 19.3 %collective-permute-start.62 = (bf16[96,768]{1,0:T(8,128)(2,1)S(1)}, bf16[96,768]{1,0:T(8,128)(2,1)S(1)}, u32[]{:S(2)}, u32[]{:S(2)}) collective-permute-start(bf16[96,768]{1,0:T(8,128)(2,1)S(1)} %get-tuple-element.78), channel_id=1, source_target_pairs={{0,2},{1,3},{2,4},{3,5},{4,6},{5,7},{6,0},{7,1},{8,10},{9,11},{10,... | collective-permute-start | bytes 442376 | tf_op jit(solution)/shard_map/ppermute | solution.py:215
  290.7 21.0 %collective-permute-start.63 = (bf16[96,768]{1,0:T(8,128)(2,1)S(1)}, bf16[96,768]{1,0:T(8,128)(2,1)S(1)}, u32[]{:S(2)}, u32[]{:S(2)}) collective-permute-start(bf16[96,768]{1,0:T(8,128)(2,1)S(1)} %get-tuple-element.77), channel_id=1, source_target_pairs={{0,4},{1,5},{2,6},{3,7},{4,0},{5,1},{6,2},{7,3},{8,12},{9,13},{10,... | collective-permute-start | bytes 442376 | tf_op jit(solution)/shard_map/ppermute | solution.py:215
  307.2 5.6 %collective-permute-start.64 = (bf16[96,768]{1,0:T(8,128)(2,1)S(1)}, bf16[96,768]{1,0:T(8,128)(2,1)S(1)}, u32[]{:S(2)}, u32[]{:S(2)}) collective-permute-start(bf16[96,768]{1,0:T(8,128)(2,1)S(1)} %get-tuple-element.76), channel_id=1, source_target_pairs={{0,6},{1,7},{2,0},{3,1},{4,2},{5,3},{6,4},{7,5},{8,14},{9,15},{10,... | collective-permute-start | bytes 442376 | tf_op jit(solution)/shard_map/ppermute | solution.py:215
  307.5 6.4 %collective-permute-start.58 = (bf16[2,24,768]{2,1,0:T(8,128)(2,1)S(1)}, bf16[2,24,768]{2,1,0:T(8,128)(2,1)S(1)}, u32[]{:S(2)}, u32[]{:S(2)}) collective-permute-start(bf16[2,24,768]{2,1,0:T(8,128)(2,1)S(1)} %get-tuple-element.96), channel_id=1, source_target_pairs={{0,24},{1,25},{2,26},{3,27},{4,28},{5,29},{6,30},{7,31},{8,0},{9,1... | collective-permute-start | bytes 221192 | tf_op jit(solution)/shard_map/ppermute | solution.py:215
  308.9 5.0 %collective-permute-start.59 = (bf16[2,24,768]{2,1,0:T(8,128)(2,1)S(1)}, bf16[2,24,768]{2,1,0:T(8,128)(2,1)S(1)}, u32[]{:S(2)}, u32[]{:S(2)}) collective-permute-start(bf16[2,24,768]{2,1,0:T(8,128)(2,1)S(1)} %get-tuple-element.97), channel_id=1, source_target_pairs={{0,16},{1,17},{2,18},{3,19},{4,20},{5,21},{6,22},{7,23},{8,24},{9,... | collective-permute-start | bytes 221192 | tf_op jit(solution)/shard_map/ppermute | solution.py:215
  311.8 5.3 %collective-permute-start.60 = (bf16[2,24,768]{2,1,0:T(8,128)(2,1)S(1)}, bf16[2,24,768]{2,1,0:T(8,128)(2,1)S(1)}, u32[]{:S(2)}, u32[]{:S(2)}) collective-permute-start(bf16[2,24,768]{2,1,0:T(8,128)(2,1)S(1)} %get-tuple-element.95), channel_id=1, source_target_pairs={{0,8},{1,9},{2,10},{3,11},{4,12},{5,13},{6,14},{7,15},{8,16},{9,17... | collective-permute-start | bytes 221192 | tf_op jit(solution)/shard_map/ppermute | solution.py:215
  317.3 8.3 %collective-permute-start.46 = (bf16[4,32,576]{2,1,0:T(8,128)(2,1)S(1)}, bf16[4,32,576]{2,1,0:T(8,128)(2,1)S(1)}, u32[]{:S(2)}, u32[]{:S(2)}) collective-permute-start(bf16[4,32,576]{2,1,0:T(8,128)(2,1)S(1)} %get-tuple-element.71), channel_id=1, source_target_pairs={{0,6},{1,7},{2,0},{3,1},{4,2},{5,3},{6,4},{7,5},{8,14},{9,15},{10,... | collective-permute-start | bytes 442376 | tf_op jit(solution)/shard_map/ppermute | solution.py:215
  320.9 12.8 %collective-permute-start.45 = (bf16[4,32,576]{2,1,0:T(8,128)(2,1)S(1)}, bf16[4,32,576]{2,1,0:T(8,128)(2,1)S(1)}, u32[]{:S(2)}, u32[]{:S(2)}) collective-permute-start(bf16[4,32,576]{2,1,0:T(8,128)(2,1)S(1)} %get-tuple-element.72), channel_id=1, source_target_pairs={{0,4},{1,5},{2,6},{3,7},{4,0},{5,1},{6,2},{7,3},{8,12},{9,13},{10,... | collective-permute-start | bytes 442376 | tf_op jit(solution)/shard_map/ppermute | solution.py:215
  320.9 12.8 %collective-permute-start.44 = (bf16[4,32,576]{2,1,0:T(8,128)(2,1)S(1)}, bf16[4,32,576]{2,1,0:T(8,128)(2,1)S(1)}, u32[]{:S(2)}, u32[]{:S(2)}) collective-permute-start(bf16[4,32,576]{2,1,0:T(8,128)(2,1)S(1)} %get-tuple-element.70), channel_id=1, source_target_pairs={{0,2},{1,3},{2,4},{3,5},{4,6},{5,7},{6,0},{7,1},{8,10},{9,11},{10,... | collective-permute-start | bytes 442376 | tf_op jit(solution)/shard_map/ppermute | solution.py:215
  334.0 4.8 %collective-permute-start.47 = (bf16[2,32,576]{2,1,0:T(8,128)(2,1)S(1)}, bf16[2,32,576]{2,1,0:T(8,128)(2,1)S(1)}, u32[]{:S(2)}, u32[]{:S(2)}) collective-permute-start(bf16[2,32,576]{2,1,0:T(8,128)(2,1)S(1)} %get-tuple-element.89), channel_id=1, source_target_pairs={{0,24},{1,25},{2,26},{3,27},{4,28},{5,29},{6,30},{7,31},{8,0},{9,1... | collective-permute-start | bytes 221192 | tf_op jit(solution)/shard_map/ppermute | solution.py:215
  334.1 6.4 %collective-permute-start.48 = (bf16[2,32,576]{2,1,0:T(8,128)(2,1)S(1)}, bf16[2,32,576]{2,1,0:T(8,128)(2,1)S(1)}, u32[]{:S(2)}, u32[]{:S(2)}) collective-permute-start(bf16[2,32,576]{2,1,0:T(8,128)(2,1)S(1)} %get-tuple-element.90), channel_id=1, source_target_pairs={{0,16},{1,17},{2,18},{3,19},{4,20},{5,21},{6,22},{7,23},{8,24},{9,... | collective-permute-start | bytes 221192 | tf_op jit(solution)/shard_map/ppermute | solution.py:215
  337.6 5.3 %collective-permute-start.49 = (bf16[2,32,576]{2,1,0:T(8,128)(2,1)S(1)}, bf16[2,32,576]{2,1,0:T(8,128)(2,1)S(1)}, u32[]{:S(2)}, u32[]{:S(2)}) collective-permute-start(bf16[2,32,576]{2,1,0:T(8,128)(2,1)S(1)} %get-tuple-element.88), channel_id=1, source_target_pairs={{0,8},{1,9},{2,10},{3,11},{4,12},{5,13},{6,14},{7,15},{8,16},{9,17... | collective-permute-start | bytes 221192 | tf_op jit(solution)/shard_map/ppermute | solution.py:215
  (63 other events, 510.9 us)

commit v2 on v0

--- a/solution.py
+++ b/solution.py
@@ -1,8 +1,11 @@
+import functools
 import math
 
 import jax
 import jax.numpy as jnp
 from jax import lax
+from jax.experimental import pallas as pl
+from jax.experimental.pallas import tpu as pltpu
 from jax.sharding import PartitionSpec as P
 
 HEADS = 12
@@ -452,6 +455,970 @@
     return (layer_out, input_grad) + shard_grads
 
 
+bf16 = jnp.bfloat16
+f32 = jnp.float32
+SMALL = 64
+score_scale = 1.0 / math.sqrt(HEAD_DIM)
+gelu_root = math.sqrt(2.0 / math.pi)
+gelu_cube = 0.044715
+SMEM = pl.BlockSpec(memory_space=pltpu.SMEM)
+
+
+def dot(a, b, ca=1, cb=0):
+    return lax.dot_general(a, b, (((ca,), (cb,)), ((), ())), preferred_element_type=f32)
+
+
+def norm_parts(values):
+    row_mean = jnp.mean(values, -1, keepdims=True)
+    centred = values - row_mean
+    row_var = jnp.mean(centred * centred, -1, keepdims=True)
+    scale = lax.rsqrt(row_var + epsilon)
+    return centred * scale, scale
+
+
+def norm_back(normal, scale, gain, grad):
+    scaled = grad * gain
+    return scale * (
+        scaled
+        - jnp.mean(scaled, -1, keepdims=True)
+        - normal * jnp.mean(scaled * normal, -1, keepdims=True)
+    )
+
+
+def head_mask(rows, width, head):
+    lane = lax.broadcasted_iota(jnp.int32, (rows, width), 1)
+    return (lane >= head * HEAD_DIM) & (lane < (head + 1) * HEAD_DIM)
+
+
+class Held:
+    def __init__(self, ref, copy):
+        self.ref, self.copy = ref, copy
+        self.shape, self.dtype = ref.shape, ref.dtype
+
+    def __getitem__(self, at):
+        if self.copy is not None:
+            self.copy.wait()
+            self.copy = None
+        return self.ref[at]
+
+
+class Made:
+    def __init__(self, ref, copy):
+        self.ref, self.copy = ref, copy
+        self.shape, self.dtype = ref.shape, ref.dtype
+        self.flushed = False
+
+    def __getitem__(self, at):
+        return self.ref[at]
+
+    def __setitem__(self, at, value):
+        self.ref[at] = value
+
+    def flush(self):
+        if not self.flushed:
+            self.copy.start()
+            self.flushed = True
+
+
+COST = 1.0
+
+
+def run(kernel, outs, *args, scalars=(), scratch=(), us=1.0, name=None):
+    shapes = [jax.ShapeDtypeStruct(shape, dtype) for shape, dtype in outs]
+    far = [k for k in range(len(args)) if k not in scalars]
+
+    def body(*refs):
+        ins, refs = list(refs[: len(args)]), refs[len(args) :]
+        targets, refs = refs[: len(outs)], refs[len(outs) :]
+        own, refs = refs[: len(scratch)], refs[len(scratch) :]
+        held, refs = refs[: len(far)], refs[len(far) :]
+        made, (in_sems, out_sems) = refs[: len(outs)], refs[len(outs) :]
+        for n, k in enumerate(far):
+            copy = pltpu.make_async_copy(ins[k], held[n], in_sems.at[n])
+            copy.start()
+            ins[k] = Held(held[n], copy)
+        results = [
+            Made(made[n], pltpu.make_async_copy(made[n], targets[n], out_sems.at[n]))
+            for n in range(len(outs))
+        ]
+        kernel(*ins, *results, *own)
+        for k in far:
+            if ins[k].copy is not None:
+                ins[k].copy.wait()
+        for result in results:
+            result.flush()
+        for result in results:
+            result.copy.wait()
+
+    hbm = pl.BlockSpec(memory_space=pltpu.HBM)
+    return pl.pallas_call(
+        body,
+        out_shape=shapes,
+        in_specs=[SMEM if k in scalars else hbm for k in range(len(args))],
+        out_specs=[hbm] * len(outs),
+        scratch_shapes=list(scratch)
+        + [pltpu.VMEM(args[k].shape, args[k].dtype) for k in far]
+        + [pltpu.VMEM(out.shape, out.dtype) for out in shapes]
+        + [
+            pltpu.SemaphoreType.DMA((max(len(far), 1),)),
+            pltpu.SemaphoreType.DMA((len(outs),)),
+        ],
+        compiler_params=pltpu.CompilerParams(vmem_limit_bytes=62 * 1024 * 1024),
+        cost_estimate=pl.CostEstimate(
+            flops=int(us * COST * 1e9), bytes_accessed=int(us * COST * 3.5e6), transcendentals=0
+        ),
+        name=name,
+    )(*args)
+
+
+def where_am_i(group):
+    place = lax.axis_index("seq")
+    return lax.axis_index("dp"), place // group, place % group
+
+
+def ties_of(tie_refs):
+    ranks = len(tie_refs)
+    rank = lax.axis_index("dp")
+
+    def tie_of(seq):
+        step = lax.rem(seq + ranks - rank, ranks)
+        tie = tie_refs[0][0]
+        for k in range(1, ranks):
+            tie = jnp.where(step == k, tie_refs[k][0], tie)
+        return tie
+
+    return tie_of
+
+
+def flat_rows(value):
+    return value.astype(f32).reshape(-1, value.shape[-1]).astype(value.dtype)
+
+
+def pack_kernel(group, ranks, *refs):
+    tie_of, refs = ties_of(refs[:ranks]), refs[ranks:]
+    qkv_ref, out_w_ref, near_ref = refs[:3]
+    vectors, out_ref, cols_refs = refs[3:11], refs[11], refs[12:]
+    ties, rows, _ = qkv_ref.shape
+    planes = ranks
+    model = qkv_ref.shape[2] // 3
+    width = model // ranks
+    rank, plane, member = where_am_i(group)
+    shape = (16, SMALL)
+    eye = lax.broadcasted_iota(jnp.int32, shape, 0) == lax.broadcasted_iota(jnp.int32, shape, 1)
+    eye = jnp.where(eye, 1.0, 0.0).astype(bf16)
+    blocks = []
+    for tie in range(ties):
+        lines = []
+        for ref in vectors:
+            line = ref[tie : tie + 1].astype(f32)
+            for at in range(line.shape[1] // rows):
+                lines.append(line[:, at * rows : (at + 1) * rows])
+        lines.append(jnp.zeros((16 - len(lines), rows), f32))
+        small = dot(jnp.concatenate(lines, 0).astype(bf16), eye, 0, 0)
+        blocks.append(small)
+    for seq in range(planes):
+        tie = tie_of(seq)
+        small = blocks[0]
+        for block in range(1, ties):
+            small = jnp.where(tie == block, blocks[block], small)
+        small = small.astype(bf16)
+        qkv = qkv_ref[tie]
+        for to in range(ranks):
+            cols = [
+                qkv[:, k * model + to * width : k * model + (to + 1) * width] for k in range(3)
+            ]
+            out_ref[to * planes + seq] = jnp.concatenate(cols + [small], 1)
+    out_ref.flush()
+    for step, ref in enumerate(cols_refs):
+        tie = tie_of(lax.rem(plane + step, planes))
+        here = out_w_ref[tie].astype(f32)
+        there = near_ref[tie].astype(f32)
+        first = jnp.where(member == 0, here, there)
+        second = jnp.where(member == 0, there, here)
+        ref[...] = jnp.concatenate([first, second], 0).astype(bf16)
+
+
+def pack_late_kernel(ranks, *refs):
+    tie_of = ties_of(refs[:ranks])
+    fc_ref, proj_ref, fc_out_ref, proj_out_ref = refs[ranks:]
+    planes = proj_out_ref.shape[0]
+    part = fc_ref.shape[2] // ranks
+    for seq in range(planes):
+        fc = fc_ref[tie_of(seq)]
+        for to in range(ranks):
+            fc_out_ref[to * planes + seq] = fc[:, to * part : (to + 1) * part]
+    fc_out_ref.flush()
+    for seq in range(planes):
+        proj_out_ref[seq] = proj_ref[tie_of(seq)]
+
+
+def project_kernel(group, x_ref, *refs):
+    w_refs, refs = refs[:group], refs[group:]
+    sel_ref, bsel_ref, mask_ref, q_ref, kv_ref, h_ref, vec_ref, fcb_ref, w_ref = refs
+    ranks, size, width = q_ref.shape
+    part = fcb_ref.shape[1]
+    normal, _ = norm_parts(x_ref[...].astype(f32))
+    rows = w_ref.shape[0] // group
+    for slot, ref in enumerate(w_refs):
+        w_ref[slot * rows : (slot + 1) * rows] = flat_rows(ref[...])
+    w_ref.flush()
+    small = w_ref[:, 3 * width :]
+    spread = dot(small, sel_ref[...], 0, 0)[:16]
+    normed = (normal * spread[0:1] + spread[1:2]).astype(bf16)
+    normed = dot(normed, sel_ref[...], 1, 1).astype(bf16)
+    mixed = dot(normed, w_ref[:, : 3 * width])
+    biases = jnp.sum(dot(small, bsel_ref[...], 0, 0)[:16] * mask_ref[...], 0, keepdims=True)
+    bias = biases[:, part:]
+    kv_ref[0] = mixed[:, width : 2 * width].astype(bf16).reshape(ranks, size, width)
+    value = (mixed[:, 2 * width :] + bias[:, width:]).astype(bf16)
+    kv_ref[1] = value.reshape(ranks, size, width)
+    kv_ref.flush()
+    query = (mixed[:, :width] + bias[:, :width]).astype(bf16) * jnp.asarray(score_scale, bf16)
+    q_ref[...] = query.reshape(ranks, size, width)
+    h_ref[...] = normed
+    vec_ref[...] = spread[:8]
+    fcb_ref[...] = jnp.broadcast_to(biases[:, :part], fcb_ref.shape)
+
+
+def attend_kernel(group, q_ref, *refs):
+    rank, plane, _ = where_am_i(group)
+    kv_refs, refs = refs[:group], refs[group:]
+    chunks, size, width = q_ref.shape
+    w_refs, refs = refs[:chunks], refs[chunks:]
+    a_ref, w_ref, sums_refs, sums_ref = refs[0], refs[1], refs[2:-1], refs[-1]
+    for chunk in range(chunks):
+        count = (chunk + 1) * size
+        keys = jnp.concatenate([r[0, : chunk + 1].reshape(count, width) for r in kv_refs], 0)
+        values = jnp.concatenate([r[1, : chunk + 1].reshape(count, width) for r in kv_refs], 0)
+        values_t = values.T
+        query = q_ref[chunk]
+        parts = []
+        for head in range(width // HEAD_DIM):
+            part = jnp.where(head_mask(size, width, head), query, jnp.zeros_like(query))
+            scores = dot(keys, part, 1, 1)
+            top = jnp.max(scores, 0, keepdims=True)
+            raised = jnp.exp(scores - top)
+            total = jnp.sum(raised, 0, keepdims=True)
+            mixed = dot(values_t[head * HEAD_DIM : (head + 1) * HEAD_DIM], raised.astype(bf16))
+            parts.append(mixed / total)
+        a_ref[chunk * size : (chunk + 1) * size] = jnp.concatenate(parts, 0).T.astype(bf16)
+    a_ref.flush()
+    step = w_ref.shape[0] // chunks
+    for k, ref in enumerate(w_refs):
+        start = pl.multiple_of(lax.rem(plane + chunks - k, chunks) * step, 16)
+        w_ref[pl.ds(start, step)] = ref[...]
+    sums = dot(a_ref[...], w_ref[...]).astype(bf16)
+    sums_ref[...] = sums.reshape(sums_ref.shape)
+    for k, ref in enumerate(sums_refs):
+        ref[...] = sums_ref[lax.rem(rank + k, chunks)]
+        ref.flush()
+
+
+def join_kernel(ranks, *refs):
+    parts, (x_ref, vec_ref, sel_ref, r_ref, h_ref) = refs[:ranks], refs[ranks:]
+    total = x_ref[...].astype(f32) + vec_ref[2:3]
+    for ref in parts:
+        total = total + ref[...].astype(f32)
+    r_ref[...] = total
+    r_ref.flush()
+    normal, _ = norm_parts(total)
+    normed = (normal * vec_ref[3:4] + vec_ref[4:5]).astype(bf16)
+    h_ref[...] = dot(normed, sel_ref[...], 1, 1).astype(bf16)
+
+
+def mlp_kernel(group, ranks, h_ref, *refs):
+    f_refs, refs = refs[:group], refs[group:]
+    fcb_ref, refs = refs[0], refs[1:]
+    g_refs, refs = refs[:ranks], refs[ranks:]
+    p_refs, refs = refs[:group], refs[group:]
+    sel_ref, refs = refs[0], refs[1:]
+    dh_refs, refs = refs[:ranks], refs[ranks:]
+    y_ref, g_ref, hid_ref, pre_ref, wf_ref, wp_ref, dh_ref = refs
+    size = y_ref.shape[1]
+    planes, hid_rows, model = p_refs[0].shape
+    rank, _, member = where_am_i(group)
+    rows = wf_ref.shape[0] // group
+    for slot, ref in enumerate(f_refs):
+        wf_ref[slot * rows : (slot + 1) * rows] = flat_rows(ref[...])
+    value = dot(h_ref[...], wf_ref[...]) + fcb_ref[0:1]
+    for slot, ref in enumerate(p_refs):
+        for plane in range(planes):
+            at = plane * group + lax.rem(member + slot, group)
+            start = pl.multiple_of(at * hid_rows, 16)
+            wp_ref[pl.ds(start, hid_rows)] = ref[plane]
+    for k, ref in enumerate(g_refs):
+        start = pl.multiple_of(lax.rem(rank + k, ranks) * size, size)
+        g_ref[pl.ds(start, size)] = ref[...]
+    g_ref.flush()
+    grad = dot(g_ref[...], wp_ref[...], 1, 1)
+    squared = value * value
+    bent = jnp.tanh(gelu_root * value * (1.0 + gelu_cube * squared))
+    half = 0.5 * (1.0 + bent)
+    slope = half + (0.5 * gelu_root) * value * (1.0 - bent * bent) * (
+        1.0 + 3.0 * gelu_cube * squared
+    )
+    pre_ref[...] = (grad * slope).astype(bf16)
+    pre_ref.flush()
+    below = dot(pre_ref[...], wf_ref[...], 1, 1).astype(bf16)
+    dh_ref[...] = dot(below, sel_ref[...]).astype(bf16).reshape(ranks, size, model)
+    for k, ref in enumerate(dh_refs):
+        ref[...] = dh_ref[lax.rem(rank + k, ranks)]
+        ref.flush()
+    hid_ref[...] = (value * half).astype(bf16)
+    hid_ref.flush()
+    y_ref[...] = dot(hid_ref[...], wp_ref[...]).astype(bf16).reshape(ranks, size, model)
+
+
+def mlp_grad_kernel(group, planes, h_ref, pre_ref, hid_ref, g_ref, *refs):
+    out_refs, fcb_ref, scr_ref = refs[:group], refs[group], refs[group + 1]
+    half = scr_ref.shape[0] // group
+    whole = dot(h_ref[...], pre_ref[...], 0, 0)
+    for slot, ref in enumerate(out_refs):
+        ref[:half] = whole[slot * half : (slot + 1) * half].astype(ref.dtype)
+    scr_ref[...] = dot(hid_ref[...], g_ref[...], 0, 0)
+    member = where_am_i(group)[2]
+    hid_rows = half // planes
+    for slot in range(group - 1, -1, -1):
+        ref = out_refs[slot]
+        for plane in range(planes):
+            at = plane * group + lax.rem(member + slot, group)
+            start = pl.multiple_of(at * hid_rows, 16)
+            to = half + plane * hid_rows
+            ref[to : to + hid_rows] = scr_ref[pl.ds(start, hid_rows)].astype(ref.dtype)
+        ref.flush()
+    fcb_ref[...] = jnp.broadcast_to(
+        jnp.sum(pre_ref[...].astype(f32), 0, keepdims=True), fcb_ref.shape
+    )
+
+
+def add_late_kernel(group, *refs):
+    parts, (fc_ref, proj_ref) = refs[:group], refs[group:]
+    total = parts[0][...]
+    for ref in parts[1:]:
+        total = total + ref[...].astype(f32)
+    half = total.shape[0] // 2
+    proj_ref[...] = total[half:].reshape(proj_ref.shape).astype(bf16)
+    proj_ref.flush()
+    fc_ref[...] = total[:half].reshape(fc_ref.shape).astype(bf16)
+
+
+def join_back_kernel(ranks, *refs):
+    parts, (r_ref, g_ref, vec_ref, dr_ref, low_ref, sums_ref) = refs[:ranks], refs[ranks:]
+    normal, scale = norm_parts(r_ref[...])
+    upstream = g_ref[...].astype(f32)
+    grad = parts[0][...].astype(f32)
+    for ref in parts[1:]:
+        grad = grad + ref[...].astype(f32)
+    total = upstream + norm_back(normal, scale, vec_ref[3:4], grad)
+    low_ref[...] = total.astype(bf16)
+    low_ref.flush()
+    dr_ref[...] = total
+    dr_ref.flush()
+    sums_ref[...] = jnp.concatenate(
+        [
+            jnp.sum(total, 0, keepdims=True),
+            jnp.sum(grad * normal, 0, keepdims=True),
+            jnp.sum(grad, 0, keepdims=True),
+            jnp.sum(upstream, 0, keepdims=True),
+        ]
+        + [jnp.zeros((4, total.shape[1]), f32)],
+        0,
+    )
+
+
+def layer_kernel(parts_ref, r_ref, vec_ref, out_ref):
+    total = r_ref[...] + vec_ref[5:6]
+    for rank in range(parts_ref.shape[0]):
+        total = total + parts_ref[rank].astype(f32)
+    out_ref[...] = total.astype(bf16)
+
+
+def attend_back_kernel(group, low_ref, wo_ref, q_ref, *refs):
+    kv_refs, refs = refs[:group], refs[group:]
+    a_ref, refs = refs[0], refs[1:]
+    dkv_refs, dq_ref, dwo_refs, (scr_ref, wo_scr) = (
+        refs[:group],
+        refs[group],
+        refs[group + 1 : -2],
+        refs[-2:],
+    )
+    chunks, size, width = q_ref.shape
+    heads = width // HEAD_DIM
+    grad_all_rows = dot(low_ref[...], wo_ref[...], 1, 1).astype(bf16)
+    for chunk in range(chunks - 1, -1, -1):
+        count = (chunk + 1) * size
+        keys = jnp.concatenate([r[0, : chunk + 1].reshape(count, width) for r in kv_refs], 0)
+        values = jnp.concatenate([r[1, : chunk + 1].reshape(count, width) for r in kv_refs], 0)
+        keys_t = keys.T
+        query = q_ref[chunk]
+        grad = grad_all_rows[chunk * size : (chunk + 1) * size]
+        parts, probs_all, grads_all, query_all, grad_all = [], [], [], [], []
+        for head in range(heads):
+            lanes = head_mask(size, width, head)
+            query_part = jnp.where(lanes, query, jnp.zeros_like(query))
+            grad_part = jnp.where(lanes, grad, jnp.zeros_like(grad))
+            scores = dot(keys, query_part, 1, 1)
+            top = jnp.max(scores, 0, keepdims=True)
+            raised = jnp.exp(scores - top)
+            probs = raised * (1.0 / jnp.sum(raised, 0, keepdims=True))
+            grad_probs = dot(values, grad_part, 1, 1)
+            delta = jnp.sum(probs * grad_probs, 0, keepdims=True)
+            grad_scores = (probs * (grad_probs - delta)).astype(bf16)
+            parts.append(dot(keys_t[head * HEAD_DIM : (head + 1) * HEAD_DIM], grad_scores))
+            probs_all.append(probs.astype(bf16))
+            grads_all.append(grad_scores)
+            query_all.append(query_part)
+            grad_all.append(grad_part)
+        dq_ref[chunk * size : (chunk + 1) * size] = (
+            jnp.concatenate(parts, 0).T * score_scale
+        ).astype(bf16)
+        both = (
+            dot(jnp.concatenate(grads_all, 1), jnp.concatenate(query_all, 0)),
+            dot(jnp.concatenate(probs_all, 1), jnp.concatenate(grad_all, 0)),
+        )
+        for slot in range(group):
+            for k in range(2):
+                value = both[k][slot * count : (slot + 1) * count].reshape(chunk + 1, size, width)
+                if chunk == chunks - 1:
+                    scr_ref[slot, k] = value
+                else:
+                    scr_ref[slot, k, : chunk + 1] = scr_ref[slot, k, : chunk + 1] + value
+    for slot in range(group - 1, -1, -1):
+        dkv_refs[slot][...] = scr_ref[slot].astype(dkv_refs[slot].dtype)
+        dkv_refs[slot].flush()
+    dq_ref.flush()
+    wo_scr[...] = dot(a_ref[...], low_ref[...], 0, 0).reshape(wo_scr.shape)
+    for slot in range(group - 1, -1, -1):
+        owner = lax.rem(where_am_i(group)[2] + slot, group)
+        for plane in range(wo_scr.shape[0]):
+            dwo_refs[slot][plane] = wo_scr[plane, owner].astype(dwo_refs[slot].dtype)
+
+
+def first_kernel(group, ranks, dq_ref, *refs):
+    dkv_refs, refs = refs[:group], refs[group:]
+    w_ref, sel_ref, refs = refs[0], refs[1], refs[2:]
+    dwo_refs, refs = refs[:group], refs[group:]
+    proj_ref, refs = refs[0], refs[1:]
+    dh_refs, (dh_ref, mix_ref, late_ref) = refs[:ranks], refs[ranks:]
+    tokens, width = dq_ref.shape
+    model = sel_ref.shape[0]
+    size = tokens // ranks
+    low = [dq_ref[...]]
+    for k in range(2):
+        total = dkv_refs[0][k]
+        for ref in dkv_refs[1:]:
+            total = total + ref[k].astype(f32)
+        low.append(total.reshape(tokens, width).astype(bf16))
+    mixed = jnp.concatenate(low, 1)
+    mix_ref[...] = mixed
+    mix_ref.flush()
+    below = dot(mixed, w_ref[:, : 3 * width], 1, 1).astype(bf16)
+    dh_ref[...] = dot(below, sel_ref[...]).astype(bf16).reshape(ranks, size, model)
+    for k, ref in enumerate(dh_refs):
+        ref[...] = dh_ref[lax.rem(where_am_i(group)[0] + k, ranks)]
+        ref.flush()
+    dh_ref.flush()
+    total = dwo_refs[0][...]
+    for ref in dwo_refs[1:]:
+        total = total + ref[...].astype(f32)
+    hid_rows = proj_ref.shape[1]
+    rest = late_ref.shape[1] - hid_rows - total.shape[1]
+    for plane in range(total.shape[0]):
+        late_ref[plane, :hid_rows] = proj_ref[plane]
+        late_ref[plane, hid_rows:] = jnp.concatenate(
+            [total[plane], jnp.zeros((rest, model), f32)], 0
+        ).astype(bf16)
+
+
+def first_grad_kernel(
+    group, h_ref, mix_ref, x_ref, dh_ref, sums_ref, fcb_ref, mask_ref, sel_ref, bsel_ref, *refs
+):
+    ranks, size, model = dh_ref.shape
+    width = mix_ref.shape[1] // 3
+    part = fcb_ref.shape[1]
+    mixed = mix_ref[...]
+    whole = dot(h_ref[...], mixed, 0, 0)
+    normal, _ = norm_parts(x_ref[...].astype(f32))
+    grad = dh_ref[...].reshape(ranks * size, model).astype(f32)
+    vec = jnp.concatenate(
+        [
+            jnp.sum(grad * normal, 0, keepdims=True),
+            jnp.sum(grad, 0, keepdims=True),
+            sums_ref[0:4],
+            jnp.zeros((2, model), f32),
+        ],
+        0,
+    )
+    cols = jnp.sum(mixed.astype(f32), 0, keepdims=True)
+    both = jnp.concatenate([cols[:, :width], cols[:, 2 * width :]], 1)
+    sums = jnp.concatenate([fcb_ref[0:1], both], 1) * mask_ref[...]
+    small = dot(sel_ref[...], vec.astype(bf16), 1, 1)
+    more = dot(bsel_ref[...], sums.astype(bf16), 1, 1)
+    rest = jnp.zeros((model, SMALL - 24), f32)
+    whole = jnp.concatenate([whole, small, more, rest], 1)
+    rows = model // group
+    for slot in range(group - 1, -1, -1):
+        refs[slot][...] = whole[slot * rows : (slot + 1) * rows].astype(refs[slot].dtype)
+        refs[slot].flush()
+
+
+def add_early_kernel(group, *refs):
+    parts, out_ref = refs[:group], refs[group]
+    total = parts[0][...]
+    for ref in parts[1:]:
+        total = total + ref[...].astype(f32)
+    out_ref[...] = total.reshape(out_ref.shape).astype(bf16)
+
+
+def last_kernel(ranks, *refs):
+    parts, (x_ref, vec_ref, dr_ref, out_ref) = refs[:ranks], refs[ranks:]
+    normal, scale = norm_parts(x_ref[...].astype(f32))
+    grad = parts[0][...].astype(f32)
+    for ref in parts[1:]:
+        grad = grad + ref[...].astype(f32)
+    out_ref[...] = (dr_ref[...] + norm_back(normal, scale, vec_ref[0:1], grad)).astype(bf16)
+
+
+def by_block(ties, parts, tie_of):
+    totals = [jnp.zeros(parts[0].shape, f32) for _ in range(ties)]
+    for seq, part in enumerate(parts):
+        value = part.astype(f32)
+        for block in range(ties):
+            totals[block] = totals[block] + jnp.where(tie_of(seq) == block, value, 0.0)
+    return totals
+
+
+def final_late_kernel(ranks, *refs):
+    tie_of = ties_of(refs[:ranks])
+    fc_in, rest_in, fc_ref, proj_ref, out_ref = refs[ranks:]
+    ties, _, inner = fc_ref.shape
+    planes = rest_in.shape[0]
+    hid_rows, rows = proj_ref.shape[1], out_ref.shape[1]
+    part = inner // ranks
+    for block, total in enumerate(by_block(ties, [rest_in[k] for k in range(planes)], tie_of)):
+        proj_ref[block] = total[:hid_rows]
+        out_ref[block] = total[hid_rows : hid_rows + rows]
+    proj_ref.flush()
+    for rank in range(ranks):
+        parts = [fc_in[rank * planes + k] for k in range(planes)]
+        for block, total in enumerate(by_block(ties, parts, tie_of)):
+            fc_ref[block, :, rank * part : (rank + 1) * part] = total
+
+
+def final_kernel(ranks, *refs):
+    tie_of = ties_of(refs[:ranks])
+    home_ref, qkv_ref, *small_refs = refs[ranks:]
+    ties, rows, wide = qkv_ref.shape
+    model = wide // 3
+    planes = home_ref.shape[0] // ranks
+    width = model // ranks
+    sums = []
+    for rank in range(ranks):
+        parts = [home_ref[rank * planes + k] for k in range(planes)]
+        sums.append(by_block(ties, parts, tie_of))
+    eye = lax.broadcasted_iota(jnp.int32, (SMALL, SMALL), 0)
+    eye = jnp.where(eye == lax.broadcasted_iota(jnp.int32, (SMALL, SMALL), 1), 1.0, 0.0)
+    eye = eye.astype(bf16)
+    for block in range(ties):
+        values = [sums[rank][block] for rank in range(ranks)]
+        qkv_ref[block] = jnp.concatenate(
+            [value[:, k * width : (k + 1) * width] for k in range(3) for value in values], 1
+        )
+        small = values[0][:, 3 * width :]
+        for value in values[1:]:
+            small = small + value[:, 3 * width :]
+        high = small.astype(bf16)
+        low = (small - high.astype(f32)).astype(bf16)
+        turned = dot(eye, high, 1, 1) + dot(eye, low, 1, 1)
+        for k in range(6):
+            small_refs[k][block : block + 1] = turned[k : k + 1]
+        small_refs[6][block : block + 1] = jnp.concatenate(
+            [turned[k : k + 1] for k in range(14, 16)], 1
+        )
+        small_refs[7][block : block + 1] = jnp.concatenate(
+            [turned[k : k + 1] for k in range(16, 20)], 1
+        )
+
+
+def fast_device(
+    n_dp,
+    n_seq,
+    tokens,
+    tie_index,
+    first_gain,
+    first_shift,
+    qkv_weight,
+    qv_bias,
+    out_weight,
+    out_bias,
+    second_gain,
+    second_shift,
+    fc_weight,
+    fc_bias,
+    proj_weight,
+    proj_bias,
+    cotangent,
+):
+    ranks, planes, group = n_dp, n_dp, n_seq // n_dp
+    axes = ("dp", "seq")
+    size, model = tokens.shape[1:]
+    ties, rows = qkv_weight.shape[:2]
+    hid_rows = proj_weight.shape[1]
+    inner = fc_weight.shape[2]
+    width = model // ranks
+    part = inner // ranks
+    count = ranks * size
+    lanes = 3 * width + SMALL
+    squads = ranks * planes
+    rank = lax.axis_index("dp")
+    place = lax.axis_index("seq")
+    plane, member = place // group, place % group
+
+    def route(where):
+        pairs = []
+        for a in range(ranks):
+            for b in range(planes):
+                for c in range(group):
+                    x, y, z = where(a, b, c)
+                    pairs.append((a * n_seq + b * group + c, x * n_seq + y * group + z))
+        return pairs
+
+    swap = route(lambda a, b, c: (b, a, c))
+    to_rank = [route(lambda a, b, c, k=k: ((a + k) % ranks, b, c)) for k in range(ranks)]
+    to_plane = [route(lambda a, b, c, k=k: (a, (b + k) % planes, c)) for k in range(planes)]
+    to_member = [route(lambda a, b, c, k=k: (a, b, (c + k) % group)) for k in range(group)]
+    same_member = [[b * group + c for b in range(planes)] for c in range(group)]
+    squad = [
+        [a * n_seq + b * group + c for a in range(ranks) for b in range(planes)]
+        for c in range(group)
+    ]
+
+    def send(values, pairs):
+        return lax.ppermute(values, axes, pairs)
+
+    def from_members(piece):
+        return [piece] + [send(piece, to_member[group - k]) for k in range(1, group)]
+
+    def over_members(parts):
+        return [parts[0]] + [send(parts[k], to_member[k]) for k in range(1, group)]
+
+    def over_planes(pieces):
+        return lax.all_to_all(pieces, "seq", 0, 0, axis_index_groups=same_member)
+
+    def over_squad(pieces):
+        return lax.all_to_all(pieces, axes, 0, 0, axis_index_groups=squad)
+
+    def scatter(parts):
+        return [parts[0]] + [send(parts[k], to_rank[k]) for k in range(1, ranks)]
+
+    def gate(value, *before):
+        return lax.optimization_barrier((value, before))[0]
+
+    ties_seen = [tie_index] + [send(tie_index, to_rank[ranks - k]) for k in range(1, ranks)]
+    scalar_ties = tuple(range(ranks))
+    near = send(out_weight, to_member[1])
+    tokens_own = send(tokens[0], swap)
+    grad_own = send(cotangent[0], swap)
+
+    early, *out_cols = run(
+        functools.partial(pack_kernel, group, ranks),
+        [((squads, rows, lanes), bf16)] + [((group * rows, model), bf16)] * planes,
+        *ties_seen,
+        qkv_weight,
+        out_weight,
+        near,
+        first_gain,
+        first_shift,
+        out_bias,
+        second_gain,
+        second_shift,
+        proj_bias,
+        qv_bias,
+        fc_bias,
+        scalars=scalar_ties,
+        us=2.0,
+        name="pack",
+    )
+    early = over_squad(early)
+    out_cols = [out_cols[0]] + [send(out_cols[k], to_plane[k]) for k in range(1, planes)]
+
+    def arrival(owner, row):
+        a, b, c = owner // n_seq, (owner % n_seq) // group, owner % group
+        slot = (c + group - member) % group
+        return (slot * squads + a * planes + b) * rows + row
+
+    flat = jnp.arange(model)
+    at_model = arrival(flat // rows, flat % rows)
+    unit = jnp.arange(part) + rank * part
+    at_fc = arrival(unit // (4 * rows), unit % rows)
+    flat_qv = jnp.arange(2 * width)
+    unit_qv = (flat_qv // width) * model + rank * width + flat_qv % width
+    at_qv = arrival(unit_qv // (2 * rows), unit_qv % rows)
+    at_bias = jnp.concatenate([at_fc, at_qv])
+    lanes_of = jnp.concatenate(
+        [
+            (jnp.arange(part) % (4 * rows)) // rows + 8,
+            (unit_qv % (2 * rows)) // rows + 6,
+        ]
+    )
+    sel = (jnp.arange(model)[:, None] == at_model[None, :]).astype(bf16)
+    bsel = (jnp.arange(model)[:, None] == at_bias[None, :]).astype(bf16)
+    row_mask = (jnp.arange(16)[:, None] == lanes_of[None, :]).astype(f32)
+
+    late_fc, late_proj = run(
+        functools.partial(pack_late_kernel, ranks),
+        [((squads, rows, part), bf16), ((planes, hid_rows, model), bf16)],
+        *ties_seen,
+        fc_weight,
+        proj_weight,
+        scalars=scalar_ties,
+        us=2.0,
+        name="pack_late",
+    )
+    tokens_all = lax.all_gather(tokens_own, "dp", axis=0, tiled=True)
+    early = gate(early, tokens_all, grad_own, sel, bsel, row_mask, late_fc, out_cols)
+    grads_seen = [grad_own] + [send(grad_own, to_rank[ranks - k]) for k in range(1, ranks)]
+    late_fc = over_squad(gate(late_fc, early))
+    early = from_members(early)
+    own = ((size, model), bf16)
+    q, kv, h_one, vec, fcb, w_early = run(
+        functools.partial(project_kernel, group),
+        [
+            ((ranks, size, width), bf16),
+            ((2, ranks, size, width), bf16),
+            ((count, model), bf16),
+            ((8, model), f32),
+            ((8, part), f32),
+            ((model, lanes), bf16),
+        ],
+        tokens_all,
+        *early,
+        sel,
+        bsel,
+        row_mask,
+        us=5.0,
+        name="project",
+    )
+    kv = from_members(kv)
+    attended, w_out, *sums = run(
+        functools.partial(attend_kernel, group),
+        [((count, width), bf16), ((width, model), bf16)] + [own] * ranks,
+        q,
+        *kv,
+        *out_cols,
+        scratch=[pltpu.VMEM((ranks, size, model), bf16)],
+        us=6.0,
+        name="attend",
+    )
+    late_proj = over_planes(gate(late_proj, attended))
+    middle, h_own = run(
+        functools.partial(join_kernel, ranks),
+        [((size, model), f32), own],
+        *scatter(sums),
+        tokens_own,
+        gate(vec, grads_seen),
+        sel,
+        us=2.0,
+        name="join",
+    )
+    late_proj = from_members(gate(late_proj, h_own))
+    late_fc = from_members(gate(late_fc, h_own))
+    h_two = lax.all_gather(h_own, "dp", axis=0, tiled=True)
+    rest = run(
+        functools.partial(mlp_kernel, group, ranks),
+        [own] * ranks
+        + [((ranks, size, model), bf16), ((count, model), bf16)]
+        + [((count, part), bf16)] * 2,
+        h_two,
+        *late_fc,
+        fcb,
+        *grads_seen,
+        *late_proj,
+        sel,
+        scratch=[
+            pltpu.VMEM((model, part), bf16),
+            pltpu.VMEM((part, model), bf16),
+            pltpu.VMEM((ranks, size, model), bf16),
+        ],
+        us=7.0,
+        name="mlp",
+    )
+    below, (layer_parts, grad_all, hidden, grad_pre) = rest[:ranks], rest[ranks:]
+    below = scatter(below)
+    half = 2 * (model // group)
+    *late, fc_sums = run(
+        functools.partial(mlp_grad_kernel, group, planes),
+        [((half, model), f32)]
+        + [((half, model), bf16)] * (group - 1)
+        + [((8, part), f32)],
+        h_two,
+        grad_pre,
+        hidden,
+        grad_all,
+        scratch=[pltpu.VMEM((part, model), f32)],
+        us=4.0,
+        name="mlp_grad",
+    )
+    late = over_members(late)
+    grad_middle, low_own, own_sums = run(
+        functools.partial(join_back_kernel, ranks),
+        [((size, model), f32), own, ((8, model), f32)],
+        *below,
+        middle,
+        grad_own,
+        vec,
+        us=30.0,
+        name="join_back",
+    )
+    late_fc, late_proj = run(
+        functools.partial(add_late_kernel, group),
+        [((squads, rows, part), bf16), ((planes, hid_rows, model), bf16)],
+        *gate(late, low_own),
+        us=2.0,
+        name="add_late",
+    )
+    low = lax.all_gather(gate(low_own, late_fc), "dp", axis=0, tiled=True)
+    late_fc = over_squad(late_fc)
+    layer_parts = lax.all_to_all(gate(layer_parts, low, late_fc), "dp", 0, 0)
+    (layer_own,) = run(
+        layer_kernel,
+        [own],
+        layer_parts,
+        middle,
+        vec,
+        us=1.0,
+        name="layer",
+    )
+    layer_out = send(layer_own, swap)[None]
+    rest = run(
+        functools.partial(attend_back_kernel, group),
+        [((2, ranks, size, width), f32)]
+        + [((2, ranks, size, width), bf16)] * (group - 1)
+        + [((count, width), bf16)]
+        + [((planes, rows, model), f32)]
+        + [((planes, rows, model), bf16)] * (group - 1),
+        low,
+        w_out,
+        q,
+        *kv,
+        attended,
+        scratch=[
+            pltpu.VMEM((group, 2, ranks, size, width), f32),
+            pltpu.VMEM((planes, group, rows, model), f32),
+        ],
+        us=10.0,
+        name="attend_back",
+    )
+    dkv, dq, dw_out = rest[:group], rest[group], rest[group + 1 :]
+    dkv = over_members(dkv)
+    dw_out = over_members(dw_out)
+    late_rows = hid_rows + (rows + 15) // 16 * 16
+    rest = run(
+        functools.partial(first_kernel, group, ranks),
+        [own] * ranks
+        + [
+            ((ranks, size, model), bf16),
+            ((count, 3 * width), bf16),
+            ((planes, late_rows, model), bf16),
+        ],
+        dq,
+        *dkv,
+        gate(w_early, layer_own),
+        sel,
+        *dw_out,
+        late_proj,
+        us=4.0,
+        name="first",
+    )
+    first_parts, (first_all, mixed, late_rest) = rest[:ranks], rest[ranks:]
+    grad_first = scatter(first_parts)
+    late_rest = over_planes(gate(late_rest, layer_parts))
+    early = run(
+        functools.partial(first_grad_kernel, group),
+        [((model // group, lanes), f32)]
+        + [((model // group, lanes), bf16)] * (group - 1),
+        h_one,
+        mixed,
+        tokens_all,
+        first_all,
+        own_sums,
+        fc_sums,
+        row_mask,
+        sel,
+        bsel,
+        us=5.0,
+        name="first_grad",
+    )
+    early = over_members(early)
+    (input_own,) = run(
+        functools.partial(last_kernel, ranks),
+        [own],
+        *grad_first,
+        tokens_own,
+        vec,
+        grad_middle,
+        us=30.0,
+        name="last",
+    )
+    (early,) = run(
+        functools.partial(add_early_kernel, group),
+        [((squads, rows, lanes), bf16)],
+        *gate(early, input_own, layer_out),
+        us=1.0,
+        name="add_early",
+    )
+    input_grad = send(input_own, swap)[None]
+    early = over_squad(early)
+    grad_fc_weight, grad_proj_weight, grad_out_weight = run(
+        functools.partial(final_late_kernel, ranks),
+        [((ties, rows, inner), f32), ((ties, hid_rows, model), f32), ((ties, rows, model), f32)],
+        *ties_seen,
+        late_fc,
+        gate(late_rest, input_own),
+        scalars=scalar_ties,
+        us=3.0,
+        name="final_late",
+    )
+    grad_qkv_weight, *small = run(
+        functools.partial(final_kernel, ranks),
+        [((ties, rows, 3 * model), f32)]
+        + [((ties, rows), f32)] * 6
+        + [((ties, 2 * rows), f32), ((ties, 4 * rows), f32)],
+        *ties_seen,
+        gate(early, grad_fc_weight),
+        scalars=scalar_ties,
+        us=1.0,
+        name="final",
+    )
+    return (
+        layer_out,
+        input_grad,
+        small[0],
+        small[1],
+        grad_qkv_weight,
+        small[6],
+        grad_out_weight,
+        small[2],
+        small[3],
+        small[4],
+        grad_fc_weight,
+        small[7],
+        grad_proj_weight,
+        small[5],
+    )
+
+
+def pick_device(n_dp, n_seq, *args):
+    tokens, qkv_weight, proj_weight = args[0], args[4], args[12]
+    size, rows, hid_rows = tokens.shape[1], qkv_weight.shape[1], proj_weight.shape[1]
+    group = n_seq // n_dp
+    whole_tiles = rows % 8 == 0 and (group * rows) % 16 == 0 and hid_rows % 16 == 0
+    one_block = tokens.shape[0] == 1 and group == 2 and size * group == BLOCK
+    if whole_tiles and one_block:
+        return fast_device(n_dp, n_seq, *args)
+    return per_device(*args)
+
+
 def solution(mesh):
     in_specs = (
         P("dp", "seq", None),
@@ -487,5 +1454,9 @@
         P(None, ("dp", "seq")),
     )
     return jax.shard_map(
-        per_device, mesh=mesh, in_specs=in_specs, out_specs=out_specs, check_vma=False
-    )
+        functools.partial(pick_device, mesh.shape["dp"], mesh.shape["seq"]),
+        mesh=mesh,
+        in_specs=in_specs,
+        out_specs=out_specs,
+        check_vma=False,
+    )

time: 1410 us -> 258 us (0.18)
  the two profiles are of different devices: /device:TPU:0 before, /device:TPU:2 now
where the time goes in v2:
time: 258 us; the launch traced here: 257 us
  Pallas kernels  82.6 us (32%)
  starting transfers between devices  78.6 us (30%)
  blocking collectives  40.6 us (16%)
  waiting for transfers between devices  39.1 us (15%)
  local copies, waits for them, and re-layouts  9.51 us (4%)
  other arithmetic  4.12 us (2%)
    pallas_call x17, Pallas kernels, run(): pl.pallas_call(body, out_shape=shapes, in_specs=[SMEM if k in scalars els...  82.6 us
    ppermute x31, starting transfers between devices, send(): return lax.ppermute(values, axes, pairs)  39.2 us
    ppermute x31, waiting for transfers between devices, send(): return lax.ppermute(values, axes, pairs)  37.3 us
    all_to_all x4, starting transfers between devices, over_squad(): return lax.all_to_all(pieces, axes, 0, 0, axis_index_groups=squad)  24.5 us
    all_gather x1, blocking collectives, fast_device(): low = lax.all_gather(gate(low_own, late_fc), 'dp', axis=0, tiled=True)  14.6 us
    all_gather x1, blocking collectives, fast_device(): h_two = lax.all_gather(h_own, 'dp', axis=0, tiled=True)  13.4 us
    all_gather x1, blocking collectives, fast_device(): tokens_all = lax.all_gather(tokens_own, 'dp', axis=0, tiled=True)  12.6 us
    unnamed x70, local copies, waits for them, and re-layouts  9.51 us
  transfers between devices with their start and end apart: 38, of which 9 were waited for; matrix products, arithmetic and copies ran while one was open for 2% of the time, Pallas kernels for 27%

profile of v2, /device:TPU:2, one launch (start us, length us, event | category | flops | bytes accessed | tf_op | source)
XLA Modules:
  0.0 256.6 jit_solution(2331078888644450176)
XLA Ops:
  0.7 1.6 collective-permute-start.2
  2.8 2.4 collective-permute-start.3
  5.2 2.5 collective-permute-start
  8.5 1.9 fusion.refs_4_.refs_8_
  10.4 4.2 %collective-permute-start.5 = (bf16[128,768]{1,0:T(8,128)(2,1)S(1)}, bf16[128,768]{1,0:T(8,128)(2,1)S(1)}, u32[]{:S(2)}, u32[]{:S(2)}) collective-permute-start(bf16[128,768]{1,0:T(8,128)(2,1)S(1)} %bitcast.7), channel_id=1, source_target_pairs={{0,0},{1,1},{2,8},{3,9},{4,16},{5,17},{6,24},{7,25},{8,2},{9,3},{1... | collective-permute-start | bytes 589832 | tf_op jit(solution)/shard_map/ppermute | solution.py:1097
  15.3 4.4 %pack.1 = (bf16[16,24,640]{2,1,0:T(8,128)(2,1)}, bf16[48,768]{1,0:T(8,128)(2,1)}, bf16[48,768]{1,0:T(8,128)(2,1)}, bf16[48,768]{1,0:T(8,128)(2,1)}, bf16[48,768]{1,0:T(8,128)(2,1)}) custom-call(s32[1]{0:T(128)S(6)} %copy.31.refs_0_, s32[1]{0:T(128)} %collective-permute-done.1.refs_1_, s32[1]{0:T(128)} %collective-permute-done.2.refs_2_, ...), custom_call_target="tpu_custom_call" | custom-call | flops 2000000000 | bytes 7000000 | tf_op jit(solution)/shard_map/pack/pallas_call | solution.py:554
  19.7 7.3 %all-to-all-start = ((bf16[16,24,640]{2,1,0:T(8,128)(2,1)}), bf16[16,24,640]{2,1,0:T(8,128)(2,1)S(1)}, u32[]{:S(2)}, u32[]{:S(2)}) async-start(bf16[16,24,640]{2,1,0:T(8,128)(2,1)} %get-tuple-element.93), calls=%async_computation | async-start | bytes 983040 | tf_op jit(solution)/shard_map/all_to_all | solution.py:1109
  27.6 1.5 fusion.1.refs_3_.refs_6_.refs_10_.refs_4_.refs_7_
  29.0 4.1 %pack_late.1 = (bf16[16,24,768]{2,1,0:T(8,128)(2,1)}, bf16[4,96,768]{2,1,0:T(8,128)(2,1)}) custom-call(s32[1]{0:T(128)S(6)} %copy.31.refs_0_, s32[1]{0:T(128)} %collective-permute-done.1.refs_1_, s32[1]{0:T(128)} %collective-permute-done.2.refs_2_, s32[1]{0:T(128)} %collective-permute-done.3.refs_3_, bf16[2,24,3072]{2,1,0:T(8,128)(2,1)} %refs_4_.3, ...), custom_call_target="tpu_custom_call" | custom-call | flops 2000000000 | bytes 7000000 | tf_op jit(solution)/shard_map/pack_late/pallas_call | solution.py:554
  33.1 1.5 collective-permute-start.6
  34.7 2.4 collective-permute-start.7
  37.0 1.5 collective-permute-start.8
  38.5 12.6 %all_gather.9.refs_0_.refs_2_ = bf16[512,768]{1,0:T(8,128)(2,1)} all-gather(bf16[128,768]{1,0:T(8,128)(2,1)S(1)} %collective-permute-done.refs_4_), channel_id=1, replica_groups=mesh['dp'=4,'seq'=8] {'dp'}, dimensions={0}, use_global_device_ids=true | all-gather | bytes 983040 | tf_op jit(solution)/shard_map/all_gather | solution.py:1178
  51.2 5.0 %all-to-all-start.1 = ((bf16[16,24,768]{2,1,0:T(8,128)(2,1)}), bf16[16,24,768]{2,1,0:T(8,128)(2,1)S(1)}, u32[]{:S(2)}, u32[]{:S(2)}) async-start(bf16[16,24,768]{2,1,0:T(8,128)(2,1)} %get-tuple-element.109), calls=%async_computation.1 | async-start | bytes 1179648 | tf_op jit(solution)/shard_map/all_to_all | solution.py:1109
  56.3 5.5 %project.1 = (bf16[4,128,192]{2,1,0:T(8,128)(2,1)}, bf16[2,4,128,192]{3,2,1,0:T(8,128)(2,1)}, bf16[512,768]{1,0:T(8,128)(2,1)}, f32[8,768]{1,0:T(8,128)}, f32[8,768]{1,0:T(8,128)}, /*index=5*/bf16[768,640]{1,0:T(8,128)(2,1)}) custom-call(bf16[512,768]{1,0:T(8,128)(2,1)} %all_gather.9.refs_0_.refs_2_, bf16[16,24,640]{2,1,0:T(8,128)(2,1)} %copy-done.5, ...), custom_call_target="tpu_custom_call" | custom-call | flops 5000000000 | bytes 17500000 | tf_op jit(solution)/shard_map/project/pallas_call | solution.py:554
  62.1 1.9 collective-permute-done.10.refs_2_.refs_4_
  64.1 0.8 copy-done.12
  64.9 7.7 %attend.1 = (bf16[512,192]{1,0:T(8,128)(2,1)}, bf16[192,768]{1,0:T(8,128)(2,1)}, bf16[128,768]{1,0:T(8,128)(2,1)}, bf16[128,768]{1,0:T(8,128)(2,1)}, bf16[128,768]{1,0:T(8,128)(2,1)}, /*index=5*/bf16[128,768]{1,0:T(8,128)(2,1)}) custom-call(bf16[4,128,192]{2,1,0:T(8,128)(2,1)} %get-tuple-element.100.refs_0_.refs_2_, ...), custom_call_target="tpu_custom_call" | custom-call | flops 6000000000 | bytes 21000000 | tf_op jit(solution)/shard_map/attend/pallas_call | solution.py:554
  72.6 4.6 %all-to-all-start.2 = ((bf16[4,96,768]{2,1,0:T(8,128)(2,1)}), bf16[4,96,768]{2,1,0:T(8,128)(2,1)S(1)}, u32[]{:S(2)}, u32[]{:S(2)}) async-start(bf16[4,96,768]{2,1,0:T(8,128)(2,1)} %get-tuple-element.114), calls=%async_computation.2 | async-start | bytes 1179648 | tf_op jit(solution)/shard_map/all_to_all | solution.py:1106
  77.2 1.5 collective-permute-start.16
  78.7 1.3 collective-permute-start.15
  80.0 0.7 collective-permute-start.14
  80.7 2.2 collective-permute-start.11
  82.9 0.7 collective-permute-start.12
  83.6 1.3 collective-permute-done.16.refs_7_
  85.0 2.3 collective-permute-start.13
  87.3 3.2 %collective-permute-done.15.refs_6_ = bf16[128,768]{1,0:T(8,128)(2,1)S(1)} collective-permute-done((bf16[128,768]{1,0:T(8,128)(2,1)S(1)}, bf16[128,768]{1,0:T(8,128)(2,1)S(1)}, u32[]{:S(2)}, u32[]{:S(2)}) %collective-permute-start.15) | collective-permute-done | bytes 196640 | tf_op jit(solution)/shard_map/ppermute | solution.py:1097
  90.5 3.1 %collective-permute-done.11.refs_1_ = bf16[128,768]{1,0:T(8,128)(2,1)} collective-permute-done((bf16[128,768]{1,0:T(8,128)(2,1)}, bf16[128,768]{1,0:T(8,128)(2,1)}, u32[]{:S(2)}, u32[]{:S(2)}) %collective-permute-start.11) | collective-permute-done | bytes 196640 | tf_op jit(solution)/shard_map/ppermute | solution.py:1097
  93.5 4.3 %collective-permute-done.12.refs_2_ = bf16[128,768]{1,0:T(8,128)(2,1)} collective-permute-done((bf16[128,768]{1,0:T(8,128)(2,1)}, bf16[128,768]{1,0:T(8,128)(2,1)}, u32[]{:S(2)}, u32[]{:S(2)}) %collective-permute-start.12) | collective-permute-done | bytes 196640 | tf_op jit(solution)/shard_map/ppermute | solution.py:1097
  97.9 3.0 %join.1 = (f32[128,768]{1,0:T(8,128)}, bf16[128,768]{1,0:T(8,128)(2,1)}) custom-call(bf16[128,768]{1,0:T(8,128)(2,1)} %get-tuple-element.102.refs_0_, bf16[128,768]{1,0:T(8,128)(2,1)} %collective-permute-done.11.refs_1_, bf16[128,768]{1,0:T(8,128)(2,1)} %collective-permute-done.12.refs_2_, bf16[128,768]{1,0:T(8,128)(2,1)} %collective-permute-done.13.refs_3_, ...), custom_call_target="tpu_custom_call" | custom-call | flops 2000000000 | bytes 7000000 | tf_op jit(solution)/shard_map/join/pallas_call | solution.py:554
  101.5 13.4 %all_gather.10.refs_0_ = bf16[512,768]{1,0:T(8,128)(2,1)} all-gather(bf16[128,768]{1,0:T(8,128)(2,1)} %get-tuple-element.108), channel_id=1, replica_groups=mesh['dp'=4,'seq'=8] {'dp'}, dimensions={0}, use_global_device_ids=true | all-gather | bytes 983040 | tf_op jit(solution)/shard_map/all_gather | solution.py:1226
  115.0 0.8 copy-done.11
  115.9 7.1 %mlp.1 = (bf16[128,768]{1,0:T(8,128)(2,1)}, bf16[128,768]{1,0:T(8,128)(2,1)}, bf16[128,768]{1,0:T(8,128)(2,1)}, bf16[128,768]{1,0:T(8,128)(2,1)}, bf16[4,128,768...) custom-call(bf16[512,768]{1,0:T(8,128)(2,1)} %all_gather.10.refs_0_, ...), custom_call_target="tpu_custom_call" | custom-call | flops 7000000000 | bytes 24500000 | tf_op jit(solution)/shard_map/mlp/pallas_call | solution.py:554
  123.1 1.5 collective-permute-start.19
  124.6 0.8 collective-permute-start.20
  126.0 5.5 %mlp_grad.1 = (f32[768,768]{1,0:T(8,128)}, bf16[768,768]{1,0:T(8,128)(2,1)}, f32[8,768]{1,0:T(8,128)}) custom-call(bf16[512,768]{1,0:T(8,128)(2,1)} %all_gather.10.refs_0_, bf16[512,768]{1,0:T(8,128)(2,1)} %get-tuple-element.123.refs_1_, bf16[512,768]{1,0:T(8,128)(2,1)} %get-tuple-element.124.refs_2_, bf16[512,768]{1,0:T(8,128)(2,1)} %get-tuple-element.125.refs_3_), custom_call_target="tpu_custom_call" | custom-call | flops 4000000000 | bytes 14000000 | tf_op jit(solution)/shard_map/mlp_grad/pallas_call | solution.py:554
  131.6 2.9 %collective-permute-done.20.refs_2_ = bf16[128,768]{1,0:T(8,128)(2,1)S(1)} collective-permute-done((bf16[128,768]{1,0:T(8,128)(2,1)}, bf16[128,768]{1,0:T(8,128)(2,1)S(1)}, u32[]{:S(2)}, u32[]{:S(2)}) %collective-permute-start.20) | collective-permute-done | bytes 196640 | tf_op jit(solution)/shard_map/ppermute | solution.py:1097
  135.3 2.9 %join_back.1 = (f32[128,768]{1,0:T(8,128)}, bf16[128,768]{1,0:T(8,128)(2,1)}, f32[8,768]{1,0:T(8,128)}) custom-call(bf16[128,768]{1,0:T(8,128)(2,1)} %get-tuple-element.117.refs_0_, bf16[128,768]{1,0:T(8,128)(2,1)} %copy-done.22, bf16[128,768]{1,0:T(8,128)(2,1)} %copy-done.23, bf16[128,768]{1,0:T(8,128)(2,1)} %copy-done.24, ...), custom_call_target="tpu_custom_call" | custom-call | flops 30000001024 | bytes 105000000 | tf_op jit(solution)/shard_map/join_back/pallas_call | solution.py:554
  138.2 1.0 copy-done.9
  139.2 3.2 %add_late.1 = (bf16[16,24,768]{2,1,0:T(8,128)(2,1)}, bf16[4,96,768]{2,1,0:T(8,128)(2,1)}) custom-call(f32[768,768]{1,0:T(8,128)} %get-tuple-element.128.refs_0_, bf16[768,768]{1,0:T(8,128)(2,1)} %copy-done.9), custom_call_target="tpu_custom_call" | custom-call | flops 2000000000 | bytes 7000000 | tf_op jit(solution)/shard_map/add_late/pallas_call | solution.py:554
  142.3 6.5 %all-to-all-start.3 = ((bf16[16,24,768]{2,1,0:T(8,128)(2,1)}), bf16[16,24,768]{2,1,0:T(8,128)(2,1)S(1)}, u32[]{:S(2)}, u32[]{:S(2)}) async-start(bf16[16,24,768]{2,1,0:T(8,128)(2,1)} %get-tuple-element.130), calls=%async_computation.3 | async-start | bytes 1179648 | tf_op jit(solution)/shard_map/all_to_all | solution.py:1109
  148.8 14.6 %all_gather.11.refs_0_ = bf16[512,768]{1,0:T(8,128)(2,1)} all-gather(bf16[128,768]{1,0:T(8,128)(2,1)S(1)} %copy-done.8), channel_id=1, replica_groups=mesh['dp'=4,'seq'=8] {'dp'}, dimensions={0}, use_global_device_ids=true | all-gather | bytes 983040 | tf_op jit(solution)/shard_map/all_gather | solution.py:1280
  163.5 5.5 %all-to-all-start.4 = ((bf16[4,128,768]{2,1,0:T(8,128)(2,1)}), bf16[4,128,768]{2,1,0:T(8,128)(2,1)S(1)}, u32[]{:S(2)}, u32[]{:S(2)}) async-start(bf16[4,128,768]{2,1,0:T(8,128)(2,1)} %get-tuple-element.132), calls=%async_computation.4 | async-start | bytes 1572864 | tf_op jit(solution)/shard_map/all_to_all | solution.py:1282
  169.0 11.9 %attend_back.1 = (f32[2,4,128,192]{3,2,1,0:T(8,128)}, bf16[2,4,128,192]{3,2,1,0:T(8,128)(2,1)}, bf16[512,192]{1,0:T(8,128)(2,1)}, f32[4,24,768]{2,1,0:T(8,128)}, bf16[4,24,768]{2,1,0:T(8,128)(2,1)}) custom-call(bf16[512,768]{1,0:T(8,128)(2,1)} %all_gather.11.refs_0_, bf16[192,768]{1,0:T(8,128)(2,1)} %get-tuple-element.133.refs_1_, ...), custom_call_target="tpu_custom_call" | custom-call | flops 10000000000 | bytes 35000000 | tf_op jit(solution)/shard_map/attend_back/pallas_call | solution.py:554
  181.5 0.9 copy-done.1
  182.4 2.1 layer.1
  184.5 2.8 %collective-permute-start.23 = (bf16[128,768]{1,0:T(8,128)(2,1)}, bf16[128,768]{1,0:T(8,128)(2,1)S(1)}, u32[]{:S(2)}, u32[]{:S(2)}) collective-permute-start(bf16[128,768]{1,0:T(8,128)(2,1)} %layer.1), channel_id=1, source_target_pairs={{0,0},{1,1},{2,8},{3,9},{4,16},{5,17},{6,24},{7,25},{8,2},{9,3},{1... | collective-permute-start | bytes 589832 | tf_op jit(solution)/shard_map/ppermute | solution.py:1097
  188.1 5.4 %first.1 = (bf16[128,768]{1,0:T(8,128)(2,1)}, bf16[128,768]{1,0:T(8,128)(2,1)}, bf16[128,768]{1,0:T(8,128)(2,1)}, bf16[128,768]{1,0:T(8,128)(2,1)}, bf16[4,128,7...) custom-call(bf16[512,192]{1,0:T(8,128)(2,1)} %get-tuple-element.134.refs_0_, ...), custom_call_target="tpu_custom_call" | custom-call | flops 4000000000 | bytes 14000000 | tf_op jit(solution)/shard_map/first/pallas_call | solution.py:554
  193.5 4.8 %all-to-all-start.6 = ((bf16[4,128,768]{2,1,0:T(8,128)(2,1)}), bf16[4,128,768]{2,1,0:T(8,128)(2,1)S(1)}, u32[]{:S(2)}, u32[]{:S(2)}) async-start(bf16[4,128,768]{2,1,0:T(8,128)(2,1)} %get-tuple-element.157), calls=%async_computation.6 | async-start | bytes 1572864 | tf_op jit(solution)/shard_map/all_to_all | solution.py:1106
  198.3 0.9 collective-permute-start.26
  199.2 2.4 collective-permute-start.27
  201.6 6.2 %first_grad.1 = (f32[384,640]{1,0:T(8,128)}, bf16[384,640]{1,0:T(8,128)(2,1)}) custom-call(bf16[512,768]{1,0:T(8,128)(2,1)} %get-tuple-element.147.refs_0_, bf16[512,576]{1,0:T(8,128)(2,1)} %get-tuple-element.148.refs_1_, bf16[512,768]{1,0:T(8,128)(2,1)} %all_gather.9.refs_0_.refs_2_, bf16[4,128,768]{2,1,0:T(8,128)(2,1)} %get-tuple-element.149.refs_3_, ...), custom_call_target="tpu_custom_call" | custom-call | flops 5000000000 | bytes 17500000 | tf_op jit(solution)/shard_map/first_grad/pallas_call | solution.py:554
  207.9 2.4 collective-permute-done.27.refs_2_
  211.0 2.6 %last.1 = bf16[128,768]{1,0:T(8,128)(2,1)} custom-call(bf16[128,768]{1,0:T(8,128)(2,1)} %get-tuple-element.142.refs_0_, bf16[128,768]{1,0:T(8,128)(2,1)} %copy-done.20, bf16[128,768]{1,0:T(8,128)(2,1)} %copy-done.21, bf16[128,768]{1,0:T(8,128)(2,1)} %collective-permute-done.28.refs_3_, bf16[128,768]{1,0:T(8,128)(2,1)} %copy-done.7, ...), custom_call_target="tpu_custom_call" | custom-call | flops 30000001024 | bytes 105000000 | tf_op jit(solution)/shard_map/last/pallas_call | solution.py:554
  213.6 0.8 copy-done.14
  214.4 2.3 add_early.1
  216.7 1.8 all-to-all-done.6.refs_5_
  218.4 5.7 %all-to-all-start.5 = ((bf16[16,24,640]{2,1,0:T(8,128)(2,1)}), bf16[16,24,640]{2,1,0:T(8,128)(2,1)S(1)}, u32[]{:S(2)}, u32[]{:S(2)}) async-start(bf16[16,24,640]{2,1,0:T(8,128)(2,1)} %add_early.1), calls=%async_computation.5 | async-start | bytes 983040 | tf_op jit(solution)/shard_map/all_to_all | solution.py:1109
  224.2 3.4 %collective-permute-start.29 = (bf16[128,768]{1,0:T(8,128)(2,1)S(1)}, bf16[128,768]{1,0:T(8,128)(2,1)S(1)}, u32[]{:S(2)}, u32[]{:S(2)}) collective-permute-start(bf16[128,768]{1,0:T(8,128)(2,1)S(1)} %copy-done.25), channel_id=1, source_target_pairs={{0,0},{1,1},{2,8},{3,9},{4,16},{5,17},{6,24},{7,25},{8,2},{9,3},{1... | collective-permute-start | bytes 589832 | tf_op jit(solution)/shard_map/ppermute | solution.py:1097
  227.5 18.1 %collective-permute-done.29 = bf16[128,768]{1,0:T(8,128)(2,1)S(1)} collective-permute-done((bf16[128,768]{1,0:T(8,128)(2,1)S(1)}, bf16[128,768]{1,0:T(8,128)(2,1)S(1)}, u32[]{:S(2)}, u32[]{:S(2)}) %collective-permute-start.29) | collective-permute-done | bytes 196640 | tf_op jit(solution)/shard_map/ppermute | solution.py:1097
  245.6 4.6 %final_late.1 = (f32[2,24,3072]{2,1,0:T(8,128)}, f32[2,96,768]{2,1,0:T(8,128)}, f32[2,24,768]{2,1,0:T(8,128)}) custom-call(s32[1]{0:T(128)S(6)} %copy.31.refs_0_, s32[1]{0:T(128)} %collective-permute-done.1.refs_1_, s32[1]{0:T(128)} %collective-permute-done.2.refs_2_, s32[1]{0:T(128)} %collective-permute-done.3.refs_3_, bf16[16,24,768]{2,1,0:T(8,128)(2,1)} %copy-done.2, ...), custom_call_target="tpu_custom_call" | custom-call | flops 3000000000 | bytes 10500000 | tf_op jit(solution)/shard_map/final_late/pallas_call | solution.py:554
  250.2 0.8 copy-done.6
  251.0 4.2 %final.1 = (f32[2,24,2304]{2,1,0:T(8,128)}, f32[2,24]{1,0:T(2,128)}, f32[2,24]{1,0:T(2,128)}, f32[2,24]{1,0:T(2,128)}, f32[2,24]{1,0:T(2,128)}, /*index=5*/f32[2...) custom-call(s32[1]{0:T(128)S(6)} %copy.31.refs_0_, s32[1]{0:T(128)} %collective-permute-done.1.refs_1_, ...), custom_call_target="tpu_custom_call" | custom-call | flops 1000000000 | bytes 3500000 | tf_op jit(solution)/shard_map/final/pallas_call | solution.py:554
  255.2 0.7 copy.32
  (111 shorter events, 7.4 us)
Async XLA Ops:
  0.6 9.8 %copy-start.15 = (bf16[1,128,768]{2,1,0:T(8,128)(2,1)S(1)}, bf16[1,128,768]{2,1,0:T(8,128)(2,1)}, u32[]{:S(2)}) copy-start(bf16[1,128,768]{2,1,0:T(8,128)(2,1)} %param.29) | copy-start | bytes 589828
  0.7 9.8 %collective-permute-start.2 = (s32[1]{0:T(128)}, s32[1]{0:T(128)}, u32[]{:S(2)}, u32[]{:S(2)}) collective-permute-start(s32[1]{0:T(128)} %param.16), channel_id=1, source_target_pairs={{0,16},{1,17},{2,18},{3,19},{4,20},{5,21},{6,22},{7,23},{8,24},{9,... | collective-permute-start | bytes 20 | tf_op jit(solution)/shard_map/ppermute | solution.py:1097
  2.2 12.4 %collective-permute-start.1 = (s32[1]{0:T(128)}, s32[1]{0:T(128)}, u32[]{:S(2)}, u32[]{:S(2)}) collective-permute-start(s32[1]{0:T(128)} %param.16), channel_id=1, source_target_pairs={{0,24},{1,25},{2,26},{3,27},{4,28},{5,29},{6,30},{7,31},{8,0},{9,1... | collective-permute-start | bytes 20 | tf_op jit(solution)/shard_map/ppermute | solution.py:1097
  2.8 11.9 %collective-permute-start.3 = (s32[1]{0:T(128)}, s32[1]{0:T(128)}, u32[]{:S(2)}, u32[]{:S(2)}) collective-permute-start(s32[1]{0:T(128)} %param.16), channel_id=1, source_target_pairs={{0,8},{1,9},{2,10},{3,11},{4,12},{5,13},{6,14},{7,15},{8,16},{9,17... | collective-permute-start | bytes 20 | tf_op jit(solution)/shard_map/ppermute | solution.py:1097
  5.2 9.5 %collective-permute-start.4 = (bf16[2,24,768]{2,1,0:T(8,128)(2,1)}, bf16[2,24,768]{2,1,0:T(8,128)(2,1)S(1)}, u32[]{:S(2)}, u32[]{:S(2)}) collective-permute-start(bf16[2,24,768]{2,1,0:T(8,128)(2,1)} %refs_5_.2), channel_id=1, source_target_pairs={{0,1},{1,0},{2,3},{3,2},{4,5},{5,4},{6,7},{7,6},{8,9},{9,8},{10,11... | collective-permute-start | bytes 221192 | tf_op jit(solution)/shard_map/ppermute | solution.py:1097
  5.2 33.3 %collective-permute-start = (bf16[128,768]{1,0:T(8,128)(2,1)}, bf16[128,768]{1,0:T(8,128)(2,1)S(1)}, u32[]{:S(2)}, u32[]{:S(2)}) collective-permute-start(bf16[128,768]{1,0:T(8,128)(2,1)} %bitcast.6), channel_id=1, source_target_pairs={{0,0},{1,1},{2,8},{3,9},{4,16},{5,17},{6,24},{7,25},{8,2},{9,3},{1... | collective-permute-start | bytes 589832 | tf_op jit(solution)/shard_map/ppermute | solution.py:1097
  10.4 40.7 %collective-permute-start.5 = (bf16[128,768]{1,0:T(8,128)(2,1)S(1)}, bf16[128,768]{1,0:T(8,128)(2,1)S(1)}, u32[]{:S(2)}, u32[]{:S(2)}) collective-permute-start(bf16[128,768]{1,0:T(8,128)(2,1)S(1)} %bitcast.7), channel_id=1, source_target_pairs={{0,0},{1,1},{2,8},{3,9},{4,16},{5,17},{6,24},{7,25},{8,2},{9,3},{1... | collective-permute-start | bytes 589832 | tf_op jit(solution)/shard_map/ppermute | solution.py:1097
  19.7 31.5 %all-to-all-start = ((bf16[16,24,640]{2,1,0:T(8,128)(2,1)}), bf16[16,24,640]{2,1,0:T(8,128)(2,1)S(1)}, u32[]{:S(2)}, u32[]{:S(2)}) async-start(bf16[16,24,640]{2,1,0:T(8,128)(2,1)} %get-tuple-element.93), calls=%async_computation | async-start | bytes 983040 | tf_op jit(solution)/shard_map/all_to_all | solution.py:1109
  29.0 4.1 %copy-start.33 = (bf16[48,768]{1,0:T(8,128)(2,1)S(1)}, bf16[48,768]{1,0:T(8,128)(2,1)}, u32[]{:S(2)}) copy-start(bf16[48,768]{1,0:T(8,128)(2,1)} %get-tuple-element.96) | copy-start | bytes 221188
  29.0 5.6 %copy-start.32 = (bf16[48,768]{1,0:T(8,128)(2,1)S(1)}, bf16[48,768]{1,0:T(8,128)(2,1)}, u32[]{:S(2)}) copy-start(bf16[48,768]{1,0:T(8,128)(2,1)} %get-tuple-element.97) | copy-start | bytes 221188
  29.0 8.0 %copy-start.31 = (bf16[48,768]{1,0:T(8,128)(2,1)S(1)}, bf16[48,768]{1,0:T(8,128)(2,1)}, u32[]{:S(2)}) copy-start(bf16[48,768]{1,0:T(8,128)(2,1)} %get-tuple-element.98) | copy-start | bytes 221188
  33.1 17.9 %collective-permute-start.6 = (bf16[48,768]{1,0:T(8,128)(2,1)S(1)}, bf16[48,768]{1,0:T(8,128)(2,1)S(1)}, u32[]{:S(2)}, u32[]{:S(2)}) collective-permute-start(bf16[48,768]{1,0:T(8,128)(2,1)S(1)} %copy-done.33), channel_id=1, source_target_pairs={{0,2},{1,3},{2,4},{3,5},{4,6},{5,7},{6,0},{7,1},{8,10},{9,11},{10,... | collective-permute-start | bytes 221192 | tf_op jit(solution)/shard_map/ppermute | solution.py:1097
  34.7 16.4 %collective-permute-start.7 = (bf16[48,768]{1,0:T(8,128)(2,1)S(1)}, bf16[48,768]{1,0:T(8,128)(2,1)S(1)}, u32[]{:S(2)}, u32[]{:S(2)}) collective-permute-start(bf16[48,768]{1,0:T(8,128)(2,1)S(1)} %copy-done.32), channel_id=1, source_target_pairs={{0,4},{1,5},{2,6},{3,7},{4,0},{5,1},{6,2},{7,3},{8,12},{9,13},{10,... | collective-permute-start | bytes 221192 | tf_op jit(solution)/shard_map/ppermute | solution.py:1097
  37.0 14.1 %collective-permute-start.8 = (bf16[48,768]{1,0:T(8,128)(2,1)S(1)}, bf16[48,768]{1,0:T(8,128)(2,1)S(1)}, u32[]{:S(2)}, u32[]{:S(2)}) collective-permute-start(bf16[48,768]{1,0:T(8,128)(2,1)S(1)} %copy-done.31), channel_id=1, source_target_pairs={{0,6},{1,7},{2,0},{3,1},{4,2},{5,3},{6,4},{7,5},{8,14},{9,15},{10,... | collective-permute-start | bytes 221192 | tf_op jit(solution)/shard_map/ppermute | solution.py:1097
  38.5 23.3 %copy-start.7 = (bf16[128,768]{1,0:T(8,128)(2,1)}, bf16[128,768]{1,0:T(8,128)(2,1)S(1)}, u32[]{:S(2)}) copy-start(bf16[128,768]{1,0:T(8,128)(2,1)S(1)} %collective-permute-done.refs_4_) | copy-start | bytes 589828
  51.1 10.8 %copy-start.28 = (bf16[48,768]{1,0:T(8,128)(2,1)}, bf16[48,768]{1,0:T(8,128)(2,1)S(1)}, u32[]{:S(2)}) copy-start(bf16[48,768]{1,0:T(8,128)(2,1)S(1)} %collective-permute-done.6.refs_4_) | copy-start | bytes 221188
  51.1 10.8 %copy-start.29 = (bf16[48,768]{1,0:T(8,128)(2,1)}, bf16[48,768]{1,0:T(8,128)(2,1)S(1)}, u32[]{:S(2)}) copy-start(bf16[48,768]{1,0:T(8,128)(2,1)S(1)} %collective-permute-done.7.refs_5_) | copy-start | bytes 221188
  51.1 10.7 %copy-start.30 = (bf16[48,768]{1,0:T(8,128)(2,1)}, bf16[48,768]{1,0:T(8,128)(2,1)S(1)}, u32[]{:S(2)}) copy-start(bf16[48,768]{1,0:T(8,128)(2,1)S(1)} %collective-permute-done.8.refs_6_) | copy-start | bytes 221188
  51.1 28.8 %copy-start.16 = (bf16[128,768]{1,0:T(8,128)(2,1)}, bf16[128,768]{1,0:T(8,128)(2,1)S(1)}, u32[]{:S(2)}) copy-start(bf16[128,768]{1,0:T(8,128)(2,1)S(1)} %collective-permute-done.5.refs_4_.refs_5_) | copy-start | bytes 589828
  51.2 5.1 %copy-start.5 = (bf16[16,24,640]{2,1,0:T(8,128)(2,1)}, bf16[16,24,640]{2,1,0:T(8,128)(2,1)S(1)}, u32[]{:S(2)}) copy-start(bf16[16,24,640]{2,1,0:T(8,128)(2,1)S(1)} %all-to-all-done.refs_1_) | copy-start | bytes 1474564
  51.2 5.1 %collective-permute-start.9 = (bf16[16,24,640]{2,1,0:T(8,128)(2,1)S(1)}, bf16[16,24,640]{2,1,0:T(8,128)(2,1)}, u32[]{:S(2)}, u32[]{:S(2)}) collective-permute-start(bf16[16,24,640]{2,1,0:T(8,128)(2,1)S(1)} %all-to-all-done.refs_1_), channel_id=1, source_target_pairs={{0,1},{1,0},{2,3},{3,2},{4,5},{5,4},{6,7},{7,6},{8,9},{9,8},{10,11... | collective-permute-start | bytes 1474568 | tf_op jit(solution)/shard_map/ppermute | solution.py:1097
  51.2 21.3 %all-to-all-start.1 = ((bf16[16,24,768]{2,1,0:T(8,128)(2,1)}), bf16[16,24,768]{2,1,0:T(8,128)(2,1)S(1)}, u32[]{:S(2)}, u32[]{:S(2)}) async-start(bf16[16,24,768]{2,1,0:T(8,128)(2,1)} %get-tuple-element.109), calls=%async_computation.1 | async-start | bytes 1179648 | tf_op jit(solution)/shard_map/all_to_all | solution.py:1109
  61.9 2.2 collective-permute-start.10
  72.6 28.3 %copy-start.3 = (bf16[16,24,768]{2,1,0:T(8,128)(2,1)}, bf16[16,24,768]{2,1,0:T(8,128)(2,1)S(1)}, u32[]{:S(2)}) copy-start(bf16[16,24,768]{2,1,0:T(8,128)(2,1)S(1)} %all-to-all-done.1.refs_1_) | copy-start | bytes 1769476
  72.6 28.4 %all-to-all-start.2 = ((bf16[4,96,768]{2,1,0:T(8,128)(2,1)}), bf16[4,96,768]{2,1,0:T(8,128)(2,1)S(1)}, u32[]{:S(2)}, u32[]{:S(2)}) async-start(bf16[4,96,768]{2,1,0:T(8,128)(2,1)} %get-tuple-element.114), calls=%async_computation.2 | async-start | bytes 1179648 | tf_op jit(solution)/shard_map/all_to_all | solution.py:1106
  77.2 7.8 %collective-permute-start.16 = (bf16[128,768]{1,0:T(8,128)(2,1)S(1)}, bf16[128,768]{1,0:T(8,128)(2,1)S(1)}, u32[]{:S(2)}, u32[]{:S(2)}) collective-permute-start(bf16[128,768]{1,0:T(8,128)(2,1)S(1)} %collective-permute-done.5.refs_4_.refs_5_), channel_id=1, source_target_pairs={{0,8},{1,9},{2,10},{3,11},{4,12},{5,13},{6,14},{7,15},{8,16},{9,17... | collective-permute-start | bytes 589832 | tf_op jit(solution)/shard_map/ppermute | solution.py:1097
  78.7 11.8 %collective-permute-start.15 = (bf16[128,768]{1,0:T(8,128)(2,1)S(1)}, bf16[128,768]{1,0:T(8,128)(2,1)S(1)}, u32[]{:S(2)}, u32[]{:S(2)}) collective-permute-start(bf16[128,768]{1,0:T(8,128)(2,1)S(1)} %collective-permute-done.5.refs_4_.refs_5_), channel_id=1, source_target_pairs={{0,16},{1,17},{2,18},{3,19},{4,20},{5,21},{6,22},{7,23},{8,24},{9,... | collective-permute-start | bytes 589832 | tf_op jit(solution)/shard_map/ppermute | solution.py:1097
  80.0 10.5 %collective-permute-start.14 = (bf16[128,768]{1,0:T(8,128)(2,1)S(1)}, bf16[128,768]{1,0:T(8,128)(2,1)S(1)}, u32[]{:S(2)}, u32[]{:S(2)}) collective-permute-start(bf16[128,768]{1,0:T(8,128)(2,1)S(1)} %collective-permute-done.5.refs_4_.refs_5_), channel_id=1, source_target_pairs={{0,24},{1,25},{2,26},{3,27},{4,28},{5,29},{6,30},{7,31},{8,0},{9,1... | collective-permute-start | bytes 589832 | tf_op jit(solution)/shard_map/ppermute | solution.py:1097
  80.7 12.8 %collective-permute-start.11 = (bf16[128,768]{1,0:T(8,128)(2,1)}, bf16[128,768]{1,0:T(8,128)(2,1)}, u32[]{:S(2)}, u32[]{:S(2)}) collective-permute-start(bf16[128,768]{1,0:T(8,128)(2,1)} %get-tuple-element.103), channel_id=1, source_target_pairs={{0,8},{1,9},{2,10},{3,11},{4,12},{5,13},{6,14},{7,15},{8,16},{9,17... | collective-permute-start | bytes 589832 | tf_op jit(solution)/shard_map/ppermute | solution.py:1097
  82.9 15.0 %collective-permute-start.12 = (bf16[128,768]{1,0:T(8,128)(2,1)}, bf16[128,768]{1,0:T(8,128)(2,1)}, u32[]{:S(2)}, u32[]{:S(2)}) collective-permute-start(bf16[128,768]{1,0:T(8,128)(2,1)} %get-tuple-element.104), channel_id=1, source_target_pairs={{0,16},{1,17},{2,18},{3,19},{4,20},{5,21},{6,22},{7,23},{8,24},{9,... | collective-permute-start | bytes 589832 | tf_op jit(solution)/shard_map/ppermute | solution.py:1097
  85.0 15.9 %copy-start.17 = (bf16[128,768]{1,0:T(8,128)(2,1)}, bf16[128,768]{1,0:T(8,128)(2,1)S(1)}, u32[]{:S(2)}) copy-start(bf16[128,768]{1,0:T(8,128)(2,1)S(1)} %collective-permute-done.16.refs_7_) | copy-start | bytes 589828
  85.0 12.9 %collective-permute-start.13 = (bf16[128,768]{1,0:T(8,128)(2,1)}, bf16[128,768]{1,0:T(8,128)(2,1)}, u32[]{:S(2)}, u32[]{:S(2)}) collective-permute-start(bf16[128,768]{1,0:T(8,128)(2,1)} %get-tuple-element.105), channel_id=1, source_target_pairs={{0,24},{1,25},{2,26},{3,27},{4,28},{5,29},{6,30},{7,31},{8,0},{9,1... | collective-permute-start | bytes 589832 | tf_op jit(solution)/shard_map/ppermute | solution.py:1097
  90.5 10.4 %copy-start.18 = (bf16[128,768]{1,0:T(8,128)(2,1)}, bf16[128,768]{1,0:T(8,128)(2,1)S(1)}, u32[]{:S(2)}) copy-start(bf16[128,768]{1,0:T(8,128)(2,1)S(1)} %collective-permute-done.15.refs_6_) | copy-start | bytes 589828
  90.5 10.4 %copy-start.19 = (bf16[128,768]{1,0:T(8,128)(2,1)}, bf16[128,768]{1,0:T(8,128)(2,1)S(1)}, u32[]{:S(2)}) copy-start(bf16[128,768]{1,0:T(8,128)(2,1)S(1)} %collective-permute-done.14.refs_5_) | copy-start | bytes 589828
  100.9 14.0 %collective-permute-start.17 = (bf16[16,24,768]{2,1,0:T(8,128)(2,1)S(1)}, bf16[16,24,768]{2,1,0:T(8,128)(2,1)S(1)}, u32[]{:S(2)}, u32[]{:S(2)}) collective-permute-start(bf16[16,24,768]{2,1,0:T(8,128)(2,1)S(1)} %all-to-all-done.1.refs_1_), channel_id=1, source_target_pairs={{0,1},{1,0},{2,3},{3,2},{4,5},{5,4},{6,7},{7,6},{8,9},{9,8},{10,11... | collective-permute-start | bytes 1769480 | tf_op jit(solution)/shard_map/ppermute | solution.py:1097
  101.0 14.8 %copy-start.4 = (bf16[4,96,768]{2,1,0:T(8,128)(2,1)}, bf16[4,96,768]{2,1,0:T(8,128)(2,1)S(1)}, u32[]{:S(2)}) copy-start(bf16[4,96,768]{2,1,0:T(8,128)(2,1)S(1)} %all-to-all-done.2.refs_8_) | copy-start | bytes 1769476
  101.0 13.9 %collective-permute-start.18 = (bf16[4,96,768]{2,1,0:T(8,128)(2,1)S(1)}, bf16[4,96,768]{2,1,0:T(8,128)(2,1)S(1)}, u32[]{:S(2)}, u32[]{:S(2)}) collective-permute-start(bf16[4,96,768]{2,1,0:T(8,128)(2,1)S(1)} %all-to-all-done.2.refs_8_), channel_id=1, source_target_pairs={{0,1},{1,0},{2,3},{3,2},{4,5},{5,4},{6,7},{7,6},{8,9},{9,8},{10,11... | collective-permute-start | bytes 1769480 | tf_op jit(solution)/shard_map/ppermute | solution.py:1097
  114.9 1.0 copy-start.10
  115.0 0.8 copy-start.11
  123.1 8.5 %collective-permute-start.19 = (bf16[128,768]{1,0:T(8,128)(2,1)}, bf16[128,768]{1,0:T(8,128)(2,1)S(1)}, u32[]{:S(2)}, u32[]{:S(2)}) collective-permute-start(bf16[128,768]{1,0:T(8,128)(2,1)} %get-tuple-element.118), channel_id=1, source_target_pairs={{0,8},{1,9},{2,10},{3,11},{4,12},{5,13},{6,14},{7,15},{8,16},{9,17... | collective-permute-start | bytes 589832 | tf_op jit(solution)/shard_map/ppermute | solution.py:1097
  124.6 9.9 %collective-permute-start.20 = (bf16[128,768]{1,0:T(8,128)(2,1)}, bf16[128,768]{1,0:T(8,128)(2,1)S(1)}, u32[]{:S(2)}, u32[]{:S(2)}) collective-permute-start(bf16[128,768]{1,0:T(8,128)(2,1)} %get-tuple-element.119), channel_id=1, source_target_pairs={{0,16},{1,17},{2,18},{3,19},{4,20},{5,21},{6,22},{7,23},{8,24},{9,... | collective-permute-start | bytes 589832 | tf_op jit(solution)/shard_map/ppermute | solution.py:1097
  125.4 9.2 %collective-permute-start.21 = (bf16[128,768]{1,0:T(8,128)(2,1)}, bf16[128,768]{1,0:T(8,128)(2,1)S(1)}, u32[]{:S(2)}, u32[]{:S(2)}) collective-permute-start(bf16[128,768]{1,0:T(8,128)(2,1)} %get-tuple-element.120), channel_id=1, source_target_pairs={{0,24},{1,25},{2,26},{3,27},{4,28},{5,29},{6,30},{7,31},{8,0},{9,1... | collective-permute-start | bytes 589832 | tf_op jit(solution)/shard_map/ppermute | solution.py:1097
  131.5 6.7 %collective-permute-start.22 = (bf16[768,768]{1,0:T(8,128)(2,1)}, bf16[768,768]{1,0:T(8,128)(2,1)S(1)}, u32[]{:S(2)}, u32[]{:S(2)}) collective-permute-start(bf16[768,768]{1,0:T(8,128)(2,1)} %get-tuple-element.127), channel_id=1, source_target_pairs={{0,1},{1,0},{2,3},{3,2},{4,5},{5,4},{6,7},{7,6},{8,9},{9,8},{10,11... | collective-permute-start | bytes 3538952 | tf_op jit(solution)/shard_map/ppermute | solution.py:1097
  131.6 3.0 %copy-start.22 = (bf16[128,768]{1,0:T(8,128)(2,1)}, bf16[128,768]{1,0:T(8,128)(2,1)S(1)}, u32[]{:S(2)}) copy-start(bf16[128,768]{1,0:T(8,128)(2,1)S(1)} %collective-permute-done.19.refs_1_) | copy-start | bytes 589828
  138.2 1.0 copy-start.9
  139.2 9.6 %copy-start.8 = (bf16[128,768]{1,0:T(8,128)(2,1)S(1)}, bf16[128,768]{1,0:T(8,128)(2,1)}, u32[]{:S(2)}) copy-start(bf16[128,768]{1,0:T(8,128)(2,1)} %get-tuple-element.131) | copy-start | bytes 589828
  142.3 21.1 %all-to-all-start.3 = ((bf16[16,24,768]{2,1,0:T(8,128)(2,1)}), bf16[16,24,768]{2,1,0:T(8,128)(2,1)S(1)}, u32[]{:S(2)}, u32[]{:S(2)}) async-start(bf16[16,24,768]{2,1,0:T(8,128)(2,1)} %get-tuple-element.130), calls=%async_computation.3 | async-start | bytes 1179648 | tf_op jit(solution)/shard_map/all_to_all | solution.py:1109
  163.4 17.5 %copy-start.2 = (bf16[16,24,768]{2,1,0:T(8,128)(2,1)}, bf16[16,24,768]{2,1,0:T(8,128)(2,1)S(1)}, u32[]{:S(2)}) copy-start(bf16[16,24,768]{2,1,0:T(8,128)(2,1)S(1)} %all-to-all-done.3.refs_4_) | copy-start | bytes 1769476
  163.5 18.0 %all-to-all-start.4 = ((bf16[4,128,768]{2,1,0:T(8,128)(2,1)}), bf16[4,128,768]{2,1,0:T(8,128)(2,1)S(1)}, u32[]{:S(2)}, u32[]{:S(2)}) async-start(bf16[4,128,768]{2,1,0:T(8,128)(2,1)} %get-tuple-element.132), calls=%async_computation.4 | async-start | bytes 1572864 | tf_op jit(solution)/shard_map/all_to_all | solution.py:1282
  180.9 6.4 %collective-permute-start.24 = (bf16[2,4,128,192]{3,2,1,0:T(8,128)(2,1)}, bf16[2,4,128,192]{3,2,1,0:T(8,128)(2,1)S(1)}, u32[]{:S(2)}, u32[]{:S(2)}) collective-permute-start(bf16[2,4,128,192]{3,2,1,0:T(8,128)(2,1)} %get-tuple-element.136), channel_id=1, source_target_pairs={{0,1},{1,0},{2,3},{3,2},{4,5},{5,4},{6,7},{7,6},{8,9},{9,8},{10,11... | collective-permute-start | bytes 1179656 | tf_op jit(solution)/shard_map/ppermute | solution.py:1097
  181.0 6.3 %collective-permute-start.25 = (bf16[4,24,768]{2,1,0:T(8,128)(2,1)}, bf16[4,24,768]{2,1,0:T(8,128)(2,1)S(1)}, u32[]{:S(2)}, u32[]{:S(2)}) collective-permute-start(bf16[4,24,768]{2,1,0:T(8,128)(2,1)} %get-tuple-element.140), channel_id=1, source_target_pairs={{0,1},{1,0},{2,3},{3,2},{4,5},{5,4},{6,7},{7,6},{8,9},{9,8},{10,11... | collective-permute-start | bytes 442376 | tf_op jit(solution)/shard_map/ppermute | solution.py:1097
  181.5 0.9 copy-start.1
  184.5 29.1 %collective-permute-start.23 = (bf16[128,768]{1,0:T(8,128)(2,1)}, bf16[128,768]{1,0:T(8,128)(2,1)S(1)}, u32[]{:S(2)}, u32[]{:S(2)}) collective-permute-start(bf16[128,768]{1,0:T(8,128)(2,1)} %layer.1), channel_id=1, source_target_pairs={{0,0},{1,1},{2,8},{3,9},{4,16},{5,17},{6,24},{7,25},{8,2},{9,3},{1... | collective-permute-start | bytes 589832 | tf_op jit(solution)/shard_map/ppermute | solution.py:1097
  187.3 0.8 copy-start.13
  193.5 24.9 %all-to-all-start.6 = ((bf16[4,128,768]{2,1,0:T(8,128)(2,1)}), bf16[4,128,768]{2,1,0:T(8,128)(2,1)S(1)}, u32[]{:S(2)}, u32[]{:S(2)}) async-start(bf16[4,128,768]{2,1,0:T(8,128)(2,1)} %get-tuple-element.157), calls=%async_computation.6 | async-start | bytes 1572864 | tf_op jit(solution)/shard_map/all_to_all | solution.py:1106
  198.3 9.5 %collective-permute-start.26 = (bf16[128,768]{1,0:T(8,128)(2,1)}, bf16[128,768]{1,0:T(8,128)(2,1)S(1)}, u32[]{:S(2)}, u32[]{:S(2)}) collective-permute-start(bf16[128,768]{1,0:T(8,128)(2,1)} %get-tuple-element.143), channel_id=1, source_target_pairs={{0,8},{1,9},{2,10},{3,11},{4,12},{5,13},{6,14},{7,15},{8,16},{9,17... | collective-permute-start | bytes 589832 | tf_op jit(solution)/shard_map/ppermute | solution.py:1097
  199.2 11.1 %collective-permute-start.27 = (bf16[128,768]{1,0:T(8,128)(2,1)}, bf16[128,768]{1,0:T(8,128)(2,1)S(1)}, u32[]{:S(2)}, u32[]{:S(2)}) collective-permute-start(bf16[128,768]{1,0:T(8,128)(2,1)} %get-tuple-element.144), channel_id=1, source_target_pairs={{0,16},{1,17},{2,18},{3,19},{4,20},{5,21},{6,22},{7,23},{8,24},{9,... | collective-permute-start | bytes 589832 | tf_op jit(solution)/shard_map/ppermute | solution.py:1097
  201.6 8.7 %collective-permute-start.28 = (bf16[128,768]{1,0:T(8,128)(2,1)}, bf16[128,768]{1,0:T(8,128)(2,1)}, u32[]{:S(2)}, u32[]{:S(2)}) collective-permute-start(bf16[128,768]{1,0:T(8,128)(2,1)} %get-tuple-element.145), channel_id=1, source_target_pairs={{0,24},{1,25},{2,26},{3,27},{4,28},{5,29},{6,30},{7,31},{8,0},{9,1... | collective-permute-start | bytes 589832 | tf_op jit(solution)/shard_map/ppermute | solution.py:1097
  207.8 5.8 %collective-permute-start.30 = (bf16[384,640]{1,0:T(8,128)(2,1)}, bf16[384,640]{1,0:T(8,128)(2,1)S(1)}, u32[]{:S(2)}, u32[]{:S(2)}) collective-permute-start(bf16[384,640]{1,0:T(8,128)(2,1)} %get-tuple-element.153), channel_id=1, source_target_pairs={{0,1},{1,0},{2,3},{3,2},{4,5},{5,4},{6,7},{7,6},{8,9},{9,8},{10,11... | collective-permute-start | bytes 1474568 | tf_op jit(solution)/shard_map/ppermute | solution.py:1097
  207.8 2.4 copy-start.20
  214.4 9.8 %copy-start.25 = (bf16[128,768]{1,0:T(8,128)(2,1)S(1)}, bf16[128,768]{1,0:T(8,128)(2,1)}, u32[]{:S(2)}) copy-start(bf16[128,768]{1,0:T(8,128)(2,1)} %last.1) | copy-start | bytes 589828
  218.4 27.2 %copy-start = (bf16[4,128,768]{2,1,0:T(8,128)(2,1)}, bf16[4,128,768]{2,1,0:T(8,128)(2,1)S(1)}, u32[]{:S(2)}) copy-start(bf16[4,128,768]{2,1,0:T(8,128)(2,1)S(1)} %all-to-all-done.6.refs_5_) | copy-start | bytes 2359300
  218.4 31.8 %all-to-all-start.5 = ((bf16[16,24,640]{2,1,0:T(8,128)(2,1)}), bf16[16,24,640]{2,1,0:T(8,128)(2,1)S(1)}, u32[]{:S(2)}, u32[]{:S(2)}) async-start(bf16[16,24,640]{2,1,0:T(8,128)(2,1)} %add_early.1), calls=%async_computation.5 | async-start | bytes 983040 | tf_op jit(solution)/shard_map/all_to_all | solution.py:1109
  224.2 21.4 %collective-permute-start.29 = (bf16[128,768]{1,0:T(8,128)(2,1)S(1)}, bf16[128,768]{1,0:T(8,128)(2,1)S(1)}, u32[]{:S(2)}, u32[]{:S(2)}) collective-permute-start(bf16[128,768]{1,0:T(8,128)(2,1)S(1)} %copy-done.25), channel_id=1, source_target_pairs={{0,0},{1,1},{2,8},{3,9},{4,16},{5,17},{6,24},{7,25},{8,2},{9,3},{1... | collective-permute-start | bytes 589832 | tf_op jit(solution)/shard_map/ppermute | solution.py:1097
  (8 other events, 5.8 us)

commit v3 on v2

--- a/solution.py
+++ b/solution.py
@@ -462,6 +462,7 @@
 gelu_root = math.sqrt(2.0 / math.pi)
 gelu_cube = 0.044715
 SMEM = pl.BlockSpec(memory_space=pltpu.SMEM)
+VMEM = pl.BlockSpec(memory_space=pltpu.VMEM)
 
 
 def dot(a, b, ca=1, cb=0):
@@ -523,7 +524,7 @@
 COST = 1.0
 
 
-def run(kernel, outs, *args, scalars=(), scratch=(), us=1.0, name=None):
+def run(kernel, outs, *args, scalars=(), scratch=(), us=1.0, room=60, name=None):
     shapes = [jax.ShapeDtypeStruct(shape, dtype) for shape, dtype in outs]
     far = [k for k in range(len(args)) if k not in scalars]
 
@@ -550,7 +551,7 @@
         for result in results:
             result.copy.wait()
 
-    hbm = pl.BlockSpec(memory_space=pltpu.HBM)
+    hbm = pl.BlockSpec(memory_space=pl.ANY)
     return pl.pallas_call(
         body,
         out_shape=shapes,
@@ -563,12 +564,24 @@
             pltpu.SemaphoreType.DMA((max(len(far), 1),)),
             pltpu.SemaphoreType.DMA((len(outs),)),
         ],
-        compiler_params=pltpu.CompilerParams(vmem_limit_bytes=62 * 1024 * 1024),
+        compiler_params=pltpu.CompilerParams(vmem_limit_bytes=room * 1024 * 1024),
         cost_estimate=pl.CostEstimate(
             flops=int(us * COST * 1e9), bytes_accessed=int(us * COST * 3.5e6), transcendentals=0
         ),
         name=name,
     )(*args)
+
+
+def by_head(values):
+    size, width = values.shape
+    blank = jnp.zeros_like(values)
+    return jnp.concatenate(
+        [
+            jnp.where(head_mask(size, width, head), values, blank)
+            for head in range(width // HEAD_DIM)
+        ],
+        0,
+    )
 
 
 def where_am_i(group):
@@ -590,23 +603,27 @@
     return tie_of
 
 
+def one_hot(at_ref, rows):
+    at = at_ref[...]
+    row = lax.broadcasted_iota(jnp.int32, (rows, at.shape[1]), 0)
+    return jnp.where(row == at, 1.0, 0.0).astype(bf16)
+
+
 def flat_rows(value):
     return value.astype(f32).reshape(-1, value.shape[-1]).astype(value.dtype)
 
 
 def pack_kernel(group, ranks, *refs):
+    refs, scr_ref = refs[:-1], refs[-1]
     tie_of, refs = ties_of(refs[:ranks]), refs[ranks:]
-    qkv_ref, out_w_ref, near_ref = refs[:3]
-    vectors, out_ref, cols_refs = refs[3:11], refs[11], refs[12:]
+    qkv_ref, out_w_ref, vectors, out_ref, cols_ref = refs[0], refs[1], refs[2:10], refs[10], refs[11]
     ties, rows, _ = qkv_ref.shape
     planes = ranks
     model = qkv_ref.shape[2] // 3
     width = model // ranks
-    rank, plane, member = where_am_i(group)
     shape = (16, SMALL)
     eye = lax.broadcasted_iota(jnp.int32, shape, 0) == lax.broadcasted_iota(jnp.int32, shape, 1)
     eye = jnp.where(eye, 1.0, 0.0).astype(bf16)
-    blocks = []
     for tie in range(ties):
         lines = []
         for ref in vectors:
@@ -614,28 +631,22 @@
             for at in range(line.shape[1] // rows):
                 lines.append(line[:, at * rows : (at + 1) * rows])
         lines.append(jnp.zeros((16 - len(lines), rows), f32))
-        small = dot(jnp.concatenate(lines, 0).astype(bf16), eye, 0, 0)
-        blocks.append(small)
-    for seq in range(planes):
-        tie = tie_of(seq)
-        small = blocks[0]
-        for block in range(1, ties):
-            small = jnp.where(tie == block, blocks[block], small)
-        small = small.astype(bf16)
+        small = dot(jnp.concatenate(lines, 0).astype(bf16), eye, 0, 0).astype(bf16)
         qkv = qkv_ref[tie]
         for to in range(ranks):
             cols = [
                 qkv[:, k * model + to * width : k * model + (to + 1) * width] for k in range(3)
             ]
-            out_ref[to * planes + seq] = jnp.concatenate(cols + [small], 1)
+            scr_ref[tie, to] = jnp.concatenate(cols + [small], 1)
+    for seq in range(planes):
+        tie = tie_of(seq)
+        for to in range(ranks):
+            out_ref[to * planes + seq] = scr_ref[tie, to]
     out_ref.flush()
-    for step, ref in enumerate(cols_refs):
-        tie = tie_of(lax.rem(plane + step, planes))
-        here = out_w_ref[tie].astype(f32)
-        there = near_ref[tie].astype(f32)
-        first = jnp.where(member == 0, here, there)
-        second = jnp.where(member == 0, there, here)
-        ref[...] = jnp.concatenate([first, second], 0).astype(bf16)
+    blank = jnp.zeros((cols_ref.shape[1] - rows, model), f32)
+    for seq in range(planes):
+        cols = jnp.concatenate([out_w_ref[tie_of(seq)].astype(f32), blank], 0)
+        cols_ref[seq] = cols.astype(bf16)
 
 
 def pack_late_kernel(ranks, *refs):
@@ -657,17 +668,20 @@
     sel_ref, bsel_ref, mask_ref, q_ref, kv_ref, h_ref, vec_ref, fcb_ref, w_ref = refs
     ranks, size, width = q_ref.shape
     part = fcb_ref.shape[1]
+    model = x_ref.shape[1]
+    sel = one_hot(sel_ref, model)
+    bsel = one_hot(bsel_ref, model)
     normal, _ = norm_parts(x_ref[...].astype(f32))
     rows = w_ref.shape[0] // group
     for slot, ref in enumerate(w_refs):
         w_ref[slot * rows : (slot + 1) * rows] = flat_rows(ref[...])
     w_ref.flush()
     small = w_ref[:, 3 * width :]
-    spread = dot(small, sel_ref[...], 0, 0)[:16]
+    spread = dot(small, sel, 0, 0)[:16]
     normed = (normal * spread[0:1] + spread[1:2]).astype(bf16)
-    normed = dot(normed, sel_ref[...], 1, 1).astype(bf16)
+    normed = dot(normed, sel, 1, 1).astype(bf16)
     mixed = dot(normed, w_ref[:, : 3 * width])
-    biases = jnp.sum(dot(small, bsel_ref[...], 0, 0)[:16] * mask_ref[...], 0, keepdims=True)
+    biases = jnp.sum(dot(small, bsel, 0, 0)[:16] * mask_ref[...], 0, keepdims=True)
     bias = biases[:, part:]
     kv_ref[0] = mixed[:, width : 2 * width].astype(bf16).reshape(ranks, size, width)
     value = (mixed[:, 2 * width :] + bias[:, width:]).astype(bf16)
@@ -680,35 +694,41 @@
     fcb_ref[...] = jnp.broadcast_to(biases[:, :part], fcb_ref.shape)
 
 
-def attend_kernel(group, q_ref, *refs):
-    rank, plane, _ = where_am_i(group)
+def attend_kernel(group, rows, q_ref, *refs):
     kv_refs, refs = refs[:group], refs[group:]
+    cols_refs, refs = refs[:group], refs[group:]
+    a_ref, lse_ref, w_ref, sums_refs, (whole_ref, sums_ref) = *refs[:3], refs[3:-2], refs[-2:]
+    rank, _, member = where_am_i(group)
     chunks, size, width = q_ref.shape
-    w_refs, refs = refs[:chunks], refs[chunks:]
-    a_ref, w_ref, sums_refs, sums_ref = refs[0], refs[1], refs[2:-1], refs[-1]
     for chunk in range(chunks):
         count = (chunk + 1) * size
         keys = jnp.concatenate([r[0, : chunk + 1].reshape(count, width) for r in kv_refs], 0)
         values = jnp.concatenate([r[1, : chunk + 1].reshape(count, width) for r in kv_refs], 0)
         values_t = values.T
-        query = q_ref[chunk]
-        parts = []
-        for head in range(width // HEAD_DIM):
-            part = jnp.where(head_mask(size, width, head), query, jnp.zeros_like(query))
-            scores = dot(keys, part, 1, 1)
-            top = jnp.max(scores, 0, keepdims=True)
-            raised = jnp.exp(scores - top)
-            total = jnp.sum(raised, 0, keepdims=True)
-            mixed = dot(values_t[head * HEAD_DIM : (head + 1) * HEAD_DIM], raised.astype(bf16))
-            parts.append(mixed / total)
+        scores = dot(keys, by_head(q_ref[chunk]), 1, 1)
+        top = jnp.max(scores, 0, keepdims=True)
+        raised = jnp.exp(scores - top)
+        total = jnp.sum(raised, 0, keepdims=True)
+        lse_ref[chunk : chunk + 1] = top + jnp.log(total)
+        mixed = dot(values_t, raised.astype(bf16)) / total
+        parts = [
+            mixed[head * HEAD_DIM : (head + 1) * HEAD_DIM, head * size : (head + 1) * size]
+            for head in range(width // HEAD_DIM)
+        ]
         a_ref[chunk * size : (chunk + 1) * size] = jnp.concatenate(parts, 0).T.astype(bf16)
     a_ref.flush()
-    step = w_ref.shape[0] // chunks
-    for k, ref in enumerate(w_refs):
-        start = pl.multiple_of(lax.rem(plane + chunks - k, chunks) * step, 16)
-        w_ref[pl.ds(start, step)] = ref[...]
-    sums = dot(a_ref[...], w_ref[...]).astype(bf16)
-    sums_ref[...] = sums.reshape(sums_ref.shape)
+    lse_ref.flush()
+    for plane in range(cols_refs[0].shape[0]):
+        pieces = [ref[plane].astype(f32)[:rows] for ref in cols_refs]
+        for owner in range(group):
+            piece = pieces[0]
+            for slot in range(1, group):
+                here = lax.rem(member + slot, group) == owner
+                piece = jnp.where(here, pieces[slot], piece)
+            at = (plane * group + owner) * rows
+            whole_ref[at : at + rows] = piece
+    w_ref[...] = whole_ref[...].astype(bf16)
+    sums_ref[...] = dot(a_ref[...], w_ref[...]).astype(bf16).reshape(sums_ref.shape)
     for k, ref in enumerate(sums_refs):
         ref[...] = sums_ref[lax.rem(rank + k, chunks)]
         ref.flush()
@@ -723,7 +743,7 @@
     r_ref.flush()
     normal, _ = norm_parts(total)
     normed = (normal * vec_ref[3:4] + vec_ref[4:5]).astype(bf16)
-    h_ref[...] = dot(normed, sel_ref[...], 1, 1).astype(bf16)
+    h_ref[...] = dot(normed, one_hot(sel_ref, normed.shape[1]), 1, 1).astype(bf16)
 
 
 def mlp_kernel(group, ranks, h_ref, *refs):
@@ -735,7 +755,8 @@
     dh_refs, refs = refs[:ranks], refs[ranks:]
     y_ref, g_ref, hid_ref, pre_ref, wf_ref, wp_ref, dh_ref = refs
     size = y_ref.shape[1]
-    planes, hid_rows, model = p_refs[0].shape
+    planes, _, model = p_refs[0].shape
+    hid_rows = wp_ref.shape[0] // (planes * group)
     rank, _, member = where_am_i(group)
     rows = wf_ref.shape[0] // group
     for slot, ref in enumerate(f_refs):
@@ -745,7 +766,7 @@
         for plane in range(planes):
             at = plane * group + lax.rem(member + slot, group)
             start = pl.multiple_of(at * hid_rows, 16)
-            wp_ref[pl.ds(start, hid_rows)] = ref[plane]
+            wp_ref[pl.ds(start, hid_rows)] = ref[plane, :hid_rows]
     for k, ref in enumerate(g_refs):
         start = pl.multiple_of(lax.rem(rank + k, ranks) * size, size)
         g_ref[pl.ds(start, size)] = ref[...]
@@ -760,7 +781,7 @@
     pre_ref[...] = (grad * slope).astype(bf16)
     pre_ref.flush()
     below = dot(pre_ref[...], wf_ref[...], 1, 1).astype(bf16)
-    dh_ref[...] = dot(below, sel_ref[...]).astype(bf16).reshape(ranks, size, model)
+    dh_ref[...] = dot(below, one_hot(sel_ref, model)).astype(bf16).reshape(ranks, size, model)
     for k, ref in enumerate(dh_refs):
         ref[...] = dh_ref[lax.rem(rank + k, ranks)]
         ref.flush()
@@ -835,7 +856,7 @@
 
 def attend_back_kernel(group, low_ref, wo_ref, q_ref, *refs):
     kv_refs, refs = refs[:group], refs[group:]
-    a_ref, refs = refs[0], refs[1:]
+    lse_ref, a_ref, refs = refs[0], refs[1], refs[2:]
     dkv_refs, dq_ref, dwo_refs, (scr_ref, wo_scr) = (
         refs[:group],
         refs[group],
@@ -850,32 +871,21 @@
         keys = jnp.concatenate([r[0, : chunk + 1].reshape(count, width) for r in kv_refs], 0)
         values = jnp.concatenate([r[1, : chunk + 1].reshape(count, width) for r in kv_refs], 0)
         keys_t = keys.T
-        query = q_ref[chunk]
-        grad = grad_all_rows[chunk * size : (chunk + 1) * size]
-        parts, probs_all, grads_all, query_all, grad_all = [], [], [], [], []
-        for head in range(heads):
-            lanes = head_mask(size, width, head)
-            query_part = jnp.where(lanes, query, jnp.zeros_like(query))
-            grad_part = jnp.where(lanes, grad, jnp.zeros_like(grad))
-            scores = dot(keys, query_part, 1, 1)
-            top = jnp.max(scores, 0, keepdims=True)
-            raised = jnp.exp(scores - top)
-            probs = raised * (1.0 / jnp.sum(raised, 0, keepdims=True))
-            grad_probs = dot(values, grad_part, 1, 1)
-            delta = jnp.sum(probs * grad_probs, 0, keepdims=True)
-            grad_scores = (probs * (grad_probs - delta)).astype(bf16)
-            parts.append(dot(keys_t[head * HEAD_DIM : (head + 1) * HEAD_DIM], grad_scores))
-            probs_all.append(probs.astype(bf16))
-            grads_all.append(grad_scores)
-            query_all.append(query_part)
-            grad_all.append(grad_part)
+        query = by_head(q_ref[chunk])
+        grad = by_head(grad_all_rows[chunk * size : (chunk + 1) * size])
+        probs = jnp.exp(dot(keys, query, 1, 1) - lse_ref[chunk : chunk + 1])
+        grad_probs = dot(values, grad, 1, 1)
+        delta = jnp.sum(probs * grad_probs, 0, keepdims=True)
+        grad_scores = (probs * (grad_probs - delta)).astype(bf16)
+        turned = dot(keys_t, grad_scores)
+        parts = [
+            turned[head * HEAD_DIM : (head + 1) * HEAD_DIM, head * size : (head + 1) * size]
+            for head in range(heads)
+        ]
         dq_ref[chunk * size : (chunk + 1) * size] = (
             jnp.concatenate(parts, 0).T * score_scale
         ).astype(bf16)
-        both = (
-            dot(jnp.concatenate(grads_all, 1), jnp.concatenate(query_all, 0)),
-            dot(jnp.concatenate(probs_all, 1), jnp.concatenate(grad_all, 0)),
-        )
+        both = (dot(grad_scores, query), dot(probs.astype(bf16), grad))
         for slot in range(group):
             for k in range(2):
                 value = both[k][slot * count : (slot + 1) * count].reshape(chunk + 1, size, width)
@@ -901,7 +911,7 @@
     proj_ref, refs = refs[0], refs[1:]
     dh_refs, (dh_ref, mix_ref, late_ref) = refs[:ranks], refs[ranks:]
     tokens, width = dq_ref.shape
-    model = sel_ref.shape[0]
+    model = sel_ref.shape[1]
     size = tokens // ranks
     low = [dq_ref[...]]
     for k in range(2):
@@ -913,7 +923,7 @@
     mix_ref[...] = mixed
     mix_ref.flush()
     below = dot(mixed, w_ref[:, : 3 * width], 1, 1).astype(bf16)
-    dh_ref[...] = dot(below, sel_ref[...]).astype(bf16).reshape(ranks, size, model)
+    dh_ref[...] = dot(below, one_hot(sel_ref, model)).astype(bf16).reshape(ranks, size, model)
     for k, ref in enumerate(dh_refs):
         ref[...] = dh_ref[lax.rem(where_am_i(group)[0] + k, ranks)]
         ref.flush()
@@ -952,8 +962,8 @@
     cols = jnp.sum(mixed.astype(f32), 0, keepdims=True)
     both = jnp.concatenate([cols[:, :width], cols[:, 2 * width :]], 1)
     sums = jnp.concatenate([fcb_ref[0:1], both], 1) * mask_ref[...]
-    small = dot(sel_ref[...], vec.astype(bf16), 1, 1)
-    more = dot(bsel_ref[...], sums.astype(bf16), 1, 1)
+    small = dot(one_hot(sel_ref, model), vec.astype(bf16), 1, 1)
+    more = dot(one_hot(bsel_ref, model), sums.astype(bf16), 1, 1)
     rest = jnp.zeros((model, SMALL - 24), f32)
     whole = jnp.concatenate([whole, small, more, rest], 1)
     rows = model // group
@@ -1069,6 +1079,7 @@
     part = inner // ranks
     count = ranks * size
     lanes = 3 * width + SMALL
+    heads_here = width // HEAD_DIM
     squads = ranks * planes
     rank = lax.axis_index("dp")
     place = lax.axis_index("seq")
@@ -1116,17 +1127,15 @@
 
     ties_seen = [tie_index] + [send(tie_index, to_rank[ranks - k]) for k in range(1, ranks)]
     scalar_ties = tuple(range(ranks))
-    near = send(out_weight, to_member[1])
     tokens_own = send(tokens[0], swap)
-    grad_own = send(cotangent[0], swap)
-
-    early, *out_cols = run(
+
+    cols_rows = (rows + 15) // 16 * 16
+    early, cols = run(
         functools.partial(pack_kernel, group, ranks),
-        [((squads, rows, lanes), bf16)] + [((group * rows, model), bf16)] * planes,
+        [((squads, rows, lanes), bf16), ((planes, cols_rows, model), bf16)],
         *ties_seen,
         qkv_weight,
         out_weight,
-        near,
         first_gain,
         first_shift,
         out_bias,
@@ -1136,11 +1145,12 @@
         qv_bias,
         fc_bias,
         scalars=scalar_ties,
+        scratch=[pltpu.VMEM((ties, ranks, rows, lanes), bf16)],
         us=2.0,
         name="pack",
     )
+    packed = early
     early = over_squad(early)
-    out_cols = [out_cols[0]] + [send(out_cols[k], to_plane[k]) for k in range(1, planes)]
 
     def arrival(owner, row):
         a, b, c = owner // n_seq, (owner % n_seq) // group, owner % group
@@ -1161,24 +1171,14 @@
             (unit_qv % (2 * rows)) // rows + 6,
         ]
     )
-    sel = (jnp.arange(model)[:, None] == at_model[None, :]).astype(bf16)
-    bsel = (jnp.arange(model)[:, None] == at_bias[None, :]).astype(bf16)
+    sel = at_model[None].astype(jnp.int32)
+    bsel = at_bias[None].astype(jnp.int32)
     row_mask = (jnp.arange(16)[:, None] == lanes_of[None, :]).astype(f32)
 
-    late_fc, late_proj = run(
-        functools.partial(pack_late_kernel, ranks),
-        [((squads, rows, part), bf16), ((planes, hid_rows, model), bf16)],
-        *ties_seen,
-        fc_weight,
-        proj_weight,
-        scalars=scalar_ties,
-        us=2.0,
-        name="pack_late",
-    )
     tokens_all = lax.all_gather(tokens_own, "dp", axis=0, tiled=True)
-    early = gate(early, tokens_all, grad_own, sel, bsel, row_mask, late_fc, out_cols)
-    grads_seen = [grad_own] + [send(grad_own, to_rank[ranks - k]) for k in range(1, ranks)]
-    late_fc = over_squad(gate(late_fc, early))
+    early = gate(early, tokens_all, sel, bsel, row_mask)
+    cols = over_planes(gate(cols, early))
+    late_rows = hid_rows + cols_rows
     early = from_members(early)
     own = ((size, model), bf16)
     q, kv, h_one, vec, fcb, w_early = run(
@@ -1196,33 +1196,51 @@
         sel,
         bsel,
         row_mask,
+        room=20,
         us=5.0,
         name="project",
     )
-    kv = from_members(kv)
-    attended, w_out, *sums = run(
-        functools.partial(attend_kernel, group),
-        [((count, width), bf16), ((width, model), bf16)] + [own] * ranks,
+    grad_own = send(gate(cotangent[0], tokens_all), swap)
+    late_fc, late_proj = run(
+        functools.partial(pack_late_kernel, ranks),
+        [((squads, rows, part), bf16), ((planes, hid_rows, model), bf16)],
+        *ties_seen,
+        gate(fc_weight, q),
+        proj_weight,
+        scalars=scalar_ties,
+        us=2.0,
+        name="pack_late",
+    )
+    cols = from_members(gate(cols, q))
+    late_fc = over_squad(gate(late_fc, grad_own, cols))
+    kv = from_members(gate(kv, grad_own))
+    grads_seen = [grad_own] + [send(grad_own, to_rank[ranks - k]) for k in range(1, ranks)]
+    attended, lse, w_out, *sums = run(
+        functools.partial(attend_kernel, group, rows),
+        [((count, width), bf16), ((8, heads_here * size), f32), ((width, model), bf16)] + [own] * ranks,
         q,
         *kv,
-        *out_cols,
-        scratch=[pltpu.VMEM((ranks, size, model), bf16)],
+        *cols,
+        scratch=[pltpu.VMEM((width, model), f32), pltpu.VMEM((ranks, size, model), bf16)],
         us=6.0,
         name="attend",
     )
-    late_proj = over_planes(gate(late_proj, attended))
+    sums = scatter(sums)
+    late_fc = gate(late_fc, attended, grads_seen)
+    late_proj = over_planes(gate(late_proj, late_fc))
+    late_fc = from_members(late_fc)
     middle, h_own = run(
         functools.partial(join_kernel, ranks),
         [((size, model), f32), own],
-        *scatter(sums),
+        *sums,
         tokens_own,
         gate(vec, grads_seen),
         sel,
+        room=16,
         us=2.0,
         name="join",
     )
     late_proj = from_members(gate(late_proj, h_own))
-    late_fc = from_members(gate(late_fc, h_own))
     h_two = lax.all_gather(h_own, "dp", axis=0, tiled=True)
     rest = run(
         functools.partial(mlp_kernel, group, ranks),
@@ -1267,13 +1285,16 @@
         middle,
         grad_own,
         vec,
+        room=16,
         us=30.0,
         name="join_back",
     )
+    late = gate(late, low_own)
     late_fc, late_proj = run(
         functools.partial(add_late_kernel, group),
         [((squads, rows, part), bf16), ((planes, hid_rows, model), bf16)],
-        *gate(late, low_own),
+        *late,
+        room=16,
         us=2.0,
         name="add_late",
     )
@@ -1286,10 +1307,11 @@
         layer_parts,
         middle,
         vec,
+        room=16,
         us=1.0,
         name="layer",
     )
-    layer_out = send(layer_own, swap)[None]
+    layer_out = send(layer_own, swap)
     rest = run(
         functools.partial(attend_back_kernel, group),
         [((2, ranks, size, width), f32)]
@@ -1301,6 +1323,7 @@
         w_out,
         q,
         *kv,
+        lse,
         attended,
         scratch=[
             pltpu.VMEM((group, 2, ranks, size, width), f32),
@@ -1312,7 +1335,6 @@
     dkv, dq, dw_out = rest[:group], rest[group], rest[group + 1 :]
     dkv = over_members(dkv)
     dw_out = over_members(dw_out)
-    late_rows = hid_rows + (rows + 15) // 16 * 16
     rest = run(
         functools.partial(first_kernel, group, ranks),
         [own] * ranks
@@ -1357,17 +1379,20 @@
         tokens_own,
         vec,
         grad_middle,
+        room=16,
         us=30.0,
         name="last",
     )
+    early = gate(early, input_own, layer_out)
     (early,) = run(
         functools.partial(add_early_kernel, group),
         [((squads, rows, lanes), bf16)],
-        *gate(early, input_own, layer_out),
+        *early,
+        room=16,
         us=1.0,
         name="add_early",
     )
-    input_grad = send(input_own, swap)[None]
+    input_grad = send(input_own, swap)
     early = over_squad(early)
     grad_fc_weight, grad_proj_weight, grad_out_weight = run(
         functools.partial(final_late_kernel, ranks),
@@ -1379,20 +1404,23 @@
         us=3.0,
         name="final_late",
     )
+    early = gate(early, grad_fc_weight)
     grad_qkv_weight, *small = run(
         functools.partial(final_kernel, ranks),
         [((ties, rows, 3 * model), f32)]
         + [((ties, rows), f32)] * 6
         + [((ties, 2 * rows), f32), ((ties, 4 * rows), f32)],
         *ties_seen,
-        gate(early, grad_fc_weight),
+        early,
         scalars=scalar_ties,
+        room=16,
         us=1.0,
         name="final",
     )
+    layer_out, input_grad = gate((layer_out, input_grad), grad_qkv_weight)
     return (
-        layer_out,
-        input_grad,
+        layer_out[None],
+        input_grad[None],
         small[0],
         small[1],
         grad_qkv_weight,

time: 258 us -> 242 us (0.938)
  the two profiles are of different devices: /device:TPU:2 before, /device:TPU:0 now
where the time goes in v3:
time: 242 us; the launch traced here: 238 us
  Pallas kernels  71.5 us (30%)
  starting transfers between devices  67.8 us (28%)
  blocking collectives  46.5 us (19%)
  waiting for transfers between devices  43 us (18%)
  local copies, waits for them, and re-layouts  6.75 us (3%)
    pallas_call x17, Pallas kernels, run(): pl.pallas_call(body, out_shape=shapes, in_specs=[SMEM if k in scalars els...  71.5 us
    ppermute x28, starting transfers between devices, send(): return lax.ppermute(values, axes, pairs)  26.7 us
    all_to_all x4, starting transfers between devices, over_squad(): return lax.all_to_all(pieces, axes, 0, 0, axis_index_groups=squad)  19.3 us
    ppermute x28, waiting for transfers between devices, send(): return lax.ppermute(values, axes, pairs)  18.2 us
    all_to_all x3, starting transfers between devices, over_planes(): return lax.all_to_all(pieces, 'seq', 0, 0, axis_index_groups=same_member)  18.1 us
    all_gather x1, blocking collectives, fast_device(): tokens_all = lax.all_gather(tokens_own, 'dp', axis=0, tiled=True)  16.7 us
    all_gather x1, blocking collectives, fast_device(): low = lax.all_gather(gate(low_own, late_fc), 'dp', axis=0, tiled=True)  16.6 us
    all_to_all x3, waiting for transfers between devices, over_planes(): return lax.all_to_all(pieces, 'seq', 0, 0, axis_index_groups=same_member)  13.8 us
  transfers between devices with their start and end apart: 36, of which 15 were waited for; matrix products, arithmetic and copies ran while one was open for 0% of the time, Pallas kernels for 26%

profile of v3, /device:TPU:0, one launch (start us, length us, event | category | flops | bytes accessed | tf_op | source)
XLA Modules:
  0.0 237.8 jit_solution(14445948705647166910)
XLA Ops:
  0.6 3.0 %collective-permute-start.2 = (s32[1]{0:T(128)}, s32[1]{0:T(128)}, u32[]{:S(2)}, u32[]{:S(2)}) collective-permute-start(s32[1]{0:T(128)} %param.16), channel_id=1, source_target_pairs={{0,16},{1,17},{2,18},{3,19},{4,20},{5,21},{6,22},{7,23},{8,24},{9,... | collective-permute-start | bytes 20 | tf_op jit(solution)/shard_map/ppermute | solution.py:1108
  3.7 1.4 collective-permute-start.1
  5.7 1.6 collective-permute-start
  8.0 1.7 collective-permute-done.3.refs_3_
  9.8 4.3 %pack.1 = (bf16[16,24,640]{2,1,0:T(8,128)(2,1)}, bf16[4,32,768]{2,1,0:T(8,128)(2,1)}) custom-call(s32[1]{0:T(128)S(6)} %copy.31.refs_0_, s32[1]{0:T(128)} %collective-permute-done.1.refs_1_, s32[1]{0:T(128)} %collective-permute-done.2.refs_2_, s32[1]{0:T(128)} %collective-permute-done.3.refs_3_, bf16[2,24,2304]{2,1,0:T(8,128)(2,1)} %refs_4_.1, ...), custom_call_target="tpu_custom_call" | custom-call | flops 2000000000 | bytes 7000000 | tf_op jit(solution)/shard_map/pack/pallas_call | solution.py:555
  14.1 6.9 %all-to-all-start = ((bf16[16,24,640]{2,1,0:T(8,128)(2,1)}), bf16[16,24,640]{2,1,0:T(8,128)(2,1)S(1)}, u32[]{:S(2)}, u32[]{:S(2)}) async-start(bf16[16,24,640]{2,1,0:T(8,128)(2,1)} %get-tuple-element.98), calls=%async_computation | async-start | bytes 983040 | tf_op jit(solution)/shard_map/all_to_all | solution.py:1120
  21.2 16.7 %all_gather.9.refs_0_.refs_2_ = bf16[512,768]{1,0:T(8,128)(2,1)S(1)} all-gather(bf16[128,768]{1,0:T(8,128)(2,1)S(1)} %collective-permute-done.refs_4_), channel_id=1, replica_groups=mesh['dp'=4,'seq'=8] {'dp'}, dimensions={0}, use_global_device_ids=true | all-gather | bytes 983040 | tf_op jit(solution)/shard_map/all_gather | solution.py:1178
  38.0 1.6 collective-permute-start.5
  39.6 6.0 %all-to-all-start.1 = ((bf16[4,32,768]{2,1,0:T(8,128)(2,1)}), bf16[4,32,768]{2,1,0:T(8,128)(2,1)S(1)}, u32[]{:S(2)}, u32[]{:S(2)}) async-start(bf16[4,32,768]{2,1,0:T(8,128)(2,1)} %get-tuple-element.105), calls=%async_computation.1 | async-start | bytes 393216 | tf_op jit(solution)/shard_map/all_to_all | solution.py:1117
  45.6 5.0 %project.1 = (bf16[4,128,192]{2,1,0:T(8,128)(2,1)S(1)}, bf16[2,4,128,192]{3,2,1,0:T(8,128)(2,1)S(1)}, bf16[512,768]{1,0:T(8,128)(2,1)S(1)}, f32[8,768]{1,0:T(8,1...) custom-call(bf16[512,768]{1,0:T(8,128)(2,1)S(1)} %all_gather.9.refs_0_.refs_2_, ...), custom_call_target="tpu_custom_call" | custom-call | flops 5000000000 | bytes 17500000 | tf_op jit(solution)/shard_map/project/pallas_call | solution.py:555
  50.7 1.0 copy-done.10
  51.7 0.9 copy-done.12
  52.6 6.7 %all-to-all-done.1.refs_3_ = bf16[4,32,768]{2,1,0:T(8,128)(2,1)S(1)} async-done(((bf16[4,32,768]{2,1,0:T(8,128)(2,1)}), bf16[4,32,768]{2,1,0:T(8,128)(2,1)S(1)}, u32[]{:S(2)}, u32[]{:S(2)}) %all-to-all-start.1) | async-done | bytes 196640 | tf_op jit(solution)/shard_map/all_to_all | solution.py:1117
  59.3 3.9 %pack_late.1 = (bf16[16,24,768]{2,1,0:T(8,128)(2,1)}, bf16[4,96,768]{2,1,0:T(8,128)(2,1)}) custom-call(s32[1]{0:T(128)S(6)} %copy.31.refs_0_, s32[1]{0:T(128)} %collective-permute-done.1.refs_1_, s32[1]{0:T(128)} %collective-permute-done.2.refs_2_, s32[1]{0:T(128)} %collective-permute-done.3.refs_3_, bf16[2,24,3072]{2,1,0:T(8,128)(2,1)} %refs_4_.2, ...), custom_call_target="tpu_custom_call" | custom-call | flops 2000000000 | bytes 7000000 | tf_op jit(solution)/shard_map/pack_late/pallas_call | solution.py:555
  63.3 4.3 %all-to-all-start.2 = ((bf16[16,24,768]{2,1,0:T(8,128)(2,1)}), bf16[16,24,768]{2,1,0:T(8,128)(2,1)S(1)}, u32[]{:S(2)}, u32[]{:S(2)}) async-start(bf16[16,24,768]{2,1,0:T(8,128)(2,1)} %get-tuple-element.116), calls=%async_computation.2 | async-start | bytes 1179648 | tf_op jit(solution)/shard_map/all_to_all | solution.py:1120
  67.9 1.8 collective-permute-start.13
  69.6 1.5 collective-permute-start.12
  71.1 1.5 collective-permute-start.11
  72.6 0.8 copy-done.25
  73.4 5.3 %attend.1 = (bf16[512,192]{1,0:T(8,128)(2,1)}, f32[8,384]{1,0:T(8,128)}, bf16[192,768]{1,0:T(8,128)(2,1)}, bf16[128,768]{1,0:T(8,128)(2,1)}, bf16[128,768]{1,0:T...) custom-call(bf16[4,128,192]{2,1,0:T(8,128)(2,1)} %copy-done.14, bf16[2,4,128,192]{3,2,1,0:T(8,128)(2,1)} %copy-done.4, ...), custom_call_target="tpu_custom_call" | custom-call | flops 6000000000 | bytes 21000000 | tf_op jit(solution)/shard_map/attend/pallas_call | solution.py:555
  78.7 3.5 %collective-permute-done.13.refs_7_ = bf16[128,768]{1,0:T(8,128)(2,1)S(1)} collective-permute-done((bf16[128,768]{1,0:T(8,128)(2,1)S(1)}, bf16[128,768]{1,0:T(8,128)(2,1)S(1)}, u32[]{:S(2)}, u32[]{:S(2)}) %collective-permute-start.13) | collective-permute-done | bytes 196640 | tf_op jit(solution)/shard_map/ppermute | solution.py:1108
  82.2 3.0 %collective-permute-done.12.refs_6_ = bf16[128,768]{1,0:T(8,128)(2,1)S(1)} collective-permute-done((bf16[128,768]{1,0:T(8,128)(2,1)S(1)}, bf16[128,768]{1,0:T(8,128)(2,1)S(1)}, u32[]{:S(2)}, u32[]{:S(2)}) %collective-permute-start.12) | collective-permute-done | bytes 196640 | tf_op jit(solution)/shard_map/ppermute | solution.py:1108
  85.9 4.2 %all-to-all-start.3 = ((bf16[4,96,768]{2,1,0:T(8,128)(2,1)}), bf16[4,96,768]{2,1,0:T(8,128)(2,1)S(1)}, u32[]{:S(2)}, u32[]{:S(2)}) async-start(bf16[4,96,768]{2,1,0:T(8,128)(2,1)} %get-tuple-element.121), calls=%async_computation.3 | async-start | bytes 1179648 | tf_op jit(solution)/shard_map/all_to_all | solution.py:1117
  90.2 1.4 collective-permute-start.8
  92.2 2.1 collective-permute-start.10
  94.3 4.6 %collective-permute-done.8.refs_1_ = bf16[128,768]{1,0:T(8,128)(2,1)S(1)} collective-permute-done((bf16[128,768]{1,0:T(8,128)(2,1)S(1)}, bf16[128,768]{1,0:T(8,128)(2,1)S(1)}, u32[]{:S(2)}, u32[]{:S(2)}) %collective-permute-start.8) | collective-permute-done | bytes 196640 | tf_op jit(solution)/shard_map/ppermute | solution.py:1108
  98.9 2.5 %collective-permute-done.9.refs_2_ = bf16[128,768]{1,0:T(8,128)(2,1)S(1)} collective-permute-done((bf16[128,768]{1,0:T(8,128)(2,1)S(1)}, bf16[128,768]{1,0:T(8,128)(2,1)S(1)}, u32[]{:S(2)}, u32[]{:S(2)}) %collective-permute-start.9) | collective-permute-done | bytes 196640 | tf_op jit(solution)/shard_map/ppermute | solution.py:1108
  101.4 2.8 %join.1 = (f32[128,768]{1,0:T(8,128)S(1)}, bf16[128,768]{1,0:T(8,128)(2,1)S(1)}) custom-call(bf16[128,768]{1,0:T(8,128)(2,1)S(1)} %copy-done.11, bf16[128,768]{1,0:T(8,128)(2,1)S(1)} %collective-permute-done.8.refs_1_, bf16[128,768]{1,0:T(8,128)(2,1)S(1)} %collective-permute-done.9.refs_2_, bf16[128,768]{1,0:T(8,128)(2,1)S(1)} %collective-permute-done.10.refs_3_, ...), custom_call_target="tpu_custom_call" | custom-call | flops 2000000000 | bytes 7000000 | tf_op jit(solution)/shard_map/join/pallas_call | solution.py:555
  104.4 1.8 all-to-all-done.3.refs_8_
  106.2 13.2 %all_gather.10.refs_0_ = bf16[512,768]{1,0:T(8,128)(2,1)} all-gather(bf16[128,768]{1,0:T(8,128)(2,1)S(1)} %get-tuple-element.113), channel_id=1, replica_groups=mesh['dp'=4,'seq'=8] {'dp'}, dimensions={0}, use_global_device_ids=true | all-gather | bytes 983040 | tf_op jit(solution)/shard_map/all_gather | solution.py:1244
  119.4 0.8 copy-done.23
  120.4 7.2 %mlp.1 = (bf16[128,768]{1,0:T(8,128)(2,1)}, bf16[128,768]{1,0:T(8,128)(2,1)}, bf16[128,768]{1,0:T(8,128)(2,1)}, bf16[128,768]{1,0:T(8,128)(2,1)}, bf16[4,128,768...) custom-call(bf16[512,768]{1,0:T(8,128)(2,1)} %all_gather.10.refs_0_, ...), custom_call_target="tpu_custom_call" | custom-call | flops 7000000000 | bytes 24500000 | tf_op jit(solution)/shard_map/mlp/pallas_call | solution.py:555
  127.7 1.0 collective-permute-start.16
  128.7 1.1 collective-permute-start.17
  129.8 1.8 collective-permute-start.18
  131.6 5.6 %mlp_grad.1 = (f32[768,768]{1,0:T(8,128)}, bf16[768,768]{1,0:T(8,128)(2,1)}, f32[8,768]{1,0:T(8,128)}) custom-call(bf16[512,768]{1,0:T(8,128)(2,1)} %all_gather.10.refs_0_, bf16[512,768]{1,0:T(8,128)(2,1)} %get-tuple-element.130.refs_1_, bf16[512,768]{1,0:T(8,128)(2,1)} %get-tuple-element.131.refs_2_, bf16[512,768]{1,0:T(8,128)(2,1)} %get-tuple-element.132.refs_3_), custom_call_target="tpu_custom_call" | custom-call | flops 4000000000 | bytes 14000000 | tf_op jit(solution)/shard_map/mlp_grad/pallas_call | solution.py:555
  137.3 1.5 collective-permute-done.17.refs_2_
  138.8 2.8 %join_back.1 = (f32[128,768]{1,0:T(8,128)S(1)}, bf16[128,768]{1,0:T(8,128)(2,1)S(1)}, f32[8,768]{1,0:T(8,128)S(1)}) custom-call(bf16[128,768]{1,0:T(8,128)(2,1)S(1)} %copy-done.15, bf16[128,768]{1,0:T(8,128)(2,1)S(1)} %collective-permute-done.16.refs_1_, bf16[128,768]{1,0:T(8,128)(2,1)S(1)} %collective-permute-done.17.refs_2_, ...), custom_call_target="tpu_custom_call" | custom-call | flops 30000001024 | bytes 105000000 | tf_op jit(solution)/shard_map/join_back/pallas_call | solution.py:555
  141.6 1.8 add_late.1
  143.5 0.8 copy-done.9
  144.3 4.4 %all-to-all-start.4 = ((bf16[16,24,768]{2,1,0:T(8,128)(2,1)}), bf16[16,24,768]{2,1,0:T(8,128)(2,1)S(1)}, u32[]{:S(2)}, u32[]{:S(2)}) async-start(bf16[16,24,768]{2,1,0:T(8,128)(2,1)} %get-tuple-element.137), calls=%async_computation.4 | async-start | bytes 1179648 | tf_op jit(solution)/shard_map/all_to_all | solution.py:1120
  148.7 16.6 %all_gather.11.refs_0_ = bf16[512,768]{1,0:T(8,128)(2,1)} all-gather(bf16[128,768]{1,0:T(8,128)(2,1)S(1)} %get-tuple-element.138), channel_id=1, replica_groups=mesh['dp'=4,'seq'=8] {'dp'}, dimensions={0}, use_global_device_ids=true | all-gather | bytes 983040 | tf_op jit(solution)/shard_map/all_gather | solution.py:1301
  165.5 3.7 %all-to-all-start.5 = ((bf16[4,128,768]{2,1,0:T(8,128)(2,1)}), bf16[4,128,768]{2,1,0:T(8,128)(2,1)S(1)}, u32[]{:S(2)}, u32[]{:S(2)}) async-start(bf16[4,128,768]{2,1,0:T(8,128)(2,1)} %get-tuple-element.139), calls=%async_computation.5 | async-start | bytes 1572864 | tf_op jit(solution)/shard_map/all_to_all | solution.py:1303
  169.2 8.4 %attend_back.1 = (f32[2,4,128,192]{3,2,1,0:T(8,128)}, bf16[2,4,128,192]{3,2,1,0:T(8,128)(2,1)}, bf16[512,192]{1,0:T(8,128)(2,1)}, f32[4,24,768]{2,1,0:T(8,128)}, bf16[4,24,768]{2,1,0:T(8,128)(2,1)}) custom-call(bf16[512,768]{1,0:T(8,128)(2,1)} %all_gather.11.refs_0_, bf16[192,768]{1,0:T(8,128)(2,1)} %get-tuple-element.140.refs_1_, ...), custom_call_target="tpu_custom_call" | custom-call | flops 10000000000 | bytes 35000000 | tf_op jit(solution)/shard_map/attend_back/pallas_call | solution.py:555
  178.2 0.7 all-to-all-done.5.refs_0_
  179.0 0.7 layer.1
  179.7 0.7 collective-permute-start.20
  180.4 0.6 copy-done.37
  181.2 5.4 %first.1 = (bf16[128,768]{1,0:T(8,128)(2,1)}, bf16[128,768]{1,0:T(8,128)(2,1)}, bf16[128,768]{1,0:T(8,128)(2,1)}, bf16[128,768]{1,0:T(8,128)(2,1)}, bf16[4,128,7...) custom-call(bf16[512,192]{1,0:T(8,128)(2,1)} %get-tuple-element.142.refs_0_, ...), custom_call_target="tpu_custom_call" | custom-call | flops 4000000000 | bytes 14000000 | tf_op jit(solution)/shard_map/first/pallas_call | solution.py:555
  186.6 7.8 %all-to-all-start.7 = ((bf16[4,128,768]{2,1,0:T(8,128)(2,1)}), bf16[4,128,768]{2,1,0:T(8,128)(2,1)S(1)}, u32[]{:S(2)}, u32[]{:S(2)}) async-start(bf16[4,128,768]{2,1,0:T(8,128)(2,1)} %get-tuple-element.165), calls=%async_computation.7 | async-start | bytes 1572864 | tf_op jit(solution)/shard_map/all_to_all | solution.py:1117
  194.9 1.4 collective-permute-start.24
  196.3 1.4 collective-permute-start.25
  197.8 6.2 %first_grad.1 = (f32[384,640]{1,0:T(8,128)}, bf16[384,640]{1,0:T(8,128)(2,1)}) custom-call(bf16[512,768]{1,0:T(8,128)(2,1)} %copy-done.12, bf16[512,576]{1,0:T(8,128)(2,1)} %get-tuple-element.156.refs_1_, bf16[512,768]{1,0:T(8,128)(2,1)} %copy-done, bf16[4,128,768]{2,1,0:T(8,128)(2,1)} %get-tuple-element.157.refs_3_, f32[8,768]{1,0:T(8,128)} %copy-done.16, ...), custom_call_target="tpu_custom_call" | custom-call | flops 5000000000 | bytes 17500000 | tf_op jit(solution)/shard_map/first_grad/pallas_call | solution.py:555
  204.1 1.0 collective-permute-done.24.refs_2_
  205.1 2.4 %last.1 = bf16[128,768]{1,0:T(8,128)(2,1)S(1)} custom-call(bf16[128,768]{1,0:T(8,128)(2,1)S(1)} %copy-done.13, bf16[128,768]{1,0:T(8,128)(2,1)S(1)} %collective-permute-done.23.refs_1_, bf16[128,768]{1,0:T(8,128)(2,1)S(1)} %collective-permute-done.24.refs_2_, bf16[128,768]{1,0:T(8,128)(2,1)S(1)} %collective-permute-done.25.refs_3_, ...), custom_call_target="tpu_custom_call" | custom-call | flops 30000001024 | bytes 105000000 | tf_op jit(solution)/shard_map/last/pallas_call | solution.py:555
  207.6 1.6 add_early.1
  209.2 5.3 %all-to-all-done.7.refs_5_ = bf16[4,128,768]{2,1,0:T(8,128)(2,1)S(1)} async-done(((bf16[4,128,768]{2,1,0:T(8,128)(2,1)}), bf16[4,128,768]{2,1,0:T(8,128)(2,1)S(1)}, u32[]{:S(2)}, u32[]{:S(2)}) %all-to-all-start.7) | async-done | bytes 786464 | tf_op jit(solution)/shard_map/all_to_all | solution.py:1117
  214.5 3.8 %all-to-all-start.6 = ((bf16[16,24,640]{2,1,0:T(8,128)(2,1)}), bf16[16,24,640]{2,1,0:T(8,128)(2,1)S(1)}, u32[]{:S(2)}, u32[]{:S(2)}) async-start(bf16[16,24,640]{2,1,0:T(8,128)(2,1)} %add_early.1), calls=%async_computation.6 | async-start | bytes 983040 | tf_op jit(solution)/shard_map/all_to_all | solution.py:1120
  218.3 0.7 collective-permute-start.26
  219.0 4.5 %final_late.1 = (f32[2,24,3072]{2,1,0:T(8,128)}, f32[2,96,768]{2,1,0:T(8,128)}, f32[2,24,768]{2,1,0:T(8,128)}) custom-call(s32[1]{0:T(128)S(6)} %copy.31.refs_0_, s32[1]{0:T(128)} %collective-permute-done.1.refs_1_, s32[1]{0:T(128)} %collective-permute-done.2.refs_2_, s32[1]{0:T(128)} %collective-permute-done.3.refs_3_, bf16[16,24,768]{2,1,0:T(8,128)(2,1)} %copy-done.19, ...), custom_call_target="tpu_custom_call" | custom-call | flops 3000000000 | bytes 10500000 | tf_op jit(solution)/shard_map/final_late/pallas_call | solution.py:555
  223.5 9.5 %all-to-all-done.6.refs_4_ = bf16[16,24,640]{2,1,0:T(8,128)(2,1)S(1)} async-done(((bf16[16,24,640]{2,1,0:T(8,128)(2,1)}), bf16[16,24,640]{2,1,0:T(8,128)(2,1)S(1)}, u32[]{:S(2)}, u32[]{:S(2)}) %all-to-all-start.6) | async-done | bytes 491552 | tf_op jit(solution)/shard_map/all_to_all | solution.py:1120
  233.1 3.3 %final.1 = (f32[2,24,2304]{2,1,0:T(8,128)}, f32[2,24]{1,0:T(2,128)}, f32[2,24]{1,0:T(2,128)}, f32[2,24]{1,0:T(2,128)}, f32[2,24]{1,0:T(2,128)}, /*index=5*/f32[2...) custom-call(s32[1]{0:T(128)S(6)} %copy.31.refs_0_, s32[1]{0:T(128)} %collective-permute-done.1.refs_1_, ...), custom_call_target="tpu_custom_call" | custom-call | flops 1000000000 | bytes 3500000 | tf_op jit(solution)/shard_map/final/pallas_call | solution.py:555
  236.4 0.7 copy.32
  237.1 0.7 copy.33
  (114 shorter events, 4.5 us)
Async XLA Ops:
  0.6 7.4 %collective-permute-start.2 = (s32[1]{0:T(128)}, s32[1]{0:T(128)}, u32[]{:S(2)}, u32[]{:S(2)}) collective-permute-start(s32[1]{0:T(128)} %param.16), channel_id=1, source_target_pairs={{0,16},{1,17},{2,18},{3,19},{4,20},{5,21},{6,22},{7,23},{8,24},{9,... | collective-permute-start | bytes 20 | tf_op jit(solution)/shard_map/ppermute | solution.py:1108
  3.7 4.4 %collective-permute-start.1 = (s32[1]{0:T(128)}, s32[1]{0:T(128)}, u32[]{:S(2)}, u32[]{:S(2)}) collective-permute-start(s32[1]{0:T(128)} %param.16), channel_id=1, source_target_pairs={{0,24},{1,25},{2,26},{3,27},{4,28},{5,29},{6,30},{7,31},{8,0},{9,1... | collective-permute-start | bytes 20 | tf_op jit(solution)/shard_map/ppermute | solution.py:1108
  5.1 4.7 %collective-permute-start.3 = (s32[1]{0:T(128)}, s32[1]{0:T(128)}, u32[]{:S(2)}, u32[]{:S(2)}) collective-permute-start(s32[1]{0:T(128)} %param.16), channel_id=1, source_target_pairs={{0,8},{1,9},{2,10},{3,11},{4,12},{5,13},{6,14},{7,15},{8,16},{9,17... | collective-permute-start | bytes 20 | tf_op jit(solution)/shard_map/ppermute | solution.py:1108
  5.7 15.5 %collective-permute-start = (bf16[128,768]{1,0:T(8,128)(2,1)}, bf16[128,768]{1,0:T(8,128)(2,1)S(1)}, u32[]{:S(2)}, u32[]{:S(2)}) collective-permute-start(bf16[128,768]{1,0:T(8,128)(2,1)} %bitcast.6), channel_id=1, source_target_pairs={{0,0},{1,1},{2,8},{3,9},{4,16},{5,17},{6,24},{7,25},{8,2},{9,3},{1... | collective-permute-start | bytes 589832 | tf_op jit(solution)/shard_map/ppermute | solution.py:1108
  14.1 23.8 %all-to-all-start = ((bf16[16,24,640]{2,1,0:T(8,128)(2,1)}), bf16[16,24,640]{2,1,0:T(8,128)(2,1)S(1)}, u32[]{:S(2)}, u32[]{:S(2)}) async-start(bf16[16,24,640]{2,1,0:T(8,128)(2,1)} %get-tuple-element.98), calls=%async_computation | async-start | bytes 983040 | tf_op jit(solution)/shard_map/all_to_all | solution.py:1120
  21.1 29.6 %copy-start.1 = (f32[16,1152]{1,0:T(8,128)}, f32[16,1152]{1,0:T(8,128)S(1)}, u32[]{:S(2)}) copy-start(f32[16,1152]{1,0:T(8,128)S(1)} %fusion.refs_5_.refs_6_) | copy-start | bytes 221188
  21.1 29.6 %copy-start.2 = (s32[1,1152]{1,0:T(1,128)}, s32[1,1152]{1,0:T(1,128)S(1)}, u32[]{:S(2)}) copy-start(s32[1,1152]{1,0:T(1,128)S(1)} %broadcast_in_dim.12.refs_4_.refs_8_) | copy-start | bytes 13828
  21.2 80.2 %copy-start.3 = (s32[1,768]{1,0:T(1,128)}, s32[1,768]{1,0:T(1,128)S(1)}, u32[]{:S(2)}) copy-start(s32[1,768]{1,0:T(1,128)S(1)} %fusion.29.refs_3_.refs_6_.refs_10_.refs_4_.refs_7_) | copy-start | bytes 9220
  37.9 12.7 %copy-start = (bf16[512,768]{1,0:T(8,128)(2,1)}, bf16[512,768]{1,0:T(8,128)(2,1)S(1)}, u32[]{:S(2)}) copy-start(bf16[512,768]{1,0:T(8,128)(2,1)S(1)} %all_gather.9.refs_0_.refs_2_) | copy-start | bytes 2359300
  37.9 7.7 %collective-permute-start.4 = (bf16[16,24,640]{2,1,0:T(8,128)(2,1)S(1)}, bf16[16,24,640]{2,1,0:T(8,128)(2,1)S(1)}, u32[]{:S(2)}, u32[]{:S(2)}) collective-permute-start(bf16[16,24,640]{2,1,0:T(8,128)(2,1)S(1)} %all-to-all-done.refs_1_), channel_id=1, source_target_pairs={{0,1},{1,0},{2,3},{3,2},{4,5},{5,4},{6,7},{7,6},{8,9},{9,8},{10,11... | collective-permute-start | bytes 1474568 | tf_op jit(solution)/shard_map/ppermute | solution.py:1108
  38.0 25.2 %collective-permute-start.5 = (bf16[128,768]{1,0:T(8,128)(2,1)}, bf16[128,768]{1,0:T(8,128)(2,1)S(1)}, u32[]{:S(2)}, u32[]{:S(2)}) collective-permute-start(bf16[128,768]{1,0:T(8,128)(2,1)} %bitcast.1), channel_id=1, source_target_pairs={{0,0},{1,1},{2,8},{3,9},{4,16},{5,17},{6,24},{7,25},{8,2},{9,3},{1... | collective-permute-start | bytes 589832 | tf_op jit(solution)/shard_map/ppermute | solution.py:1108
  39.6 19.7 %all-to-all-start.1 = ((bf16[4,32,768]{2,1,0:T(8,128)(2,1)}), bf16[4,32,768]{2,1,0:T(8,128)(2,1)S(1)}, u32[]{:S(2)}, u32[]{:S(2)}) async-start(bf16[4,32,768]{2,1,0:T(8,128)(2,1)} %get-tuple-element.105), calls=%async_computation.1 | async-start | bytes 393216 | tf_op jit(solution)/shard_map/all_to_all | solution.py:1117
  52.6 10.7 %copy-start.14 = (bf16[4,128,192]{2,1,0:T(8,128)(2,1)}, bf16[4,128,192]{2,1,0:T(8,128)(2,1)S(1)}, u32[]{:S(2)}) copy-start(bf16[4,128,192]{2,1,0:T(8,128)(2,1)S(1)} %get-tuple-element.100.refs_0_.refs_2_) | copy-start | bytes 589828
  52.6 10.7 %copy-start.17 = (f32[8,768]{1,0:T(8,128)}, f32[8,768]{1,0:T(8,128)S(1)}, u32[]{:S(2)}) copy-start(f32[8,768]{1,0:T(8,128)S(1)} %get-tuple-element.119.refs_3_) | copy-start | bytes 73732
  52.6 15.0 %copy-start.4 = (bf16[2,4,128,192]{3,2,1,0:T(8,128)(2,1)}, bf16[2,4,128,192]{3,2,1,0:T(8,128)(2,1)S(1)}, u32[]{:S(2)}) copy-start(bf16[2,4,128,192]{3,2,1,0:T(8,128)(2,1)S(1)} %get-tuple-element.103.refs_1_.refs_3_) | copy-start | bytes 1179652
  59.3 4.0 %copy-start.22 = (bf16[4,32,768]{2,1,0:T(8,128)(2,1)}, bf16[4,32,768]{2,1,0:T(8,128)(2,1)S(1)}, u32[]{:S(2)}) copy-start(bf16[4,32,768]{2,1,0:T(8,128)(2,1)S(1)} %all-to-all-done.1.refs_3_) | copy-start | bytes 589828
  59.3 4.0 %collective-permute-start.7 = (bf16[4,32,768]{2,1,0:T(8,128)(2,1)S(1)}, bf16[4,32,768]{2,1,0:T(8,128)(2,1)S(1)}, u32[]{:S(2)}, u32[]{:S(2)}) collective-permute-start(bf16[4,32,768]{2,1,0:T(8,128)(2,1)S(1)} %all-to-all-done.1.refs_3_), channel_id=1, source_target_pairs={{0,1},{1,0},{2,3},{3,2},{4,5},{5,4},{6,7},{7,6},{8,9},{9,8},{10,11... | collective-permute-start | bytes 589832 | tf_op jit(solution)/shard_map/ppermute | solution.py:1108
  63.2 15.4 %copy-start.5 = (bf16[128,768]{1,0:T(8,128)(2,1)}, bf16[128,768]{1,0:T(8,128)(2,1)S(1)}, u32[]{:S(2)}) copy-start(bf16[128,768]{1,0:T(8,128)(2,1)S(1)} %collective-permute-done.5.refs_4_.refs_5_) | copy-start | bytes 589828
  63.3 9.3 %copy-start.35 = (bf16[4,32,768]{2,1,0:T(8,128)(2,1)}, bf16[4,32,768]{2,1,0:T(8,128)(2,1)S(1)}, u32[]{:S(2)}) copy-start(bf16[4,32,768]{2,1,0:T(8,128)(2,1)S(1)} %collective-permute-done.7.refs_4_) | copy-start | bytes 589828
  63.3 22.7 %all-to-all-start.2 = ((bf16[16,24,768]{2,1,0:T(8,128)(2,1)}), bf16[16,24,768]{2,1,0:T(8,128)(2,1)S(1)}, u32[]{:S(2)}, u32[]{:S(2)}) async-start(bf16[16,24,768]{2,1,0:T(8,128)(2,1)} %get-tuple-element.116), calls=%async_computation.2 | async-start | bytes 1179648 | tf_op jit(solution)/shard_map/all_to_all | solution.py:1120
  67.6 5.0 %collective-permute-start.6 = (bf16[2,4,128,192]{3,2,1,0:T(8,128)(2,1)S(1)}, bf16[2,4,128,192]{3,2,1,0:T(8,128)(2,1)S(1)}, u32[]{:S(2)}, u32[]{:S(2)}) collective-permute-start(bf16[2,4,128,192]{3,2,1,0:T(8,128)(2,1)S(1)} %get-tuple-element.103.refs_1_.refs_3_), channel_id=1, source_target_pairs={{0,1},{1,0},{2,3},{3,2},{4,5},{5,4},{6,7},{7,6},{8,9},{9,8},{10,11... | collective-permute-start | bytes 1179656 | tf_op jit(solution)/shard_map/ppermute | solution.py:1108
  67.9 14.3 %collective-permute-start.13 = (bf16[128,768]{1,0:T(8,128)(2,1)S(1)}, bf16[128,768]{1,0:T(8,128)(2,1)S(1)}, u32[]{:S(2)}, u32[]{:S(2)}) collective-permute-start(bf16[128,768]{1,0:T(8,128)(2,1)S(1)} %collective-permute-done.5.refs_4_.refs_5_), channel_id=1, source_target_pairs={{0,8},{1,9},{2,10},{3,11},{4,12},{5,13},{6,14},{7,15},{8,16},{9,17... | collective-permute-start | bytes 589832 | tf_op jit(solution)/shard_map/ppermute | solution.py:1108
  69.6 15.6 %collective-permute-start.12 = (bf16[128,768]{1,0:T(8,128)(2,1)S(1)}, bf16[128,768]{1,0:T(8,128)(2,1)S(1)}, u32[]{:S(2)}, u32[]{:S(2)}) collective-permute-start(bf16[128,768]{1,0:T(8,128)(2,1)S(1)} %collective-permute-done.5.refs_4_.refs_5_), channel_id=1, source_target_pairs={{0,16},{1,17},{2,18},{3,19},{4,20},{5,21},{6,22},{7,23},{8,24},{9,... | collective-permute-start | bytes 589832 | tf_op jit(solution)/shard_map/ppermute | solution.py:1108
  71.1 14.4 %collective-permute-start.11 = (bf16[128,768]{1,0:T(8,128)(2,1)S(1)}, bf16[128,768]{1,0:T(8,128)(2,1)S(1)}, u32[]{:S(2)}, u32[]{:S(2)}) collective-permute-start(bf16[128,768]{1,0:T(8,128)(2,1)S(1)} %collective-permute-done.5.refs_4_.refs_5_), channel_id=1, source_target_pairs={{0,24},{1,25},{2,26},{3,27},{4,28},{5,29},{6,30},{7,31},{8,0},{9,1... | collective-permute-start | bytes 589832 | tf_op jit(solution)/shard_map/ppermute | solution.py:1108
  78.7 11.5 %copy-start.36 = (bf16[128,768]{1,0:T(8,128)(2,1)S(1)}, bf16[128,768]{1,0:T(8,128)(2,1)}, u32[]{:S(2)}) copy-start(bf16[128,768]{1,0:T(8,128)(2,1)} %get-tuple-element.108) | copy-start | bytes 589828
  78.7 12.9 %copy-start.34 = (bf16[128,768]{1,0:T(8,128)(2,1)S(1)}, bf16[128,768]{1,0:T(8,128)(2,1)}, u32[]{:S(2)}) copy-start(bf16[128,768]{1,0:T(8,128)(2,1)} %get-tuple-element.109) | copy-start | bytes 589828
  78.7 13.5 %copy-start.32 = (bf16[128,768]{1,0:T(8,128)(2,1)S(1)}, bf16[128,768]{1,0:T(8,128)(2,1)}, u32[]{:S(2)}) copy-start(bf16[128,768]{1,0:T(8,128)(2,1)} %get-tuple-element.110) | copy-start | bytes 589828
  78.7 22.7 %copy-start.11 = (bf16[128,768]{1,0:T(8,128)(2,1)S(1)}, bf16[128,768]{1,0:T(8,128)(2,1)}, u32[]{:S(2)}) copy-start(bf16[128,768]{1,0:T(8,128)(2,1)} %get-tuple-element.107.refs_0_) | copy-start | bytes 589828
  82.2 22.1 %copy-start.27 = (bf16[128,768]{1,0:T(8,128)(2,1)}, bf16[128,768]{1,0:T(8,128)(2,1)S(1)}, u32[]{:S(2)}) copy-start(bf16[128,768]{1,0:T(8,128)(2,1)S(1)} %collective-permute-done.13.refs_7_) | copy-start | bytes 589828
  85.2 16.2 %copy-start.28 = (bf16[128,768]{1,0:T(8,128)(2,1)}, bf16[128,768]{1,0:T(8,128)(2,1)S(1)}, u32[]{:S(2)}) copy-start(bf16[128,768]{1,0:T(8,128)(2,1)S(1)} %collective-permute-done.12.refs_6_) | copy-start | bytes 589828
  85.5 15.9 %copy-start.29 = (bf16[128,768]{1,0:T(8,128)(2,1)}, bf16[128,768]{1,0:T(8,128)(2,1)S(1)}, u32[]{:S(2)}) copy-start(bf16[128,768]{1,0:T(8,128)(2,1)S(1)} %collective-permute-done.11.refs_5_) | copy-start | bytes 589828
  85.9 18.4 %copy-start.20 = (bf16[16,24,768]{2,1,0:T(8,128)(2,1)}, bf16[16,24,768]{2,1,0:T(8,128)(2,1)S(1)}, u32[]{:S(2)}) copy-start(bf16[16,24,768]{2,1,0:T(8,128)(2,1)S(1)} %all-to-all-done.2.refs_1_) | copy-start | bytes 1769476
  85.9 20.2 %all-to-all-start.3 = ((bf16[4,96,768]{2,1,0:T(8,128)(2,1)}), bf16[4,96,768]{2,1,0:T(8,128)(2,1)S(1)}, u32[]{:S(2)}, u32[]{:S(2)}) async-start(bf16[4,96,768]{2,1,0:T(8,128)(2,1)} %get-tuple-element.121), calls=%async_computation.3 | async-start | bytes 1179648 | tf_op jit(solution)/shard_map/all_to_all | solution.py:1117
  90.2 8.7 %collective-permute-start.8 = (bf16[128,768]{1,0:T(8,128)(2,1)S(1)}, bf16[128,768]{1,0:T(8,128)(2,1)S(1)}, u32[]{:S(2)}, u32[]{:S(2)}) collective-permute-start(bf16[128,768]{1,0:T(8,128)(2,1)S(1)} %copy-done.36), channel_id=1, source_target_pairs={{0,8},{1,9},{2,10},{3,11},{4,12},{5,13},{6,14},{7,15},{8,16},{9,17... | collective-permute-start | bytes 589832 | tf_op jit(solution)/shard_map/ppermute | solution.py:1108
  91.6 9.8 %collective-permute-start.9 = (bf16[128,768]{1,0:T(8,128)(2,1)S(1)}, bf16[128,768]{1,0:T(8,128)(2,1)S(1)}, u32[]{:S(2)}, u32[]{:S(2)}) collective-permute-start(bf16[128,768]{1,0:T(8,128)(2,1)S(1)} %copy-done.34), channel_id=1, source_target_pairs={{0,16},{1,17},{2,18},{3,19},{4,20},{5,21},{6,22},{7,23},{8,24},{9,... | collective-permute-start | bytes 589832 | tf_op jit(solution)/shard_map/ppermute | solution.py:1108
  92.2 9.3 %collective-permute-start.10 = (bf16[128,768]{1,0:T(8,128)(2,1)S(1)}, bf16[128,768]{1,0:T(8,128)(2,1)S(1)}, u32[]{:S(2)}, u32[]{:S(2)}) collective-permute-start(bf16[128,768]{1,0:T(8,128)(2,1)S(1)} %copy-done.32), channel_id=1, source_target_pairs={{0,24},{1,25},{2,26},{3,27},{4,28},{5,29},{6,30},{7,31},{8,0},{9,1... | collective-permute-start | bytes 589832 | tf_op jit(solution)/shard_map/ppermute | solution.py:1108
  104.3 15.1 %collective-permute-start.14 = (bf16[16,24,768]{2,1,0:T(8,128)(2,1)S(1)}, bf16[16,24,768]{2,1,0:T(8,128)(2,1)S(1)}, u32[]{:S(2)}, u32[]{:S(2)}) collective-permute-start(bf16[16,24,768]{2,1,0:T(8,128)(2,1)S(1)} %all-to-all-done.2.refs_1_), channel_id=1, source_target_pairs={{0,1},{1,0},{2,3},{3,2},{4,5},{5,4},{6,7},{7,6},{8,9},{9,8},{10,11... | collective-permute-start | bytes 1769480 | tf_op jit(solution)/shard_map/ppermute | solution.py:1108
  106.2 13.2 %copy-start.21 = (bf16[4,96,768]{2,1,0:T(8,128)(2,1)}, bf16[4,96,768]{2,1,0:T(8,128)(2,1)S(1)}, u32[]{:S(2)}) copy-start(bf16[4,96,768]{2,1,0:T(8,128)(2,1)S(1)} %all-to-all-done.3.refs_8_) | copy-start | bytes 1769476
  106.2 13.2 %collective-permute-start.15 = (bf16[4,96,768]{2,1,0:T(8,128)(2,1)S(1)}, bf16[4,96,768]{2,1,0:T(8,128)(2,1)S(1)}, u32[]{:S(2)}, u32[]{:S(2)}) collective-permute-start(bf16[4,96,768]{2,1,0:T(8,128)(2,1)S(1)} %all-to-all-done.3.refs_8_), channel_id=1, source_target_pairs={{0,1},{1,0},{2,3},{3,2},{4,5},{5,4},{6,7},{7,6},{8,9},{9,8},{10,11... | collective-permute-start | bytes 1769480 | tf_op jit(solution)/shard_map/ppermute | solution.py:1108
  127.7 9.6 %collective-permute-start.16 = (bf16[128,768]{1,0:T(8,128)(2,1)}, bf16[128,768]{1,0:T(8,128)(2,1)S(1)}, u32[]{:S(2)}, u32[]{:S(2)}) collective-permute-start(bf16[128,768]{1,0:T(8,128)(2,1)} %get-tuple-element.125), channel_id=1, source_target_pairs={{0,8},{1,9},{2,10},{3,11},{4,12},{5,13},{6,14},{7,15},{8,16},{9,17... | collective-permute-start | bytes 589832 | tf_op jit(solution)/shard_map/ppermute | solution.py:1108
  128.7 10.1 %collective-permute-start.17 = (bf16[128,768]{1,0:T(8,128)(2,1)}, bf16[128,768]{1,0:T(8,128)(2,1)S(1)}, u32[]{:S(2)}, u32[]{:S(2)}) collective-permute-start(bf16[128,768]{1,0:T(8,128)(2,1)} %get-tuple-element.126), channel_id=1, source_target_pairs={{0,16},{1,17},{2,18},{3,19},{4,20},{5,21},{6,22},{7,23},{8,24},{9,... | collective-permute-start | bytes 589832 | tf_op jit(solution)/shard_map/ppermute | solution.py:1108
  129.8 9.0 %collective-permute-start.18 = (bf16[128,768]{1,0:T(8,128)(2,1)}, bf16[128,768]{1,0:T(8,128)(2,1)S(1)}, u32[]{:S(2)}, u32[]{:S(2)}) collective-permute-start(bf16[128,768]{1,0:T(8,128)(2,1)} %get-tuple-element.127), channel_id=1, source_target_pairs={{0,24},{1,25},{2,26},{3,27},{4,28},{5,29},{6,30},{7,31},{8,0},{9,1... | collective-permute-start | bytes 589832 | tf_op jit(solution)/shard_map/ppermute | solution.py:1108
  131.6 7.2 %copy-start.6 = (bf16[128,768]{1,0:T(8,128)(2,1)S(1)}, bf16[128,768]{1,0:T(8,128)(2,1)}, u32[]{:S(2)}) copy-start(bf16[128,768]{1,0:T(8,128)(2,1)} %copy-done.5) | copy-start | bytes 589828
  131.6 7.2 %copy-start.15 = (bf16[128,768]{1,0:T(8,128)(2,1)S(1)}, bf16[128,768]{1,0:T(8,128)(2,1)}, u32[]{:S(2)}) copy-start(bf16[128,768]{1,0:T(8,128)(2,1)} %get-tuple-element.124.refs_0_) | copy-start | bytes 589828
  137.2 4.4 %collective-permute-start.19 = (bf16[768,768]{1,0:T(8,128)(2,1)}, bf16[768,768]{1,0:T(8,128)(2,1)S(1)}, u32[]{:S(2)}, u32[]{:S(2)}) collective-permute-start(bf16[768,768]{1,0:T(8,128)(2,1)} %get-tuple-element.134), channel_id=1, source_target_pairs={{0,1},{1,0},{2,3},{3,2},{4,5},{5,4},{6,7},{7,6},{8,9},{9,8},{10,11... | collective-permute-start | bytes 3538952 | tf_op jit(solution)/shard_map/ppermute | solution.py:1108
  138.8 2.8 %copy-start.8 = (f32[768,768]{1,0:T(8,128)S(1)}, f32[768,768]{1,0:T(8,128)}, u32[]{:S(2)}) copy-start(f32[768,768]{1,0:T(8,128)} %get-tuple-element.135.refs_0_) | copy-start | bytes 7077892
  144.3 21.2 %all-to-all-start.4 = ((bf16[16,24,768]{2,1,0:T(8,128)(2,1)}), bf16[16,24,768]{2,1,0:T(8,128)(2,1)S(1)}, u32[]{:S(2)}, u32[]{:S(2)}) async-start(bf16[16,24,768]{2,1,0:T(8,128)(2,1)} %get-tuple-element.137), calls=%async_computation.4 | async-start | bytes 1179648 | tf_op jit(solution)/shard_map/all_to_all | solution.py:1120
  165.5 12.2 %copy-start.19 = (bf16[16,24,768]{2,1,0:T(8,128)(2,1)}, bf16[16,24,768]{2,1,0:T(8,128)(2,1)S(1)}, u32[]{:S(2)}) copy-start(bf16[16,24,768]{2,1,0:T(8,128)(2,1)S(1)} %all-to-all-done.4.refs_4_) | copy-start | bytes 1769476
  165.5 13.5 %all-to-all-start.5 = ((bf16[4,128,768]{2,1,0:T(8,128)(2,1)}), bf16[4,128,768]{2,1,0:T(8,128)(2,1)S(1)}, u32[]{:S(2)}, u32[]{:S(2)}) async-start(bf16[4,128,768]{2,1,0:T(8,128)(2,1)} %get-tuple-element.139), calls=%async_computation.5 | async-start | bytes 1572864 | tf_op jit(solution)/shard_map/all_to_all | solution.py:1303
  177.6 2.7 %collective-permute-start.21 = (bf16[2,4,128,192]{3,2,1,0:T(8,128)(2,1)}, bf16[2,4,128,192]{3,2,1,0:T(8,128)(2,1)S(1)}, u32[]{:S(2)}, u32[]{:S(2)}) collective-permute-start(bf16[2,4,128,192]{3,2,1,0:T(8,128)(2,1)} %get-tuple-element.144), channel_id=1, source_target_pairs={{0,1},{1,0},{2,3},{3,2},{4,5},{5,4},{6,7},{7,6},{8,9},{9,8},{10,11... | collective-permute-start | bytes 1179656 | tf_op jit(solution)/shard_map/ppermute | solution.py:1108
  177.7 2.6 %collective-permute-start.22 = (bf16[4,24,768]{2,1,0:T(8,128)(2,1)}, bf16[4,24,768]{2,1,0:T(8,128)(2,1)S(1)}, u32[]{:S(2)}, u32[]{:S(2)}) collective-permute-start(bf16[4,24,768]{2,1,0:T(8,128)(2,1)} %get-tuple-element.148), channel_id=1, source_target_pairs={{0,1},{1,0},{2,3},{3,2},{4,5},{5,4},{6,7},{7,6},{8,9},{9,8},{10,11... | collective-permute-start | bytes 442376 | tf_op jit(solution)/shard_map/ppermute | solution.py:1108
  179.7 27.9 %collective-permute-start.20 = (bf16[128,768]{1,0:T(8,128)(2,1)S(1)}, bf16[128,768]{1,0:T(8,128)(2,1)S(1)}, u32[]{:S(2)}, u32[]{:S(2)}) collective-permute-start(bf16[128,768]{1,0:T(8,128)(2,1)S(1)} %layer.1), channel_id=1, source_target_pairs={{0,0},{1,1},{2,8},{3,9},{4,16},{5,17},{6,24},{7,25},{8,2},{9,3},{1... | collective-permute-start | bytes 589832 | tf_op jit(solution)/shard_map/ppermute | solution.py:1108
  186.6 7.9 %copy-start.33 = (bf16[128,768]{1,0:T(8,128)(2,1)S(1)}, bf16[128,768]{1,0:T(8,128)(2,1)}, u32[]{:S(2)}) copy-start(bf16[128,768]{1,0:T(8,128)(2,1)} %get-tuple-element.151) | copy-start | bytes 589828
  186.6 8.3 %copy-start.31 = (bf16[128,768]{1,0:T(8,128)(2,1)S(1)}, bf16[128,768]{1,0:T(8,128)(2,1)}, u32[]{:S(2)}) copy-start(bf16[128,768]{1,0:T(8,128)(2,1)} %get-tuple-element.152) | copy-start | bytes 589828
  186.6 9.7 %copy-start.30 = (bf16[128,768]{1,0:T(8,128)(2,1)S(1)}, bf16[128,768]{1,0:T(8,128)(2,1)}, u32[]{:S(2)}) copy-start(bf16[128,768]{1,0:T(8,128)(2,1)} %get-tuple-element.153) | copy-start | bytes 589828
  186.6 27.9 %all-to-all-start.7 = ((bf16[4,128,768]{2,1,0:T(8,128)(2,1)}), bf16[4,128,768]{2,1,0:T(8,128)(2,1)S(1)}, u32[]{:S(2)}, u32[]{:S(2)}) async-start(bf16[4,128,768]{2,1,0:T(8,128)(2,1)} %get-tuple-element.165), calls=%async_computation.7 | async-start | bytes 1572864 | tf_op jit(solution)/shard_map/all_to_all | solution.py:1117
  194.5 9.7 %collective-permute-start.23 = (bf16[128,768]{1,0:T(8,128)(2,1)S(1)}, bf16[128,768]{1,0:T(8,128)(2,1)S(1)}, u32[]{:S(2)}, u32[]{:S(2)}) collective-permute-start(bf16[128,768]{1,0:T(8,128)(2,1)S(1)} %copy-done.33), channel_id=1, source_target_pairs={{0,8},{1,9},{2,10},{3,11},{4,12},{5,13},{6,14},{7,15},{8,16},{9,17... | collective-permute-start | bytes 589832 | tf_op jit(solution)/shard_map/ppermute | solution.py:1108
  194.9 10.2 %collective-permute-start.24 = (bf16[128,768]{1,0:T(8,128)(2,1)S(1)}, bf16[128,768]{1,0:T(8,128)(2,1)S(1)}, u32[]{:S(2)}, u32[]{:S(2)}) collective-permute-start(bf16[128,768]{1,0:T(8,128)(2,1)S(1)} %copy-done.31), channel_id=1, source_target_pairs={{0,16},{1,17},{2,18},{3,19},{4,20},{5,21},{6,22},{7,23},{8,24},{9,... | collective-permute-start | bytes 589832 | tf_op jit(solution)/shard_map/ppermute | solution.py:1108
  196.3 8.8 %collective-permute-start.25 = (bf16[128,768]{1,0:T(8,128)(2,1)S(1)}, bf16[128,768]{1,0:T(8,128)(2,1)S(1)}, u32[]{:S(2)}, u32[]{:S(2)}) collective-permute-start(bf16[128,768]{1,0:T(8,128)(2,1)S(1)} %copy-done.30), channel_id=1, source_target_pairs={{0,24},{1,25},{2,26},{3,27},{4,28},{5,29},{6,30},{7,31},{8,0},{9,1... | collective-permute-start | bytes 589832 | tf_op jit(solution)/shard_map/ppermute | solution.py:1108
  197.8 7.4 %copy-start.13 = (bf16[128,768]{1,0:T(8,128)(2,1)S(1)}, bf16[128,768]{1,0:T(8,128)(2,1)}, u32[]{:S(2)}) copy-start(bf16[128,768]{1,0:T(8,128)(2,1)} %get-tuple-element.150.refs_0_) | copy-start | bytes 589828
  204.0 3.5 %collective-permute-start.27 = (bf16[384,640]{1,0:T(8,128)(2,1)}, bf16[384,640]{1,0:T(8,128)(2,1)S(1)}, u32[]{:S(2)}, u32[]{:S(2)}) collective-permute-start(bf16[384,640]{1,0:T(8,128)(2,1)} %get-tuple-element.161), channel_id=1, source_target_pairs={{0,1},{1,0},{2,3},{3,2},{4,5},{5,4},{6,7},{7,6},{8,9},{9,8},{10,11... | collective-permute-start | bytes 1474568 | tf_op jit(solution)/shard_map/ppermute | solution.py:1108
  214.5 4.5 %copy-start.18 = (bf16[4,128,768]{2,1,0:T(8,128)(2,1)}, bf16[4,128,768]{2,1,0:T(8,128)(2,1)S(1)}, u32[]{:S(2)}) copy-start(bf16[4,128,768]{2,1,0:T(8,128)(2,1)S(1)} %all-to-all-done.7.refs_5_) | copy-start | bytes 2359300
  214.5 18.5 %all-to-all-start.6 = ((bf16[16,24,640]{2,1,0:T(8,128)(2,1)}), bf16[16,24,640]{2,1,0:T(8,128)(2,1)S(1)}, u32[]{:S(2)}, u32[]{:S(2)}) async-start(bf16[16,24,640]{2,1,0:T(8,128)(2,1)} %add_early.1), calls=%async_computation.6 | async-start | bytes 983040 | tf_op jit(solution)/shard_map/all_to_all | solution.py:1120
  218.3 18.1 %collective-permute-start.26 = (bf16[128,768]{1,0:T(8,128)(2,1)S(1)}, bf16[128,768]{1,0:T(8,128)(2,1)S(1)}, u32[]{:S(2)}, u32[]{:S(2)}) collective-permute-start(bf16[128,768]{1,0:T(8,128)(2,1)S(1)} %last.1), channel_id=1, source_target_pairs={{0,0},{1,1},{2,8},{3,9},{4,16},{5,17},{6,24},{7,25},{8,2},{9,3},{1... | collective-permute-start | bytes 589832 | tf_op jit(solution)/shard_map/ppermute | solution.py:1108
  (10 other events, 11.1 us)

commit v4 on v3

--- a/solution.py
+++ b/solution.py
@@ -1146,7 +1146,7 @@
         fc_bias,
         scalars=scalar_ties,
         scratch=[pltpu.VMEM((ties, ranks, rows, lanes), bf16)],
-        us=2.0,
+        us=0.1,
         name="pack",
     )
     packed = early
@@ -1211,7 +1211,7 @@
         us=2.0,
         name="pack_late",
     )
-    cols = from_members(gate(cols, q))
+    cols = from_members(gate(cols, q, late_fc))
     late_fc = over_squad(gate(late_fc, grad_own, cols))
     kv = from_members(gate(kv, grad_own))
     grads_seen = [grad_own] + [send(grad_own, to_rank[ranks - k]) for k in range(1, ranks)]
@@ -1329,7 +1329,7 @@
             pltpu.VMEM((group, 2, ranks, size, width), f32),
             pltpu.VMEM((planes, group, rows, model), f32),
         ],
-        us=10.0,
+        us=0.5,
         name="attend_back",
     )
     dkv, dq, dw_out = rest[:group], rest[group], rest[group + 1 :]
@@ -1401,7 +1401,7 @@
         late_fc,
         gate(late_rest, input_own),
         scalars=scalar_ties,
-        us=3.0,
+        us=60.0,
         name="final_late",
     )
     early = gate(early, grad_fc_weight)

time: 242 us -> 239 us (0.988); the launches traced: 238 us -> 238 us
  starting transfers between devices: 67.8 us -> 70.5 us
    all_to_all x3, waiting for transfers between devices: 13.8 us -> 9.48 us  [over_planes(): return lax.all_to_all(pieces, 'seq', 0, 0, axis_index_groups=same_member)]
    unnamed x78 -> x76, local copies, waits for them, and re-layouts: 6.75 us -> 6.72 us
  transfers between devices with their start and end apart: 36 -> 36, of which waited for: 15 -> 16; matrix products, arithmetic and copies ran while one was open for 0% -> 0% of each run, Pallas kernels for 26% -> 26%
where the time goes in v4:
time: 239 us; the launch traced here: 238 us
  Pallas kernels  71.5 us (30%)
  starting transfers between devices  70.5 us (29%)
  blocking collectives  46.2 us (19%)
  waiting for transfers between devices  40.8 us (17%)
  local copies, waits for them, and re-layouts  6.72 us (3%)
    pallas_call x17, Pallas kernels, run(): pl.pallas_call(body, out_shape=shapes, in_specs=[SMEM if k in scalars els...  71.5 us
    ppermute x28, starting transfers between devices, send(): return lax.ppermute(values, axes, pairs)  27.9 us
    all_to_all x4, starting transfers between devices, over_squad(): return lax.all_to_all(pieces, axes, 0, 0, axis_index_groups=squad)  20.7 us
    ppermute x28, waiting for transfers between devices, send(): return lax.ppermute(values, axes, pairs)  18.8 us
    all_to_all x3, starting transfers between devices, over_planes(): return lax.all_to_all(pieces, 'seq', 0, 0, axis_index_groups=same_member)  18.2 us
    all_gather x1, blocking collectives, fast_device(): tokens_all = lax.all_gather(tokens_own, 'dp', axis=0, tiled=True)  16.7 us
    all_gather x1, blocking collectives, fast_device(): low = lax.all_gather(gate(low_own, late_fc), 'dp', axis=0, tiled=True)  16.3 us
    all_gather x1, blocking collectives, fast_device(): h_two = lax.all_gather(h_own, 'dp', axis=0, tiled=True)  13.2 us
  transfers between devices with their start and end apart: 36, of which 16 were waited for; matrix products, arithmetic and copies ran while one was open for 0% of the time, Pallas kernels for 26%

profile of v4, /device:TPU:0, one launch (start us, length us, event | category | flops | bytes accessed | tf_op | source)
XLA Modules:
  0.0 237.9 jit_solution(15647883140136601551)
XLA Ops:
  0.6 3.0 %collective-permute-start.2 = (s32[1]{0:T(128)}, s32[1]{0:T(128)}, u32[]{:S(2)}, u32[]{:S(2)}) collective-permute-start(s32[1]{0:T(128)} %param.16), channel_id=1, source_target_pairs={{0,16},{1,17},{2,18},{3,19},{4,20},{5,21},{6,22},{7,23},{8,24},{9,... | collective-permute-start | bytes 20 | tf_op jit(solution)/shard_map/ppermute | solution.py:1108
  3.7 1.4 collective-permute-start.1
  5.7 1.6 collective-permute-start
  8.0 1.7 collective-permute-done.3.refs_3_
  9.8 4.3 %pack.1 = (bf16[16,24,640]{2,1,0:T(8,128)(2,1)}, bf16[4,32,768]{2,1,0:T(8,128)(2,1)}) custom-call(s32[1]{0:T(128)S(6)} %copy.31.refs_0_, s32[1]{0:T(128)} %collective-permute-done.1.refs_1_, s32[1]{0:T(128)} %collective-permute-done.2.refs_2_, s32[1]{0:T(128)} %collective-permute-done.3.refs_3_, bf16[2,24,2304]{2,1,0:T(8,128)(2,1)} %refs_4_.1, ...), custom_call_target="tpu_custom_call" | custom-call | flops 100000000 | bytes 350000 | tf_op jit(solution)/shard_map/pack/pallas_call | solution.py:555
  14.1 6.9 %all-to-all-start = ((bf16[16,24,640]{2,1,0:T(8,128)(2,1)}), bf16[16,24,640]{2,1,0:T(8,128)(2,1)S(1)}, u32[]{:S(2)}, u32[]{:S(2)}) async-start(bf16[16,24,640]{2,1,0:T(8,128)(2,1)} %get-tuple-element.98), calls=%async_computation | async-start | bytes 983040 | tf_op jit(solution)/shard_map/all_to_all | solution.py:1120
  21.2 16.7 %all_gather.9.refs_0_.refs_2_ = bf16[512,768]{1,0:T(8,128)(2,1)S(1)} all-gather(bf16[128,768]{1,0:T(8,128)(2,1)S(1)} %collective-permute-done.refs_4_), channel_id=1, replica_groups=mesh['dp'=4,'seq'=8] {'dp'}, dimensions={0}, use_global_device_ids=true | all-gather | bytes 983040 | tf_op jit(solution)/shard_map/all_gather | solution.py:1178
  38.0 1.6 collective-permute-start.5
  39.6 6.0 %all-to-all-start.1 = ((bf16[4,32,768]{2,1,0:T(8,128)(2,1)}), bf16[4,32,768]{2,1,0:T(8,128)(2,1)S(1)}, u32[]{:S(2)}, u32[]{:S(2)}) async-start(bf16[4,32,768]{2,1,0:T(8,128)(2,1)} %get-tuple-element.105), calls=%async_computation.1 | async-start | bytes 393216 | tf_op jit(solution)/shard_map/all_to_all | solution.py:1117
  45.6 5.0 %project.1 = (bf16[4,128,192]{2,1,0:T(8,128)(2,1)S(1)}, bf16[2,4,128,192]{3,2,1,0:T(8,128)(2,1)S(1)}, bf16[512,768]{1,0:T(8,128)(2,1)S(1)}, f32[8,768]{1,0:T(8,1...) custom-call(bf16[512,768]{1,0:T(8,128)(2,1)S(1)} %all_gather.9.refs_0_.refs_2_, ...), custom_call_target="tpu_custom_call" | custom-call | flops 5000000000 | bytes 17500000 | tf_op jit(solution)/shard_map/project/pallas_call | solution.py:555
  50.7 1.0 copy-done.11
  51.7 0.9 copy-done.13
  52.6 3.9 %pack_late.1 = (bf16[16,24,768]{2,1,0:T(8,128)(2,1)}, bf16[4,96,768]{2,1,0:T(8,128)(2,1)}) custom-call(s32[1]{0:T(128)S(6)} %copy.31.refs_0_, s32[1]{0:T(128)} %collective-permute-done.1.refs_1_, s32[1]{0:T(128)} %collective-permute-done.2.refs_2_, s32[1]{0:T(128)} %collective-permute-done.3.refs_3_, bf16[2,24,3072]{2,1,0:T(8,128)(2,1)} %refs_4_.2, ...), custom_call_target="tpu_custom_call" | custom-call | flops 2000000000 | bytes 7000000 | tf_op jit(solution)/shard_map/pack_late/pallas_call | solution.py:555
  56.5 2.7 %all-to-all-done.1.refs_3_ = bf16[4,32,768]{2,1,0:T(8,128)(2,1)S(1)} async-done(((bf16[4,32,768]{2,1,0:T(8,128)(2,1)}), bf16[4,32,768]{2,1,0:T(8,128)(2,1)S(1)}, u32[]{:S(2)}, u32[]{:S(2)}) %all-to-all-start.1) | async-done | bytes 196640 | tf_op jit(solution)/shard_map/all_to_all | solution.py:1117
  59.3 1.4 collective-permute-done.7.refs_4_
  60.7 5.3 %all-to-all-start.2 = ((bf16[16,24,768]{2,1,0:T(8,128)(2,1)}), bf16[16,24,768]{2,1,0:T(8,128)(2,1)S(1)}, u32[]{:S(2)}, u32[]{:S(2)}) async-start(bf16[16,24,768]{2,1,0:T(8,128)(2,1)} %get-tuple-element.116), calls=%async_computation.2 | async-start | bytes 1179648 | tf_op jit(solution)/shard_map/all_to_all | solution.py:1120
  66.1 2.0 collective-permute-start.13
  68.1 1.5 collective-permute-start.12
  69.6 1.5 collective-permute-start.11
  71.0 0.8 copy-done.21
  71.8 5.3 %attend.1 = (bf16[512,192]{1,0:T(8,128)(2,1)}, f32[8,384]{1,0:T(8,128)}, bf16[192,768]{1,0:T(8,128)(2,1)}, bf16[128,768]{1,0:T(8,128)(2,1)}, bf16[128,768]{1,0:T...) custom-call(bf16[4,128,192]{2,1,0:T(8,128)(2,1)} %copy-done.2, bf16[2,4,128,192]{3,2,1,0:T(8,128)(2,1)} %copy-done.1, ...), custom_call_target="tpu_custom_call" | custom-call | flops 6000000000 | bytes 21000000 | tf_op jit(solution)/shard_map/attend/pallas_call | solution.py:555
  77.2 3.3 %collective-permute-done.13.refs_7_ = bf16[128,768]{1,0:T(8,128)(2,1)S(1)} collective-permute-done((bf16[128,768]{1,0:T(8,128)(2,1)S(1)}, bf16[128,768]{1,0:T(8,128)(2,1)S(1)}, u32[]{:S(2)}, u32[]{:S(2)}) %collective-permute-start.13) | collective-permute-done | bytes 196640 | tf_op jit(solution)/shard_map/ppermute | solution.py:1108
  80.5 2.9 %collective-permute-done.12.refs_6_ = bf16[128,768]{1,0:T(8,128)(2,1)S(1)} collective-permute-done((bf16[128,768]{1,0:T(8,128)(2,1)S(1)}, bf16[128,768]{1,0:T(8,128)(2,1)S(1)}, u32[]{:S(2)}, u32[]{:S(2)}) %collective-permute-start.12) | collective-permute-done | bytes 196640 | tf_op jit(solution)/shard_map/ppermute | solution.py:1108
  84.0 4.3 %all-to-all-start.3 = ((bf16[4,96,768]{2,1,0:T(8,128)(2,1)}), bf16[4,96,768]{2,1,0:T(8,128)(2,1)S(1)}, u32[]{:S(2)}, u32[]{:S(2)}) async-start(bf16[4,96,768]{2,1,0:T(8,128)(2,1)} %get-tuple-element.121), calls=%async_computation.3 | async-start | bytes 1179648 | tf_op jit(solution)/shard_map/all_to_all | solution.py:1117
  88.4 1.5 collective-permute-start.8
  90.4 2.0 collective-permute-start.10
  92.4 4.7 %collective-permute-done.8.refs_1_ = bf16[128,768]{1,0:T(8,128)(2,1)S(1)} collective-permute-done((bf16[128,768]{1,0:T(8,128)(2,1)S(1)}, bf16[128,768]{1,0:T(8,128)(2,1)S(1)}, u32[]{:S(2)}, u32[]{:S(2)}) %collective-permute-start.8) | collective-permute-done | bytes 196640 | tf_op jit(solution)/shard_map/ppermute | solution.py:1108
  97.1 2.3 collective-permute-done.9.refs_2_
  99.5 2.8 %join.1 = (f32[128,768]{1,0:T(8,128)S(1)}, bf16[128,768]{1,0:T(8,128)(2,1)S(1)}) custom-call(bf16[128,768]{1,0:T(8,128)(2,1)S(1)} %copy-done.12, bf16[128,768]{1,0:T(8,128)(2,1)S(1)} %collective-permute-done.8.refs_1_, bf16[128,768]{1,0:T(8,128)(2,1)S(1)} %collective-permute-done.9.refs_2_, bf16[128,768]{1,0:T(8,128)(2,1)S(1)} %collective-permute-done.10.refs_3_, ...), custom_call_target="tpu_custom_call" | custom-call | flops 2000000000 | bytes 7000000 | tf_op jit(solution)/shard_map/join/pallas_call | solution.py:555
  102.5 1.8 all-to-all-done.3.refs_8_
  104.3 13.2 %all_gather.10.refs_0_ = bf16[512,768]{1,0:T(8,128)(2,1)} all-gather(bf16[128,768]{1,0:T(8,128)(2,1)S(1)} %get-tuple-element.115), channel_id=1, replica_groups=mesh['dp'=4,'seq'=8] {'dp'}, dimensions={0}, use_global_device_ids=true | all-gather | bytes 983040 | tf_op jit(solution)/shard_map/all_gather | solution.py:1244
  117.5 0.8 copy-done.23
  118.5 7.2 %mlp.1 = (bf16[128,768]{1,0:T(8,128)(2,1)}, bf16[128,768]{1,0:T(8,128)(2,1)}, bf16[128,768]{1,0:T(8,128)(2,1)}, bf16[128,768]{1,0:T(8,128)(2,1)}, bf16[4,128,768...) custom-call(bf16[512,768]{1,0:T(8,128)(2,1)} %all_gather.10.refs_0_, ...), custom_call_target="tpu_custom_call" | custom-call | flops 7000000000 | bytes 24500000 | tf_op jit(solution)/shard_map/mlp/pallas_call | solution.py:555
  125.7 1.0 collective-permute-start.16
  126.7 1.1 collective-permute-start.17
  127.8 1.9 collective-permute-start.18
  129.7 5.6 %mlp_grad.1 = (f32[768,768]{1,0:T(8,128)}, bf16[768,768]{1,0:T(8,128)(2,1)}, f32[8,768]{1,0:T(8,128)}) custom-call(bf16[512,768]{1,0:T(8,128)(2,1)} %all_gather.10.refs_0_, bf16[512,768]{1,0:T(8,128)(2,1)} %get-tuple-element.130.refs_1_, bf16[512,768]{1,0:T(8,128)(2,1)} %get-tuple-element.131.refs_2_, bf16[512,768]{1,0:T(8,128)(2,1)} %get-tuple-element.132.refs_3_), custom_call_target="tpu_custom_call" | custom-call | flops 4000000000 | bytes 14000000 | tf_op jit(solution)/shard_map/mlp_grad/pallas_call | solution.py:555
  135.4 1.5 collective-permute-done.17.refs_2_
  136.9 2.8 %join_back.1 = (f32[128,768]{1,0:T(8,128)S(1)}, bf16[128,768]{1,0:T(8,128)(2,1)S(1)}, f32[8,768]{1,0:T(8,128)S(1)}) custom-call(bf16[128,768]{1,0:T(8,128)(2,1)S(1)} %copy-done.15, bf16[128,768]{1,0:T(8,128)(2,1)S(1)} %collective-permute-done.16.refs_1_, bf16[128,768]{1,0:T(8,128)(2,1)S(1)} %collective-permute-done.17.refs_2_, ...), custom_call_target="tpu_custom_call" | custom-call | flops 30000001024 | bytes 105000000 | tf_op jit(solution)/shard_map/join_back/pallas_call | solution.py:555
  139.7 1.8 add_late.1
  141.5 0.8 copy-done.10
  142.3 4.6 %all-to-all-start.4 = ((bf16[16,24,768]{2,1,0:T(8,128)(2,1)}), bf16[16,24,768]{2,1,0:T(8,128)(2,1)S(1)}, u32[]{:S(2)}, u32[]{:S(2)}) async-start(bf16[16,24,768]{2,1,0:T(8,128)(2,1)} %get-tuple-element.137), calls=%async_computation.4 | async-start | bytes 1179648 | tf_op jit(solution)/shard_map/all_to_all | solution.py:1120
  146.9 16.3 %all_gather.11.refs_0_ = bf16[512,768]{1,0:T(8,128)(2,1)} all-gather(bf16[128,768]{1,0:T(8,128)(2,1)S(1)} %get-tuple-element.138), channel_id=1, replica_groups=mesh['dp'=4,'seq'=8] {'dp'}, dimensions={0}, use_global_device_ids=true | all-gather | bytes 983040 | tf_op jit(solution)/shard_map/all_gather | solution.py:1301
  163.5 3.7 %all-to-all-start.5 = ((bf16[4,128,768]{2,1,0:T(8,128)(2,1)}), bf16[4,128,768]{2,1,0:T(8,128)(2,1)S(1)}, u32[]{:S(2)}, u32[]{:S(2)}) async-start(bf16[4,128,768]{2,1,0:T(8,128)(2,1)} %get-tuple-element.139), calls=%async_computation.5 | async-start | bytes 1572864 | tf_op jit(solution)/shard_map/all_to_all | solution.py:1303
  167.3 8.4 %attend_back.1 = (f32[2,4,128,192]{3,2,1,0:T(8,128)}, bf16[2,4,128,192]{3,2,1,0:T(8,128)(2,1)}, bf16[512,192]{1,0:T(8,128)(2,1)}, f32[4,24,768]{2,1,0:T(8,128)}, bf16[4,24,768]{2,1,0:T(8,128)(2,1)}) custom-call(bf16[512,768]{1,0:T(8,128)(2,1)} %all_gather.11.refs_0_, bf16[192,768]{1,0:T(8,128)(2,1)} %get-tuple-element.140.refs_1_, ...), custom_call_target="tpu_custom_call" | custom-call | flops 500000000 | bytes 1750000 | tf_op jit(solution)/shard_map/attend_back/pallas_call | solution.py:555
  176.3 0.7 all-to-all-done.5.refs_0_
  177.0 0.7 layer.1
  177.7 0.7 collective-permute-start.20
  179.3 5.4 %first.1 = (bf16[128,768]{1,0:T(8,128)(2,1)}, bf16[128,768]{1,0:T(8,128)(2,1)}, bf16[128,768]{1,0:T(8,128)(2,1)}, bf16[128,768]{1,0:T(8,128)(2,1)}, bf16[4,128,7...) custom-call(bf16[512,192]{1,0:T(8,128)(2,1)} %get-tuple-element.142.refs_0_, ...), custom_call_target="tpu_custom_call" | custom-call | flops 4000000000 | bytes 14000000 | tf_op jit(solution)/shard_map/first/pallas_call | solution.py:555
  184.7 7.8 %all-to-all-start.7 = ((bf16[4,128,768]{2,1,0:T(8,128)(2,1)}), bf16[4,128,768]{2,1,0:T(8,128)(2,1)}, u32[]{:S(2)}, u32[]{:S(2)}) async-start(bf16[4,128,768]{2,1,0:T(8,128)(2,1)} %get-tuple-element.165), calls=%async_computation.7 | async-start | bytes 1572864 | tf_op jit(solution)/shard_map/all_to_all | solution.py:1117
  192.5 1.1 collective-permute-start.23
  193.6 1.4 collective-permute-start.24
  195.0 2.0 collective-permute-start.25
  197.0 6.2 %first_grad.1 = (f32[384,640]{1,0:T(8,128)}, bf16[384,640]{1,0:T(8,128)(2,1)}) custom-call(bf16[512,768]{1,0:T(8,128)(2,1)} %copy-done.13, bf16[512,576]{1,0:T(8,128)(2,1)} %get-tuple-element.156.refs_1_, bf16[512,768]{1,0:T(8,128)(2,1)} %copy-done, bf16[4,128,768]{2,1,0:T(8,128)(2,1)} %get-tuple-element.157.refs_3_, f32[8,768]{1,0:T(8,128)} %copy-done.16, ...), custom_call_target="tpu_custom_call" | custom-call | flops 5000000000 | bytes 17500000 | tf_op jit(solution)/shard_map/first_grad/pallas_call | solution.py:555
  203.8 2.4 %last.1 = bf16[128,768]{1,0:T(8,128)(2,1)S(1)} custom-call(bf16[128,768]{1,0:T(8,128)(2,1)S(1)} %copy-done.14, bf16[128,768]{1,0:T(8,128)(2,1)S(1)} %collective-permute-done.23.refs_1_, bf16[128,768]{1,0:T(8,128)(2,1)S(1)} %collective-permute-done.24.refs_2_, bf16[128,768]{1,0:T(8,128)(2,1)S(1)} %collective-permute-done.25.refs_3_, ...), custom_call_target="tpu_custom_call" | custom-call | flops 30000001024 | bytes 105000000 | tf_op jit(solution)/shard_map/last/pallas_call | solution.py:555
  206.2 0.7 collective-permute-start.26
  206.9 1.6 add_early.1
  208.5 4.9 %all-to-all-done.7.refs_5_ = bf16[4,128,768]{2,1,0:T(8,128)(2,1)} async-done(((bf16[4,128,768]{2,1,0:T(8,128)(2,1)}), bf16[4,128,768]{2,1,0:T(8,128)(2,1)}, u32[]{:S(2)}, u32[]{:S(2)}) %all-to-all-start.7) | async-done | bytes 786464 | tf_op jit(solution)/shard_map/all_to_all | solution.py:1117
  213.5 4.0 %all-to-all-start.6 = ((bf16[16,24,640]{2,1,0:T(8,128)(2,1)}), bf16[16,24,640]{2,1,0:T(8,128)(2,1)S(1)}, u32[]{:S(2)}, u32[]{:S(2)}) async-start(bf16[16,24,640]{2,1,0:T(8,128)(2,1)} %add_early.1), calls=%async_computation.6 | async-start | bytes 983040 | tf_op jit(solution)/shard_map/all_to_all | solution.py:1120
  217.5 4.5 %final_late.1 = (f32[2,24,3072]{2,1,0:T(8,128)}, f32[2,96,768]{2,1,0:T(8,128)}, f32[2,24,768]{2,1,0:T(8,128)}) custom-call(s32[1]{0:T(128)S(6)} %copy.31.refs_0_, s32[1]{0:T(128)} %collective-permute-done.1.refs_1_, s32[1]{0:T(128)} %collective-permute-done.2.refs_2_, s32[1]{0:T(128)} %collective-permute-done.3.refs_3_, bf16[16,24,768]{2,1,0:T(8,128)(2,1)} %copy-done.18, ...), custom_call_target="tpu_custom_call" | custom-call | flops 60000002048 | bytes 210000000 | tf_op jit(solution)/shard_map/final_late/pallas_call | solution.py:555
  222.0 11.2 %all-to-all-done.6.refs_4_ = bf16[16,24,640]{2,1,0:T(8,128)(2,1)S(1)} async-done(((bf16[16,24,640]{2,1,0:T(8,128)(2,1)}), bf16[16,24,640]{2,1,0:T(8,128)(2,1)S(1)}, u32[]{:S(2)}, u32[]{:S(2)}) %all-to-all-start.6) | async-done | bytes 491552 | tf_op jit(solution)/shard_map/all_to_all | solution.py:1120
  233.1 3.3 %final.1 = (f32[2,24,2304]{2,1,0:T(8,128)}, f32[2,24]{1,0:T(2,128)}, f32[2,24]{1,0:T(2,128)}, f32[2,24]{1,0:T(2,128)}, f32[2,24]{1,0:T(2,128)}, /*index=5*/f32[2...) custom-call(s32[1]{0:T(128)S(6)} %copy.31.refs_0_, s32[1]{0:T(128)} %collective-permute-done.1.refs_1_, ...), custom_call_target="tpu_custom_call" | custom-call | flops 1000000000 | bytes 3500000 | tf_op jit(solution)/shard_map/final/pallas_call | solution.py:555
  236.5 0.7 copy.32
  237.2 0.7 copy.33
  (112 shorter events, 4.8 us)
Async XLA Ops:
  0.6 7.4 %collective-permute-start.2 = (s32[1]{0:T(128)}, s32[1]{0:T(128)}, u32[]{:S(2)}, u32[]{:S(2)}) collective-permute-start(s32[1]{0:T(128)} %param.16), channel_id=1, source_target_pairs={{0,16},{1,17},{2,18},{3,19},{4,20},{5,21},{6,22},{7,23},{8,24},{9,... | collective-permute-start | bytes 20 | tf_op jit(solution)/shard_map/ppermute | solution.py:1108
  3.7 4.4 %collective-permute-start.1 = (s32[1]{0:T(128)}, s32[1]{0:T(128)}, u32[]{:S(2)}, u32[]{:S(2)}) collective-permute-start(s32[1]{0:T(128)} %param.16), channel_id=1, source_target_pairs={{0,24},{1,25},{2,26},{3,27},{4,28},{5,29},{6,30},{7,31},{8,0},{9,1... | collective-permute-start | bytes 20 | tf_op jit(solution)/shard_map/ppermute | solution.py:1108
  5.1 4.7 %collective-permute-start.3 = (s32[1]{0:T(128)}, s32[1]{0:T(128)}, u32[]{:S(2)}, u32[]{:S(2)}) collective-permute-start(s32[1]{0:T(128)} %param.16), channel_id=1, source_target_pairs={{0,8},{1,9},{2,10},{3,11},{4,12},{5,13},{6,14},{7,15},{8,16},{9,17... | collective-permute-start | bytes 20 | tf_op jit(solution)/shard_map/ppermute | solution.py:1108
  5.7 15.5 %collective-permute-start = (bf16[128,768]{1,0:T(8,128)(2,1)}, bf16[128,768]{1,0:T(8,128)(2,1)S(1)}, u32[]{:S(2)}, u32[]{:S(2)}) collective-permute-start(bf16[128,768]{1,0:T(8,128)(2,1)} %bitcast.6), channel_id=1, source_target_pairs={{0,0},{1,1},{2,8},{3,9},{4,16},{5,17},{6,24},{7,25},{8,2},{9,3},{1... | collective-permute-start | bytes 589832 | tf_op jit(solution)/shard_map/ppermute | solution.py:1108
  14.1 23.8 %all-to-all-start = ((bf16[16,24,640]{2,1,0:T(8,128)(2,1)}), bf16[16,24,640]{2,1,0:T(8,128)(2,1)S(1)}, u32[]{:S(2)}, u32[]{:S(2)}) async-start(bf16[16,24,640]{2,1,0:T(8,128)(2,1)} %get-tuple-element.98), calls=%async_computation | async-start | bytes 983040 | tf_op jit(solution)/shard_map/all_to_all | solution.py:1120
  21.1 29.6 %copy-start.3 = (f32[16,1152]{1,0:T(8,128)}, f32[16,1152]{1,0:T(8,128)S(1)}, u32[]{:S(2)}) copy-start(f32[16,1152]{1,0:T(8,128)S(1)} %fusion.refs_5_.refs_6_) | copy-start | bytes 221188
  21.1 29.6 %copy-start.4 = (s32[1,1152]{1,0:T(1,128)}, s32[1,1152]{1,0:T(1,128)S(1)}, u32[]{:S(2)}) copy-start(s32[1,1152]{1,0:T(1,128)S(1)} %broadcast_in_dim.12.refs_4_.refs_8_) | copy-start | bytes 13828
  21.2 78.3 %copy-start.5 = (s32[1,768]{1,0:T(1,128)}, s32[1,768]{1,0:T(1,128)S(1)}, u32[]{:S(2)}) copy-start(s32[1,768]{1,0:T(1,128)S(1)} %fusion.29.refs_3_.refs_6_.refs_10_.refs_4_.refs_7_) | copy-start | bytes 9220
  37.9 12.7 %copy-start = (bf16[512,768]{1,0:T(8,128)(2,1)}, bf16[512,768]{1,0:T(8,128)(2,1)S(1)}, u32[]{:S(2)}) copy-start(bf16[512,768]{1,0:T(8,128)(2,1)S(1)} %all_gather.9.refs_0_.refs_2_) | copy-start | bytes 2359300
  37.9 7.7 %collective-permute-start.4 = (bf16[16,24,640]{2,1,0:T(8,128)(2,1)S(1)}, bf16[16,24,640]{2,1,0:T(8,128)(2,1)S(1)}, u32[]{:S(2)}, u32[]{:S(2)}) collective-permute-start(bf16[16,24,640]{2,1,0:T(8,128)(2,1)S(1)} %all-to-all-done.refs_1_), channel_id=1, source_target_pairs={{0,1},{1,0},{2,3},{3,2},{4,5},{5,4},{6,7},{7,6},{8,9},{9,8},{10,11... | collective-permute-start | bytes 1474568 | tf_op jit(solution)/shard_map/ppermute | solution.py:1108
  38.0 21.2 %collective-permute-start.5 = (bf16[128,768]{1,0:T(8,128)(2,1)}, bf16[128,768]{1,0:T(8,128)(2,1)S(1)}, u32[]{:S(2)}, u32[]{:S(2)}) collective-permute-start(bf16[128,768]{1,0:T(8,128)(2,1)} %bitcast.1), channel_id=1, source_target_pairs={{0,0},{1,1},{2,8},{3,9},{4,16},{5,17},{6,24},{7,25},{8,2},{9,3},{1... | collective-permute-start | bytes 589832 | tf_op jit(solution)/shard_map/ppermute | solution.py:1108
  39.6 19.7 %all-to-all-start.1 = ((bf16[4,32,768]{2,1,0:T(8,128)(2,1)}), bf16[4,32,768]{2,1,0:T(8,128)(2,1)S(1)}, u32[]{:S(2)}, u32[]{:S(2)}) async-start(bf16[4,32,768]{2,1,0:T(8,128)(2,1)} %get-tuple-element.105), calls=%async_computation.1 | async-start | bytes 393216 | tf_op jit(solution)/shard_map/all_to_all | solution.py:1117
  52.6 3.9 %copy-start.2 = (bf16[4,128,192]{2,1,0:T(8,128)(2,1)}, bf16[4,128,192]{2,1,0:T(8,128)(2,1)S(1)}, u32[]{:S(2)}) copy-start(bf16[4,128,192]{2,1,0:T(8,128)(2,1)S(1)} %get-tuple-element.100.refs_0_.refs_2_) | copy-start | bytes 589828
  52.6 4.0 %copy-start.17 = (f32[8,768]{1,0:T(8,128)}, f32[8,768]{1,0:T(8,128)S(1)}, u32[]{:S(2)}) copy-start(f32[8,768]{1,0:T(8,128)S(1)} %get-tuple-element.119.refs_3_) | copy-start | bytes 73732
  52.6 13.5 %copy-start.1 = (bf16[2,4,128,192]{3,2,1,0:T(8,128)(2,1)}, bf16[2,4,128,192]{3,2,1,0:T(8,128)(2,1)S(1)}, u32[]{:S(2)}) copy-start(bf16[2,4,128,192]{3,2,1,0:T(8,128)(2,1)S(1)} %get-tuple-element.103.refs_1_.refs_3_) | copy-start | bytes 1179652
  59.3 11.8 %copy-start.22 = (bf16[4,32,768]{2,1,0:T(8,128)(2,1)}, bf16[4,32,768]{2,1,0:T(8,128)(2,1)S(1)}, u32[]{:S(2)}) copy-start(bf16[4,32,768]{2,1,0:T(8,128)(2,1)S(1)} %all-to-all-done.1.refs_3_) | copy-start | bytes 589828
  59.3 1.4 collective-permute-start.7
  59.3 17.8 %copy-start.6 = (bf16[128,768]{1,0:T(8,128)(2,1)}, bf16[128,768]{1,0:T(8,128)(2,1)S(1)}, u32[]{:S(2)}) copy-start(bf16[128,768]{1,0:T(8,128)(2,1)S(1)} %collective-permute-done.5.refs_4_.refs_5_) | copy-start | bytes 589828
  60.7 10.3 %copy-start.35 = (bf16[4,32,768]{2,1,0:T(8,128)(2,1)}, bf16[4,32,768]{2,1,0:T(8,128)(2,1)S(1)}, u32[]{:S(2)}) copy-start(bf16[4,32,768]{2,1,0:T(8,128)(2,1)S(1)} %collective-permute-done.7.refs_4_) | copy-start | bytes 589828
  60.7 23.3 %all-to-all-start.2 = ((bf16[16,24,768]{2,1,0:T(8,128)(2,1)}), bf16[16,24,768]{2,1,0:T(8,128)(2,1)S(1)}, u32[]{:S(2)}, u32[]{:S(2)}) async-start(bf16[16,24,768]{2,1,0:T(8,128)(2,1)} %get-tuple-element.116), calls=%async_computation.2 | async-start | bytes 1179648 | tf_op jit(solution)/shard_map/all_to_all | solution.py:1120
  66.0 5.0 %collective-permute-start.6 = (bf16[2,4,128,192]{3,2,1,0:T(8,128)(2,1)S(1)}, bf16[2,4,128,192]{3,2,1,0:T(8,128)(2,1)S(1)}, u32[]{:S(2)}, u32[]{:S(2)}) collective-permute-start(bf16[2,4,128,192]{3,2,1,0:T(8,128)(2,1)S(1)} %get-tuple-element.103.refs_1_.refs_3_), channel_id=1, source_target_pairs={{0,1},{1,0},{2,3},{3,2},{4,5},{5,4},{6,7},{7,6},{8,9},{9,8},{10,11... | collective-permute-start | bytes 1179656 | tf_op jit(solution)/shard_map/ppermute | solution.py:1108
  66.1 14.4 %collective-permute-start.13 = (bf16[128,768]{1,0:T(8,128)(2,1)S(1)}, bf16[128,768]{1,0:T(8,128)(2,1)S(1)}, u32[]{:S(2)}, u32[]{:S(2)}) collective-permute-start(bf16[128,768]{1,0:T(8,128)(2,1)S(1)} %collective-permute-done.5.refs_4_.refs_5_), channel_id=1, source_target_pairs={{0,8},{1,9},{2,10},{3,11},{4,12},{5,13},{6,14},{7,15},{8,16},{9,17... | collective-permute-start | bytes 589832 | tf_op jit(solution)/shard_map/ppermute | solution.py:1108
  68.1 15.4 %collective-permute-start.12 = (bf16[128,768]{1,0:T(8,128)(2,1)S(1)}, bf16[128,768]{1,0:T(8,128)(2,1)S(1)}, u32[]{:S(2)}, u32[]{:S(2)}) collective-permute-start(bf16[128,768]{1,0:T(8,128)(2,1)S(1)} %collective-permute-done.5.refs_4_.refs_5_), channel_id=1, source_target_pairs={{0,16},{1,17},{2,18},{3,19},{4,20},{5,21},{6,22},{7,23},{8,24},{9,... | collective-permute-start | bytes 589832 | tf_op jit(solution)/shard_map/ppermute | solution.py:1108
  69.6 14.2 %collective-permute-start.11 = (bf16[128,768]{1,0:T(8,128)(2,1)S(1)}, bf16[128,768]{1,0:T(8,128)(2,1)S(1)}, u32[]{:S(2)}, u32[]{:S(2)}) collective-permute-start(bf16[128,768]{1,0:T(8,128)(2,1)S(1)} %collective-permute-done.5.refs_4_.refs_5_), channel_id=1, source_target_pairs={{0,24},{1,25},{2,26},{3,27},{4,28},{5,29},{6,30},{7,31},{8,0},{9,1... | collective-permute-start | bytes 589832 | tf_op jit(solution)/shard_map/ppermute | solution.py:1108
  77.1 11.3 %copy-start.34 = (bf16[128,768]{1,0:T(8,128)(2,1)S(1)}, bf16[128,768]{1,0:T(8,128)(2,1)}, u32[]{:S(2)}) copy-start(bf16[128,768]{1,0:T(8,128)(2,1)} %get-tuple-element.110) | copy-start | bytes 589828
  77.1 12.7 %copy-start.33 = (bf16[128,768]{1,0:T(8,128)(2,1)S(1)}, bf16[128,768]{1,0:T(8,128)(2,1)}, u32[]{:S(2)}) copy-start(bf16[128,768]{1,0:T(8,128)(2,1)} %get-tuple-element.111) | copy-start | bytes 589828
  77.1 13.3 %copy-start.31 = (bf16[128,768]{1,0:T(8,128)(2,1)S(1)}, bf16[128,768]{1,0:T(8,128)(2,1)}, u32[]{:S(2)}) copy-start(bf16[128,768]{1,0:T(8,128)(2,1)} %get-tuple-element.112) | copy-start | bytes 589828
  77.2 22.3 %copy-start.12 = (bf16[128,768]{1,0:T(8,128)(2,1)S(1)}, bf16[128,768]{1,0:T(8,128)(2,1)}, u32[]{:S(2)}) copy-start(bf16[128,768]{1,0:T(8,128)(2,1)} %get-tuple-element.109.refs_0_) | copy-start | bytes 589828
  80.5 19.0 %copy-start.26 = (bf16[128,768]{1,0:T(8,128)(2,1)}, bf16[128,768]{1,0:T(8,128)(2,1)S(1)}, u32[]{:S(2)}) copy-start(bf16[128,768]{1,0:T(8,128)(2,1)S(1)} %collective-permute-done.13.refs_7_) | copy-start | bytes 589828
  83.4 16.0 %copy-start.27 = (bf16[128,768]{1,0:T(8,128)(2,1)}, bf16[128,768]{1,0:T(8,128)(2,1)S(1)}, u32[]{:S(2)}) copy-start(bf16[128,768]{1,0:T(8,128)(2,1)S(1)} %collective-permute-done.12.refs_6_) | copy-start | bytes 589828
  83.8 15.7 %copy-start.28 = (bf16[128,768]{1,0:T(8,128)(2,1)}, bf16[128,768]{1,0:T(8,128)(2,1)S(1)}, u32[]{:S(2)}) copy-start(bf16[128,768]{1,0:T(8,128)(2,1)S(1)} %collective-permute-done.11.refs_5_) | copy-start | bytes 589828
  84.0 18.3 %copy-start.19 = (bf16[16,24,768]{2,1,0:T(8,128)(2,1)}, bf16[16,24,768]{2,1,0:T(8,128)(2,1)S(1)}, u32[]{:S(2)}) copy-start(bf16[16,24,768]{2,1,0:T(8,128)(2,1)S(1)} %all-to-all-done.2.refs_1_) | copy-start | bytes 1769476
  84.0 20.2 %all-to-all-start.3 = ((bf16[4,96,768]{2,1,0:T(8,128)(2,1)}), bf16[4,96,768]{2,1,0:T(8,128)(2,1)S(1)}, u32[]{:S(2)}, u32[]{:S(2)}) async-start(bf16[4,96,768]{2,1,0:T(8,128)(2,1)} %get-tuple-element.121), calls=%async_computation.3 | async-start | bytes 1179648 | tf_op jit(solution)/shard_map/all_to_all | solution.py:1117
  88.4 8.7 %collective-permute-start.8 = (bf16[128,768]{1,0:T(8,128)(2,1)S(1)}, bf16[128,768]{1,0:T(8,128)(2,1)S(1)}, u32[]{:S(2)}, u32[]{:S(2)}) collective-permute-start(bf16[128,768]{1,0:T(8,128)(2,1)S(1)} %copy-done.34), channel_id=1, source_target_pairs={{0,8},{1,9},{2,10},{3,11},{4,12},{5,13},{6,14},{7,15},{8,16},{9,17... | collective-permute-start | bytes 589832 | tf_op jit(solution)/shard_map/ppermute | solution.py:1108
  89.9 9.6 %collective-permute-start.9 = (bf16[128,768]{1,0:T(8,128)(2,1)S(1)}, bf16[128,768]{1,0:T(8,128)(2,1)S(1)}, u32[]{:S(2)}, u32[]{:S(2)}) collective-permute-start(bf16[128,768]{1,0:T(8,128)(2,1)S(1)} %copy-done.33), channel_id=1, source_target_pairs={{0,16},{1,17},{2,18},{3,19},{4,20},{5,21},{6,22},{7,23},{8,24},{9,... | collective-permute-start | bytes 589832 | tf_op jit(solution)/shard_map/ppermute | solution.py:1108
  90.4 9.1 %collective-permute-start.10 = (bf16[128,768]{1,0:T(8,128)(2,1)S(1)}, bf16[128,768]{1,0:T(8,128)(2,1)S(1)}, u32[]{:S(2)}, u32[]{:S(2)}) collective-permute-start(bf16[128,768]{1,0:T(8,128)(2,1)S(1)} %copy-done.31), channel_id=1, source_target_pairs={{0,24},{1,25},{2,26},{3,27},{4,28},{5,29},{6,30},{7,31},{8,0},{9,1... | collective-permute-start | bytes 589832 | tf_op jit(solution)/shard_map/ppermute | solution.py:1108
  102.4 15.1 %collective-permute-start.14 = (bf16[16,24,768]{2,1,0:T(8,128)(2,1)S(1)}, bf16[16,24,768]{2,1,0:T(8,128)(2,1)S(1)}, u32[]{:S(2)}, u32[]{:S(2)}) collective-permute-start(bf16[16,24,768]{2,1,0:T(8,128)(2,1)S(1)} %all-to-all-done.2.refs_1_), channel_id=1, source_target_pairs={{0,1},{1,0},{2,3},{3,2},{4,5},{5,4},{6,7},{7,6},{8,9},{9,8},{10,11... | collective-permute-start | bytes 1769480 | tf_op jit(solution)/shard_map/ppermute | solution.py:1108
  104.3 13.2 %copy-start.20 = (bf16[4,96,768]{2,1,0:T(8,128)(2,1)}, bf16[4,96,768]{2,1,0:T(8,128)(2,1)S(1)}, u32[]{:S(2)}) copy-start(bf16[4,96,768]{2,1,0:T(8,128)(2,1)S(1)} %all-to-all-done.3.refs_8_) | copy-start | bytes 1769476
  104.3 13.2 %collective-permute-start.15 = (bf16[4,96,768]{2,1,0:T(8,128)(2,1)S(1)}, bf16[4,96,768]{2,1,0:T(8,128)(2,1)S(1)}, u32[]{:S(2)}, u32[]{:S(2)}) collective-permute-start(bf16[4,96,768]{2,1,0:T(8,128)(2,1)S(1)} %all-to-all-done.3.refs_8_), channel_id=1, source_target_pairs={{0,1},{1,0},{2,3},{3,2},{4,5},{5,4},{6,7},{7,6},{8,9},{9,8},{10,11... | collective-permute-start | bytes 1769480 | tf_op jit(solution)/shard_map/ppermute | solution.py:1108
  125.7 9.7 %collective-permute-start.16 = (bf16[128,768]{1,0:T(8,128)(2,1)}, bf16[128,768]{1,0:T(8,128)(2,1)S(1)}, u32[]{:S(2)}, u32[]{:S(2)}) collective-permute-start(bf16[128,768]{1,0:T(8,128)(2,1)} %get-tuple-element.125), channel_id=1, source_target_pairs={{0,8},{1,9},{2,10},{3,11},{4,12},{5,13},{6,14},{7,15},{8,16},{9,17... | collective-permute-start | bytes 589832 | tf_op jit(solution)/shard_map/ppermute | solution.py:1108
  126.7 10.1 %collective-permute-start.17 = (bf16[128,768]{1,0:T(8,128)(2,1)}, bf16[128,768]{1,0:T(8,128)(2,1)S(1)}, u32[]{:S(2)}, u32[]{:S(2)}) collective-permute-start(bf16[128,768]{1,0:T(8,128)(2,1)} %get-tuple-element.126), channel_id=1, source_target_pairs={{0,16},{1,17},{2,18},{3,19},{4,20},{5,21},{6,22},{7,23},{8,24},{9,... | collective-permute-start | bytes 589832 | tf_op jit(solution)/shard_map/ppermute | solution.py:1108
  127.8 9.0 %collective-permute-start.18 = (bf16[128,768]{1,0:T(8,128)(2,1)}, bf16[128,768]{1,0:T(8,128)(2,1)S(1)}, u32[]{:S(2)}, u32[]{:S(2)}) collective-permute-start(bf16[128,768]{1,0:T(8,128)(2,1)} %get-tuple-element.127), channel_id=1, source_target_pairs={{0,24},{1,25},{2,26},{3,27},{4,28},{5,29},{6,30},{7,31},{8,0},{9,1... | collective-permute-start | bytes 589832 | tf_op jit(solution)/shard_map/ppermute | solution.py:1108
  129.7 7.2 %copy-start.7 = (bf16[128,768]{1,0:T(8,128)(2,1)S(1)}, bf16[128,768]{1,0:T(8,128)(2,1)}, u32[]{:S(2)}) copy-start(bf16[128,768]{1,0:T(8,128)(2,1)} %copy-done.6) | copy-start | bytes 589828
  129.7 7.2 %copy-start.15 = (bf16[128,768]{1,0:T(8,128)(2,1)S(1)}, bf16[128,768]{1,0:T(8,128)(2,1)}, u32[]{:S(2)}) copy-start(bf16[128,768]{1,0:T(8,128)(2,1)} %get-tuple-element.124.refs_0_) | copy-start | bytes 589828
  135.3 4.3 %collective-permute-start.19 = (bf16[768,768]{1,0:T(8,128)(2,1)}, bf16[768,768]{1,0:T(8,128)(2,1)S(1)}, u32[]{:S(2)}, u32[]{:S(2)}) collective-permute-start(bf16[768,768]{1,0:T(8,128)(2,1)} %get-tuple-element.134), channel_id=1, source_target_pairs={{0,1},{1,0},{2,3},{3,2},{4,5},{5,4},{6,7},{7,6},{8,9},{9,8},{10,11... | collective-permute-start | bytes 3538952 | tf_op jit(solution)/shard_map/ppermute | solution.py:1108
  136.8 2.8 %copy-start.9 = (f32[768,768]{1,0:T(8,128)S(1)}, f32[768,768]{1,0:T(8,128)}, u32[]{:S(2)}) copy-start(f32[768,768]{1,0:T(8,128)} %get-tuple-element.135.refs_0_) | copy-start | bytes 7077892
  142.3 21.2 %all-to-all-start.4 = ((bf16[16,24,768]{2,1,0:T(8,128)(2,1)}), bf16[16,24,768]{2,1,0:T(8,128)(2,1)S(1)}, u32[]{:S(2)}, u32[]{:S(2)}) async-start(bf16[16,24,768]{2,1,0:T(8,128)(2,1)} %get-tuple-element.137), calls=%async_computation.4 | async-start | bytes 1179648 | tf_op jit(solution)/shard_map/all_to_all | solution.py:1120
  163.5 12.2 %copy-start.18 = (bf16[16,24,768]{2,1,0:T(8,128)(2,1)}, bf16[16,24,768]{2,1,0:T(8,128)(2,1)S(1)}, u32[]{:S(2)}) copy-start(bf16[16,24,768]{2,1,0:T(8,128)(2,1)S(1)} %all-to-all-done.4.refs_4_) | copy-start | bytes 1769476
  163.5 13.5 %all-to-all-start.5 = ((bf16[4,128,768]{2,1,0:T(8,128)(2,1)}), bf16[4,128,768]{2,1,0:T(8,128)(2,1)S(1)}, u32[]{:S(2)}, u32[]{:S(2)}) async-start(bf16[4,128,768]{2,1,0:T(8,128)(2,1)} %get-tuple-element.139), calls=%async_computation.5 | async-start | bytes 1572864 | tf_op jit(solution)/shard_map/all_to_all | solution.py:1303
  175.7 2.7 %collective-permute-start.21 = (bf16[2,4,128,192]{3,2,1,0:T(8,128)(2,1)}, bf16[2,4,128,192]{3,2,1,0:T(8,128)(2,1)S(1)}, u32[]{:S(2)}, u32[]{:S(2)}) collective-permute-start(bf16[2,4,128,192]{3,2,1,0:T(8,128)(2,1)} %get-tuple-element.144), channel_id=1, source_target_pairs={{0,1},{1,0},{2,3},{3,2},{4,5},{5,4},{6,7},{7,6},{8,9},{9,8},{10,11... | collective-permute-start | bytes 1179656 | tf_op jit(solution)/shard_map/ppermute | solution.py:1108
  175.8 2.6 %collective-permute-start.22 = (bf16[4,24,768]{2,1,0:T(8,128)(2,1)}, bf16[4,24,768]{2,1,0:T(8,128)(2,1)S(1)}, u32[]{:S(2)}, u32[]{:S(2)}) collective-permute-start(bf16[4,24,768]{2,1,0:T(8,128)(2,1)} %get-tuple-element.148), channel_id=1, source_target_pairs={{0,1},{1,0},{2,3},{3,2},{4,5},{5,4},{6,7},{7,6},{8,9},{9,8},{10,11... | collective-permute-start | bytes 442376 | tf_op jit(solution)/shard_map/ppermute | solution.py:1108
  177.7 29.2 %collective-permute-start.20 = (bf16[128,768]{1,0:T(8,128)(2,1)S(1)}, bf16[128,768]{1,0:T(8,128)(2,1)S(1)}, u32[]{:S(2)}, u32[]{:S(2)}) collective-permute-start(bf16[128,768]{1,0:T(8,128)(2,1)S(1)} %layer.1), channel_id=1, source_target_pairs={{0,0},{1,1},{2,8},{3,9},{4,16},{5,17},{6,24},{7,25},{8,2},{9,3},{1... | collective-permute-start | bytes 589832 | tf_op jit(solution)/shard_map/ppermute | solution.py:1108
  184.6 7.9 %copy-start.32 = (bf16[128,768]{1,0:T(8,128)(2,1)S(1)}, bf16[128,768]{1,0:T(8,128)(2,1)}, u32[]{:S(2)}) copy-start(bf16[128,768]{1,0:T(8,128)(2,1)} %get-tuple-element.151) | copy-start | bytes 589828
  184.7 9.0 %copy-start.30 = (bf16[128,768]{1,0:T(8,128)(2,1)S(1)}, bf16[128,768]{1,0:T(8,128)(2,1)}, u32[]{:S(2)}) copy-start(bf16[128,768]{1,0:T(8,128)(2,1)} %get-tuple-element.152) | copy-start | bytes 589828
  184.7 10.4 %copy-start.29 = (bf16[128,768]{1,0:T(8,128)(2,1)S(1)}, bf16[128,768]{1,0:T(8,128)(2,1)}, u32[]{:S(2)}) copy-start(bf16[128,768]{1,0:T(8,128)(2,1)} %get-tuple-element.153) | copy-start | bytes 589828
  184.7 28.8 %all-to-all-start.7 = ((bf16[4,128,768]{2,1,0:T(8,128)(2,1)}), bf16[4,128,768]{2,1,0:T(8,128)(2,1)}, u32[]{:S(2)}, u32[]{:S(2)}) async-start(bf16[4,128,768]{2,1,0:T(8,128)(2,1)} %get-tuple-element.165), calls=%async_computation.7 | async-start | bytes 1572864 | tf_op jit(solution)/shard_map/all_to_all | solution.py:1117
  192.5 10.8 %collective-permute-start.23 = (bf16[128,768]{1,0:T(8,128)(2,1)S(1)}, bf16[128,768]{1,0:T(8,128)(2,1)S(1)}, u32[]{:S(2)}, u32[]{:S(2)}) collective-permute-start(bf16[128,768]{1,0:T(8,128)(2,1)S(1)} %copy-done.32), channel_id=1, source_target_pairs={{0,8},{1,9},{2,10},{3,11},{4,12},{5,13},{6,14},{7,15},{8,16},{9,17... | collective-permute-start | bytes 589832 | tf_op jit(solution)/shard_map/ppermute | solution.py:1108
  193.6 10.2 %collective-permute-start.24 = (bf16[128,768]{1,0:T(8,128)(2,1)S(1)}, bf16[128,768]{1,0:T(8,128)(2,1)S(1)}, u32[]{:S(2)}, u32[]{:S(2)}) collective-permute-start(bf16[128,768]{1,0:T(8,128)(2,1)S(1)} %copy-done.30), channel_id=1, source_target_pairs={{0,16},{1,17},{2,18},{3,19},{4,20},{5,21},{6,22},{7,23},{8,24},{9,... | collective-permute-start | bytes 589832 | tf_op jit(solution)/shard_map/ppermute | solution.py:1108
  195.0 8.8 %collective-permute-start.25 = (bf16[128,768]{1,0:T(8,128)(2,1)S(1)}, bf16[128,768]{1,0:T(8,128)(2,1)S(1)}, u32[]{:S(2)}, u32[]{:S(2)}) collective-permute-start(bf16[128,768]{1,0:T(8,128)(2,1)S(1)} %copy-done.29), channel_id=1, source_target_pairs={{0,24},{1,25},{2,26},{3,27},{4,28},{5,29},{6,30},{7,31},{8,0},{9,1... | collective-permute-start | bytes 589832 | tf_op jit(solution)/shard_map/ppermute | solution.py:1108
  197.0 6.8 %copy-start.14 = (bf16[128,768]{1,0:T(8,128)(2,1)S(1)}, bf16[128,768]{1,0:T(8,128)(2,1)}, u32[]{:S(2)}) copy-start(bf16[128,768]{1,0:T(8,128)(2,1)} %get-tuple-element.150.refs_0_) | copy-start | bytes 589828
  203.3 3.6 %collective-permute-start.27 = (bf16[384,640]{1,0:T(8,128)(2,1)}, bf16[384,640]{1,0:T(8,128)(2,1)S(1)}, u32[]{:S(2)}, u32[]{:S(2)}) collective-permute-start(bf16[384,640]{1,0:T(8,128)(2,1)} %get-tuple-element.161), channel_id=1, source_target_pairs={{0,1},{1,0},{2,3},{3,2},{4,5},{5,4},{6,7},{7,6},{8,9},{9,8},{10,11... | collective-permute-start | bytes 1474568 | tf_op jit(solution)/shard_map/ppermute | solution.py:1108
  203.8 3.1 %copy-start.8 = (f32[384,640]{1,0:T(8,128)S(1)}, f32[384,640]{1,0:T(8,128)}, u32[]{:S(2)}) copy-start(f32[384,640]{1,0:T(8,128)} %get-tuple-element.162.refs_0_) | copy-start | bytes 2949124
  206.2 30.3 %collective-permute-start.26 = (bf16[128,768]{1,0:T(8,128)(2,1)S(1)}, bf16[128,768]{1,0:T(8,128)(2,1)S(1)}, u32[]{:S(2)}, u32[]{:S(2)}) collective-permute-start(bf16[128,768]{1,0:T(8,128)(2,1)S(1)} %last.1), channel_id=1, source_target_pairs={{0,0},{1,1},{2,8},{3,9},{4,16},{5,17},{6,24},{7,25},{8,2},{9,3},{1... | collective-permute-start | bytes 589832 | tf_op jit(solution)/shard_map/ppermute | solution.py:1108
  213.5 19.7 %all-to-all-start.6 = ((bf16[16,24,640]{2,1,0:T(8,128)(2,1)}), bf16[16,24,640]{2,1,0:T(8,128)(2,1)S(1)}, u32[]{:S(2)}, u32[]{:S(2)}) async-start(bf16[16,24,640]{2,1,0:T(8,128)(2,1)} %add_early.1), calls=%async_computation.6 | async-start | bytes 983040 | tf_op jit(solution)/shard_map/all_to_all | solution.py:1120
  (9 other events, 8.7 us)

commit v5 on v4

--- a/solution.py
+++ b/solution.py
@@ -524,25 +524,26 @@
 COST = 1.0
 
 
-def run(kernel, outs, *args, scalars=(), scratch=(), us=1.0, room=60, name=None):
+def run(kernel, outs, *args, scalars=(), scalar_out=False, scratch=(), us=1.0, room=60, name=None):
     shapes = [jax.ShapeDtypeStruct(shape, dtype) for shape, dtype in outs]
     far = [k for k in range(len(args)) if k not in scalars]
+    made_count = len(outs) - scalar_out
 
     def body(*refs):
         ins, refs = list(refs[: len(args)]), refs[len(args) :]
         targets, refs = refs[: len(outs)], refs[len(outs) :]
         own, refs = refs[: len(scratch)], refs[len(scratch) :]
         held, refs = refs[: len(far)], refs[len(far) :]
-        made, (in_sems, out_sems) = refs[: len(outs)], refs[len(outs) :]
+        made, (in_sems, out_sems) = refs[:made_count], refs[made_count:]
         for n, k in enumerate(far):
             copy = pltpu.make_async_copy(ins[k], held[n], in_sems.at[n])
             copy.start()
             ins[k] = Held(held[n], copy)
         results = [
             Made(made[n], pltpu.make_async_copy(made[n], targets[n], out_sems.at[n]))
-            for n in range(len(outs))
+            for n in range(made_count)
         ]
-        kernel(*ins, *results, *own)
+        kernel(*ins, *results, *targets[made_count:], *own)
         for k in far:
             if ins[k].copy is not None:
                 ins[k].copy.wait()
@@ -556,13 +557,13 @@
         body,
         out_shape=shapes,
         in_specs=[SMEM if k in scalars else hbm for k in range(len(args))],
-        out_specs=[hbm] * len(outs),
+        out_specs=[hbm] * made_count + [SMEM] * (len(outs) - made_count),
         scratch_shapes=list(scratch)
         + [pltpu.VMEM(args[k].shape, args[k].dtype) for k in far]
-        + [pltpu.VMEM(out.shape, out.dtype) for out in shapes]
+        + [pltpu.VMEM(out.shape, out.dtype) for out in shapes[:made_count]]
         + [
             pltpu.SemaphoreType.DMA((max(len(far), 1),)),
-            pltpu.SemaphoreType.DMA((len(outs),)),
+            pltpu.SemaphoreType.DMA((made_count,)),
         ],
         compiler_params=pltpu.CompilerParams(vmem_limit_bytes=room * 1024 * 1024),
         cost_estimate=pl.CostEstimate(
@@ -617,6 +618,7 @@
     refs, scr_ref = refs[:-1], refs[-1]
     tie_of, refs = ties_of(refs[:ranks]), refs[ranks:]
     qkv_ref, out_w_ref, vectors, out_ref, cols_ref = refs[0], refs[1], refs[2:10], refs[10], refs[11]
+    ties_ref = refs[12]
     ties, rows, _ = qkv_ref.shape
     planes = ranks
     model = qkv_ref.shape[2] // 3
@@ -640,6 +642,7 @@
             scr_ref[tie, to] = jnp.concatenate(cols + [small], 1)
     for seq in range(planes):
         tie = tie_of(seq)
+        ties_ref[seq] = tie
         for to in range(ranks):
             out_ref[to * planes + seq] = scr_ref[tie, to]
     out_ref.flush()
@@ -650,8 +653,8 @@
 
 
 def pack_late_kernel(ranks, *refs):
-    tie_of = ties_of(refs[:ranks])
-    fc_ref, proj_ref, fc_out_ref, proj_out_ref = refs[ranks:]
+    tie_of = lambda seq: refs[0][seq]
+    fc_ref, proj_ref, fc_out_ref, proj_out_ref = refs[1:]
     planes = proj_out_ref.shape[0]
     part = fc_ref.shape[2] // ranks
     for seq in range(planes):
@@ -999,8 +1002,8 @@
 
 
 def final_late_kernel(ranks, *refs):
-    tie_of = ties_of(refs[:ranks])
-    fc_in, rest_in, fc_ref, proj_ref, out_ref = refs[ranks:]
+    tie_of = lambda seq: refs[0][seq]
+    fc_in, rest_in, fc_ref, proj_ref, out_ref = refs[1:]
     ties, _, inner = fc_ref.shape
     planes = rest_in.shape[0]
     hid_rows, rows = proj_ref.shape[1], out_ref.shape[1]
@@ -1016,8 +1019,8 @@
 
 
 def final_kernel(ranks, *refs):
-    tie_of = ties_of(refs[:ranks])
-    home_ref, qkv_ref, *small_refs = refs[ranks:]
+    tie_of = lambda seq: refs[0][seq]
+    home_ref, qkv_ref, *small_refs = refs[1:]
     ties, rows, wide = qkv_ref.shape
     model = wide // 3
     planes = home_ref.shape[0] // ranks
@@ -1130,9 +1133,13 @@
     tokens_own = send(tokens[0], swap)
 
     cols_rows = (rows + 15) // 16 * 16
-    early, cols = run(
+    early, cols, all_ties = run(
         functools.partial(pack_kernel, group, ranks),
-        [((squads, rows, lanes), bf16), ((planes, cols_rows, model), bf16)],
+        [
+            ((squads, rows, lanes), bf16),
+            ((planes, cols_rows, model), bf16),
+            ((planes,), jnp.int32),
+        ],
         *ties_seen,
         qkv_weight,
         out_weight,
@@ -1145,6 +1152,7 @@
         qv_bias,
         fc_bias,
         scalars=scalar_ties,
+        scalar_out=True,
         scratch=[pltpu.VMEM((ties, ranks, rows, lanes), bf16)],
         us=0.1,
         name="pack",
@@ -1204,10 +1212,10 @@
     late_fc, late_proj = run(
         functools.partial(pack_late_kernel, ranks),
         [((squads, rows, part), bf16), ((planes, hid_rows, model), bf16)],
-        *ties_seen,
+        all_ties,
         gate(fc_weight, q),
         proj_weight,
-        scalars=scalar_ties,
+        scalars=(0,),
         us=2.0,
         name="pack_late",
     )
@@ -1397,10 +1405,10 @@
     grad_fc_weight, grad_proj_weight, grad_out_weight = run(
         functools.partial(final_late_kernel, ranks),
         [((ties, rows, inner), f32), ((ties, hid_rows, model), f32), ((ties, rows, model), f32)],
-        *ties_seen,
+        all_ties,
         late_fc,
         gate(late_rest, input_own),
-        scalars=scalar_ties,
+        scalars=(0,),
         us=60.0,
         name="final_late",
     )
@@ -1410,9 +1418,9 @@
         [((ties, rows, 3 * model), f32)]
         + [((ties, rows), f32)] * 6
         + [((ties, 2 * rows), f32), ((ties, 4 * rows), f32)],
-        *ties_seen,
+        all_ties,
         early,
-        scalars=scalar_ties,
+        scalars=(0,),
         room=16,
         us=1.0,
         name="final",

time: 239 us -> 237 us (level)
  Pallas kernels: 71.5 us -> 68.3 us
    pallas_call x17, Pallas kernels: 71.5 us -> 68.3 us  [run(): pl.pallas_call(body, out_shape=shapes, in_specs=[SMEM if k in scalars els...]
    unnamed x76 -> x78, local copies, waits for them, and re-layouts: 6.72 us -> 6.73 us
  transfers between devices with their start and end apart: 36 -> 36, of which waited for: 16 -> 16; matrix products, arithmetic and copies ran while one was open for 0% -> 0% of each run, Pallas kernels for 26% -> 25%
where the time goes in v5:
time: 237 us; the launch traced here: 235 us
  starting transfers between devices  70.4 us (30%)
  Pallas kernels  68.3 us (29%)
  blocking collectives  45 us (19%)
  waiting for transfers between devices  42.9 us (18%)
  local copies, waits for them, and re-layouts  6.73 us (3%)
    pallas_call x17, Pallas kernels, run(): pl.pallas_call(body, out_shape=shapes, in_specs=[SMEM if k in scalars els...  68.3 us
    ppermute x28, starting transfers between devices, send(): return lax.ppermute(values, axes, pairs)  27.7 us
    all_to_all x4, starting transfers between devices, over_squad(): return lax.all_to_all(pieces, axes, 0, 0, axis_index_groups=squad)  20.4 us
    ppermute x28, waiting for transfers between devices, send(): return lax.ppermute(values, axes, pairs)  18.8 us
    all_to_all x3, starting transfers between devices, over_planes(): return lax.all_to_all(pieces, 'seq', 0, 0, axis_index_groups=same_member)  18.5 us
    all_gather x1, blocking collectives, fast_device(): low = lax.all_gather(gate(low_own, late_fc), 'dp', axis=0, tiled=True)  16.4 us
    all_gather x1, blocking collectives, fast_device(): tokens_all = lax.all_gather(tokens_own, 'dp', axis=0, tiled=True)  15.4 us
    all_gather x1, blocking collectives, fast_device(): h_two = lax.all_gather(h_own, 'dp', axis=0, tiled=True)  13.1 us
  transfers between devices with their start and end apart: 36, of which 16 were waited for; matrix products, arithmetic and copies ran while one was open for 0% of the time, Pallas kernels for 25%

profile of v5, /device:TPU:0, one launch (start us, length us, event | category | flops | bytes accessed | tf_op | source)
XLA Modules:
  0.0 235.4 jit_solution(16860827829171573620)
XLA Ops:
  0.6 3.0 %collective-permute-start.2 = (s32[1]{0:T(128)}, s32[1]{0:T(128)}, u32[]{:S(2)}, u32[]{:S(2)}) collective-permute-start(s32[1]{0:T(128)} %param.16), channel_id=1, source_target_pairs={{0,16},{1,17},{2,18},{3,19},{4,20},{5,21},{6,22},{7,23},{8,24},{9,... | collective-permute-start | bytes 20 | tf_op jit(solution)/shard_map/ppermute | solution.py:1111
  3.7 1.4 collective-permute-start.1
  5.7 1.6 collective-permute-start
  8.0 1.6 collective-permute-done.3.refs_3_
  9.6 4.9 %pack.1 = (bf16[16,24,640]{2,1,0:T(8,128)(2,1)}, bf16[4,32,768]{2,1,0:T(8,128)(2,1)}, s32[4]{0:T(128)}) custom-call(s32[1]{0:T(128)S(6)} %copy.31.refs_0_, s32[1]{0:T(128)} %collective-permute-done.1.refs_1_, s32[1]{0:T(128)} %collective-permute-done.2.refs_2_, s32[1]{0:T(128)} %collective-permute-done.3.refs_3_, bf16[2,24,2304]{2,1,0:T(8,128)(2,1)} %refs_4_.1, ...), custom_call_target="tpu_custom_call" | custom-call | flops 100000000 | bytes 350000 | tf_op jit(solution)/shard_map/pack/pallas_call | solution.py:556
  14.5 7.0 %all-to-all-start = ((bf16[16,24,640]{2,1,0:T(8,128)(2,1)}), bf16[16,24,640]{2,1,0:T(8,128)(2,1)S(1)}, u32[]{:S(2)}, u32[]{:S(2)}) async-start(bf16[16,24,640]{2,1,0:T(8,128)(2,1)} %get-tuple-element.99), calls=%async_computation | async-start | bytes 983040 | tf_op jit(solution)/shard_map/all_to_all | solution.py:1123
  21.8 15.4 %all_gather.9.refs_0_.refs_2_ = bf16[512,768]{1,0:T(8,128)(2,1)S(1)} all-gather(bf16[128,768]{1,0:T(8,128)(2,1)S(1)} %collective-permute-done.refs_4_), channel_id=1, replica_groups=mesh['dp'=4,'seq'=8] {'dp'}, dimensions={0}, use_global_device_ids=true | all-gather | bytes 983040 | tf_op jit(solution)/shard_map/all_gather | solution.py:1186
  37.3 1.6 collective-permute-start.5
  38.9 6.3 %all-to-all-start.1 = ((bf16[4,32,768]{2,1,0:T(8,128)(2,1)}), bf16[4,32,768]{2,1,0:T(8,128)(2,1)S(1)}, u32[]{:S(2)}, u32[]{:S(2)}) async-start(bf16[4,32,768]{2,1,0:T(8,128)(2,1)} %get-tuple-element.106), calls=%async_computation.1 | async-start | bytes 393216 | tf_op jit(solution)/shard_map/all_to_all | solution.py:1120
  45.1 5.0 %project.1 = (bf16[4,128,192]{2,1,0:T(8,128)(2,1)S(1)}, bf16[2,4,128,192]{3,2,1,0:T(8,128)(2,1)S(1)}, bf16[512,768]{1,0:T(8,128)(2,1)S(1)}, f32[8,768]{1,0:T(8,1...) custom-call(bf16[512,768]{1,0:T(8,128)(2,1)S(1)} %all_gather.9.refs_0_.refs_2_, ...), custom_call_target="tpu_custom_call" | custom-call | flops 5000000000 | bytes 17500000 | tf_op jit(solution)/shard_map/project/pallas_call | solution.py:556
  50.2 1.0 copy-done.12
  51.2 0.9 copy-done.14
  52.1 2.7 %pack_late.1 = (bf16[16,24,768]{2,1,0:T(8,128)(2,1)}, bf16[4,96,768]{2,1,0:T(8,128)(2,1)}) custom-call(s32[4]{0:T(128)} %get-tuple-element.107.refs_0_, bf16[2,24,3072]{2,1,0:T(8,128)(2,1)} %refs_1_, bf16[2,96,768]{2,1,0:T(8,128)(2,1)} %refs_2_.1), custom_call_target="tpu_custom_call" | custom-call | flops 2000000000 | bytes 7000000 | tf_op jit(solution)/shard_map/pack_late/pallas_call | solution.py:556
  54.8 3.5 %all-to-all-done.1.refs_3_ = bf16[4,32,768]{2,1,0:T(8,128)(2,1)S(1)} async-done(((bf16[4,32,768]{2,1,0:T(8,128)(2,1)}), bf16[4,32,768]{2,1,0:T(8,128)(2,1)S(1)}, u32[]{:S(2)}, u32[]{:S(2)}) %all-to-all-start.1) | async-done | bytes 196640 | tf_op jit(solution)/shard_map/all_to_all | solution.py:1120
  58.4 1.4 collective-permute-done.7.refs_4_
  59.8 5.1 %all-to-all-start.2 = ((bf16[16,24,768]{2,1,0:T(8,128)(2,1)}), bf16[16,24,768]{2,1,0:T(8,128)(2,1)S(1)}, u32[]{:S(2)}, u32[]{:S(2)}) async-start(bf16[16,24,768]{2,1,0:T(8,128)(2,1)} %get-tuple-element.118), calls=%async_computation.2 | async-start | bytes 1179648 | tf_op jit(solution)/shard_map/all_to_all | solution.py:1123
  65.0 2.0 collective-permute-start.13
  66.9 1.5 collective-permute-start.12
  68.4 1.5 collective-permute-start.11
  69.9 0.8 copy-done.22
  70.7 5.3 %attend.1 = (bf16[512,192]{1,0:T(8,128)(2,1)}, f32[8,384]{1,0:T(8,128)}, bf16[192,768]{1,0:T(8,128)(2,1)}, bf16[128,768]{1,0:T(8,128)(2,1)}, bf16[128,768]{1,0:T...) custom-call(bf16[4,128,192]{2,1,0:T(8,128)(2,1)} %copy-done.2, bf16[2,4,128,192]{3,2,1,0:T(8,128)(2,1)} %copy-done.1, ...), custom_call_target="tpu_custom_call" | custom-call | flops 6000000000 | bytes 21000000 | tf_op jit(solution)/shard_map/attend/pallas_call | solution.py:556
  76.0 3.3 %collective-permute-done.13.refs_7_ = bf16[128,768]{1,0:T(8,128)(2,1)S(1)} collective-permute-done((bf16[128,768]{1,0:T(8,128)(2,1)S(1)}, bf16[128,768]{1,0:T(8,128)(2,1)S(1)}, u32[]{:S(2)}, u32[]{:S(2)}) %collective-permute-start.13) | collective-permute-done | bytes 196640 | tf_op jit(solution)/shard_map/ppermute | solution.py:1111
  79.3 2.9 %collective-permute-done.12.refs_6_ = bf16[128,768]{1,0:T(8,128)(2,1)S(1)} collective-permute-done((bf16[128,768]{1,0:T(8,128)(2,1)S(1)}, bf16[128,768]{1,0:T(8,128)(2,1)S(1)}, u32[]{:S(2)}, u32[]{:S(2)}) %collective-permute-start.12) | collective-permute-done | bytes 196640 | tf_op jit(solution)/shard_map/ppermute | solution.py:1111
  82.9 4.3 %all-to-all-start.3 = ((bf16[4,96,768]{2,1,0:T(8,128)(2,1)}), bf16[4,96,768]{2,1,0:T(8,128)(2,1)S(1)}, u32[]{:S(2)}, u32[]{:S(2)}) async-start(bf16[4,96,768]{2,1,0:T(8,128)(2,1)} %get-tuple-element.123), calls=%async_computation.3 | async-start | bytes 1179648 | tf_op jit(solution)/shard_map/all_to_all | solution.py:1120
  87.2 1.5 collective-permute-start.8
  89.3 2.0 collective-permute-start.10
  91.3 4.7 %collective-permute-done.8.refs_1_ = bf16[128,768]{1,0:T(8,128)(2,1)S(1)} collective-permute-done((bf16[128,768]{1,0:T(8,128)(2,1)S(1)}, bf16[128,768]{1,0:T(8,128)(2,1)S(1)}, u32[]{:S(2)}, u32[]{:S(2)}) %collective-permute-start.8) | collective-permute-done | bytes 196640 | tf_op jit(solution)/shard_map/ppermute | solution.py:1111
  96.0 2.3 collective-permute-done.9.refs_2_
  98.4 2.8 %join.1 = (f32[128,768]{1,0:T(8,128)S(1)}, bf16[128,768]{1,0:T(8,128)(2,1)S(1)}) custom-call(bf16[128,768]{1,0:T(8,128)(2,1)S(1)} %copy-done.13, bf16[128,768]{1,0:T(8,128)(2,1)S(1)} %collective-permute-done.8.refs_1_, bf16[128,768]{1,0:T(8,128)(2,1)S(1)} %collective-permute-done.9.refs_2_, bf16[128,768]{1,0:T(8,128)(2,1)S(1)} %collective-permute-done.10.refs_3_, ...), custom_call_target="tpu_custom_call" | custom-call | flops 2000000000 | bytes 7000000 | tf_op jit(solution)/shard_map/join/pallas_call | solution.py:556
  101.3 1.8 all-to-all-done.3.refs_8_
  103.1 13.1 %all_gather.10.refs_0_ = bf16[512,768]{1,0:T(8,128)(2,1)} all-gather(bf16[128,768]{1,0:T(8,128)(2,1)S(1)} %get-tuple-element.117), channel_id=1, replica_groups=mesh['dp'=4,'seq'=8] {'dp'}, dimensions={0}, use_global_device_ids=true | all-gather | bytes 983040 | tf_op jit(solution)/shard_map/all_gather | solution.py:1252
  116.3 0.9 copy-done.25
  117.3 7.2 %mlp.1 = (bf16[128,768]{1,0:T(8,128)(2,1)}, bf16[128,768]{1,0:T(8,128)(2,1)}, bf16[128,768]{1,0:T(8,128)(2,1)}, bf16[128,768]{1,0:T(8,128)(2,1)}, bf16[4,128,768...) custom-call(bf16[512,768]{1,0:T(8,128)(2,1)} %all_gather.10.refs_0_, ...), custom_call_target="tpu_custom_call" | custom-call | flops 7000000000 | bytes 24500000 | tf_op jit(solution)/shard_map/mlp/pallas_call | solution.py:556
  124.5 1.1 collective-permute-start.16
  125.6 1.0 collective-permute-start.17
  126.6 1.9 collective-permute-start.18
  128.5 5.6 %mlp_grad.1 = (f32[768,768]{1,0:T(8,128)}, bf16[768,768]{1,0:T(8,128)(2,1)}, f32[8,768]{1,0:T(8,128)}) custom-call(bf16[512,768]{1,0:T(8,128)(2,1)} %all_gather.10.refs_0_, bf16[512,768]{1,0:T(8,128)(2,1)} %get-tuple-element.132.refs_1_, bf16[512,768]{1,0:T(8,128)(2,1)} %get-tuple-element.133.refs_2_, bf16[512,768]{1,0:T(8,128)(2,1)} %get-tuple-element.134.refs_3_), custom_call_target="tpu_custom_call" | custom-call | flops 4000000000 | bytes 14000000 | tf_op jit(solution)/shard_map/mlp_grad/pallas_call | solution.py:556
  134.2 1.5 collective-permute-done.17.refs_2_
  135.7 2.8 %join_back.1 = (f32[128,768]{1,0:T(8,128)S(1)}, bf16[128,768]{1,0:T(8,128)(2,1)S(1)}, f32[8,768]{1,0:T(8,128)S(1)}) custom-call(bf16[128,768]{1,0:T(8,128)(2,1)S(1)} %copy-done.16, bf16[128,768]{1,0:T(8,128)(2,1)S(1)} %collective-permute-done.16.refs_1_, bf16[128,768]{1,0:T(8,128)(2,1)S(1)} %collective-permute-done.17.refs_2_, ...), custom_call_target="tpu_custom_call" | custom-call | flops 30000001024 | bytes 105000000 | tf_op jit(solution)/shard_map/join_back/pallas_call | solution.py:556
  138.5 1.8 add_late.1
  140.4 0.8 copy-done.11
  141.2 4.6 %all-to-all-start.4 = ((bf16[16,24,768]{2,1,0:T(8,128)(2,1)}), bf16[16,24,768]{2,1,0:T(8,128)(2,1)S(1)}, u32[]{:S(2)}, u32[]{:S(2)}) async-start(bf16[16,24,768]{2,1,0:T(8,128)(2,1)} %get-tuple-element.139), calls=%async_computation.4 | async-start | bytes 1179648 | tf_op jit(solution)/shard_map/all_to_all | solution.py:1123
  145.8 16.4 %all_gather.11.refs_0_ = bf16[512,768]{1,0:T(8,128)(2,1)} all-gather(bf16[128,768]{1,0:T(8,128)(2,1)S(1)} %get-tuple-element.140), channel_id=1, replica_groups=mesh['dp'=4,'seq'=8] {'dp'}, dimensions={0}, use_global_device_ids=true | all-gather | bytes 983040 | tf_op jit(solution)/shard_map/all_gather | solution.py:1309
  162.5 3.7 %all-to-all-start.5 = ((bf16[4,128,768]{2,1,0:T(8,128)(2,1)}), bf16[4,128,768]{2,1,0:T(8,128)(2,1)S(1)}, u32[]{:S(2)}, u32[]{:S(2)}) async-start(bf16[4,128,768]{2,1,0:T(8,128)(2,1)} %get-tuple-element.141), calls=%async_computation.5 | async-start | bytes 1572864 | tf_op jit(solution)/shard_map/all_to_all | solution.py:1311
  166.2 8.4 %attend_back.1 = (f32[2,4,128,192]{3,2,1,0:T(8,128)}, bf16[2,4,128,192]{3,2,1,0:T(8,128)(2,1)}, bf16[512,192]{1,0:T(8,128)(2,1)}, f32[4,24,768]{2,1,0:T(8,128)}, bf16[4,24,768]{2,1,0:T(8,128)(2,1)}) custom-call(bf16[512,768]{1,0:T(8,128)(2,1)} %all_gather.11.refs_0_, bf16[192,768]{1,0:T(8,128)(2,1)} %get-tuple-element.142.refs_1_, ...), custom_call_target="tpu_custom_call" | custom-call | flops 500000000 | bytes 1750000 | tf_op jit(solution)/shard_map/attend_back/pallas_call | solution.py:556
  175.2 0.7 all-to-all-done.5.refs_0_
  176.0 0.7 layer.1
  176.7 0.7 collective-permute-start.20
  178.2 5.4 %first.1 = (bf16[128,768]{1,0:T(8,128)(2,1)}, bf16[128,768]{1,0:T(8,128)(2,1)}, bf16[128,768]{1,0:T(8,128)(2,1)}, bf16[128,768]{1,0:T(8,128)(2,1)}, bf16[4,128,7...) custom-call(bf16[512,192]{1,0:T(8,128)(2,1)} %get-tuple-element.144.refs_0_, ...), custom_call_target="tpu_custom_call" | custom-call | flops 4000000000 | bytes 14000000 | tf_op jit(solution)/shard_map/first/pallas_call | solution.py:556
  183.6 7.8 %all-to-all-start.7 = ((bf16[4,128,768]{2,1,0:T(8,128)(2,1)}), bf16[4,128,768]{2,1,0:T(8,128)(2,1)}, u32[]{:S(2)}, u32[]{:S(2)}) async-start(bf16[4,128,768]{2,1,0:T(8,128)(2,1)} %get-tuple-element.167), calls=%async_computation.7 | async-start | bytes 1572864 | tf_op jit(solution)/shard_map/all_to_all | solution.py:1120
  191.5 1.1 collective-permute-start.23
  192.6 1.3 collective-permute-start.24
  193.9 1.9 collective-permute-start.25
  195.8 6.2 %first_grad.1 = (f32[384,640]{1,0:T(8,128)}, bf16[384,640]{1,0:T(8,128)(2,1)}) custom-call(bf16[512,768]{1,0:T(8,128)(2,1)} %copy-done.14, bf16[512,576]{1,0:T(8,128)(2,1)} %get-tuple-element.158.refs_1_, bf16[512,768]{1,0:T(8,128)(2,1)} %copy-done, bf16[4,128,768]{2,1,0:T(8,128)(2,1)} %get-tuple-element.159.refs_3_, f32[8,768]{1,0:T(8,128)} %copy-done.17, ...), custom_call_target="tpu_custom_call" | custom-call | flops 5000000000 | bytes 17500000 | tf_op jit(solution)/shard_map/first_grad/pallas_call | solution.py:556
  202.7 2.4 %last.1 = bf16[128,768]{1,0:T(8,128)(2,1)S(1)} custom-call(bf16[128,768]{1,0:T(8,128)(2,1)S(1)} %copy-done.15, bf16[128,768]{1,0:T(8,128)(2,1)S(1)} %collective-permute-done.23.refs_1_, bf16[128,768]{1,0:T(8,128)(2,1)S(1)} %collective-permute-done.24.refs_2_, bf16[128,768]{1,0:T(8,128)(2,1)S(1)} %collective-permute-done.25.refs_3_, ...), custom_call_target="tpu_custom_call" | custom-call | flops 30000001024 | bytes 105000000 | tf_op jit(solution)/shard_map/last/pallas_call | solution.py:556
  205.1 0.7 collective-permute-start.26
  205.8 1.6 add_early.1
  207.4 5.1 %all-to-all-done.7.refs_2_ = bf16[4,128,768]{2,1,0:T(8,128)(2,1)} async-done(((bf16[4,128,768]{2,1,0:T(8,128)(2,1)}), bf16[4,128,768]{2,1,0:T(8,128)(2,1)}, u32[]{:S(2)}, u32[]{:S(2)}) %all-to-all-start.7) | async-done | bytes 786464 | tf_op jit(solution)/shard_map/all_to_all | solution.py:1120
  212.6 3.7 %all-to-all-start.6 = ((bf16[16,24,640]{2,1,0:T(8,128)(2,1)}), bf16[16,24,640]{2,1,0:T(8,128)(2,1)S(1)}, u32[]{:S(2)}, u32[]{:S(2)}) async-start(bf16[16,24,640]{2,1,0:T(8,128)(2,1)} %add_early.1), calls=%async_computation.6 | async-start | bytes 983040 | tf_op jit(solution)/shard_map/all_to_all | solution.py:1123
  216.3 3.4 %final_late.1 = (f32[2,24,3072]{2,1,0:T(8,128)}, f32[2,96,768]{2,1,0:T(8,128)}, f32[2,24,768]{2,1,0:T(8,128)}) custom-call(s32[4]{0:T(128)} %get-tuple-element.107.refs_0_, bf16[16,24,768]{2,1,0:T(8,128)(2,1)} %copy-done.19, bf16[4,128,768]{2,1,0:T(8,128)(2,1)} %all-to-all-done.7.refs_2_), custom_call_target="tpu_custom_call" | custom-call | flops 60000002048 | bytes 210000000 | tf_op jit(solution)/shard_map/final_late/pallas_call | solution.py:556
  219.7 12.4 %all-to-all-done.6.refs_1_ = bf16[16,24,640]{2,1,0:T(8,128)(2,1)S(1)} async-done(((bf16[16,24,640]{2,1,0:T(8,128)(2,1)}), bf16[16,24,640]{2,1,0:T(8,128)(2,1)S(1)}, u32[]{:S(2)}, u32[]{:S(2)}) %all-to-all-start.6) | async-done | bytes 491552 | tf_op jit(solution)/shard_map/all_to_all | solution.py:1123
  232.1 2.0 final.1
  234.1 0.7 copy.32
  234.8 0.7 copy.33
  (114 shorter events, 4.8 us)
Async XLA Ops:
  0.6 7.4 %collective-permute-start.2 = (s32[1]{0:T(128)}, s32[1]{0:T(128)}, u32[]{:S(2)}, u32[]{:S(2)}) collective-permute-start(s32[1]{0:T(128)} %param.16), channel_id=1, source_target_pairs={{0,16},{1,17},{2,18},{3,19},{4,20},{5,21},{6,22},{7,23},{8,24},{9,... | collective-permute-start | bytes 20 | tf_op jit(solution)/shard_map/ppermute | solution.py:1111
  3.7 4.4 %collective-permute-start.1 = (s32[1]{0:T(128)}, s32[1]{0:T(128)}, u32[]{:S(2)}, u32[]{:S(2)}) collective-permute-start(s32[1]{0:T(128)} %param.16), channel_id=1, source_target_pairs={{0,24},{1,25},{2,26},{3,27},{4,28},{5,29},{6,30},{7,31},{8,0},{9,1... | collective-permute-start | bytes 20 | tf_op jit(solution)/shard_map/ppermute | solution.py:1111
  5.1 4.5 %collective-permute-start.3 = (s32[1]{0:T(128)}, s32[1]{0:T(128)}, u32[]{:S(2)}, u32[]{:S(2)}) collective-permute-start(s32[1]{0:T(128)} %param.16), channel_id=1, source_target_pairs={{0,8},{1,9},{2,10},{3,11},{4,12},{5,13},{6,14},{7,15},{8,16},{9,17... | collective-permute-start | bytes 20 | tf_op jit(solution)/shard_map/ppermute | solution.py:1111
  5.7 16.0 %collective-permute-start = (bf16[128,768]{1,0:T(8,128)(2,1)}, bf16[128,768]{1,0:T(8,128)(2,1)S(1)}, u32[]{:S(2)}, u32[]{:S(2)}) collective-permute-start(bf16[128,768]{1,0:T(8,128)(2,1)} %bitcast.6), channel_id=1, source_target_pairs={{0,0},{1,1},{2,8},{3,9},{4,16},{5,17},{6,24},{7,25},{8,2},{9,3},{1... | collective-permute-start | bytes 589832 | tf_op jit(solution)/shard_map/ppermute | solution.py:1111
  14.5 22.7 %all-to-all-start = ((bf16[16,24,640]{2,1,0:T(8,128)(2,1)}), bf16[16,24,640]{2,1,0:T(8,128)(2,1)S(1)}, u32[]{:S(2)}, u32[]{:S(2)}) async-start(bf16[16,24,640]{2,1,0:T(8,128)(2,1)} %get-tuple-element.99), calls=%async_computation | async-start | bytes 983040 | tf_op jit(solution)/shard_map/all_to_all | solution.py:1123
  21.6 28.6 %copy-start.3 = (f32[16,1152]{1,0:T(8,128)}, f32[16,1152]{1,0:T(8,128)S(1)}, u32[]{:S(2)}) copy-start(f32[16,1152]{1,0:T(8,128)S(1)} %fusion.refs_5_.refs_6_) | copy-start | bytes 221188
  21.6 28.6 %copy-start.4 = (s32[1,1152]{1,0:T(1,128)}, s32[1,1152]{1,0:T(1,128)S(1)}, u32[]{:S(2)}) copy-start(s32[1,1152]{1,0:T(1,128)S(1)} %broadcast_in_dim.12.refs_4_.refs_8_) | copy-start | bytes 13828
  21.7 76.6 %copy-start.5 = (s32[1,768]{1,0:T(1,128)}, s32[1,768]{1,0:T(1,128)S(1)}, u32[]{:S(2)}) copy-start(s32[1,768]{1,0:T(1,128)S(1)} %fusion.29.refs_3_.refs_6_.refs_10_.refs_4_.refs_7_) | copy-start | bytes 9220
  37.2 13.0 %copy-start = (bf16[512,768]{1,0:T(8,128)(2,1)}, bf16[512,768]{1,0:T(8,128)(2,1)S(1)}, u32[]{:S(2)}) copy-start(bf16[512,768]{1,0:T(8,128)(2,1)S(1)} %all_gather.9.refs_0_.refs_2_) | copy-start | bytes 2359300
  37.2 8.0 %collective-permute-start.4 = (bf16[16,24,640]{2,1,0:T(8,128)(2,1)S(1)}, bf16[16,24,640]{2,1,0:T(8,128)(2,1)S(1)}, u32[]{:S(2)}, u32[]{:S(2)}) collective-permute-start(bf16[16,24,640]{2,1,0:T(8,128)(2,1)S(1)} %all-to-all-done.refs_1_), channel_id=1, source_target_pairs={{0,1},{1,0},{2,3},{3,2},{4,5},{5,4},{6,7},{7,6},{8,9},{9,8},{10,11... | collective-permute-start | bytes 1474568 | tf_op jit(solution)/shard_map/ppermute | solution.py:1111
  37.3 21.1 %collective-permute-start.5 = (bf16[128,768]{1,0:T(8,128)(2,1)}, bf16[128,768]{1,0:T(8,128)(2,1)S(1)}, u32[]{:S(2)}, u32[]{:S(2)}) collective-permute-start(bf16[128,768]{1,0:T(8,128)(2,1)} %bitcast.1), channel_id=1, source_target_pairs={{0,0},{1,1},{2,8},{3,9},{4,16},{5,17},{6,24},{7,25},{8,2},{9,3},{1... | collective-permute-start | bytes 589832 | tf_op jit(solution)/shard_map/ppermute | solution.py:1111
  38.9 19.5 %all-to-all-start.1 = ((bf16[4,32,768]{2,1,0:T(8,128)(2,1)}), bf16[4,32,768]{2,1,0:T(8,128)(2,1)S(1)}, u32[]{:S(2)}, u32[]{:S(2)}) async-start(bf16[4,32,768]{2,1,0:T(8,128)(2,1)} %get-tuple-element.106), calls=%async_computation.1 | async-start | bytes 393216 | tf_op jit(solution)/shard_map/all_to_all | solution.py:1120
  52.1 2.7 %copy-start.18 = (f32[8,768]{1,0:T(8,128)}, f32[8,768]{1,0:T(8,128)S(1)}, u32[]{:S(2)}) copy-start(f32[8,768]{1,0:T(8,128)S(1)} %get-tuple-element.121.refs_3_) | copy-start | bytes 73732
  52.1 12.8 %copy-start.1 = (bf16[2,4,128,192]{3,2,1,0:T(8,128)(2,1)}, bf16[2,4,128,192]{3,2,1,0:T(8,128)(2,1)S(1)}, u32[]{:S(2)}) copy-start(bf16[2,4,128,192]{3,2,1,0:T(8,128)(2,1)S(1)} %get-tuple-element.104.refs_1_.refs_3_) | copy-start | bytes 1179652
  58.3 11.5 %copy-start.23 = (bf16[4,32,768]{2,1,0:T(8,128)(2,1)}, bf16[4,32,768]{2,1,0:T(8,128)(2,1)S(1)}, u32[]{:S(2)}) copy-start(bf16[4,32,768]{2,1,0:T(8,128)(2,1)S(1)} %all-to-all-done.1.refs_3_) | copy-start | bytes 589828
  58.3 1.4 collective-permute-start.7
  58.3 17.6 %copy-start.6 = (bf16[128,768]{1,0:T(8,128)(2,1)}, bf16[128,768]{1,0:T(8,128)(2,1)S(1)}, u32[]{:S(2)}) copy-start(bf16[128,768]{1,0:T(8,128)(2,1)S(1)} %collective-permute-done.5.refs_4_.refs_5_) | copy-start | bytes 589828
  59.8 10.1 %copy-start.36 = (bf16[4,32,768]{2,1,0:T(8,128)(2,1)}, bf16[4,32,768]{2,1,0:T(8,128)(2,1)S(1)}, u32[]{:S(2)}) copy-start(bf16[4,32,768]{2,1,0:T(8,128)(2,1)S(1)} %collective-permute-done.7.refs_4_) | copy-start | bytes 589828
  59.8 23.1 %all-to-all-start.2 = ((bf16[16,24,768]{2,1,0:T(8,128)(2,1)}), bf16[16,24,768]{2,1,0:T(8,128)(2,1)S(1)}, u32[]{:S(2)}, u32[]{:S(2)}) async-start(bf16[16,24,768]{2,1,0:T(8,128)(2,1)} %get-tuple-element.118), calls=%async_computation.2 | async-start | bytes 1179648 | tf_op jit(solution)/shard_map/all_to_all | solution.py:1123
  64.9 5.0 %collective-permute-start.6 = (bf16[2,4,128,192]{3,2,1,0:T(8,128)(2,1)S(1)}, bf16[2,4,128,192]{3,2,1,0:T(8,128)(2,1)S(1)}, u32[]{:S(2)}, u32[]{:S(2)}) collective-permute-start(bf16[2,4,128,192]{3,2,1,0:T(8,128)(2,1)S(1)} %get-tuple-element.104.refs_1_.refs_3_), channel_id=1, source_target_pairs={{0,1},{1,0},{2,3},{3,2},{4,5},{5,4},{6,7},{7,6},{8,9},{9,8},{10,11... | collective-permute-start | bytes 1179656 | tf_op jit(solution)/shard_map/ppermute | solution.py:1111
  65.0 14.4 %collective-permute-start.13 = (bf16[128,768]{1,0:T(8,128)(2,1)S(1)}, bf16[128,768]{1,0:T(8,128)(2,1)S(1)}, u32[]{:S(2)}, u32[]{:S(2)}) collective-permute-start(bf16[128,768]{1,0:T(8,128)(2,1)S(1)} %collective-permute-done.5.refs_4_.refs_5_), channel_id=1, source_target_pairs={{0,8},{1,9},{2,10},{3,11},{4,12},{5,13},{6,14},{7,15},{8,16},{9,17... | collective-permute-start | bytes 589832 | tf_op jit(solution)/shard_map/ppermute | solution.py:1111
  66.9 15.4 %collective-permute-start.12 = (bf16[128,768]{1,0:T(8,128)(2,1)S(1)}, bf16[128,768]{1,0:T(8,128)(2,1)S(1)}, u32[]{:S(2)}, u32[]{:S(2)}) collective-permute-start(bf16[128,768]{1,0:T(8,128)(2,1)S(1)} %collective-permute-done.5.refs_4_.refs_5_), channel_id=1, source_target_pairs={{0,16},{1,17},{2,18},{3,19},{4,20},{5,21},{6,22},{7,23},{8,24},{9,... | collective-permute-start | bytes 589832 | tf_op jit(solution)/shard_map/ppermute | solution.py:1111
  68.4 14.2 %collective-permute-start.11 = (bf16[128,768]{1,0:T(8,128)(2,1)S(1)}, bf16[128,768]{1,0:T(8,128)(2,1)S(1)}, u32[]{:S(2)}, u32[]{:S(2)}) collective-permute-start(bf16[128,768]{1,0:T(8,128)(2,1)S(1)} %collective-permute-done.5.refs_4_.refs_5_), channel_id=1, source_target_pairs={{0,24},{1,25},{2,26},{3,27},{4,28},{5,29},{6,30},{7,31},{8,0},{9,1... | collective-permute-start | bytes 589832 | tf_op jit(solution)/shard_map/ppermute | solution.py:1111
  76.0 11.3 %copy-start.35 = (bf16[128,768]{1,0:T(8,128)(2,1)S(1)}, bf16[128,768]{1,0:T(8,128)(2,1)}, u32[]{:S(2)}) copy-start(bf16[128,768]{1,0:T(8,128)(2,1)} %get-tuple-element.112) | copy-start | bytes 589828
  76.0 12.7 %copy-start.34 = (bf16[128,768]{1,0:T(8,128)(2,1)S(1)}, bf16[128,768]{1,0:T(8,128)(2,1)}, u32[]{:S(2)}) copy-start(bf16[128,768]{1,0:T(8,128)(2,1)} %get-tuple-element.113) | copy-start | bytes 589828
  76.0 13.3 %copy-start.32 = (bf16[128,768]{1,0:T(8,128)(2,1)S(1)}, bf16[128,768]{1,0:T(8,128)(2,1)}, u32[]{:S(2)}) copy-start(bf16[128,768]{1,0:T(8,128)(2,1)} %get-tuple-element.114) | copy-start | bytes 589828
  76.0 22.3 %copy-start.13 = (bf16[128,768]{1,0:T(8,128)(2,1)S(1)}, bf16[128,768]{1,0:T(8,128)(2,1)}, u32[]{:S(2)}) copy-start(bf16[128,768]{1,0:T(8,128)(2,1)} %get-tuple-element.111.refs_0_) | copy-start | bytes 589828
  79.3 19.0 %copy-start.27 = (bf16[128,768]{1,0:T(8,128)(2,1)}, bf16[128,768]{1,0:T(8,128)(2,1)S(1)}, u32[]{:S(2)}) copy-start(bf16[128,768]{1,0:T(8,128)(2,1)S(1)} %collective-permute-done.13.refs_7_) | copy-start | bytes 589828
  82.3 16.0 %copy-start.28 = (bf16[128,768]{1,0:T(8,128)(2,1)}, bf16[128,768]{1,0:T(8,128)(2,1)S(1)}, u32[]{:S(2)}) copy-start(bf16[128,768]{1,0:T(8,128)(2,1)S(1)} %collective-permute-done.12.refs_6_) | copy-start | bytes 589828
  82.6 15.7 %copy-start.29 = (bf16[128,768]{1,0:T(8,128)(2,1)}, bf16[128,768]{1,0:T(8,128)(2,1)S(1)}, u32[]{:S(2)}) copy-start(bf16[128,768]{1,0:T(8,128)(2,1)S(1)} %collective-permute-done.11.refs_5_) | copy-start | bytes 589828
  82.9 18.3 %copy-start.20 = (bf16[16,24,768]{2,1,0:T(8,128)(2,1)}, bf16[16,24,768]{2,1,0:T(8,128)(2,1)S(1)}, u32[]{:S(2)}) copy-start(bf16[16,24,768]{2,1,0:T(8,128)(2,1)S(1)} %all-to-all-done.2.refs_1_) | copy-start | bytes 1769476
  82.9 20.2 %all-to-all-start.3 = ((bf16[4,96,768]{2,1,0:T(8,128)(2,1)}), bf16[4,96,768]{2,1,0:T(8,128)(2,1)S(1)}, u32[]{:S(2)}, u32[]{:S(2)}) async-start(bf16[4,96,768]{2,1,0:T(8,128)(2,1)} %get-tuple-element.123), calls=%async_computation.3 | async-start | bytes 1179648 | tf_op jit(solution)/shard_map/all_to_all | solution.py:1120
  87.2 8.7 %collective-permute-start.8 = (bf16[128,768]{1,0:T(8,128)(2,1)S(1)}, bf16[128,768]{1,0:T(8,128)(2,1)S(1)}, u32[]{:S(2)}, u32[]{:S(2)}) collective-permute-start(bf16[128,768]{1,0:T(8,128)(2,1)S(1)} %copy-done.35), channel_id=1, source_target_pairs={{0,8},{1,9},{2,10},{3,11},{4,12},{5,13},{6,14},{7,15},{8,16},{9,17... | collective-permute-start | bytes 589832 | tf_op jit(solution)/shard_map/ppermute | solution.py:1111
  88.7 9.6 %collective-permute-start.9 = (bf16[128,768]{1,0:T(8,128)(2,1)S(1)}, bf16[128,768]{1,0:T(8,128)(2,1)S(1)}, u32[]{:S(2)}, u32[]{:S(2)}) collective-permute-start(bf16[128,768]{1,0:T(8,128)(2,1)S(1)} %copy-done.34), channel_id=1, source_target_pairs={{0,16},{1,17},{2,18},{3,19},{4,20},{5,21},{6,22},{7,23},{8,24},{9,... | collective-permute-start | bytes 589832 | tf_op jit(solution)/shard_map/ppermute | solution.py:1111
  89.3 9.1 %collective-permute-start.10 = (bf16[128,768]{1,0:T(8,128)(2,1)S(1)}, bf16[128,768]{1,0:T(8,128)(2,1)S(1)}, u32[]{:S(2)}, u32[]{:S(2)}) collective-permute-start(bf16[128,768]{1,0:T(8,128)(2,1)S(1)} %copy-done.32), channel_id=1, source_target_pairs={{0,24},{1,25},{2,26},{3,27},{4,28},{5,29},{6,30},{7,31},{8,0},{9,1... | collective-permute-start | bytes 589832 | tf_op jit(solution)/shard_map/ppermute | solution.py:1111
  101.2 15.0 %collective-permute-start.14 = (bf16[16,24,768]{2,1,0:T(8,128)(2,1)S(1)}, bf16[16,24,768]{2,1,0:T(8,128)(2,1)S(1)}, u32[]{:S(2)}, u32[]{:S(2)}) collective-permute-start(bf16[16,24,768]{2,1,0:T(8,128)(2,1)S(1)} %all-to-all-done.2.refs_1_), channel_id=1, source_target_pairs={{0,1},{1,0},{2,3},{3,2},{4,5},{5,4},{6,7},{7,6},{8,9},{9,8},{10,11... | collective-permute-start | bytes 1769480 | tf_op jit(solution)/shard_map/ppermute | solution.py:1111
  103.1 14.1 %copy-start.21 = (bf16[4,96,768]{2,1,0:T(8,128)(2,1)}, bf16[4,96,768]{2,1,0:T(8,128)(2,1)S(1)}, u32[]{:S(2)}) copy-start(bf16[4,96,768]{2,1,0:T(8,128)(2,1)S(1)} %all-to-all-done.3.refs_8_) | copy-start | bytes 1769476
  103.1 13.2 %collective-permute-start.15 = (bf16[4,96,768]{2,1,0:T(8,128)(2,1)S(1)}, bf16[4,96,768]{2,1,0:T(8,128)(2,1)S(1)}, u32[]{:S(2)}, u32[]{:S(2)}) collective-permute-start(bf16[4,96,768]{2,1,0:T(8,128)(2,1)S(1)} %all-to-all-done.3.refs_8_), channel_id=1, source_target_pairs={{0,1},{1,0},{2,3},{3,2},{4,5},{5,4},{6,7},{7,6},{8,9},{9,8},{10,11... | collective-permute-start | bytes 1769480 | tf_op jit(solution)/shard_map/ppermute | solution.py:1111
  124.5 9.7 %collective-permute-start.16 = (bf16[128,768]{1,0:T(8,128)(2,1)}, bf16[128,768]{1,0:T(8,128)(2,1)S(1)}, u32[]{:S(2)}, u32[]{:S(2)}) collective-permute-start(bf16[128,768]{1,0:T(8,128)(2,1)} %get-tuple-element.127), channel_id=1, source_target_pairs={{0,8},{1,9},{2,10},{3,11},{4,12},{5,13},{6,14},{7,15},{8,16},{9,17... | collective-permute-start | bytes 589832 | tf_op jit(solution)/shard_map/ppermute | solution.py:1111
  125.6 10.1 %collective-permute-start.17 = (bf16[128,768]{1,0:T(8,128)(2,1)}, bf16[128,768]{1,0:T(8,128)(2,1)S(1)}, u32[]{:S(2)}, u32[]{:S(2)}) collective-permute-start(bf16[128,768]{1,0:T(8,128)(2,1)} %get-tuple-element.128), channel_id=1, source_target_pairs={{0,16},{1,17},{2,18},{3,19},{4,20},{5,21},{6,22},{7,23},{8,24},{9,... | collective-permute-start | bytes 589832 | tf_op jit(solution)/shard_map/ppermute | solution.py:1111
  126.6 9.1 %collective-permute-start.18 = (bf16[128,768]{1,0:T(8,128)(2,1)}, bf16[128,768]{1,0:T(8,128)(2,1)S(1)}, u32[]{:S(2)}, u32[]{:S(2)}) collective-permute-start(bf16[128,768]{1,0:T(8,128)(2,1)} %get-tuple-element.129), channel_id=1, source_target_pairs={{0,24},{1,25},{2,26},{3,27},{4,28},{5,29},{6,30},{7,31},{8,0},{9,1... | collective-permute-start | bytes 589832 | tf_op jit(solution)/shard_map/ppermute | solution.py:1111
  128.5 7.2 %copy-start.7 = (bf16[128,768]{1,0:T(8,128)(2,1)S(1)}, bf16[128,768]{1,0:T(8,128)(2,1)}, u32[]{:S(2)}) copy-start(bf16[128,768]{1,0:T(8,128)(2,1)} %copy-done.6) | copy-start | bytes 589828
  128.5 7.2 %copy-start.16 = (bf16[128,768]{1,0:T(8,128)(2,1)S(1)}, bf16[128,768]{1,0:T(8,128)(2,1)}, u32[]{:S(2)}) copy-start(bf16[128,768]{1,0:T(8,128)(2,1)} %get-tuple-element.126.refs_0_) | copy-start | bytes 589828
  134.1 4.4 %collective-permute-start.19 = (bf16[768,768]{1,0:T(8,128)(2,1)}, bf16[768,768]{1,0:T(8,128)(2,1)S(1)}, u32[]{:S(2)}, u32[]{:S(2)}) collective-permute-start(bf16[768,768]{1,0:T(8,128)(2,1)} %get-tuple-element.136), channel_id=1, source_target_pairs={{0,1},{1,0},{2,3},{3,2},{4,5},{5,4},{6,7},{7,6},{8,9},{9,8},{10,11... | collective-permute-start | bytes 3538952 | tf_op jit(solution)/shard_map/ppermute | solution.py:1111
  135.7 2.8 %copy-start.9 = (f32[768,768]{1,0:T(8,128)S(1)}, f32[768,768]{1,0:T(8,128)}, u32[]{:S(2)}) copy-start(f32[768,768]{1,0:T(8,128)} %get-tuple-element.137.refs_0_) | copy-start | bytes 7077892
  141.2 21.3 %all-to-all-start.4 = ((bf16[16,24,768]{2,1,0:T(8,128)(2,1)}), bf16[16,24,768]{2,1,0:T(8,128)(2,1)S(1)}, u32[]{:S(2)}, u32[]{:S(2)}) async-start(bf16[16,24,768]{2,1,0:T(8,128)(2,1)} %get-tuple-element.139), calls=%async_computation.4 | async-start | bytes 1179648 | tf_op jit(solution)/shard_map/all_to_all | solution.py:1123
  162.5 12.2 %copy-start.19 = (bf16[16,24,768]{2,1,0:T(8,128)(2,1)}, bf16[16,24,768]{2,1,0:T(8,128)(2,1)S(1)}, u32[]{:S(2)}) copy-start(bf16[16,24,768]{2,1,0:T(8,128)(2,1)S(1)} %all-to-all-done.4.refs_1_) | copy-start | bytes 1769476
  162.5 13.5 %all-to-all-start.5 = ((bf16[4,128,768]{2,1,0:T(8,128)(2,1)}), bf16[4,128,768]{2,1,0:T(8,128)(2,1)S(1)}, u32[]{:S(2)}, u32[]{:S(2)}) async-start(bf16[4,128,768]{2,1,0:T(8,128)(2,1)} %get-tuple-element.141), calls=%async_computation.5 | async-start | bytes 1572864 | tf_op jit(solution)/shard_map/all_to_all | solution.py:1311
  174.7 2.7 %collective-permute-start.21 = (bf16[2,4,128,192]{3,2,1,0:T(8,128)(2,1)}, bf16[2,4,128,192]{3,2,1,0:T(8,128)(2,1)S(1)}, u32[]{:S(2)}, u32[]{:S(2)}) collective-permute-start(bf16[2,4,128,192]{3,2,1,0:T(8,128)(2,1)} %get-tuple-element.146), channel_id=1, source_target_pairs={{0,1},{1,0},{2,3},{3,2},{4,5},{5,4},{6,7},{7,6},{8,9},{9,8},{10,11... | collective-permute-start | bytes 1179656 | tf_op jit(solution)/shard_map/ppermute | solution.py:1111
  174.7 2.6 %collective-permute-start.22 = (bf16[4,24,768]{2,1,0:T(8,128)(2,1)}, bf16[4,24,768]{2,1,0:T(8,128)(2,1)S(1)}, u32[]{:S(2)}, u32[]{:S(2)}) collective-permute-start(bf16[4,24,768]{2,1,0:T(8,128)(2,1)} %get-tuple-element.150), channel_id=1, source_target_pairs={{0,1},{1,0},{2,3},{3,2},{4,5},{5,4},{6,7},{7,6},{8,9},{9,8},{10,11... | collective-permute-start | bytes 442376 | tf_op jit(solution)/shard_map/ppermute | solution.py:1111
  176.7 29.1 %collective-permute-start.20 = (bf16[128,768]{1,0:T(8,128)(2,1)S(1)}, bf16[128,768]{1,0:T(8,128)(2,1)S(1)}, u32[]{:S(2)}, u32[]{:S(2)}) collective-permute-start(bf16[128,768]{1,0:T(8,128)(2,1)S(1)} %layer.1), channel_id=1, source_target_pairs={{0,0},{1,1},{2,8},{3,9},{4,16},{5,17},{6,24},{7,25},{8,2},{9,3},{1... | collective-permute-start | bytes 589832 | tf_op jit(solution)/shard_map/ppermute | solution.py:1111
  183.6 7.9 %copy-start.33 = (bf16[128,768]{1,0:T(8,128)(2,1)S(1)}, bf16[128,768]{1,0:T(8,128)(2,1)}, u32[]{:S(2)}) copy-start(bf16[128,768]{1,0:T(8,128)(2,1)} %get-tuple-element.153) | copy-start | bytes 589828
  183.6 9.0 %copy-start.31 = (bf16[128,768]{1,0:T(8,128)(2,1)S(1)}, bf16[128,768]{1,0:T(8,128)(2,1)}, u32[]{:S(2)}) copy-start(bf16[128,768]{1,0:T(8,128)(2,1)} %get-tuple-element.154) | copy-start | bytes 589828
  183.6 10.3 %copy-start.30 = (bf16[128,768]{1,0:T(8,128)(2,1)S(1)}, bf16[128,768]{1,0:T(8,128)(2,1)}, u32[]{:S(2)}) copy-start(bf16[128,768]{1,0:T(8,128)(2,1)} %get-tuple-element.155) | copy-start | bytes 589828
  183.6 28.9 %all-to-all-start.7 = ((bf16[4,128,768]{2,1,0:T(8,128)(2,1)}), bf16[4,128,768]{2,1,0:T(8,128)(2,1)}, u32[]{:S(2)}, u32[]{:S(2)}) async-start(bf16[4,128,768]{2,1,0:T(8,128)(2,1)} %get-tuple-element.167), calls=%async_computation.7 | async-start | bytes 1572864 | tf_op jit(solution)/shard_map/all_to_all | solution.py:1120
  191.5 10.7 %collective-permute-start.23 = (bf16[128,768]{1,0:T(8,128)(2,1)S(1)}, bf16[128,768]{1,0:T(8,128)(2,1)S(1)}, u32[]{:S(2)}, u32[]{:S(2)}) collective-permute-start(bf16[128,768]{1,0:T(8,128)(2,1)S(1)} %copy-done.33), channel_id=1, source_target_pairs={{0,8},{1,9},{2,10},{3,11},{4,12},{5,13},{6,14},{7,15},{8,16},{9,17... | collective-permute-start | bytes 589832 | tf_op jit(solution)/shard_map/ppermute | solution.py:1111
  192.6 10.1 %collective-permute-start.24 = (bf16[128,768]{1,0:T(8,128)(2,1)S(1)}, bf16[128,768]{1,0:T(8,128)(2,1)S(1)}, u32[]{:S(2)}, u32[]{:S(2)}) collective-permute-start(bf16[128,768]{1,0:T(8,128)(2,1)S(1)} %copy-done.31), channel_id=1, source_target_pairs={{0,16},{1,17},{2,18},{3,19},{4,20},{5,21},{6,22},{7,23},{8,24},{9,... | collective-permute-start | bytes 589832 | tf_op jit(solution)/shard_map/ppermute | solution.py:1111
  193.9 8.8 %collective-permute-start.25 = (bf16[128,768]{1,0:T(8,128)(2,1)S(1)}, bf16[128,768]{1,0:T(8,128)(2,1)S(1)}, u32[]{:S(2)}, u32[]{:S(2)}) collective-permute-start(bf16[128,768]{1,0:T(8,128)(2,1)S(1)} %copy-done.30), channel_id=1, source_target_pairs={{0,24},{1,25},{2,26},{3,27},{4,28},{5,29},{6,30},{7,31},{8,0},{9,1... | collective-permute-start | bytes 589832 | tf_op jit(solution)/shard_map/ppermute | solution.py:1111
  195.8 6.9 %copy-start.15 = (bf16[128,768]{1,0:T(8,128)(2,1)S(1)}, bf16[128,768]{1,0:T(8,128)(2,1)}, u32[]{:S(2)}) copy-start(bf16[128,768]{1,0:T(8,128)(2,1)} %get-tuple-element.152.refs_0_) | copy-start | bytes 589828
  202.1 3.7 %collective-permute-start.27 = (bf16[384,640]{1,0:T(8,128)(2,1)}, bf16[384,640]{1,0:T(8,128)(2,1)S(1)}, u32[]{:S(2)}, u32[]{:S(2)}) collective-permute-start(bf16[384,640]{1,0:T(8,128)(2,1)} %get-tuple-element.163), channel_id=1, source_target_pairs={{0,1},{1,0},{2,3},{3,2},{4,5},{5,4},{6,7},{7,6},{8,9},{9,8},{10,11... | collective-permute-start | bytes 1474568 | tf_op jit(solution)/shard_map/ppermute | solution.py:1111
  202.7 3.1 %copy-start.8 = (f32[384,640]{1,0:T(8,128)S(1)}, f32[384,640]{1,0:T(8,128)}, u32[]{:S(2)}) copy-start(f32[384,640]{1,0:T(8,128)} %get-tuple-element.164.refs_0_) | copy-start | bytes 2949124
  205.1 29.0 %collective-permute-start.26 = (bf16[128,768]{1,0:T(8,128)(2,1)S(1)}, bf16[128,768]{1,0:T(8,128)(2,1)S(1)}, u32[]{:S(2)}, u32[]{:S(2)}) collective-permute-start(bf16[128,768]{1,0:T(8,128)(2,1)S(1)} %last.1), channel_id=1, source_target_pairs={{0,0},{1,1},{2,8},{3,9},{4,16},{5,17},{6,24},{7,25},{8,2},{9,3},{1... | collective-permute-start | bytes 589832 | tf_op jit(solution)/shard_map/ppermute | solution.py:1111
  212.6 19.5 %all-to-all-start.6 = ((bf16[16,24,640]{2,1,0:T(8,128)(2,1)}), bf16[16,24,640]{2,1,0:T(8,128)(2,1)S(1)}, u32[]{:S(2)}, u32[]{:S(2)}) async-start(bf16[16,24,640]{2,1,0:T(8,128)(2,1)} %add_early.1), calls=%async_computation.6 | async-start | bytes 983040 | tf_op jit(solution)/shard_map/all_to_all | solution.py:1123
  216.2 15.8 %copy-start.10 = (s32[4]{0:T(128)S(1)}, s32[4]{0:T(128)}, u32[]{:S(2)}) copy-start(s32[4]{0:T(128)} %get-tuple-element.107.refs_0_) | copy-start | bytes 52
  (10 other events, 11.4 us)
